TPU v7x, 32 devices: a whole 2x2x4 slice. The times are simulated.
32 devices in a mesh: gx: 4 (over y, core), gy: 8 (over z, x).
Axes of the slice: x: 2, y: 2, z: 4, core: 2. Of those that a mesh axis runs over, the one named last changes fastest.
Arguments:
- leaf_values: float32 [4096, 64], P(('gx', 'gy')), may hold values from -6 to 6
- leaf_inverse: bfloat16 [32, 128, 128], P(('gx', 'gy'))
- leaf_coupling: bfloat16 [32, 5, 256, 128], P(('gx', 'gy')), may hold values from -0.5 to 0.5
- block_values: float32 [32, 5, 256, 64], P(('gx', 'gy')), may hold values from -6 to 6
- block_inverse: bfloat16 [32, 5, 256, 256], P(('gx', 'gy'))
- block_coupling: bfloat16 [32, 4, 1, 2, 256, 256], P(('gx', 'gy')), may hold values from -0.375 to 0.375
Outputs:
- leaf_solution: float32 [4096, 64], P(('gx', 'gy'))
- block_solution: float32 [32, 5, 256, 64], P(('gx', 'gy'))
All inputs are finite; a program needn't handle non-finite values.
Results may differ from a plain program's by a relative error of at most 0.025.
Values may be sent and summed in bfloat16 or wider, within the bound.
No kernel may reach another device: no remote copies, remote signals or barrier semaphores. Data moves between devices by JAX's collectives and lax.ppermute only.
A program may use at most 64 MiB of HBM per device.

v0:
```python
import jax
import jax.numpy as jnp
from jax import lax
from jax.sharding import PartitionSpec as P


def from_partner(value, axis, bit):
    mask = 2**bit
    pairs = [(source, source ^ mask) for source in range(lax.axis_size(axis))]
    return lax.ppermute(value, axis, pairs)


def forward_mirror(values, level, gy_levels):
    if level < gy_levels:
        return from_partner(values, "gy", level)
    return from_partner(values, "gx", level - gy_levels)


def backward_mirror(values, level, gy_levels):
    if level < gy_levels:
        return from_partner(values, "gy", level)
    return from_partner(values, "gx", level - gy_levels)


def apply_block(matrix, values):
    return jnp.dot(matrix, values.astype(jnp.bfloat16), preferred_element_type=jnp.float32)


def apply_transpose(matrix, values):
    return lax.dot_general(
        matrix,
        values.astype(jnp.bfloat16),
        (((0,), (0,)), ((), ())),
        preferred_element_type=jnp.float32,
    )


def shards(leaf_values, leaf_inverse, leaf_coupling, block_values, block_inverse, block_coupling):
    levels = block_inverse.shape[1]
    band = block_coupling.shape[2]
    gy_levels = lax.axis_size("gy").bit_length() - 1
    leaf_forward = apply_block(leaf_inverse[0], leaf_values)
    leaf_terms = jnp.einsum(
        "kwn,nr->kwr",
        leaf_coupling[0],
        leaf_forward.astype(jnp.bfloat16),
        preferred_element_type=jnp.float32,
    )
    outgoing = [leaf_terms[level] for level in range(levels)]
    retained = [jnp.zeros_like(leaf_terms[0]) for level in range(levels)]
    forward = []
    received_top = None
    for level in range(levels):
        partial_value = block_values[0, level] - retained[level]
        if level == levels - 1:
            mine = outgoing[level]
            other_send, other_partial = from_partner((mine, partial_value), "gx", level - gy_levels)
            other_matrix = from_partner(block_inverse[0, level], "gx", level - gy_levels)
            solved = apply_block(block_inverse[0, level], partial_value - other_send)
            other_solved = apply_block(other_matrix, other_partial - mine)
            received_top = apply_transpose(other_matrix, other_solved).astype(jnp.bfloat16)
        else:
            incoming = forward_mirror(outgoing[level], level, gy_levels)
            solved = apply_block(block_inverse[0, level], partial_value - incoming)
        forward.append(solved)
        offset = 0
        upper = level + 1 + offset
        if upper < levels:
            term = jnp.einsum(
                "swv,vr->swr",
                block_coupling[0, level, offset],
                solved.astype(jnp.bfloat16),
                preferred_element_type=jnp.float32,
            )
            retained[upper] = term[0]
            outgoing[upper] = outgoing[upper] + term[1]
    backward = [None] * levels
    mirrored = [None] * levels
    for level in reversed(range(levels)):
        base = forward[level]
        offset = 0
        upper = level + 1 + offset
        if upper < levels:
            stacked = jnp.stack([backward[upper].astype(jnp.bfloat16), mirrored[upper]])
            base = base - lax.dot_general(
                block_coupling[0, level, offset],
                stacked,
                (((0, 1), (0, 1)), ((), ())),
                preferred_element_type=jnp.float32,
            )
        backward[level] = apply_transpose(block_inverse[0, level], base)
        if level == levels - 1:
            mirrored[level] = received_top
        else:
            mirrored[level] = backward_mirror(
                backward[level].astype(jnp.bfloat16), level, gy_levels
            )
    stacked_all = jnp.stack(mirrored)
    gathered = jnp.einsum(
        "kwn,kwr->nr", leaf_coupling[0], stacked_all, preferred_element_type=jnp.float32
    )
    leaf_solution = apply_transpose(leaf_inverse[0], leaf_forward - gathered)
    return (leaf_solution, jnp.stack(backward)[None])


def solution(mesh):
    return jax.shard_map(
        shards,
        mesh=mesh,
        in_specs=(
            P(("gx", "gy"), None),
            P(("gx", "gy"), None, None),
            P(("gx", "gy"), None, None, None),
            P(("gx", "gy"), None, None, None),
            P(("gx", "gy"), None, None, None),
            P(("gx", "gy"), None, None, None, None, None),
        ),
        out_specs=(P(("gx", "gy"), None), P(("gx", "gy"), None, None, None)),
        check_vma=False,
    )
```

profile of v0, /device:TPU:0, one launch (start us, length us, event | category | flops | bytes accessed | tf_op | source)
XLA Modules:
  0.0 46.4 jit_solution(6094539365161988901)
XLA Ops:
  0.7 1.0 %fusion.112 = f32[128,64]{0,1:T(8,128)S(1)} fusion(bf16[1,128,128]{2,1,0:T(8,128)(2,1)} %param.7, f32[128,64]{0,1:T(8,128)} %param.6), kind=kOutput, calls=%fused_computation.125 | convolution fusion | flops 2105344 | bytes 98304 | tf_op jit(solution)/shard_map/dot_general | solution.py:26
  1.7 0.3 convolution_bitcast_fusion
  1.9 3.0 %collective-permute-start = (f32[256,64]{0,1:T(8,128)S(1)}, f32[256,64]{0,1:T(8,128)S(1)}, u32[]{:S(2)}, u32[]{:S(2)}) collective-permute-start(f32[256,64]{0,1:T(8,128)S(1)} %slice_bitcast_fusion.5), channel_id=1, source_target_pairs={{0,1},{1,0},{2,3},{3,2},{4,5},{5,4},{6,7},{7,6},{8,9},{9,8},{10,11... | collective-permute-start | bytes 196616 | tf_op jit(solution)/shard_map/ppermute | solution.py:10
  4.9 2.2 %collective-permute-done = f32[256,64]{0,1:T(8,128)S(1)} collective-permute-done((f32[256,64]{0,1:T(8,128)S(1)}, f32[256,64]{0,1:T(8,128)S(1)}, u32[]{:S(2)}, u32[]{:S(2)}) %collective-permute-start) | collective-permute-done | bytes 65568 | tf_op jit(solution)/shard_map/ppermute | solution.py:10
  7.2 1.1 %fusion.53 = f32[64,256]{1,0:T(8,128)S(1)} fusion(bf16[1,5,256,256]{3,2,1,0:T(8,128)(2,1)} %param.10, f32[256,64]{0,1:T(8,128)S(1)} %collective-permute-done, f32[1,5,256,64]{2,3,1,0:T(8,128)} %param.9), kind=kOutput, calls=%fused_computation.58 | convolution fusion | flops 8421376 | bytes 327680 | tf_op jit(solution)/shard_map/dot_general | solution.py:26
  8.3 0.2 convolution_bitcast_fusion.4
  8.5 2.2 %collective-permute-start.1 = (f32[256,64]{0,1:T(8,128)S(1)}, f32[256,64]{0,1:T(8,128)S(1)}, u32[]{:S(2)}, u32[]{:S(2)}) collective-permute-start(f32[256,64]{0,1:T(8,128)S(1)} %fusion.73), channel_id=1, source_target_pairs={{0,2},{1,3},{2,0},{3,1},{4,6},{5,7},{6,4},{7,5},{8,10},{9,11},{10,... | collective-permute-start | bytes 196616 | tf_op jit(solution)/shard_map/ppermute | solution.py:10
  10.7 2.2 %collective-permute-done.1 = f32[256,64]{0,1:T(8,128)S(1)} collective-permute-done((f32[256,64]{0,1:T(8,128)S(1)}, f32[256,64]{0,1:T(8,128)S(1)}, u32[]{:S(2)}, u32[]{:S(2)}) %collective-permute-start.1) | collective-permute-done | bytes 65568 | tf_op jit(solution)/shard_map/ppermute | solution.py:10
  13.0 1.0 %fusion.50 = f32[64,256]{1,0:T(8,128)S(1)} fusion(bf16[1,5,256,256]{3,2,1,0:T(8,128)(2,1)S(1)} %copy-done.2, f32[256,64]{0,1:T(8,128)S(1)} %collective-permute-done.1, f32[2,256,64]{1,2,0:T(8,128)S(1)} %convolution_bitcast_fusion.4, f32[1,5,256,64]{2,3,1,0:T(8,128)} %param.9), kind=kOutput, calls=%fused_computation.55 | convolution fusion | flops 8437760 | bytes 393216 | tf_op jit(solution)/shard_map/dot_general | solution.py:26
  14.2 3.1 %collective-permute-start.2 = (f32[256,64]{0,1:T(8,128)S(1)}, f32[256,64]{0,1:T(8,128)S(1)}, u32[]{:S(2)}, u32[]{:S(2)}) collective-permute-start(f32[256,64]{0,1:T(8,128)S(1)} %fusion.69), channel_id=1, source_target_pairs={{0,4},{1,5},{2,6},{3,7},{4,0},{5,1},{6,2},{7,3},{8,12},{9,13},{10,... | collective-permute-start | bytes 196616 | tf_op jit(solution)/shard_map/ppermute | solution.py:10
  17.3 2.2 %collective-permute-done.2 = f32[256,64]{0,1:T(8,128)S(1)} collective-permute-done((f32[256,64]{0,1:T(8,128)S(1)}, f32[256,64]{0,1:T(8,128)S(1)}, u32[]{:S(2)}, u32[]{:S(2)}) %collective-permute-start.2) | collective-permute-done | bytes 65568 | tf_op jit(solution)/shard_map/ppermute | solution.py:10
  20.1 1.9 %collective-permute-start.6 = (bf16[256,256]{1,0:T(8,128)(2,1)S(1)}, bf16[256,256]{1,0:T(8,128)(2,1)S(1)}, u32[]{:S(2)}, u32[]{:S(2)}) collective-permute-start(bf16[256,256]{1,0:T(8,128)(2,1)S(1)} %slice_bitcast_fusion), channel_id=1, source_target_pairs={{0,16},{8,24},{16,0},{24,8},{1,17},{9,25},{17,1},{25,9},{2,18},{10... | collective-permute-start | bytes 393224 | tf_op jit(solution)/shard_map/ppermute | solution.py:10
  22.1 0.2 convolution_bitcast_fusion.1
  22.4 1.2 %collective-permute-start.4 = (f32[256,64]{0,1:T(8,128)S(1)}, f32[256,64]{0,1:T(8,128)S(1)}, u32[]{:S(2)}, u32[]{:S(2)}) collective-permute-start(f32[256,64]{0,1:T(8,128)S(1)} %fusion.63), channel_id=1, source_target_pairs={{0,16},{8,24},{16,0},{24,8},{1,17},{9,25},{17,1},{25,9},{2,18},{10... | collective-permute-start | bytes 196616 | tf_op jit(solution)/shard_map/ppermute | solution.py:10
  23.6 0.9 %collective-permute-start.5 = (f32[256,64]{0,1:T(8,128)S(1)}, f32[256,64]{0,1:T(8,128)S(1)}, u32[]{:S(2)}, u32[]{:S(2)}) collective-permute-start(f32[256,64]{0,1:T(8,128)S(1)} %fusion.64), channel_id=1, source_target_pairs={{0,16},{8,24},{16,0},{24,8},{1,17},{9,25},{17,1},{25,9},{2,18},{10... | collective-permute-start | bytes 196616 | tf_op jit(solution)/shard_map/ppermute | solution.py:10
  24.6 3.3 %collective-permute-done.4 = f32[256,64]{0,1:T(8,128)S(1)} collective-permute-done((f32[256,64]{0,1:T(8,128)S(1)}, f32[256,64]{0,1:T(8,128)S(1)}, u32[]{:S(2)}, u32[]{:S(2)}) %collective-permute-start.4) | collective-permute-done | bytes 65568 | tf_op jit(solution)/shard_map/ppermute | solution.py:10
  27.8 0.3 fusion.8
  28.2 0.8 %collective-permute-done.5 = f32[256,64]{0,1:T(8,128)S(1)} collective-permute-done((f32[256,64]{0,1:T(8,128)S(1)}, f32[256,64]{0,1:T(8,128)S(1)}, u32[]{:S(2)}, u32[]{:S(2)}) %collective-permute-start.5) | collective-permute-done | bytes 65568 | tf_op jit(solution)/shard_map/ppermute | solution.py:10
  29.0 0.3 fusion.9
  29.3 0.3 bitcast_convert_fusion.3
  29.7 1.2 %collective-permute-done.7 = bf16[256,64]{0,1:T(8,128)(2,1)S(1)} collective-permute-done((bf16[256,64]{0,1:T(8,128)(2,1)S(1)}, bf16[256,64]{0,1:T(8,128)(2,1)S(1)}, u32[]{:S(2)}, u32[]{:S(2)}) %collective-permute-start.7) | collective-permute-done | bytes 32800 | tf_op jit(solution)/shard_map/ppermute | solution.py:10
  30.9 0.3 bitcast_convert_fusion.2
  31.2 2.9 %collective-permute-start.8 = (bf16[256,64]{0,1:T(8,128)(2,1)S(1)}, bf16[256,64]{0,1:T(8,128)(2,1)S(1)}, u32[]{:S(2)}, u32[]{:S(2)}) collective-permute-start(bf16[256,64]{0,1:T(8,128)(2,1)S(1)} %get-tuple-element.4), channel_id=1, source_target_pairs={{0,4},{1,5},{2,6},{3,7},{4,0},{5,1},{6,2},{7,3},{8,12},{9,13},{10,... | collective-permute-start | bytes 98312 | tf_op jit(solution)/shard_map/ppermute | solution.py:10
  34.1 1.9 %collective-permute-done.8 = bf16[256,64]{0,1:T(8,128)(2,1)S(1)} collective-permute-done((bf16[256,64]{0,1:T(8,128)(2,1)S(1)}, bf16[256,64]{0,1:T(8,128)(2,1)S(1)}, u32[]{:S(2)}, u32[]{:S(2)}) %collective-permute-start.8) | collective-permute-done | bytes 32800 | tf_op jit(solution)/shard_map/ppermute | solution.py:10
  36.1 0.3 bitcast_convert_fusion.1
  36.4 2.1 %collective-permute-start.9 = (bf16[256,64]{0,1:T(8,128)(2,1)S(1)}, bf16[256,64]{0,1:T(8,128)(2,1)S(1)}, u32[]{:S(2)}, u32[]{:S(2)}) collective-permute-start(bf16[256,64]{0,1:T(8,128)(2,1)S(1)} %get-tuple-element.6), channel_id=1, source_target_pairs={{0,2},{1,3},{2,0},{3,1},{4,6},{5,7},{6,4},{7,5},{8,10},{9,11},{10,... | collective-permute-start | bytes 98312 | tf_op jit(solution)/shard_map/ppermute | solution.py:10
  38.5 1.9 %collective-permute-done.9 = bf16[256,64]{0,1:T(8,128)(2,1)S(1)} collective-permute-done((bf16[256,64]{0,1:T(8,128)(2,1)S(1)}, bf16[256,64]{0,1:T(8,128)(2,1)S(1)}, u32[]{:S(2)}, u32[]{:S(2)}) %collective-permute-start.9) | collective-permute-done | bytes 32800 | tf_op jit(solution)/shard_map/ppermute | solution.py:10
  40.4 0.3 bitcast_convert_fusion
  40.7 1.7 %collective-permute-start.10 = (bf16[256,64]{0,1:T(8,128)(2,1)S(1)}, bf16[256,64]{0,1:T(8,128)(2,1)S(1)}, u32[]{:S(2)}, u32[]{:S(2)}) collective-permute-start(bf16[256,64]{0,1:T(8,128)(2,1)S(1)} %get-tuple-element.8), channel_id=1, source_target_pairs={{0,1},{1,0},{2,3},{3,2},{4,5},{5,4},{6,7},{7,6},{8,9},{9,8},{10,11... | collective-permute-start | bytes 98312 | tf_op jit(solution)/shard_map/ppermute | solution.py:10
  42.5 2.2 %collective-permute-done.10 = bf16[256,64]{0,1:T(8,128)(2,1)S(1)} collective-permute-done((bf16[256,64]{0,1:T(8,128)(2,1)S(1)}, bf16[256,64]{0,1:T(8,128)(2,1)S(1)}, u32[]{:S(2)}, u32[]{:S(2)}) %collective-permute-start.10) | collective-permute-done | bytes 32800 | tf_op jit(solution)/shard_map/ppermute | solution.py:10
  44.7 0.7 %copy-done.4 = bf16[1,128,128]{2,1,0:T(8,128)(2,1)S(1)} copy-done((bf16[1,128,128]{2,1,0:T(8,128)(2,1)S(1)}, bf16[1,128,128]{2,1,0:T(8,128)(2,1)}, u32[]{:S(2)}) %copy-start.4) | copy-done | bytes 32792
  45.5 0.9 %convolution_bitcast_fusion.9 = f32[128,64]{0,1:T(8,128)} fusion(f32[128,64]{0,1:T(8,128)S(1)} %fusion.112, bf16[5,256,64]{1,2,0:T(8,128)(2,1)S(1)} %constant_dynamic-update-slice_fusion, bf16[1,5,256,128]{3,2,1,0:T(8,128)(2,1)S(1)} %copy-done, bf16[1,128,128]{2,1,0:T(8,128)(2,1)S(1)} %copy-done.4), kind=kOutput, calls=%fused_computation.22 | convolution fusion | flops 23085056 | bytes 589824 | tf_op jit(solution)/shard_map/dot_general | solution.py:30
  (37 shorter events, 1.1 us)
Async XLA Ops:
  0.6 1.0 %copy-start = (bf16[1,5,256,128]{3,2,1,0:T(8,128)(2,1)S(1)}, bf16[1,5,256,128]{3,2,1,0:T(8,128)(2,1)}, u32[]{:S(2)}) copy-start(bf16[1,5,256,128]{3,2,1,0:T(8,128)(2,1)} %param.8) | copy-start | bytes 983044
  0.6 7.6 %copy-start.1 = (bf16[1,4,1,2,256,256]{5,4,3,2,1,0:T(8,128)(2,1)S(1)}, bf16[1,4,1,2,256,256]{5,4,3,2,1,0:T(8,128)(2,1)}, u32[]{:S(2)}) copy-start(bf16[1,4,1,2,256,256]{5,4,3,2,1,0:T(8,128)(2,1)} %param.11) | copy-start | bytes 3145732
  1.9 11.0 %copy-start.2 = (bf16[1,5,256,256]{3,2,1,0:T(8,128)(2,1)S(1)}, bf16[1,5,256,256]{3,2,1,0:T(8,128)(2,1)}, u32[]{:S(2)}) copy-start(bf16[1,5,256,256]{3,2,1,0:T(8,128)(2,1)} %param.10) | copy-start | bytes 1966084
  1.9 5.2 %collective-permute-start = (f32[256,64]{0,1:T(8,128)S(1)}, f32[256,64]{0,1:T(8,128)S(1)}, u32[]{:S(2)}, u32[]{:S(2)}) collective-permute-start(f32[256,64]{0,1:T(8,128)S(1)} %slice_bitcast_fusion.5), channel_id=1, source_target_pairs={{0,1},{1,0},{2,3},{3,2},{4,5},{5,4},{6,7},{7,6},{8,9},{9,8},{10,11... | collective-permute-start | bytes 196616 | tf_op jit(solution)/shard_map/ppermute | solution.py:10
  8.5 4.4 %collective-permute-start.1 = (f32[256,64]{0,1:T(8,128)S(1)}, f32[256,64]{0,1:T(8,128)S(1)}, u32[]{:S(2)}, u32[]{:S(2)}) collective-permute-start(f32[256,64]{0,1:T(8,128)S(1)} %fusion.73), channel_id=1, source_target_pairs={{0,2},{1,3},{2,0},{3,1},{4,6},{5,7},{6,4},{7,5},{8,10},{9,11},{10,... | collective-permute-start | bytes 196616 | tf_op jit(solution)/shard_map/ppermute | solution.py:10
  14.0 5.6 %copy-start.3 = (f32[1,5,256,64]{2,3,1,0:T(8,128)S(1)}, f32[1,5,256,64]{2,3,1,0:T(8,128)}, u32[]{:S(2)}) copy-start(f32[1,5,256,64]{2,3,1,0:T(8,128)} %param.9) | copy-start | bytes 983044
  14.2 5.3 %collective-permute-start.2 = (f32[256,64]{0,1:T(8,128)S(1)}, f32[256,64]{0,1:T(8,128)S(1)}, u32[]{:S(2)}, u32[]{:S(2)}) collective-permute-start(f32[256,64]{0,1:T(8,128)S(1)} %fusion.69), channel_id=1, source_target_pairs={{0,4},{1,5},{2,6},{3,7},{4,0},{5,1},{6,2},{7,3},{8,12},{9,13},{10,... | collective-permute-start | bytes 196616 | tf_op jit(solution)/shard_map/ppermute | solution.py:10
  20.0 2.0 %collective-permute-start.3 = (f32[256,64]{0,1:T(8,128)S(1)}, f32[256,64]{0,1:T(8,128)S(1)}, u32[]{:S(2)}, u32[]{:S(2)}) collective-permute-start(f32[256,64]{0,1:T(8,128)S(1)} %fusion.65), channel_id=1, source_target_pairs={{0,8},{8,0},{16,24},{24,16},{1,9},{9,1},{17,25},{25,17},{2,10},{10... | collective-permute-start | bytes 196616 | tf_op jit(solution)/shard_map/ppermute | solution.py:10
  20.1 8.1 %collective-permute-start.6 = (bf16[256,256]{1,0:T(8,128)(2,1)S(1)}, bf16[256,256]{1,0:T(8,128)(2,1)S(1)}, u32[]{:S(2)}, u32[]{:S(2)}) collective-permute-start(bf16[256,256]{1,0:T(8,128)(2,1)S(1)} %slice_bitcast_fusion), channel_id=1, source_target_pairs={{0,16},{8,24},{16,0},{24,8},{1,17},{9,25},{17,1},{25,9},{2,18},{10... | collective-permute-start | bytes 393224 | tf_op jit(solution)/shard_map/ppermute | solution.py:10
  22.4 5.4 %collective-permute-start.4 = (f32[256,64]{0,1:T(8,128)S(1)}, f32[256,64]{0,1:T(8,128)S(1)}, u32[]{:S(2)}, u32[]{:S(2)}) collective-permute-start(f32[256,64]{0,1:T(8,128)S(1)} %fusion.63), channel_id=1, source_target_pairs={{0,16},{8,24},{16,0},{24,8},{1,17},{9,25},{17,1},{25,9},{2,18},{10... | collective-permute-start | bytes 196616 | tf_op jit(solution)/shard_map/ppermute | solution.py:10
  23.6 5.3 %collective-permute-start.5 = (f32[256,64]{0,1:T(8,128)S(1)}, f32[256,64]{0,1:T(8,128)S(1)}, u32[]{:S(2)}, u32[]{:S(2)}) collective-permute-start(f32[256,64]{0,1:T(8,128)S(1)} %fusion.64), channel_id=1, source_target_pairs={{0,16},{8,24},{16,0},{24,8},{1,17},{9,25},{17,1},{25,9},{2,18},{10... | collective-permute-start | bytes 196616 | tf_op jit(solution)/shard_map/ppermute | solution.py:10
  29.6 1.3 %collective-permute-start.7 = (bf16[256,64]{0,1:T(8,128)(2,1)S(1)}, bf16[256,64]{0,1:T(8,128)(2,1)S(1)}, u32[]{:S(2)}, u32[]{:S(2)}) collective-permute-start(bf16[256,64]{0,1:T(8,128)(2,1)S(1)} %get-tuple-element.2), channel_id=1, source_target_pairs={{0,8},{8,0},{16,24},{24,16},{1,9},{9,1},{17,25},{25,17},{2,10},{10... | collective-permute-start | bytes 98312 | tf_op jit(solution)/shard_map/ppermute | solution.py:10
  31.2 4.9 %collective-permute-start.8 = (bf16[256,64]{0,1:T(8,128)(2,1)S(1)}, bf16[256,64]{0,1:T(8,128)(2,1)S(1)}, u32[]{:S(2)}, u32[]{:S(2)}) collective-permute-start(bf16[256,64]{0,1:T(8,128)(2,1)S(1)} %get-tuple-element.4), channel_id=1, source_target_pairs={{0,4},{1,5},{2,6},{3,7},{4,0},{5,1},{6,2},{7,3},{8,12},{9,13},{10,... | collective-permute-start | bytes 98312 | tf_op jit(solution)/shard_map/ppermute | solution.py:10
  36.4 4.0 %collective-permute-start.9 = (bf16[256,64]{0,1:T(8,128)(2,1)S(1)}, bf16[256,64]{0,1:T(8,128)(2,1)S(1)}, u32[]{:S(2)}, u32[]{:S(2)}) collective-permute-start(bf16[256,64]{0,1:T(8,128)(2,1)S(1)} %get-tuple-element.6), channel_id=1, source_target_pairs={{0,2},{1,3},{2,0},{3,1},{4,6},{5,7},{6,4},{7,5},{8,10},{9,11},{10,... | collective-permute-start | bytes 98312 | tf_op jit(solution)/shard_map/ppermute | solution.py:10
  40.7 4.0 %collective-permute-start.10 = (bf16[256,64]{0,1:T(8,128)(2,1)S(1)}, bf16[256,64]{0,1:T(8,128)(2,1)S(1)}, u32[]{:S(2)}, u32[]{:S(2)}) collective-permute-start(bf16[256,64]{0,1:T(8,128)(2,1)S(1)} %get-tuple-element.8), channel_id=1, source_target_pairs={{0,1},{1,0},{2,3},{3,2},{4,5},{5,4},{6,7},{7,6},{8,9},{9,8},{10,11... | collective-permute-start | bytes 98312 | tf_op jit(solution)/shard_map/ppermute | solution.py:10
  42.5 3.9 %copy-start.5 = (f32[5,256,64]{1,2,0:T(8,128)}, f32[5,256,64]{1,2,0:T(8,128)S(1)}, u32[]{:S(2)}) copy-start(f32[5,256,64]{1,2,0:T(8,128)S(1)} %bitcast_dynamic-update-slice_fusion) | copy-start | bytes 983044
  44.7 0.8 %copy-start.4 = (bf16[1,128,128]{2,1,0:T(8,128)(2,1)S(1)}, bf16[1,128,128]{2,1,0:T(8,128)(2,1)}, u32[]{:S(2)}) copy-start(bf16[1,128,128]{2,1,0:T(8,128)(2,1)} %param.7) | copy-start | bytes 98308
where the time goes:
time: 46.7 us; the launch traced here: 46.4 us
  starting transfers between devices  19.3 us (41%)
  waiting for transfers between devices  18 us (39%)
  matrix products  7.39 us (16%)
  between operations  0.85 us (2%)
  local copies, waits for them, and re-layouts  0.84 us (2%)
    ppermute x11, starting transfers between devices, from_partner(): return lax.ppermute(value, axis, pairs)  19.3 us
    ppermute x11, waiting for transfers between devices, from_partner(): return lax.ppermute(value, axis, pairs)  18 us
    dot_general x5, matrix products, apply_block(): jnp.dot(matrix, values.astype(jnp.bfloat16), preferred_element_type=jnp.f...  3.41 us
    dot_general x7, matrix products, apply_transpose(): lax.dot_general(matrix, values.astype(jnp.bfloat16), (((0,), (0,)), ((),...  2.8 us
  transfers between devices with their start and end apart: 11, of which 9 were waited for; matrix products, arithmetic and copies ran while one was open for 2% of the time, Pallas kernels for 0%

commit v1 on v0

v1 whole, which is shorter than its diff:
```python
import jax
import jax.numpy as jnp
from jax import lax
from jax.experimental import pallas as pl
from jax.experimental.pallas import tpu as pltpu
from jax.sharding import PartitionSpec as P

BF = jnp.bfloat16
F32 = jnp.float32
VMEM = pl.BlockSpec(memory_space=pltpu.VMEM)


def times(values, matrix):
    return lax.dot_general(values, matrix, (((1,), (0,)), ((), ())), preferred_element_type=F32)


def times_t(values, matrix):
    return lax.dot_general(values, matrix, (((1,), (1,)), ((), ())), preferred_element_type=F32)


def gram(left, right):
    return lax.dot_general(left, right, (((0,), (0,)), ((), ())), preferred_element_type=F32)


def from_partner(value, level, gy_levels):
    axis, bit = ("gy", level) if level < gy_levels else ("gx", level - gy_levels)
    mask = 2**bit
    pairs = [(source, source ^ mask) for source in range(lax.axis_size(axis))]
    return lax.ppermute(value, axis, pairs)


def call(body, outs, *args, flops=0):
    moved = sum(a.size * a.dtype.itemsize for a in args)
    return pl.pallas_call(
        body,
        out_shape=[jax.ShapeDtypeStruct(shape, kind) for shape, kind in outs],
        in_specs=[VMEM] * len(args),
        out_specs=[VMEM] * len(outs),
        compiler_params=pltpu.CompilerParams(vmem_limit_bytes=32 * 2**20),
        cost_estimate=pl.CostEstimate(flops=flops, bytes_accessed=moved, transcendentals=0),
    )(*args)


def head(values, inverse, coupling, leaf, out):
    solved = times_t(values[...].astype(BF), inverse[...])
    leaf[...] = solved
    out[...] = times_t(solved.astype(BF), coupling[0]).astype(BF)


def leaf_terms(leaf, coupling, out):
    solved = leaf[...].astype(BF)
    for level in range(1, coupling.shape[0]):
        out[level - 1] = times_t(solved, coupling[level])


def products(inverse, coupling, out, *, level):
    for side in range(2):
        out[side] = times(coupling[level, side], inverse[level]).astype(BF)


def top_gram(inverse, out):
    matrix = inverse[inverse.shape[0] - 1]
    out[...] = gram(matrix, matrix).astype(BF)


def top_products(own, mirror, product, out):
    out[0] = times(own[...], product[0]).astype(BF)
    out[1] = times(mirror[...], product[1]).astype(BF)


def leaf_products(inverse, coupling, out):
    for level in range(coupling.shape[0]):
        out[level] = times(coupling[level], inverse[...]).astype(BF)


def forward(residue, received, product, terms, delta, out, *, level):
    change = (residue[...] - received[...].astype(F32)).astype(BF)
    delta[...] = change
    out[...] = (terms[level] + times_t(change, product[1])).astype(BF)


def forward_side(delta, product, inverse, values, residue, solved, *, level):
    residue[...] = values[level + 1] - times_t(delta[...], product[0])
    step = times_t(delta[...], inverse[level]).astype(BF)
    solved[...] = times(step, inverse[level])


def forward_top(residue, received, product, terms, values, delta, out, *, level):
    change = (residue[...] - received[...].astype(F32)).astype(BF)
    delta[...] = change
    rows = change.shape[0]
    out[:rows] = (terms[level] + times_t(change, product[1])).astype(BF)
    out[rows:] = (values[level + 1] - times_t(change, product[0])).astype(BF)


def solve(delta, inverse, solved, *, level):
    step = times_t(delta[...], inverse[level]).astype(BF)
    solved[...] = times(step, inverse[level])


def top(mine, received, product, solved, out, out_bf, delta):
    rows = solved.shape[0]
    own = (mine[rows:].astype(F32) - received[:rows].astype(F32)).astype(BF)
    other = (received[rows:].astype(F32) - mine[:rows].astype(F32)).astype(BF)
    value = solved[...] - times(own, product[0]) - times(other, product[1])
    out[...] = value
    out_bf[...] = value.astype(BF)
    delta[0] = own
    delta[1] = other


def top_values(delta, own, mirror, out, mirrored):
    out[...] = times(delta[0], own[...])
    mirrored[...] = times(delta[1], mirror[...]).astype(BF)


def back_own(solved, upper, product, out):
    out[...] = solved[...] - times(upper[...], product[0])


def back(own, received, product, out, out_bf):
    value = own[...] - times(received[...], product[1])
    out[...] = value
    out_bf[...] = value.astype(BF)


def leaf_own(leaf, inverse, products_, *refs):
    *mirrored, out = refs
    total = times(leaf[...].astype(BF), inverse[...])
    for level, block in enumerate(mirrored):
        total = total - times(block[...], products_[level + 1])
    out[...] = total


def leaf_last(own, received, products_, out):
    out[...] = own[...] - times(received[...], products_[0])


def gather_blocks(*refs):
    *blocks, out = refs
    for level, block in enumerate(blocks):
        out[level] = block[...]


def shards(leaf_values, leaf_inverse, leaf_coupling, block_values, block_inverse, block_coupling):
    levels, width = block_inverse.shape[1], block_inverse.shape[2]
    size, cols = leaf_values.shape
    gy_levels = lax.axis_size("gy").bit_length() - 1
    inverse, coupling = block_inverse[0], block_coupling[0, :, 0]
    leaf_inv, leaf_cpl = leaf_inverse[0], leaf_coupling[0]
    values = jnp.swapaxes(block_values[0], 1, 2)
    vec, vec_bf, pair = ((cols, width), F32), ((cols, width), BF), ((2, width, width), BF)

    def swap(value, level):
        return from_partner(value, level, gy_levels)

    leaf, out = call(head, [((cols, size), F32), vec_bf], leaf_values.T, leaf_inv, leaf_cpl)
    received = swap(out, 0)
    (terms,) = call(leaf_terms, [((levels - 1, cols, width), F32)], leaf, leaf_cpl)
    product, delta, solved = [], [], []
    residue = values[0]
    own_gram = mirror_gram = None
    for level in range(levels - 1):
        (made,) = call(
            lambda *refs, level=level: products(*refs, level=level), [pair], inverse, coupling
        )
        product.append(made)
        if level == 0:
            (own_gram,) = call(top_gram, [((width, width), BF)], inverse)
        if level < levels - 2:
            change, out = call(
                lambda *refs, level=level: forward(*refs, level=level),
                [vec_bf, vec_bf], residue, received, made, terms,
            )
            received = swap(out, level + 1)
            residue, ahead = call(
                lambda *refs, level=level: forward_side(*refs, level=level),
                [vec, vec], change, made, inverse, values,
            )
            if level == min(1, levels - 3):
                mirror_gram = swap(own_gram, levels - 1)
        else:
            change, out = call(
                lambda *refs, level=level: forward_top(*refs, level=level),
                [vec_bf, ((2 * cols, width), BF)], residue, received, made, terms, values,
            )
            received = swap(out, levels - 1)
            (ahead,) = call(
                lambda *refs, level=level: solve(*refs, level=level), [vec], change, inverse
            )
        delta.append(change)
        solved.append(ahead)
    (top_pair,) = call(top_products, [pair], own_gram, mirror_gram, product[-1])
    (leaf_prod,) = call(leaf_products, [((levels, width, size), BF)], leaf_inv, leaf_cpl)

    blocks, mirrored = [None] * levels, [None] * levels
    block, block_bf, deltas = call(
        top, [vec, vec_bf, ((2, cols, width), BF)], out, received, top_pair, solved[-1]
    )
    blocks[levels - 2] = block
    mirrored[levels - 2] = swap(block_bf, levels - 2)
    blocks[-1], mirrored[-1] = call(top_values, [vec, vec_bf], deltas, own_gram, mirror_gram)
    for level in reversed(range(levels - 2)):
        (own,) = call(back_own, [vec], solved[level], block_bf, product[level])
        block, block_bf = call(back, [vec, vec_bf], own, mirrored[level + 1], product[level])
        blocks[level] = block
        mirrored[level] = swap(block_bf, level)
    (own,) = call(leaf_own, [((cols, size), F32)], leaf, leaf_inv, leaf_prod, *mirrored[1:])
    (stacked,) = call(gather_blocks, [((levels, cols, width), F32)], *blocks)
    (leaf_solution,) = call(leaf_last, [((cols, size), F32)], own, mirrored[0], leaf_prod)
    return leaf_solution.T, jnp.swapaxes(stacked, 1, 2)[None]


def solution(mesh):
    both = ("gx", "gy")
    return jax.shard_map(
        shards,
        mesh=mesh,
        in_specs=tuple(P(both, *[None] * rank) for rank in (1, 2, 3, 3, 3, 5)),
        out_specs=(P(both, None), P(both, None, None, None)),
        check_vma=False,
    )
```

time: 46.7 us -> 40.5 us (0.87)
  matrix products: 7.39 us -> 0 us
  Pallas kernels: 0 us -> 6.86 us
  waiting for transfers between devices: 18 us -> 12.6 us
  starting transfers between devices: 19.3 us -> 15.1 us
  local copies, waits for them, and re-layouts: 0.84 us -> 4.78 us
    dot_general x17 -> x0, matrix products: 7.39 us -> none  [the longest x5 3.41 us: apply_block(): jnp.dot(matrix, values.astype(jnp.bfloat16), preferred_element_type=jnp.f...]
    pallas_call x0 -> x28, Pallas kernels: none -> 6.86 us  [call(): pl.pallas_call(body, out_shape=[jax.ShapeDtypeStruct(shape, kind) for sha...]
    ppermute x11 -> x10, waiting for transfers between devices: 18 us -> 12.6 us  [from_partner(): return lax.ppermute(value, axis, pairs)]
    ppermute x11 -> x10, starting transfers between devices: 19.3 us -> 15.1 us  [from_partner(): return lax.ppermute(value, axis, pairs)]
    unnamed x20, local copies, waits for them, and re-layouts: 0.81 us -> 4.77 us
  transfers between devices with their start and end apart: 11 -> 10, of which waited for: 9 -> 7; matrix products, arithmetic and copies ran while one was open for 2% -> 0% of each run, Pallas kernels for 0% -> 12%
where the time goes in v1:
time: 40.5 us; the launch traced here: 40.2 us
  starting transfers between devices  15.1 us (37%)
  waiting for transfers between devices  12.6 us (31%)
  Pallas kernels  6.86 us (17%)
  local copies, waits for them, and re-layouts  4.78 us (12%)
  between operations  0.85 us (2%)
    ppermute x10, starting transfers between devices, from_partner(): return lax.ppermute(value, axis, pairs)  15.1 us
    ppermute x10, waiting for transfers between devices, from_partner(): return lax.ppermute(value, axis, pairs)  12.6 us
    pallas_call x28, Pallas kernels, call(): pl.pallas_call(body, out_shape=[jax.ShapeDtypeStruct(shape, kind) for sha...  6.86 us
    unnamed x20, local copies, waits for them, and re-layouts  4.77 us
  transfers between devices with their start and end apart: 10, of which 7 were waited for; matrix products, arithmetic and copies ran while one was open for 0% of the time, Pallas kernels for 12%

profile of v1, /device:TPU:0, one launch (start us, length us, event | category | flops | bytes accessed | tf_op | source)
XLA Modules:
  0.0 40.2 jit_solution(3738883402877946802)
XLA Ops:
  0.7 1.0 %copy-done.4 = bf16[1,5,256,128]{3,2,1,0:T(8,128)(2,1)S(1)} copy-done((bf16[1,5,256,128]{3,2,1,0:T(8,128)(2,1)S(1)}, bf16[1,5,256,128]{3,2,1,0:T(8,128)(2,1)}, u32[]{:S(2)}) %copy-start.4) | copy-done | bytes 327704
  1.7 0.8 %copy-done.7 = bf16[1,128,128]{2,1,0:T(8,128)(2,1)S(1)} copy-done((bf16[1,128,128]{2,1,0:T(8,128)(2,1)S(1)}, bf16[1,128,128]{2,1,0:T(8,128)(2,1)}, u32[]{:S(2)}) %copy-start.7) | copy-done | bytes 32792
  2.5 0.8 %copy-done.9 = f32[128,64]{0,1:T(8,128)S(1)} copy-done((f32[128,64]{0,1:T(8,128)S(1)}, f32[128,64]{0,1:T(8,128)}, u32[]{:S(2)}) %copy-start.9) | copy-done | bytes 32792
  3.2 0.3 shard_map.77
  3.5 3.0 %collective-permute-start = (bf16[64,256]{1,0:T(8,128)(2,1)S(1)}, bf16[64,256]{1,0:T(8,128)(2,1)S(1)}, u32[]{:S(2)}, u32[]{:S(2)}) collective-permute-start(bf16[64,256]{1,0:T(8,128)(2,1)S(1)} %get-tuple-element.30), channel_id=1, source_target_pairs={{0,1},{1,0},{2,3},{3,2},{4,5},{5,4},{6,7},{7,6},{8,9},{9,8},{10,11... | collective-permute-start | bytes 98312 | tf_op jit(solution)/shard_map/ppermute | solution.py:29
  6.5 1.0 %copy-done.5 = bf16[1,5,256,128]{3,2,1,0:T(8,128)(2,1)S(1)} copy-done((bf16[1,5,256,128]{3,2,1,0:T(8,128)(2,1)S(1)}, bf16[1,5,256,128]{3,2,1,0:T(8,128)(2,1)}, u32[]{:S(2)}) %copy-start.5) | copy-done | bytes 327704
  7.7 1.2 %copy-done.1 = bf16[1,4,1,2,256,256]{5,4,3,2,1,0:T(8,128)(2,1)S(1)} copy-done((bf16[1,4,1,2,256,256]{5,4,3,2,1,0:T(8,128)(2,1)S(1)}, bf16[1,4,1,2,256,256]{5,4,3,2,1,0:T(8,128)(2,1)}, u32[]{:S(2)}) %copy-start.1) | copy-done | bytes 1048600
  9.3 1.6 %collective-permute-start.1 = (bf16[64,256]{1,0:T(8,128)(2,1)S(1)}, bf16[64,256]{1,0:T(8,128)(2,1)S(1)}, u32[]{:S(2)}, u32[]{:S(2)}) collective-permute-start(bf16[64,256]{1,0:T(8,128)(2,1)S(1)} %get-tuple-element.33), channel_id=1, source_target_pairs={{0,2},{1,3},{2,0},{3,1},{4,6},{5,7},{6,4},{7,5},{8,10},{9,11},{10,... | collective-permute-start | bytes 98312 | tf_op jit(solution)/shard_map/ppermute | solution.py:29
  11.0 0.2 shard_map.83.refs_2_.refs_1_.product
  11.2 0.3 shard_map.82
  11.5 1.8 %collective-permute-done.1.refs_1_ = bf16[64,256]{1,0:T(8,128)(2,1)S(1)} collective-permute-done((bf16[64,256]{1,0:T(8,128)(2,1)S(1)}, bf16[64,256]{1,0:T(8,128)(2,1)S(1)}, u32[]{:S(2)}, u32[]{:S(2)}) %collective-permute-start.1) | collective-permute-done | bytes 32800 | tf_op jit(solution)/shard_map/ppermute | solution.py:29
  13.4 2.6 %collective-permute-start.2 = (bf16[64,256]{1,0:T(8,128)(2,1)S(1)}, bf16[64,256]{1,0:T(8,128)(2,1)S(1)}, u32[]{:S(2)}, u32[]{:S(2)}) collective-permute-start(bf16[64,256]{1,0:T(8,128)(2,1)S(1)} %get-tuple-element.37), channel_id=1, source_target_pairs={{0,4},{1,5},{2,6},{3,7},{4,0},{5,1},{6,2},{7,3},{8,12},{9,13},{10,... | collective-permute-start | bytes 98312 | tf_op jit(solution)/shard_map/ppermute | solution.py:29
  16.1 0.2 shard_map.91.own
  16.3 1.6 %collective-permute-start.5 = (bf16[256,256]{1,0:T(8,128)(2,1)S(1)}, bf16[256,256]{1,0:T(8,128)(2,1)S(1)}, u32[]{:S(2)}, u32[]{:S(2)}) collective-permute-start(bf16[256,256]{1,0:T(8,128)(2,1)S(1)} %shard_map.91.own), channel_id=1, source_target_pairs={{0,16},{8,24},{16,0},{24,8},{1,17},{9,25},{17,1},{25,9},{2,18},{10... | collective-permute-start | bytes 393224 | tf_op jit(solution)/shard_map/ppermute | solution.py:29
  17.9 0.2 shard_map.86.refs_2_.refs_1_.product
  18.1 0.3 shard_map.85
  18.9 0.3 shard_map.88
  19.2 0.7 %collective-permute-done.3.refs_1_ = bf16[64,256]{1,0:T(8,128)(2,1)S(1)} collective-permute-done((bf16[64,256]{1,0:T(8,128)(2,1)S(1)}, bf16[64,256]{1,0:T(8,128)(2,1)S(1)}, u32[]{:S(2)}, u32[]{:S(2)}) %collective-permute-start.3) | collective-permute-done | bytes 32800 | tf_op jit(solution)/shard_map/ppermute | solution.py:29
  20.0 1.4 %collective-permute-start.4 = (bf16[128,256]{1,0:T(8,128)(2,1)S(1)}, bf16[128,256]{1,0:T(8,128)(2,1)S(1)}, u32[]{:S(2)}, u32[]{:S(2)}) collective-permute-start(bf16[128,256]{1,0:T(8,128)(2,1)S(1)} %get-tuple-element.42.mine), channel_id=1, source_target_pairs={{0,16},{8,24},{16,0},{24,8},{1,17},{9,25},{17,1},{25,9},{2,18},{10... | collective-permute-start | bytes 196616 | tf_op jit(solution)/shard_map/ppermute | solution.py:29
  21.5 0.3 shard_map.93.solved
  21.8 0.2 shard_map.92.product
  22.0 2.3 %collective-permute-done.4.received = bf16[128,256]{1,0:T(8,128)(2,1)S(1)} collective-permute-done((bf16[128,256]{1,0:T(8,128)(2,1)S(1)}, bf16[128,256]{1,0:T(8,128)(2,1)S(1)}, u32[]{:S(2)}, u32[]{:S(2)}) %collective-permute-start.4) | collective-permute-done | bytes 65568 | tf_op jit(solution)/shard_map/ppermute | solution.py:29
  24.8 1.1 %collective-permute-done.6.received.refs_2_ = bf16[64,256]{1,0:T(8,128)(2,1)S(1)} collective-permute-done((bf16[64,256]{1,0:T(8,128)(2,1)S(1)}, bf16[64,256]{1,0:T(8,128)(2,1)S(1)}, u32[]{:S(2)}, u32[]{:S(2)}) %collective-permute-start.6) | collective-permute-done | bytes 32800 | tf_op jit(solution)/shard_map/ppermute | solution.py:29
  26.0 2.5 %collective-permute-start.7 = (bf16[64,256]{1,0:T(8,128)(2,1)S(1)}, bf16[64,256]{1,0:T(8,128)(2,1)S(1)}, u32[]{:S(2)}, u32[]{:S(2)}) collective-permute-start(bf16[64,256]{1,0:T(8,128)(2,1)S(1)} %get-tuple-element.45.upper), channel_id=1, source_target_pairs={{0,4},{1,5},{2,6},{3,7},{4,0},{5,1},{6,2},{7,3},{8,12},{9,13},{10,... | collective-permute-start | bytes 98312 | tf_op jit(solution)/shard_map/ppermute | solution.py:29
  28.6 2.6 %collective-permute-done.7.received.refs_1_ = bf16[64,256]{1,0:T(8,128)(2,1)S(1)} collective-permute-done((bf16[64,256]{1,0:T(8,128)(2,1)S(1)}, bf16[64,256]{1,0:T(8,128)(2,1)S(1)}, u32[]{:S(2)}, u32[]{:S(2)}) %collective-permute-start.7) | collective-permute-done | bytes 32800 | tf_op jit(solution)/shard_map/ppermute | solution.py:29
  31.3 1.3 %collective-permute-start.8 = (bf16[64,256]{1,0:T(8,128)(2,1)S(1)}, bf16[64,256]{1,0:T(8,128)(2,1)S(1)}, u32[]{:S(2)}, u32[]{:S(2)}) collective-permute-start(bf16[64,256]{1,0:T(8,128)(2,1)S(1)} %get-tuple-element.46.upper), channel_id=1, source_target_pairs={{0,2},{1,3},{2,0},{3,1},{4,6},{5,7},{6,4},{7,5},{8,10},{9,11},{10,... | collective-permute-start | bytes 98312 | tf_op jit(solution)/shard_map/ppermute | solution.py:29
  32.8 2.5 %collective-permute-done.8.refs_0_.received = bf16[64,256]{1,0:T(8,128)(2,1)S(1)} collective-permute-done((bf16[64,256]{1,0:T(8,128)(2,1)S(1)}, bf16[64,256]{1,0:T(8,128)(2,1)S(1)}, u32[]{:S(2)}, u32[]{:S(2)}) %collective-permute-start.8) | collective-permute-done | bytes 32800 | tf_op jit(solution)/shard_map/ppermute | solution.py:29
  35.5 1.0 %collective-permute-start.9 = (bf16[64,256]{1,0:T(8,128)(2,1)S(1)}, bf16[64,256]{1,0:T(8,128)(2,1)S(1)}, u32[]{:S(2)}, u32[]{:S(2)}) collective-permute-start(bf16[64,256]{1,0:T(8,128)(2,1)S(1)} %get-tuple-element.50), channel_id=1, source_target_pairs={{0,1},{1,0},{2,3},{3,2},{4,5},{5,4},{6,7},{7,6},{8,9},{9,8},{10,11... | collective-permute-start | bytes 98312 | tf_op jit(solution)/shard_map/ppermute | solution.py:29
  36.5 0.2 shard_map.78.products_
  36.9 0.8 %shard_map.104 = f32[5,64,256]{2,1,0:T(8,128)} custom-call(f32[64,256]{1,0:T(8,128)S(1)} %get-tuple-element.51.refs_0_, f32[64,256]{1,0:T(8,128)S(1)} %get-tuple-element.52.refs_1_, f32[64,256]{1,0:T(8,128)S(1)} %get-tuple-element.53.refs_2_, f32[64,256]{1,0:T(8,128)S(1)} %get-tuple-element.54.refs_3_, f32[64,256]{1,0:T(8,128)S(1)} %get-tuple-element.55.refs_4_), custom_call_target="tpu_custom_call" | custom-call | bytes 327680 | tf_op jit(solution)/shard_map/pallas_call | solution.py:34
  37.8 1.7 %collective-permute-done.9.received = bf16[64,256]{1,0:T(8,128)(2,1)S(1)} collective-permute-done((bf16[64,256]{1,0:T(8,128)(2,1)S(1)}, bf16[64,256]{1,0:T(8,128)(2,1)S(1)}, u32[]{:S(2)}, u32[]{:S(2)}) %collective-permute-start.9) | collective-permute-done | bytes 32800 | tf_op jit(solution)/shard_map/ppermute | solution.py:29
  39.5 0.8 %shard_map.103 = f32[64,128]{1,0:T(8,128)} custom-call(f32[64,128]{1,0:T(8,128)S(1)} %shard_map.100.own, bf16[64,256]{1,0:T(8,128)(2,1)S(1)} %collective-permute-done.9.received, bf16[5,256,128]{2,1,0:T(8,128)(2,1)S(1)} %shard_map.78.products_), custom_call_target="tpu_custom_call" | custom-call | bytes 393216 | tf_op jit(solution)/shard_map/pallas_call | solution.py:34
  (37 shorter events, 2.8 us)
Async XLA Ops:
  0.6 5.9 %copy-start.3 = (f32[1,5,256,64]{2,3,1,0:T(8,128)S(1)}, f32[1,5,256,64]{2,3,1,0:T(8,128)}, u32[]{:S(2)}) copy-start(f32[1,5,256,64]{2,3,1,0:T(8,128)} %param.9) | copy-start | bytes 983044
  0.6 7.1 %copy-start = (bf16[1,5,256,256]{3,2,1,0:T(8,128)(2,1)S(1)}, bf16[1,5,256,256]{3,2,1,0:T(8,128)(2,1)}, u32[]{:S(2)}) copy-start(bf16[1,5,256,256]{3,2,1,0:T(8,128)(2,1)} %param.10) | copy-start | bytes 1966084
  0.6 1.1 %copy-start.4 = (bf16[1,5,256,128]{3,2,1,0:T(8,128)(2,1)S(1)}, bf16[1,5,256,128]{3,2,1,0:T(8,128)(2,1)}, u32[]{:S(2)}) copy-start(bf16[1,5,256,128]{3,2,1,0:T(8,128)(2,1)} %param.8) | copy-start | bytes 983044
  1.7 0.8 %copy-start.7 = (bf16[1,128,128]{2,1,0:T(8,128)(2,1)S(1)}, bf16[1,128,128]{2,1,0:T(8,128)(2,1)}, u32[]{:S(2)}) copy-start(bf16[1,128,128]{2,1,0:T(8,128)(2,1)} %param.7) | copy-start | bytes 98308
  2.5 0.8 %copy-start.9 = (f32[128,64]{0,1:T(8,128)S(1)}, f32[128,64]{0,1:T(8,128)}, u32[]{:S(2)}) copy-start(f32[128,64]{0,1:T(8,128)} %param.6) | copy-start | bytes 98308
  3.5 5.7 %collective-permute-start = (bf16[64,256]{1,0:T(8,128)(2,1)S(1)}, bf16[64,256]{1,0:T(8,128)(2,1)S(1)}, u32[]{:S(2)}, u32[]{:S(2)}) collective-permute-start(bf16[64,256]{1,0:T(8,128)(2,1)S(1)} %get-tuple-element.30), channel_id=1, source_target_pairs={{0,1},{1,0},{2,3},{3,2},{4,5},{5,4},{6,7},{7,6},{8,9},{9,8},{10,11... | collective-permute-start | bytes 98312 | tf_op jit(solution)/shard_map/ppermute | solution.py:29
  6.5 1.0 %copy-start.5 = (bf16[1,5,256,128]{3,2,1,0:T(8,128)(2,1)S(1)}, bf16[1,5,256,128]{3,2,1,0:T(8,128)(2,1)}, u32[]{:S(2)}) copy-start(bf16[1,5,256,128]{3,2,1,0:T(8,128)(2,1)} %param.8) | copy-start | bytes 983044
  7.7 1.2 %copy-start.1 = (bf16[1,4,1,2,256,256]{5,4,3,2,1,0:T(8,128)(2,1)S(1)}, bf16[1,4,1,2,256,256]{5,4,3,2,1,0:T(8,128)(2,1)}, u32[]{:S(2)}) copy-start(bf16[1,4,1,2,256,256]{5,4,3,2,1,0:T(8,128)(2,1)} %param.11) | copy-start | bytes 3145732
  8.9 2.0 %copy-start.2 = (bf16[1,4,1,2,256,256]{5,4,3,2,1,0:T(8,128)(2,1)S(1)}, bf16[1,4,1,2,256,256]{5,4,3,2,1,0:T(8,128)(2,1)}, u32[]{:S(2)}) copy-start(bf16[1,4,1,2,256,256]{5,4,3,2,1,0:T(8,128)(2,1)} %param.11) | copy-start | bytes 3145732
  9.3 4.0 %collective-permute-start.1 = (bf16[64,256]{1,0:T(8,128)(2,1)S(1)}, bf16[64,256]{1,0:T(8,128)(2,1)S(1)}, u32[]{:S(2)}, u32[]{:S(2)}) collective-permute-start(bf16[64,256]{1,0:T(8,128)(2,1)S(1)} %get-tuple-element.33), channel_id=1, source_target_pairs={{0,2},{1,3},{2,0},{3,1},{4,6},{5,7},{6,4},{7,5},{8,10},{9,11},{10,... | collective-permute-start | bytes 98312 | tf_op jit(solution)/shard_map/ppermute | solution.py:29
  13.4 5.0 %collective-permute-start.2 = (bf16[64,256]{1,0:T(8,128)(2,1)S(1)}, bf16[64,256]{1,0:T(8,128)(2,1)S(1)}, u32[]{:S(2)}, u32[]{:S(2)}) collective-permute-start(bf16[64,256]{1,0:T(8,128)(2,1)S(1)} %get-tuple-element.37), channel_id=1, source_target_pairs={{0,4},{1,5},{2,6},{3,7},{4,0},{5,1},{6,2},{7,3},{8,12},{9,13},{10,... | collective-permute-start | bytes 98312 | tf_op jit(solution)/shard_map/ppermute | solution.py:29
  16.3 5.5 %collective-permute-start.5 = (bf16[256,256]{1,0:T(8,128)(2,1)S(1)}, bf16[256,256]{1,0:T(8,128)(2,1)S(1)}, u32[]{:S(2)}, u32[]{:S(2)}) collective-permute-start(bf16[256,256]{1,0:T(8,128)(2,1)S(1)} %shard_map.91.own), channel_id=1, source_target_pairs={{0,16},{8,24},{16,0},{24,8},{1,17},{9,25},{17,1},{25,9},{2,18},{10... | collective-permute-start | bytes 393224 | tf_op jit(solution)/shard_map/ppermute | solution.py:29
  18.6 1.2 %collective-permute-start.3 = (bf16[64,256]{1,0:T(8,128)(2,1)S(1)}, bf16[64,256]{1,0:T(8,128)(2,1)S(1)}, u32[]{:S(2)}, u32[]{:S(2)}) collective-permute-start(bf16[64,256]{1,0:T(8,128)(2,1)S(1)} %get-tuple-element.41), channel_id=1, source_target_pairs={{0,8},{8,0},{16,24},{24,16},{1,9},{9,1},{17,25},{25,17},{2,10},{10... | collective-permute-start | bytes 98312 | tf_op jit(solution)/shard_map/ppermute | solution.py:29
  20.0 4.3 %collective-permute-start.4 = (bf16[128,256]{1,0:T(8,128)(2,1)S(1)}, bf16[128,256]{1,0:T(8,128)(2,1)S(1)}, u32[]{:S(2)}, u32[]{:S(2)}) collective-permute-start(bf16[128,256]{1,0:T(8,128)(2,1)S(1)} %get-tuple-element.42.mine), channel_id=1, source_target_pairs={{0,16},{8,24},{16,0},{24,8},{1,17},{9,25},{17,1},{25,9},{2,18},{10... | collective-permute-start | bytes 196616 | tf_op jit(solution)/shard_map/ppermute | solution.py:29
  24.5 1.3 %collective-permute-start.6 = (bf16[64,256]{1,0:T(8,128)(2,1)S(1)}, bf16[64,256]{1,0:T(8,128)(2,1)S(1)}, u32[]{:S(2)}, u32[]{:S(2)}) collective-permute-start(bf16[64,256]{1,0:T(8,128)(2,1)S(1)} %get-tuple-element.44.upper), channel_id=1, source_target_pairs={{0,8},{8,0},{16,24},{24,16},{1,9},{9,1},{17,25},{25,17},{2,10},{10... | collective-permute-start | bytes 98312 | tf_op jit(solution)/shard_map/ppermute | solution.py:29
  26.0 5.2 %collective-permute-start.7 = (bf16[64,256]{1,0:T(8,128)(2,1)S(1)}, bf16[64,256]{1,0:T(8,128)(2,1)S(1)}, u32[]{:S(2)}, u32[]{:S(2)}) collective-permute-start(bf16[64,256]{1,0:T(8,128)(2,1)S(1)} %get-tuple-element.45.upper), channel_id=1, source_target_pairs={{0,4},{1,5},{2,6},{3,7},{4,0},{5,1},{6,2},{7,3},{8,12},{9,13},{10,... | collective-permute-start | bytes 98312 | tf_op jit(solution)/shard_map/ppermute | solution.py:29
  31.3 4.0 %collective-permute-start.8 = (bf16[64,256]{1,0:T(8,128)(2,1)S(1)}, bf16[64,256]{1,0:T(8,128)(2,1)S(1)}, u32[]{:S(2)}, u32[]{:S(2)}) collective-permute-start(bf16[64,256]{1,0:T(8,128)(2,1)S(1)} %get-tuple-element.46.upper), channel_id=1, source_target_pairs={{0,2},{1,3},{2,0},{3,1},{4,6},{5,7},{6,4},{7,5},{8,10},{9,11},{10,... | collective-permute-start | bytes 98312 | tf_op jit(solution)/shard_map/ppermute | solution.py:29
  32.6 3.8 %copy-start.6 = (bf16[1,5,256,128]{3,2,1,0:T(8,128)(2,1)S(1)}, bf16[1,5,256,128]{3,2,1,0:T(8,128)(2,1)}, u32[]{:S(2)}) copy-start(bf16[1,5,256,128]{3,2,1,0:T(8,128)(2,1)} %param.8) | copy-start | bytes 983044
  32.8 3.7 %copy-start.8 = (bf16[1,128,128]{2,1,0:T(8,128)(2,1)S(1)}, bf16[1,128,128]{2,1,0:T(8,128)(2,1)}, u32[]{:S(2)}) copy-start(bf16[1,128,128]{2,1,0:T(8,128)(2,1)} %param.7) | copy-start | bytes 98308
  35.5 4.0 %collective-permute-start.9 = (bf16[64,256]{1,0:T(8,128)(2,1)S(1)}, bf16[64,256]{1,0:T(8,128)(2,1)S(1)}, u32[]{:S(2)}, u32[]{:S(2)}) collective-permute-start(bf16[64,256]{1,0:T(8,128)(2,1)S(1)} %get-tuple-element.50), channel_id=1, source_target_pairs={{0,1},{1,0},{2,3},{3,2},{4,5},{5,4},{6,7},{7,6},{8,9},{9,8},{10,11... | collective-permute-start | bytes 98312 | tf_op jit(solution)/shard_map/ppermute | solution.py:29

commit v2 on v1

--- a/solution.py
+++ b/solution.py
@@ -29,7 +29,7 @@
     return lax.ppermute(value, axis, pairs)
 
 
-def call(body, outs, *args, flops=0):
+def call(body, outs, *args, flops=3 * 10**8):
     moved = sum(a.size * a.dtype.itemsize for a in args)
     return pl.pallas_call(
         body,
@@ -41,18 +41,6 @@
     )(*args)
 
 
-def head(values, inverse, coupling, leaf, out):
-    solved = times_t(values[...].astype(BF), inverse[...])
-    leaf[...] = solved
-    out[...] = times_t(solved.astype(BF), coupling[0]).astype(BF)
-
-
-def leaf_terms(leaf, coupling, out):
-    solved = leaf[...].astype(BF)
-    for level in range(1, coupling.shape[0]):
-        out[level - 1] = times_t(solved, coupling[level])
-
-
 def products(inverse, coupling, out, *, level):
     for side in range(2):
         out[side] = times(coupling[level, side], inverse[level]).astype(BF)
@@ -68,28 +56,23 @@
     out[1] = times(mirror[...], product[1]).astype(BF)
 
 
-def leaf_products(inverse, coupling, out):
-    for level in range(coupling.shape[0]):
-        out[level] = times(coupling[level], inverse[...]).astype(BF)
-
-
 def forward(residue, received, product, terms, delta, out, *, level):
-    change = (residue[...] - received[...].astype(F32)).astype(BF)
+    change = (residue[0] - received[...].astype(F32)).astype(BF)
     delta[...] = change
-    out[...] = (terms[level] + times_t(change, product[1])).astype(BF)
+    out[...] = (terms[level + 1] + times_t(change, product[1])).astype(BF)
 
 
 def forward_side(delta, product, inverse, values, residue, solved, *, level):
-    residue[...] = values[level + 1] - times_t(delta[...], product[0])
+    residue[0] = values[level + 1] - times_t(delta[...], product[0])
     step = times_t(delta[...], inverse[level]).astype(BF)
     solved[...] = times(step, inverse[level])
 
 
 def forward_top(residue, received, product, terms, values, delta, out, *, level):
-    change = (residue[...] - received[...].astype(F32)).astype(BF)
+    change = (residue[0] - received[...].astype(F32)).astype(BF)
     delta[...] = change
     rows = change.shape[0]
-    out[:rows] = (terms[level] + times_t(change, product[1])).astype(BF)
+    out[:rows] = (terms[level + 1] + times_t(change, product[1])).astype(BF)
     out[rows:] = (values[level + 1] - times_t(change, product[0])).astype(BF)
 
 
@@ -154,11 +137,11 @@
     def swap(value, level):
         return from_partner(value, level, gy_levels)
 
-    leaf, out = call(head, [((cols, size), F32), vec_bf], leaf_values.T, leaf_inv, leaf_cpl)
-    received = swap(out, 0)
-    (terms,) = call(leaf_terms, [((levels - 1, cols, width), F32)], leaf, leaf_cpl)
+    leaf = times_t(leaf_values.T.astype(BF), leaf_inv)
+    terms = jnp.einsum("kwn,rn->krw", leaf_cpl, leaf.astype(BF), preferred_element_type=F32)
+    received = swap(terms[0].astype(BF), 0)
     product, delta, solved = [], [], []
-    residue = values[0]
+    residue = values
     own_gram = mirror_gram = None
     for level in range(levels - 1):
         (made,) = call(
@@ -175,9 +158,10 @@
             received = swap(out, level + 1)
             residue, ahead = call(
                 lambda *refs, level=level: forward_side(*refs, level=level),
-                [vec, vec], change, made, inverse, values,
+                [((1, cols, width), F32), vec], change, made, inverse, values,
             )
             if level == min(1, levels - 3):
+                own_gram, _ = lax.optimization_barrier((own_gram, out))
                 mirror_gram = swap(own_gram, levels - 1)
         else:
             change, out = call(
@@ -191,7 +175,7 @@
         delta.append(change)
         solved.append(ahead)
     (top_pair,) = call(top_products, [pair], own_gram, mirror_gram, product[-1])
-    (leaf_prod,) = call(leaf_products, [((levels, width, size), BF)], leaf_inv, leaf_cpl)
+    leaf_prod = jnp.einsum("kwn,nm->kwm", leaf_cpl, leaf_inv, preferred_element_type=F32).astype(BF)
 
     blocks, mirrored = [None] * levels, [None] * levels
     block, block_bf, deltas = call(

time: 40.5 us -> 38 us (0.938)
  local copies, waits for them, and re-layouts: 4.78 us -> 0.04 us
  starting transfers between devices: 15.1 us -> 17.7 us
  matrix products: 0 us -> 1.53 us
  waiting for transfers between devices: 12.6 us -> 11.7 us
  Pallas kernels: 6.86 us -> 6.16 us
    unnamed x20 -> x10, local copies, waits for them, and re-layouts: 4.77 us -> 0.03 us
    ppermute x10, starting transfers between devices: 15.1 us -> 17.7 us  [from_partner(): return lax.ppermute(value, axis, pairs)]
    dot_general x0 -> x3, matrix products: none -> 1.53 us  [the longest x1 1.04 us: times_t(): lax.dot_general(values, matrix, (((1,), (1,)), ((), ())), preferred_eleme...]
    ppermute x10, waiting for transfers between devices: 12.6 us -> 11.7 us  [from_partner(): return lax.ppermute(value, axis, pairs)]
    pallas_call x28 -> x25, Pallas kernels: 6.86 us -> 6.16 us  [call(): pl.pallas_call(body, out_shape=[jax.ShapeDtypeStruct(shape, kind) for sha...]
  transfers between devices with their start and end apart: 10 -> 10, of which waited for: 7 -> 8; matrix products, arithmetic and copies ran while one was open for 0% -> 1% of each run, Pallas kernels for 12% -> 12%
where the time goes in v2:
time: 38 us; the launch traced here: 37.9 us
  starting transfers between devices  17.7 us (47%)
  waiting for transfers between devices  11.7 us (31%)
  Pallas kernels  6.16 us (16%)
  matrix products  1.53 us (4%)
  between operations  0.82 us (2%)
    ppermute x10, starting transfers between devices, from_partner(): return lax.ppermute(value, axis, pairs)  17.7 us
    ppermute x10, waiting for transfers between devices, from_partner(): return lax.ppermute(value, axis, pairs)  11.7 us
    pallas_call x25, Pallas kernels, call(): pl.pallas_call(body, out_shape=[jax.ShapeDtypeStruct(shape, kind) for sha...  6.16 us
    dot_general x1, matrix products, times_t(): lax.dot_general(values, matrix, (((1,), (1,)), ((), ())), preferred_eleme...  1.04 us
  transfers between devices with their start and end apart: 10, of which 8 were waited for; matrix products, arithmetic and copies ran while one was open for 1% of the time, Pallas kernels for 12%

profile of v2, /device:TPU:0, one launch (start us, length us, event | category | flops | bytes accessed | tf_op | source)
XLA Modules:
  0.0 37.9 jit_solution(7764773223235517222)
XLA Ops:
  0.7 1.0 %fusion.6.leaf = f32[64,128]{1,0:T(8,128)S(1)} fusion(f32[128,64]{0,1:T(8,128)} %param.6, bf16[1,128,128]{2,1,0:T(8,128)(2,1)} %param.7), kind=kOutput, calls=%fused_computation.9 | convolution fusion | flops 2105344 | bytes 98304 | tf_op jit(solution)/shard_map/dot_general | solution.py:18
  1.7 0.3 convolution_bitcast_fusion.refs_3_
  2.0 3.0 %collective-permute-start = (bf16[64,256]{1,0:T(8,128)(2,1)S(1)}, bf16[64,256]{1,0:T(8,128)(2,1)S(1)}, u32[]{:S(2)}, u32[]{:S(2)}) collective-permute-start(bf16[64,256]{1,0:T(8,128)(2,1)S(1)} %fusion.2), channel_id=1, source_target_pairs={{0,1},{1,0},{2,3},{3,2},{4,5},{5,4},{6,7},{7,6},{8,9},{9,8},{10,11... | collective-permute-start | bytes 98312 | tf_op jit(solution)/shard_map/ppermute | solution.py:29
  5.0 0.2 shard_map.88.own
  5.2 0.2 shard_map.77.refs_2_.refs_1_.product
  5.5 1.4 %collective-permute-done.refs_1_ = bf16[64,256]{1,0:T(8,128)(2,1)S(1)} collective-permute-done((bf16[64,256]{1,0:T(8,128)(2,1)S(1)}, bf16[64,256]{1,0:T(8,128)(2,1)S(1)}, u32[]{:S(2)}, u32[]{:S(2)}) %collective-permute-start) | collective-permute-done | bytes 32800 | tf_op jit(solution)/shard_map/ppermute | solution.py:29
  7.0 2.1 %collective-permute-start.1 = (bf16[64,256]{1,0:T(8,128)(2,1)S(1)}, bf16[64,256]{1,0:T(8,128)(2,1)S(1)}, u32[]{:S(2)}, u32[]{:S(2)}) collective-permute-start(bf16[64,256]{1,0:T(8,128)(2,1)S(1)} %get-tuple-element.30), channel_id=1, source_target_pairs={{0,2},{1,3},{2,0},{3,1},{4,6},{5,7},{6,4},{7,5},{8,10},{9,11},{10,... | collective-permute-start | bytes 98312 | tf_op jit(solution)/shard_map/ppermute | solution.py:29
  9.2 0.2 shard_map.80.refs_2_.refs_1_.product
  9.4 0.3 shard_map.79
  9.7 1.3 %collective-permute-done.1.refs_1_ = bf16[64,256]{1,0:T(8,128)(2,1)S(1)} collective-permute-done((bf16[64,256]{1,0:T(8,128)(2,1)S(1)}, bf16[64,256]{1,0:T(8,128)(2,1)S(1)}, u32[]{:S(2)}, u32[]{:S(2)}) %collective-permute-start.1) | collective-permute-done | bytes 32800 | tf_op jit(solution)/shard_map/ppermute | solution.py:29
  11.2 3.1 %collective-permute-start.2 = (bf16[64,256]{1,0:T(8,128)(2,1)S(1)}, bf16[64,256]{1,0:T(8,128)(2,1)S(1)}, u32[]{:S(2)}, u32[]{:S(2)}) collective-permute-start(bf16[64,256]{1,0:T(8,128)(2,1)S(1)} %get-tuple-element.34), channel_id=1, source_target_pairs={{0,4},{1,5},{2,6},{3,7},{4,0},{5,1},{6,2},{7,3},{8,12},{9,13},{10,... | collective-permute-start | bytes 98312 | tf_op jit(solution)/shard_map/ppermute | solution.py:29
  14.3 0.2 shard_map.83.refs_2_.refs_1_.product
  14.5 1.6 %collective-permute-start.5 = (bf16[256,256]{1,0:T(8,128)(2,1)S(1)}, bf16[256,256]{1,0:T(8,128)(2,1)S(1)}, u32[]{:S(2)}, u32[]{:S(2)}) collective-permute-start(bf16[256,256]{1,0:T(8,128)(2,1)S(1)} %shard_map.88.own), channel_id=1, source_target_pairs={{0,16},{8,24},{16,0},{24,8},{1,17},{9,25},{17,1},{25,9},{2,18},{10... | collective-permute-start | bytes 393224 | tf_op jit(solution)/shard_map/ppermute | solution.py:29
  16.1 0.3 shard_map.82
  16.6 0.2 shard_map.86.refs_2_.product
  16.9 0.3 shard_map.85
  17.2 0.7 %collective-permute-done.3.refs_1_ = bf16[64,256]{1,0:T(8,128)(2,1)S(1)} collective-permute-done((bf16[64,256]{1,0:T(8,128)(2,1)S(1)}, bf16[64,256]{1,0:T(8,128)(2,1)S(1)}, u32[]{:S(2)}, u32[]{:S(2)}) %collective-permute-start.3) | collective-permute-done | bytes 32800 | tf_op jit(solution)/shard_map/ppermute | solution.py:29
  17.8 0.2 shard_map.87
  18.1 1.7 %collective-permute-start.4 = (bf16[128,256]{1,0:T(8,128)(2,1)S(1)}, bf16[128,256]{1,0:T(8,128)(2,1)S(1)}, u32[]{:S(2)}, u32[]{:S(2)}) collective-permute-start(bf16[128,256]{1,0:T(8,128)(2,1)S(1)} %get-tuple-element.39.mine), channel_id=1, source_target_pairs={{0,16},{8,24},{16,0},{24,8},{1,17},{9,25},{17,1},{25,9},{2,18},{10... | collective-permute-start | bytes 196616 | tf_op jit(solution)/shard_map/ppermute | solution.py:29
  19.7 0.3 shard_map.90.solved
  20.0 0.2 shard_map.89.product
  20.3 2.1 %collective-permute-done.4.received = bf16[128,256]{1,0:T(8,128)(2,1)S(1)} collective-permute-done((bf16[128,256]{1,0:T(8,128)(2,1)S(1)}, bf16[128,256]{1,0:T(8,128)(2,1)S(1)}, u32[]{:S(2)}, u32[]{:S(2)}) %collective-permute-start.4) | collective-permute-done | bytes 65568 | tf_op jit(solution)/shard_map/ppermute | solution.py:29
  22.8 1.0 %collective-permute-done.6.received.refs_2_ = bf16[64,256]{1,0:T(8,128)(2,1)S(1)} collective-permute-done((bf16[64,256]{1,0:T(8,128)(2,1)S(1)}, bf16[64,256]{1,0:T(8,128)(2,1)S(1)}, u32[]{:S(2)}, u32[]{:S(2)}) %collective-permute-start.6) | collective-permute-done | bytes 32800 | tf_op jit(solution)/shard_map/ppermute | solution.py:29
  24.0 2.8 %collective-permute-start.7 = (bf16[64,256]{1,0:T(8,128)(2,1)S(1)}, bf16[64,256]{1,0:T(8,128)(2,1)S(1)}, u32[]{:S(2)}, u32[]{:S(2)}) collective-permute-start(bf16[64,256]{1,0:T(8,128)(2,1)S(1)} %get-tuple-element.43.upper), channel_id=1, source_target_pairs={{0,4},{1,5},{2,6},{3,7},{4,0},{5,1},{6,2},{7,3},{8,12},{9,13},{10,... | collective-permute-start | bytes 98312 | tf_op jit(solution)/shard_map/ppermute | solution.py:29
  26.7 0.2 convolution_convert_fusion.products_
  27.1 1.7 %collective-permute-done.7.received.refs_1_ = bf16[64,256]{1,0:T(8,128)(2,1)S(1)} collective-permute-done((bf16[64,256]{1,0:T(8,128)(2,1)S(1)}, bf16[64,256]{1,0:T(8,128)(2,1)S(1)}, u32[]{:S(2)}, u32[]{:S(2)}) %collective-permute-start.7) | collective-permute-done | bytes 32800 | tf_op jit(solution)/shard_map/ppermute | solution.py:29
  29.0 1.7 %collective-permute-start.8 = (bf16[64,256]{1,0:T(8,128)(2,1)S(1)}, bf16[64,256]{1,0:T(8,128)(2,1)S(1)}, u32[]{:S(2)}, u32[]{:S(2)}) collective-permute-start(bf16[64,256]{1,0:T(8,128)(2,1)S(1)} %get-tuple-element.44.upper), channel_id=1, source_target_pairs={{0,2},{1,3},{2,0},{3,1},{4,6},{5,7},{6,4},{7,5},{8,10},{9,11},{10,... | collective-permute-start | bytes 98312 | tf_op jit(solution)/shard_map/ppermute | solution.py:29
  31.0 1.9 %collective-permute-done.8.refs_0_.received = bf16[64,256]{1,0:T(8,128)(2,1)S(1)} collective-permute-done((bf16[64,256]{1,0:T(8,128)(2,1)S(1)}, bf16[64,256]{1,0:T(8,128)(2,1)S(1)}, u32[]{:S(2)}, u32[]{:S(2)}) %collective-permute-start.8) | collective-permute-done | bytes 32800 | tf_op jit(solution)/shard_map/ppermute | solution.py:29
  33.1 1.6 %collective-permute-start.9 = (bf16[64,256]{1,0:T(8,128)(2,1)S(1)}, bf16[64,256]{1,0:T(8,128)(2,1)S(1)}, u32[]{:S(2)}, u32[]{:S(2)}) collective-permute-start(bf16[64,256]{1,0:T(8,128)(2,1)S(1)} %get-tuple-element.48), channel_id=1, source_target_pairs={{0,1},{1,0},{2,3},{3,2},{4,5},{5,4},{6,7},{7,6},{8,9},{9,8},{10,11... | collective-permute-start | bytes 98312 | tf_op jit(solution)/shard_map/ppermute | solution.py:29
  34.8 0.7 %shard_map.101 = f32[5,64,256]{2,1,0:T(8,128)} custom-call(f32[64,256]{1,0:T(8,128)S(1)} %get-tuple-element.49.refs_0_, f32[64,256]{1,0:T(8,128)S(1)} %get-tuple-element.50.refs_1_, f32[64,256]{1,0:T(8,128)S(1)} %get-tuple-element.51.refs_2_, f32[64,256]{1,0:T(8,128)S(1)} %get-tuple-element.52.refs_3_, f32[64,256]{1,0:T(8,128)S(1)} %get-tuple-element.53.refs_4_), custom_call_target="tpu_custom_call" | custom-call | flops 300000000 | bytes 327680 | tf_op jit(solution)/shard_map/pallas_call | solution.py:34
  35.7 1.4 %collective-permute-done.9.received = bf16[64,256]{1,0:T(8,128)(2,1)S(1)} collective-permute-done((bf16[64,256]{1,0:T(8,128)(2,1)S(1)}, bf16[64,256]{1,0:T(8,128)(2,1)S(1)}, u32[]{:S(2)}, u32[]{:S(2)}) %collective-permute-start.9) | collective-permute-done | bytes 32800 | tf_op jit(solution)/shard_map/ppermute | solution.py:29
  37.1 0.8 %shard_map.100 = f32[64,128]{1,0:T(8,128)} custom-call(f32[64,128]{1,0:T(8,128)S(1)} %shard_map.97.own, bf16[64,256]{1,0:T(8,128)(2,1)S(1)} %collective-permute-done.9.received, bf16[5,256,128]{2,1,0:T(8,128)(2,1)S(1)} %convolution_convert_fusion.products_), custom_call_target="tpu_custom_call" | custom-call | flops 300000000 | bytes 393216 | tf_op jit(solution)/shard_map/pallas_call | solution.py:34
  (27 shorter events, 2.0 us)
Async XLA Ops:
  0.6 1.1 %copy-start = (bf16[1,5,256,128]{3,2,1,0:T(8,128)(2,1)S(1)}, bf16[1,5,256,128]{3,2,1,0:T(8,128)(2,1)}, u32[]{:S(2)}) copy-start(bf16[1,5,256,128]{3,2,1,0:T(8,128)(2,1)} %param.8) | copy-start | bytes 983044
  0.6 4.3 %copy-start.1 = (bf16[1,5,256,256]{3,2,1,0:T(8,128)(2,1)S(1)}, bf16[1,5,256,256]{3,2,1,0:T(8,128)(2,1)}, u32[]{:S(2)}) copy-start(bf16[1,5,256,256]{3,2,1,0:T(8,128)(2,1)} %param.10) | copy-start | bytes 1966084
  0.7 4.6 %copy-start.2 = (bf16[1,4,1,2,256,256]{5,4,3,2,1,0:T(8,128)(2,1)S(1)}, bf16[1,4,1,2,256,256]{5,4,3,2,1,0:T(8,128)(2,1)}, u32[]{:S(2)}) copy-start(bf16[1,4,1,2,256,256]{5,4,3,2,1,0:T(8,128)(2,1)} %param.11) | copy-start | bytes 3145732
  2.0 4.9 %collective-permute-start = (bf16[64,256]{1,0:T(8,128)(2,1)S(1)}, bf16[64,256]{1,0:T(8,128)(2,1)S(1)}, u32[]{:S(2)}, u32[]{:S(2)}) collective-permute-start(bf16[64,256]{1,0:T(8,128)(2,1)S(1)} %fusion.2), channel_id=1, source_target_pairs={{0,1},{1,0},{2,3},{3,2},{4,5},{5,4},{6,7},{7,6},{8,9},{9,8},{10,11... | collective-permute-start | bytes 98312 | tf_op jit(solution)/shard_map/ppermute | solution.py:29
  5.2 1.7 %copy-start.3 = (f32[1,5,256,64]{2,3,1,0:T(8,128)S(1)}, f32[1,5,256,64]{2,3,1,0:T(8,128)}, u32[]{:S(2)}) copy-start(f32[1,5,256,64]{2,3,1,0:T(8,128)} %param.9) | copy-start | bytes 983044
  7.0 4.0 %collective-permute-start.1 = (bf16[64,256]{1,0:T(8,128)(2,1)S(1)}, bf16[64,256]{1,0:T(8,128)(2,1)S(1)}, u32[]{:S(2)}, u32[]{:S(2)}) collective-permute-start(bf16[64,256]{1,0:T(8,128)(2,1)S(1)} %get-tuple-element.30), channel_id=1, source_target_pairs={{0,2},{1,3},{2,0},{3,1},{4,6},{5,7},{6,4},{7,5},{8,10},{9,11},{10,... | collective-permute-start | bytes 98312 | tf_op jit(solution)/shard_map/ppermute | solution.py:29
  11.2 5.2 %collective-permute-start.2 = (bf16[64,256]{1,0:T(8,128)(2,1)S(1)}, bf16[64,256]{1,0:T(8,128)(2,1)S(1)}, u32[]{:S(2)}, u32[]{:S(2)}) collective-permute-start(bf16[64,256]{1,0:T(8,128)(2,1)S(1)} %get-tuple-element.34), channel_id=1, source_target_pairs={{0,4},{1,5},{2,6},{3,7},{4,0},{5,1},{6,2},{7,3},{8,12},{9,13},{10,... | collective-permute-start | bytes 98312 | tf_op jit(solution)/shard_map/ppermute | solution.py:29
  14.5 5.5 %collective-permute-start.5 = (bf16[256,256]{1,0:T(8,128)(2,1)S(1)}, bf16[256,256]{1,0:T(8,128)(2,1)S(1)}, u32[]{:S(2)}, u32[]{:S(2)}) collective-permute-start(bf16[256,256]{1,0:T(8,128)(2,1)S(1)} %shard_map.88.own), channel_id=1, source_target_pairs={{0,16},{8,24},{16,0},{24,8},{1,17},{9,25},{17,1},{25,9},{2,18},{10... | collective-permute-start | bytes 393224 | tf_op jit(solution)/shard_map/ppermute | solution.py:29
  16.6 1.2 %collective-permute-start.3 = (bf16[64,256]{1,0:T(8,128)(2,1)S(1)}, bf16[64,256]{1,0:T(8,128)(2,1)S(1)}, u32[]{:S(2)}, u32[]{:S(2)}) collective-permute-start(bf16[64,256]{1,0:T(8,128)(2,1)S(1)} %get-tuple-element.38), channel_id=1, source_target_pairs={{0,8},{8,0},{16,24},{24,16},{1,9},{9,1},{17,25},{25,17},{2,10},{10... | collective-permute-start | bytes 98312 | tf_op jit(solution)/shard_map/ppermute | solution.py:29
  18.1 4.3 %collective-permute-start.4 = (bf16[128,256]{1,0:T(8,128)(2,1)S(1)}, bf16[128,256]{1,0:T(8,128)(2,1)S(1)}, u32[]{:S(2)}, u32[]{:S(2)}) collective-permute-start(bf16[128,256]{1,0:T(8,128)(2,1)S(1)} %get-tuple-element.39.mine), channel_id=1, source_target_pairs={{0,16},{8,24},{16,0},{24,8},{1,17},{9,25},{17,1},{25,9},{2,18},{10... | collective-permute-start | bytes 196616 | tf_op jit(solution)/shard_map/ppermute | solution.py:29
  22.6 1.3 %collective-permute-start.6 = (bf16[64,256]{1,0:T(8,128)(2,1)S(1)}, bf16[64,256]{1,0:T(8,128)(2,1)S(1)}, u32[]{:S(2)}, u32[]{:S(2)}) collective-permute-start(bf16[64,256]{1,0:T(8,128)(2,1)S(1)} %get-tuple-element.42.upper), channel_id=1, source_target_pairs={{0,8},{8,0},{16,24},{24,16},{1,9},{9,1},{17,25},{25,17},{2,10},{10... | collective-permute-start | bytes 98312 | tf_op jit(solution)/shard_map/ppermute | solution.py:29
  22.8 4.0 %copy-start.4 = (bf16[1,128,128]{2,1,0:T(8,128)(2,1)S(1)}, bf16[1,128,128]{2,1,0:T(8,128)(2,1)}, u32[]{:S(2)}) copy-start(bf16[1,128,128]{2,1,0:T(8,128)(2,1)} %param.7) | copy-start | bytes 98308
  24.0 4.9 %collective-permute-start.7 = (bf16[64,256]{1,0:T(8,128)(2,1)S(1)}, bf16[64,256]{1,0:T(8,128)(2,1)S(1)}, u32[]{:S(2)}, u32[]{:S(2)}) collective-permute-start(bf16[64,256]{1,0:T(8,128)(2,1)S(1)} %get-tuple-element.43.upper), channel_id=1, source_target_pairs={{0,4},{1,5},{2,6},{3,7},{4,0},{5,1},{6,2},{7,3},{8,12},{9,13},{10,... | collective-permute-start | bytes 98312 | tf_op jit(solution)/shard_map/ppermute | solution.py:29
  29.0 4.0 %collective-permute-start.8 = (bf16[64,256]{1,0:T(8,128)(2,1)S(1)}, bf16[64,256]{1,0:T(8,128)(2,1)S(1)}, u32[]{:S(2)}, u32[]{:S(2)}) collective-permute-start(bf16[64,256]{1,0:T(8,128)(2,1)S(1)} %get-tuple-element.44.upper), channel_id=1, source_target_pairs={{0,2},{1,3},{2,0},{3,1},{4,6},{5,7},{6,4},{7,5},{8,10},{9,11},{10,... | collective-permute-start | bytes 98312 | tf_op jit(solution)/shard_map/ppermute | solution.py:29
  33.1 4.0 %collective-permute-start.9 = (bf16[64,256]{1,0:T(8,128)(2,1)S(1)}, bf16[64,256]{1,0:T(8,128)(2,1)S(1)}, u32[]{:S(2)}, u32[]{:S(2)}) collective-permute-start(bf16[64,256]{1,0:T(8,128)(2,1)S(1)} %get-tuple-element.48), channel_id=1, source_target_pairs={{0,1},{1,0},{2,3},{3,2},{4,5},{5,4},{6,7},{7,6},{8,9},{9,8},{10,11... | collective-permute-start | bytes 98312 | tf_op jit(solution)/shard_map/ppermute | solution.py:29

commit v3 on v2

v3 whole, which is shorter than its diff:
```python
import functools

import jax
import jax.numpy as jnp
from jax import lax
from jax.experimental import pallas as pl
from jax.experimental.pallas import tpu as pltpu
from jax.sharding import PartitionSpec as P

BF = jnp.bfloat16
F32 = jnp.float32
VMEM = pl.BlockSpec(memory_space=pltpu.VMEM)


def times(values, matrix):
    return lax.dot_general(values, matrix, (((1,), (0,)), ((), ())), preferred_element_type=F32)


def times_t(values, matrix):
    return lax.dot_general(values, matrix, (((1,), (1,)), ((), ())), preferred_element_type=F32)


def gram(left, right):
    return lax.dot_general(left, right, (((0,), (0,)), ((), ())), preferred_element_type=F32)


def exchange(value, level, gy_levels, cross=False):
    inner, outer = lax.axis_size("gy"), lax.axis_size("gx")
    mask = 2**level ^ (inner if cross else 0)
    pairs = [(source, source ^ mask) for source in range(inner * outer)]
    return lax.ppermute(value, ("gx", "gy"), pairs)


def call(body, outs, *args, cost=1, **static):
    moved = sum(a.size * a.dtype.itemsize for a in args)
    made = pl.pallas_call(
        functools.partial(body, **static),
        out_shape=[jax.ShapeDtypeStruct(shape, kind) for shape, kind in outs],
        in_specs=[VMEM] * len(args),
        out_specs=[VMEM] * len(outs),
        compiler_params=pltpu.CompilerParams(vmem_limit_bytes=32 * 2**20),
        cost_estimate=pl.CostEstimate(flops=cost * 3 * 10**8, bytes_accessed=moved, transcendentals=0),
    )(*args)
    return made if len(outs) > 1 else made[0]


def products(inverse, coupling, out, *, level):
    for side in range(2):
        out[side] = times(coupling[level, side], inverse[level]).astype(BF)


def products_ahead(inverse, coupling, terms, out, ahead, *, level):
    rows = inverse.shape[1]
    out[0] = times(coupling[level, 0], inverse[level]).astype(BF)
    mirror = times(coupling[level, 1], inverse[level]).astype(BF)
    out[1] = mirror
    ahead[:rows] = mirror
    ahead[rows:] = terms[level + 1].astype(BF)


def top_gram(inverse, out):
    matrix = inverse[inverse.shape[0] - 1]
    out[...] = gram(matrix, matrix).astype(BF)


def top_products(own, mirror, product, out):
    out[0] = times(own[...], product[0]).astype(BF)
    out[1] = times(mirror[...], product[1]).astype(BF)


def forward(residue, received, product, terms, delta, out, *, level):
    change = (residue[0] - received[...].astype(F32)).astype(BF)
    delta[...] = change
    out[...] = (terms[level + 1] + times_t(change, product[1])).astype(BF)


def forward_ahead(residue, received, product, terms, values, delta, out, ahead, *, level):
    change = (residue[0] - received[...].astype(F32)).astype(BF)
    delta[...] = change
    out[...] = (terms[level + 1] + times_t(change, product[1])).astype(BF)
    ahead[...] = (values[level + 1] - times_t(change, product[0])).astype(BF)


def forward_mate(received, residue, ahead, delta, out):
    rows = ahead.shape[1]
    change = (residue[...].astype(F32) - received[...].astype(F32)).astype(BF)
    delta[...] = change
    out[...] = (ahead[rows:].astype(F32) + times_t(change, ahead[:rows])).astype(BF)


def forward_back(received, below, product_below, product, terms, values, delta, out, *, level):
    residue = values[level] - times_t(below[...], product_below[0])
    change = (residue - received[...].astype(F32)).astype(BF)
    delta[...] = change
    out[...] = (terms[level + 1] + times_t(change, product[1])).astype(BF)


def forward_residue(delta, product, values, residue, *, level):
    residue[0] = values[level + 1] - times_t(delta[...], product[0])


def forward_top(residue, received, product, terms, values, delta, out, *, level):
    change = (residue[0] - received[...].astype(F32)).astype(BF)
    delta[...] = change
    rows = change.shape[0]
    out[:rows] = (terms[level + 1] + times_t(change, product[1])).astype(BF)
    out[rows:] = (values[level + 1] - times_t(change, product[0])).astype(BF)


def solve(delta, inverse, solved, *, level):
    step = times_t(delta[...], inverse[level]).astype(BF)
    solved[...] = times(step, inverse[level])


def top(mine, received, product, solved, out, out_bf, delta):
    rows = solved.shape[0]
    own = (mine[rows:].astype(F32) - received[:rows].astype(F32)).astype(BF)
    other = (received[rows:].astype(F32) - mine[:rows].astype(F32)).astype(BF)
    value = solved[...] - times(own, product[0]) - times(other, product[1])
    out[...] = value
    out_bf[...] = value.astype(BF)
    delta[0] = own
    delta[1] = other


def top_values(delta, own, mirror, out, mirrored):
    out[...] = times(delta[0], own[...])
    mirrored[...] = times(delta[1], mirror[...]).astype(BF)


def back_part(solved, known, product, out, *, side):
    out[...] = solved[...] - times(known[...].astype(BF), product[side])


def back(part, received, product, *outs, side):
    value = part[...] - times(received[...].astype(BF), product[side])
    for out in outs:
        out[...] = value.astype(out.dtype)


def back_both(received, known, solved, product, *outs):
    value = solved[...] - times(known[...], product[0])
    value = value - times(received[...].astype(BF), product[1])
    for out in outs:
        out[...] = value.astype(out.dtype)


def leaf_part(leaf, inverse, leaf_products, *refs, early):
    *mirrored, out = refs
    total = times(leaf[...].astype(BF), inverse[...])
    for level, block in zip(early, mirrored, strict=True):
        total = total - times(block[...], leaf_products[level])
    out[...] = total


def finish(part, leaf_products, *refs, late):
    *refs, leaf, out = refs
    mirrored, blocks = refs[: len(late)], refs[len(late) :]
    total = part[...]
    for level, block in zip(late, mirrored, strict=True):
        total = total - times(block[...].astype(BF), leaf_products[level])
    leaf[...] = total
    for level, block in enumerate(blocks):
        out[level] = block[...].astype(F32)


def shards(leaf_values, leaf_inverse, leaf_coupling, block_values, block_inverse, block_coupling):
    levels, width = block_inverse.shape[1], block_inverse.shape[2]
    size, cols = leaf_values.shape
    core = lax.axis_size("gy").bit_length() - 1
    inverse, coupling = block_inverse[0], block_coupling[0, :, 0]
    leaf_inv, leaf_cpl = leaf_inverse[0], leaf_coupling[0]
    values = jnp.swapaxes(block_values[0], 1, 2)
    vec, vec_bf, pair = ((cols, width), F32), ((cols, width), BF), ((2, width, width), BF)
    slab = ((1, cols, width), F32)

    def send(value, level, cross=False):
        return exchange(value, level, core, cross)

    def mate(value):
        return exchange(value, core, core)

    def arrived(value):
        return value.astype(F32)

    def after(value, other):
        return lax.optimization_barrier((value, other))[0]

    below_top = levels - 1
    first_across = 1 + (core - 1) % 2
    at_home = [
        level < first_across or level >= core or (level - first_across) % 2 == 1
        for level in range(levels)
    ]
    leaf = times_t(leaf_values.T.astype(BF), leaf_inv)
    terms = jnp.einsum("kwn,rn->krw", leaf_cpl, leaf.astype(BF), preferred_element_type=F32)
    received = send(terms[0].astype(BF), 0)
    product, ahead, solved = [None] * below_top, [None] * below_top, [None] * below_top
    own_gram = call(top_gram, [((width, width), BF)], inverse)
    inverse = after(inverse, own_gram)
    for level in range(below_top):
        if at_home[level]:
            product[level] = call(products, [pair], inverse, coupling, level=level, cost=1 if level < 2 else 1)
        else:
            product[level], ahead[level] = call(
                products_ahead, [pair, ((width + cols, width), BF)], inverse, coupling, terms, level=level
            )

    residue, change = values, None
    for level in range(below_top):
        below = change
        if level == levels - 2:
            received, mirror_gram = lax.optimization_barrier((received, mirror_gram))
            change, out = call(
                forward_top, [vec_bf, ((2 * cols, width), BF)],
                residue, received, product[level], terms, values, level=level,
            )
            received = send(out, below_top)
        else:
            across = first_across <= level + 1 < core
            if not at_home[level]:
                change, out = call(forward_mate, [vec_bf, vec_bf], arrived(received), residue, ahead[level])
            elif level and not at_home[level - 1]:
                change, out = call(
                    forward_back, [vec_bf, vec_bf], arrived(received), below,
                    product[level - 1], product[level], terms, values, level=level, cost=1,
                )
            elif not at_home[level + 1]:
                change, out, residue = call(
                    forward_ahead, [vec_bf, vec_bf, vec_bf],
                    residue, received, product[level], terms, values, level=level,
                )
            else:
                change, out = call(
                    forward, [vec_bf, vec_bf], residue, received, product[level], terms, level=level
                )
            received = send(out, level + 1, across)
            if level == 0:
                mirror_gram = send(after(own_gram, out), below_top)
            if not at_home[level]:
                change = mate(change)
            elif not at_home[level + 1]:
                residue = mate(residue)
                ahead[level + 1] = mate(after(ahead[level + 1], out))
            else:
                residue = call(
                    forward_residue, [slab], change, product[level], values, level=level, cost=0
                )
        solved[level] = call(solve, [vec], change, inverse, level=level)
    top_pair = call(top_products, [pair], own_gram, mirror_gram, product[-1], cost=8)
    leaf_prod = jnp.einsum("kwn,nm->kwm", leaf_cpl, leaf_inv, preferred_element_type=F32).astype(BF)

    mates = [level for level in range(core) if level % 2 == 0]
    for level in mates:
        product[level] = mate(after(product[level], out))
        solved[level] = mate(after(solved[level], out))
    blocks, mirrored = [None] * levels, [None] * levels
    block, block_bf, deltas = call(
        top, [vec, vec_bf, ((2, cols, width), BF)], out, received, top_pair, solved[-1]
    )
    blocks[levels - 2] = block
    received = mirrored[levels - 2] = send(block_bf, levels - 2)
    blocks[-1], mirrored[-1] = call(top_values, [vec, vec_bf], deltas, own_gram, mirror_gram)
    late = [0]
    for level in reversed(range(levels - 2)):
        home = level not in mates
        outs = [vec, vec_bf] if home else [vec_bf]
        if level + 1 >= core:
            side = 0 if home else 1
            part = call(back_part, [vec], solved[level], block_bf, product[level], side=side)
            made = call(back, outs, part, received, product[level], side=1 - side)
        else:
            known = mate(block_bf)
            if home:
                blocks[level + 1] = known
            made = call(back_both, outs, arrived(received), known, solved[level], product[level])
        if home:
            blocks[level], block_bf = made
        else:
            block_bf = made
        received = send(block_bf, level, level < core)
        if home == (level < core):
            mirrored[level] = mate(received)
            late.append(level)
        else:
            mirrored[level] = received
    if 0 in mates:
        blocks[0] = mate(block_bf)
    early = tuple(level for level in range(levels) if level not in late)
    part = call(
        leaf_part, [((cols, size), F32)],
        leaf, leaf_inv, leaf_prod, *[mirrored[level] for level in early], early=early,
    )
    mirrored[0] = arrived(mirrored[0])
    leaf_solution, stacked = call(
        finish, [((cols, size), F32), ((levels, cols, width), F32)],
        part, leaf_prod, *[mirrored[level] for level in late], *blocks, late=tuple(late),
    )
    return leaf_solution.T, jnp.swapaxes(stacked, 1, 2)[None]


def solution(mesh):
    both = ("gx", "gy")
    return jax.shard_map(
        shards,
        mesh=mesh,
        in_specs=tuple(P(both, *[None] * rank) for rank in (1, 2, 3, 3, 3, 5)),
        out_specs=(P(both, None), P(both, None, None, None)),
        check_vma=False,
    )
```

time: 38 us -> 35.9 us (0.945)
  waiting for transfers between devices: 11.7 us -> 8.4 us
  starting transfers between devices: 17.7 us -> 19.3 us
  Pallas kernels: 6.16 us -> 5.59 us
    ppermute x10 -> x21, waiting for transfers between devices: 11.7 us -> 8.4 us  [exchange(): return lax.ppermute(value, ('gx', 'gy'), pairs)]
    ppermute x10 -> x21, starting transfers between devices: 17.7 us -> 19.3 us  [exchange(): return lax.ppermute(value, ('gx', 'gy'), pairs)]
    pallas_call x25 -> x23, Pallas kernels: 6.16 us -> 5.59 us  [call(): pl.pallas_call(functools.partial(body, **static), out_shape=[jax.ShapeDty...]
  transfers between devices with their start and end apart: 10 -> 21, of which waited for: 8 -> 9; matrix products, arithmetic and copies ran while one was open for 1% -> 1% of each run, Pallas kernels for 12% -> 11%
where the time goes in v3:
time: 35.9 us; the launch traced here: 35.7 us
  starting transfers between devices  19.3 us (54%)
  waiting for transfers between devices  8.4 us (23%)
  Pallas kernels  5.59 us (16%)
  matrix products  1.52 us (4%)
  between operations  0.88 us (2%)
    ppermute x21, starting transfers between devices, exchange(): return lax.ppermute(value, ('gx', 'gy'), pairs)  19.3 us
    ppermute x21, waiting for transfers between devices, exchange(): return lax.ppermute(value, ('gx', 'gy'), pairs)  8.4 us
    pallas_call x23, Pallas kernels, call(): pl.pallas_call(functools.partial(body, **static), out_shape=[jax.ShapeDty...  5.59 us
    dot_general x1, matrix products, times_t(): lax.dot_general(values, matrix, (((1,), (1,)), ((), ())), preferred_eleme...  1.04 us
  transfers between devices with their start and end apart: 21, of which 9 were waited for; matrix products, arithmetic and copies ran while one was open for 1% of the time, Pallas kernels for 11%

profile of v3, /device:TPU:0, one launch (start us, length us, event | category | flops | bytes accessed | tf_op | source)
XLA Modules:
  0.0 35.7 jit_solution(9837396567342010278)
XLA Ops:
  0.7 1.0 %fusion.6.leaf = f32[64,128]{1,0:T(8,128)S(1)} fusion(f32[128,64]{0,1:T(8,128)} %param.6, bf16[1,128,128]{2,1,0:T(8,128)(2,1)} %param.7), kind=kOutput, calls=%fused_computation.9 | convolution fusion | flops 2105344 | bytes 98304 | tf_op jit(solution)/shard_map/dot_general | solution.py:20
  1.7 0.3 convolution_bitcast_fusion.terms
  2.0 3.0 %collective-permute-start = (bf16[64,256]{1,0:T(8,128)(2,1)S(1)}, bf16[64,256]{1,0:T(8,128)(2,1)S(1)}, u32[]{:S(2)}, u32[]{:S(2)}) collective-permute-start(bf16[64,256]{1,0:T(8,128)(2,1)S(1)} %fusion.2), channel_id=1, source_target_pairs={{0,1},{1,0},{2,3},{3,2},{4,5},{5,4},{6,7},{7,6},{8,9},{9,8},{10,11... | collective-permute-start | bytes 98312 | tf_op jit(solution)/shard_map/ppermute | solution.py:31
  5.2 0.2 shard_map.78.product
  5.7 1.2 %collective-permute-done.received = bf16[64,256]{1,0:T(8,128)(2,1)S(1)} collective-permute-done((bf16[64,256]{1,0:T(8,128)(2,1)S(1)}, bf16[64,256]{1,0:T(8,128)(2,1)S(1)}, u32[]{:S(2)}, u32[]{:S(2)}) %collective-permute-start) | collective-permute-done | bytes 32800 | tf_op jit(solution)/shard_map/ppermute | solution.py:31
  7.2 2.2 %collective-permute-start.1 = (bf16[64,256]{1,0:T(8,128)(2,1)S(1)}, bf16[64,256]{1,0:T(8,128)(2,1)S(1)}, u32[]{:S(2)}, u32[]{:S(2)}) collective-permute-start(bf16[64,256]{1,0:T(8,128)(2,1)S(1)} %get-tuple-element.32), channel_id=1, source_target_pairs={{0,10},{1,11},{2,8},{3,9},{4,14},{5,15},{6,12},{7,13},{8,2},{9,3},... | collective-permute-start | bytes 98312 | tf_op jit(solution)/shard_map/ppermute | solution.py:31
  9.5 1.5 %collective-permute-start.7 = (bf16[256,256]{1,0:T(8,128)(2,1)S(1)}, bf16[256,256]{1,0:T(8,128)(2,1)S(1)}, u32[]{:S(2)}, u32[]{:S(2)}) collective-permute-start(bf16[256,256]{1,0:T(8,128)(2,1)S(1)} %shard_map.77.own), channel_id=1, source_target_pairs={{0,16},{1,17},{2,18},{3,19},{4,20},{5,21},{6,22},{7,23},{8,24},{9,... | collective-permute-start | bytes 393224 | tf_op jit(solution)/shard_map/ppermute | solution.py:31
  11.2 2.7 %collective-permute-start.4 = (bf16[64,256]{1,0:T(8,128)(2,1)S(1)}, bf16[64,256]{1,0:T(8,128)(2,1)S(1)}, u32[]{:S(2)}, u32[]{:S(2)}) collective-permute-start(bf16[64,256]{1,0:T(8,128)(2,1)S(1)} %get-tuple-element.36), channel_id=1, source_target_pairs={{0,12},{1,13},{2,14},{3,15},{4,8},{5,9},{6,10},{7,11},{8,4},{9,5},... | collective-permute-start | bytes 98312 | tf_op jit(solution)/shard_map/ppermute | solution.py:31
  14.0 0.2 shard_map.82.product
  14.3 1.4 %collective-permute-done.4 = bf16[64,256]{1,0:T(8,128)(2,1)S(1)} collective-permute-done((bf16[64,256]{1,0:T(8,128)(2,1)S(1)}, bf16[64,256]{1,0:T(8,128)(2,1)S(1)}, u32[]{:S(2)}, u32[]{:S(2)}) %collective-permute-start.4) | collective-permute-done | bytes 32800 | tf_op jit(solution)/shard_map/ppermute | solution.py:31
  15.7 0.3 shard_map.83
  16.6 0.3 shard_map.84
  16.9 0.3 collective-permute-done.6.received
  17.5 1.6 %collective-permute-start.9 = (bf16[128,256]{1,0:T(8,128)(2,1)S(1)}, bf16[128,256]{1,0:T(8,128)(2,1)S(1)}, u32[]{:S(2)}, u32[]{:S(2)}) collective-permute-start(bf16[128,256]{1,0:T(8,128)(2,1)S(1)} %get-tuple-element.43.mine), channel_id=1, source_target_pairs={{0,16},{1,17},{2,18},{3,19},{4,20},{5,21},{6,22},{7,23},{8,24},{9,... | collective-permute-start | bytes 196616 | tf_op jit(solution)/shard_map/ppermute | solution.py:31
  19.1 0.4 %collective-permute-start.8 = (f32[64,256]{1,0:T(8,128)S(1)}, f32[64,256]{1,0:T(8,128)S(1)}, u32[]{:S(2)}, u32[]{:S(2)}) collective-permute-start(f32[64,256]{1,0:T(8,128)S(1)} %shard_map.84), channel_id=1, source_target_pairs={{0,8},{1,9},{2,10},{3,11},{4,12},{5,13},{6,14},{7,15},{8,0},{9,1},... | collective-permute-start | bytes 196616 | tf_op jit(solution)/shard_map/ppermute | solution.py:31
  19.6 0.2 shard_map.88.product
  19.8 0.3 shard_map.89.solved
  20.1 1.7 %collective-permute-done.9.received = bf16[128,256]{1,0:T(8,128)(2,1)S(1)} collective-permute-done((bf16[128,256]{1,0:T(8,128)(2,1)S(1)}, bf16[128,256]{1,0:T(8,128)(2,1)S(1)}, u32[]{:S(2)}, u32[]{:S(2)}) %collective-permute-start.9) | collective-permute-done | bytes 65568 | tf_op jit(solution)/shard_map/ppermute | solution.py:31
  22.2 1.0 %collective-permute-done.11.received.refs_1_ = bf16[64,256]{1,0:T(8,128)(2,1)S(1)} collective-permute-done((bf16[64,256]{1,0:T(8,128)(2,1)S(1)}, bf16[64,256]{1,0:T(8,128)(2,1)S(1)}, u32[]{:S(2)}, u32[]{:S(2)}) %collective-permute-start.11) | collective-permute-done | bytes 32800 | tf_op jit(solution)/shard_map/ppermute | solution.py:31
  23.4 2.5 %collective-permute-start.12 = (bf16[64,256]{1,0:T(8,128)(2,1)S(1)}, bf16[64,256]{1,0:T(8,128)(2,1)S(1)}, u32[]{:S(2)}, u32[]{:S(2)}) collective-permute-start(bf16[64,256]{1,0:T(8,128)(2,1)S(1)} %shard_map.92), channel_id=1, source_target_pairs={{0,12},{1,13},{2,14},{3,15},{4,8},{5,9},{6,10},{7,11},{8,4},{9,5},... | collective-permute-start | bytes 98312 | tf_op jit(solution)/shard_map/ppermute | solution.py:31
  25.8 0.3 collective-permute-start.13
  26.2 0.3 shard_map.97
  26.5 0.3 shard_map.95.solved
  26.8 0.2 collective-permute-start.16
  27.0 0.3 collective-permute-start.17
  27.4 0.3 collective-permute-done.12.refs_0_
  27.8 1.9 %collective-permute-start.14 = (bf16[64,256]{1,0:T(8,128)(2,1)S(1)}, bf16[64,256]{1,0:T(8,128)(2,1)S(1)}, u32[]{:S(2)}, u32[]{:S(2)}) collective-permute-start(bf16[64,256]{1,0:T(8,128)(2,1)S(1)} %get-tuple-element.51), channel_id=1, source_target_pairs={{0,10},{1,11},{2,8},{3,9},{4,14},{5,15},{6,12},{7,13},{8,2},{9,3},... | collective-permute-start | bytes 98312 | tf_op jit(solution)/shard_map/ppermute | solution.py:31
  30.1 1.2 %collective-permute-done.14 = bf16[64,256]{1,0:T(8,128)(2,1)S(1)} collective-permute-done((bf16[64,256]{1,0:T(8,128)(2,1)S(1)}, bf16[64,256]{1,0:T(8,128)(2,1)S(1)}, u32[]{:S(2)}, u32[]{:S(2)}) %collective-permute-start.14) | collective-permute-done | bytes 32800 | tf_op jit(solution)/shard_map/ppermute | solution.py:31
  31.5 1.3 %collective-permute-start.18 = (bf16[64,256]{1,0:T(8,128)(2,1)S(1)}, bf16[64,256]{1,0:T(8,128)(2,1)S(1)}, u32[]{:S(2)}, u32[]{:S(2)}) collective-permute-start(bf16[64,256]{1,0:T(8,128)(2,1)S(1)} %shard_map.98), channel_id=1, source_target_pairs={{0,9},{1,8},{2,11},{3,10},{4,13},{5,12},{6,15},{7,14},{8,1},{9,0},... | collective-permute-start | bytes 98312 | tf_op jit(solution)/shard_map/ppermute | solution.py:31
  32.9 0.3 collective-permute-start.20
  33.7 1.2 %collective-permute-done.18 = bf16[64,256]{1,0:T(8,128)(2,1)S(1)} collective-permute-done((bf16[64,256]{1,0:T(8,128)(2,1)S(1)}, bf16[64,256]{1,0:T(8,128)(2,1)S(1)}, u32[]{:S(2)}, u32[]{:S(2)}) %collective-permute-start.18) | collective-permute-done | bytes 32800 | tf_op jit(solution)/shard_map/ppermute | solution.py:31
  34.9 0.8 %shard_map.99 = (f32[64,128]{1,0:T(8,128)}, f32[5,64,256]{2,1,0:T(8,128)}) custom-call(f32[64,128]{1,0:T(8,128)S(1)} %shard_map.94.part, bf16[5,256,128]{2,1,0:T(8,128)(2,1)S(1)} %convolution_convert_fusion.leaf_products, f32[64,256]{1,0:T(8,128)S(1)} %convert_element_type.37.refs_0_, bf16[64,256]{1,0:T(8,128)(2,1)S(1)} %collective-permute-done.19.refs_1_, ...), custom_call_target="tpu_custom_call" | custom-call | flops 300000000 | bytes 720896 | tf_op jit(solution)/shard_map/pallas_call | solution.py:36
  (52 shorter events, 3.8 us)
Async XLA Ops:
  0.6 1.1 %copy-start = (bf16[1,5,256,128]{3,2,1,0:T(8,128)(2,1)S(1)}, bf16[1,5,256,128]{3,2,1,0:T(8,128)(2,1)}, u32[]{:S(2)}) copy-start(bf16[1,5,256,128]{3,2,1,0:T(8,128)(2,1)} %param.8) | copy-start | bytes 983044
  0.6 4.3 %copy-start.2 = (bf16[1,5,256,256]{3,2,1,0:T(8,128)(2,1)S(1)}, bf16[1,5,256,256]{3,2,1,0:T(8,128)(2,1)}, u32[]{:S(2)}) copy-start(bf16[1,5,256,256]{3,2,1,0:T(8,128)(2,1)} %param.10) | copy-start | bytes 1966084
  0.7 4.6 %copy-start.1 = (bf16[1,4,1,2,256,256]{5,4,3,2,1,0:T(8,128)(2,1)S(1)}, bf16[1,4,1,2,256,256]{5,4,3,2,1,0:T(8,128)(2,1)}, u32[]{:S(2)}) copy-start(bf16[1,4,1,2,256,256]{5,4,3,2,1,0:T(8,128)(2,1)} %param.11) | copy-start | bytes 3145732
  2.0 4.9 %collective-permute-start = (bf16[64,256]{1,0:T(8,128)(2,1)S(1)}, bf16[64,256]{1,0:T(8,128)(2,1)S(1)}, u32[]{:S(2)}, u32[]{:S(2)}) collective-permute-start(bf16[64,256]{1,0:T(8,128)(2,1)S(1)} %fusion.2), channel_id=1, source_target_pairs={{0,1},{1,0},{2,3},{3,2},{4,5},{5,4},{6,7},{7,6},{8,9},{9,8},{10,11... | collective-permute-start | bytes 98312 | tf_op jit(solution)/shard_map/ppermute | solution.py:31
  5.5 1.4 %copy-start.3 = (f32[1,5,256,64]{2,3,1,0:T(8,128)S(1)}, f32[1,5,256,64]{2,3,1,0:T(8,128)}, u32[]{:S(2)}) copy-start(f32[1,5,256,64]{2,3,1,0:T(8,128)} %param.9) | copy-start | bytes 983044
  7.1 4.0 %collective-permute-start.3 = (bf16[320,256]{1,0:T(8,128)(2,1)S(1)}, bf16[320,256]{1,0:T(8,128)(2,1)S(1)}, u32[]{:S(2)}, u32[]{:S(2)}) collective-permute-start(bf16[320,256]{1,0:T(8,128)(2,1)S(1)} %get-tuple-element.35), channel_id=1, source_target_pairs={{0,8},{1,9},{2,10},{3,11},{4,12},{5,13},{6,14},{7,15},{8,0},{9,1},... | collective-permute-start | bytes 491528 | tf_op jit(solution)/shard_map/ppermute | solution.py:31
  7.2 3.9 %collective-permute-start.1 = (bf16[64,256]{1,0:T(8,128)(2,1)S(1)}, bf16[64,256]{1,0:T(8,128)(2,1)S(1)}, u32[]{:S(2)}, u32[]{:S(2)}) collective-permute-start(bf16[64,256]{1,0:T(8,128)(2,1)S(1)} %get-tuple-element.32), channel_id=1, source_target_pairs={{0,10},{1,11},{2,8},{3,9},{4,14},{5,15},{6,12},{7,13},{8,2},{9,3},... | collective-permute-start | bytes 98312 | tf_op jit(solution)/shard_map/ppermute | solution.py:31
  9.4 1.7 %collective-permute-start.2 = (bf16[64,256]{1,0:T(8,128)(2,1)S(1)}, bf16[64,256]{1,0:T(8,128)(2,1)S(1)}, u32[]{:S(2)}, u32[]{:S(2)}) collective-permute-start(bf16[64,256]{1,0:T(8,128)(2,1)S(1)} %get-tuple-element.33), channel_id=1, source_target_pairs={{0,8},{1,9},{2,10},{3,11},{4,12},{5,13},{6,14},{7,15},{8,0},{9,1},... | collective-permute-start | bytes 98312 | tf_op jit(solution)/shard_map/ppermute | solution.py:31
  9.5 7.4 %collective-permute-start.7 = (bf16[256,256]{1,0:T(8,128)(2,1)S(1)}, bf16[256,256]{1,0:T(8,128)(2,1)S(1)}, u32[]{:S(2)}, u32[]{:S(2)}) collective-permute-start(bf16[256,256]{1,0:T(8,128)(2,1)S(1)} %shard_map.77.own), channel_id=1, source_target_pairs={{0,16},{1,17},{2,18},{3,19},{4,20},{5,21},{6,22},{7,23},{8,24},{9,... | collective-permute-start | bytes 393224 | tf_op jit(solution)/shard_map/ppermute | solution.py:31
  11.2 4.4 %collective-permute-start.4 = (bf16[64,256]{1,0:T(8,128)(2,1)S(1)}, bf16[64,256]{1,0:T(8,128)(2,1)S(1)}, u32[]{:S(2)}, u32[]{:S(2)}) collective-permute-start(bf16[64,256]{1,0:T(8,128)(2,1)S(1)} %get-tuple-element.36), channel_id=1, source_target_pairs={{0,12},{1,13},{2,14},{3,15},{4,8},{5,9},{6,10},{7,11},{8,4},{9,5},... | collective-permute-start | bytes 98312 | tf_op jit(solution)/shard_map/ppermute | solution.py:31
  14.0 1.7 %collective-permute-start.5 = (bf16[64,256]{1,0:T(8,128)(2,1)S(1)}, bf16[64,256]{1,0:T(8,128)(2,1)S(1)}, u32[]{:S(2)}, u32[]{:S(2)}) collective-permute-start(bf16[64,256]{1,0:T(8,128)(2,1)S(1)} %get-tuple-element.37), channel_id=1, source_target_pairs={{0,8},{1,9},{2,10},{3,11},{4,12},{5,13},{6,14},{7,15},{8,0},{9,1},... | collective-permute-start | bytes 98312 | tf_op jit(solution)/shard_map/ppermute | solution.py:31
  16.0 1.3 %collective-permute-start.6 = (bf16[64,256]{1,0:T(8,128)(2,1)S(1)}, bf16[64,256]{1,0:T(8,128)(2,1)S(1)}, u32[]{:S(2)}, u32[]{:S(2)}) collective-permute-start(bf16[64,256]{1,0:T(8,128)(2,1)S(1)} %get-tuple-element.40), channel_id=1, source_target_pairs={{0,8},{1,9},{2,10},{3,11},{4,12},{5,13},{6,14},{7,15},{8,0},{9,1},... | collective-permute-start | bytes 98312 | tf_op jit(solution)/shard_map/ppermute | solution.py:31
  17.5 4.3 %collective-permute-start.9 = (bf16[128,256]{1,0:T(8,128)(2,1)S(1)}, bf16[128,256]{1,0:T(8,128)(2,1)S(1)}, u32[]{:S(2)}, u32[]{:S(2)}) collective-permute-start(bf16[128,256]{1,0:T(8,128)(2,1)S(1)} %get-tuple-element.43.mine), channel_id=1, source_target_pairs={{0,16},{1,17},{2,18},{3,19},{4,20},{5,21},{6,22},{7,23},{8,24},{9,... | collective-permute-start | bytes 196616 | tf_op jit(solution)/shard_map/ppermute | solution.py:31
  19.1 3.0 %collective-permute-start.10 = (bf16[2,256,256]{2,1,0:T(8,128)(2,1)S(1)}, bf16[2,256,256]{2,1,0:T(8,128)(2,1)S(1)}, u32[]{:S(2)}, u32[]{:S(2)}) collective-permute-start(bf16[2,256,256]{2,1,0:T(8,128)(2,1)S(1)} %shard_map.82.product), channel_id=1, source_target_pairs={{0,8},{1,9},{2,10},{3,11},{4,12},{5,13},{6,14},{7,15},{8,0},{9,1},... | collective-permute-start | bytes 786440 | tf_op jit(solution)/shard_map/ppermute | solution.py:31
  19.1 2.9 %collective-permute-start.8 = (f32[64,256]{1,0:T(8,128)S(1)}, f32[64,256]{1,0:T(8,128)S(1)}, u32[]{:S(2)}, u32[]{:S(2)}) collective-permute-start(f32[64,256]{1,0:T(8,128)S(1)} %shard_map.84), channel_id=1, source_target_pairs={{0,8},{1,9},{2,10},{3,11},{4,12},{5,13},{6,14},{7,15},{8,0},{9,1},... | collective-permute-start | bytes 196616 | tf_op jit(solution)/shard_map/ppermute | solution.py:31
  22.0 1.3 %collective-permute-start.11 = (bf16[64,256]{1,0:T(8,128)(2,1)S(1)}, bf16[64,256]{1,0:T(8,128)(2,1)S(1)}, u32[]{:S(2)}, u32[]{:S(2)}) collective-permute-start(bf16[64,256]{1,0:T(8,128)(2,1)S(1)} %get-tuple-element.47.known), channel_id=1, source_target_pairs={{0,8},{1,9},{2,10},{3,11},{4,12},{5,13},{6,14},{7,15},{8,0},{9,1},... | collective-permute-start | bytes 98312 | tf_op jit(solution)/shard_map/ppermute | solution.py:31
  23.4 4.3 %collective-permute-start.12 = (bf16[64,256]{1,0:T(8,128)(2,1)S(1)}, bf16[64,256]{1,0:T(8,128)(2,1)S(1)}, u32[]{:S(2)}, u32[]{:S(2)}) collective-permute-start(bf16[64,256]{1,0:T(8,128)(2,1)S(1)} %shard_map.92), channel_id=1, source_target_pairs={{0,12},{1,13},{2,14},{3,15},{4,8},{5,9},{6,10},{7,11},{8,4},{9,5},... | collective-permute-start | bytes 98312 | tf_op jit(solution)/shard_map/ppermute | solution.py:31
  25.8 1.8 %collective-permute-start.13 = (bf16[64,256]{1,0:T(8,128)(2,1)S(1)}, bf16[64,256]{1,0:T(8,128)(2,1)S(1)}, u32[]{:S(2)}, u32[]{:S(2)}) collective-permute-start(bf16[64,256]{1,0:T(8,128)(2,1)S(1)} %shard_map.92), channel_id=1, source_target_pairs={{0,8},{1,9},{2,10},{3,11},{4,12},{5,13},{6,14},{7,15},{8,0},{9,1},... | collective-permute-start | bytes 98312 | tf_op jit(solution)/shard_map/ppermute | solution.py:31
  26.8 4.5 %collective-permute-start.16 = (f32[64,256]{1,0:T(8,128)S(1)}, f32[64,256]{1,0:T(8,128)S(1)}, u32[]{:S(2)}, u32[]{:S(2)}) collective-permute-start(f32[64,256]{1,0:T(8,128)S(1)} %shard_map.97), channel_id=1, source_target_pairs={{0,8},{1,9},{2,10},{3,11},{4,12},{5,13},{6,14},{7,15},{8,0},{9,1},... | collective-permute-start | bytes 196616 | tf_op jit(solution)/shard_map/ppermute | solution.py:31
  27.0 4.3 %collective-permute-start.17 = (bf16[2,256,256]{2,1,0:T(8,128)(2,1)S(1)}, bf16[2,256,256]{2,1,0:T(8,128)(2,1)S(1)}, u32[]{:S(2)}, u32[]{:S(2)}) collective-permute-start(bf16[2,256,256]{2,1,0:T(8,128)(2,1)S(1)} %shard_map.78.product), channel_id=1, source_target_pairs={{0,8},{1,9},{2,10},{3,11},{4,12},{5,13},{6,14},{7,15},{8,0},{9,1},... | collective-permute-start | bytes 786440 | tf_op jit(solution)/shard_map/ppermute | solution.py:31
  27.6 2.2 %copy-start.4 = (bf16[1,128,128]{2,1,0:T(8,128)(2,1)S(1)}, bf16[1,128,128]{2,1,0:T(8,128)(2,1)}, u32[]{:S(2)}) copy-start(bf16[1,128,128]{2,1,0:T(8,128)(2,1)} %param.7) | copy-start | bytes 98308
  27.8 3.5 %collective-permute-start.14 = (bf16[64,256]{1,0:T(8,128)(2,1)S(1)}, bf16[64,256]{1,0:T(8,128)(2,1)S(1)}, u32[]{:S(2)}, u32[]{:S(2)}) collective-permute-start(bf16[64,256]{1,0:T(8,128)(2,1)S(1)} %get-tuple-element.51), channel_id=1, source_target_pairs={{0,10},{1,11},{2,8},{3,9},{4,14},{5,15},{6,12},{7,13},{8,2},{9,3},... | collective-permute-start | bytes 98312 | tf_op jit(solution)/shard_map/ppermute | solution.py:31
  29.7 1.6 %collective-permute-start.15 = (bf16[64,256]{1,0:T(8,128)(2,1)S(1)}, bf16[64,256]{1,0:T(8,128)(2,1)S(1)}, u32[]{:S(2)}, u32[]{:S(2)}) collective-permute-start(bf16[64,256]{1,0:T(8,128)(2,1)S(1)} %get-tuple-element.51), channel_id=1, source_target_pairs={{0,8},{1,9},{2,10},{3,11},{4,12},{5,13},{6,14},{7,15},{8,0},{9,1},... | collective-permute-start | bytes 98312 | tf_op jit(solution)/shard_map/ppermute | solution.py:31
  31.5 3.4 %collective-permute-start.18 = (bf16[64,256]{1,0:T(8,128)(2,1)S(1)}, bf16[64,256]{1,0:T(8,128)(2,1)S(1)}, u32[]{:S(2)}, u32[]{:S(2)}) collective-permute-start(bf16[64,256]{1,0:T(8,128)(2,1)S(1)} %shard_map.98), channel_id=1, source_target_pairs={{0,9},{1,8},{2,11},{3,10},{4,13},{5,12},{6,15},{7,14},{8,1},{9,0},... | collective-permute-start | bytes 98312 | tf_op jit(solution)/shard_map/ppermute | solution.py:31
  32.9 2.1 %collective-permute-start.20 = (bf16[64,256]{1,0:T(8,128)(2,1)S(1)}, bf16[64,256]{1,0:T(8,128)(2,1)S(1)}, u32[]{:S(2)}, u32[]{:S(2)}) collective-permute-start(bf16[64,256]{1,0:T(8,128)(2,1)S(1)} %shard_map.98), channel_id=1, source_target_pairs={{0,8},{1,9},{2,10},{3,11},{4,12},{5,13},{6,14},{7,15},{8,0},{9,1},... | collective-permute-start | bytes 98312 | tf_op jit(solution)/shard_map/ppermute | solution.py:31
  33.2 1.7 %collective-permute-start.19 = (bf16[64,256]{1,0:T(8,128)(2,1)S(1)}, bf16[64,256]{1,0:T(8,128)(2,1)S(1)}, u32[]{:S(2)}, u32[]{:S(2)}) collective-permute-start(bf16[64,256]{1,0:T(8,128)(2,1)S(1)} %collective-permute-done.14), channel_id=1, source_target_pairs={{0,8},{1,9},{2,10},{3,11},{4,12},{5,13},{6,14},{7,15},{8,0},{9,1},... | collective-permute-start | bytes 98312 | tf_op jit(solution)/shard_map/ppermute | solution.py:31

commit v4 on v3

--- a/solution.py
+++ b/solution.py
@@ -107,6 +107,94 @@
     out[rows:] = (values[level + 1] - times_t(change, product[0])).astype(BF)
 
 
+def forward_first(residue, received, inverse, coupling, terms, values, delta, out, ahead):
+    change = (residue[0] - received[...].astype(F32)).astype(BF)
+    delta[...] = change
+    step = times_t(change, inverse[0]).astype(BF)
+    out[...] = (terms[1] + times_t(step, coupling[0, 1])).astype(BF)
+    ahead[...] = (values[1] - times_t(step, coupling[0, 0])).astype(BF)
+
+
+def forward_last(received, below, product_below, product, terms, values, delta, out, *, level):
+    residue = values[level] - times_t(below[...], product_below[0])
+    change = (residue - received[...].astype(F32)).astype(BF)
+    delta[...] = change
+    rows = change.shape[0]
+    out[:rows] = (terms[level + 1] + times_t(change, product[1])).astype(BF)
+    out[rows:] = (values[level + 1] - times_t(change, product[0])).astype(BF)
+
+
+def pack_top(own_gram, inverse, coupling, out, *, level):
+    width = inverse.shape[1]
+    out[:width] = own_gram[...]
+    for side in range(2):
+        made = times(coupling[level, side], inverse[level]).astype(BF)
+        out[(side + 1) * width : (side + 2) * width] = made
+
+
+def top_ends(terms, values, out):
+    cols = values.shape[1]
+    out[:cols] = values[values.shape[0] - 1].astype(BF)
+    out[cols:] = terms[terms.shape[0] - 1].astype(BF)
+
+
+def join_top(mine, mirror, ends, mirror_ends, inverse, out, *, level):
+    width = inverse.shape[1]
+    gram_mine, gram_mirror = mine[:width], mirror[:width]
+    own, other = mine[width : 2 * width], mine[2 * width : 3 * width]
+    mirror_own, mirror_other = mirror[width : 2 * width], mirror[2 * width : 3 * width]
+    first = times(gram_mine, own).astype(BF)
+    second = times(gram_mirror, other).astype(BF)
+    matrix = inverse[level]
+    out[:width] = (gram(matrix, matrix) + gram(own, first) + gram(other, second)).astype(BF)
+    out[width : 2 * width] = (gram(mirror_other, first) + gram(mirror_own, second)).astype(BF)
+    right, mirror_right = top_rights(ends, mirror_ends)
+    out[2 * width :] = (-times(right, first) - times(mirror_right, second)).astype(BF)
+
+
+def top_rights(mine, mirror):
+    cols = mine.shape[0] // 2
+    right = mine[:cols].astype(F32) - mirror[cols:].astype(F32)
+    mirror_right = mirror[:cols].astype(F32) - mine[cols:].astype(F32)
+    return right.astype(BF), mirror_right.astype(BF)
+
+
+def join_own(mine, mate, joined, joined_mate, out, delta):
+    rows, width = out.shape[1], joined.shape[1]
+    for at, (a, b, matrices) in enumerate(((mine, mate, joined), (mate, mine, joined_mate))):
+        change = (a[rows:].astype(F32) - b[:rows].astype(F32)).astype(BF)
+        delta[at] = change
+        out[at] = times(change, matrices[:width]) + matrices[2 * width :].astype(F32)
+
+
+def join(theirs, across, part, joined, joined_mate, solved, product, block, block_mate, delta, below, *, home):
+    rows, width = part.shape[1], joined.shape[1]
+    found = []
+    pairs = ((theirs, across, joined), (across, theirs, joined_mate))
+    for at, (a, b, matrices) in enumerate(pairs):
+        change = (a[rows:].astype(F32) - b[:rows].astype(F32)).astype(BF)
+        value = part[at] + times(change, matrices[width : 2 * width])
+        found.append(value.astype(BF))
+        if at == 0:
+            block[...] = value
+            delta[0] = change
+    block_mate[...] = found[1]
+    own, other = found if home else found[::-1]
+    below[...] = (solved[...] - times(own, product[0]) - times(other, product[1])).astype(BF)
+
+
+def top_blocks(mine, mirror, ends, mirror_ends, delta, delta_mirror, out, mirrored):
+    width = out.shape[1]
+    right, mirror_right = top_rights(ends, mirror_ends)
+    change, other = delta[0], delta_mirror[0]
+    own = right.astype(F32) - times_t(change, mine[width : 2 * width])
+    own = own - times_t(other, mirror[2 * width : 3 * width])
+    theirs = mirror_right.astype(F32) - times_t(other, mirror[width : 2 * width])
+    theirs = theirs - times_t(change, mine[2 * width : 3 * width])
+    out[...] = times(own.astype(BF), mine[:width])
+    mirrored[...] = times(theirs.astype(BF), mirror[:width]).astype(BF)
+
+
 def solve(delta, inverse, solved, *, level):
     step = times_t(delta[...], inverse[level]).astype(BF)
     solved[...] = times(step, inverse[level])
@@ -196,20 +284,35 @@
     terms = jnp.einsum("kwn,rn->krw", leaf_cpl, leaf.astype(BF), preferred_element_type=F32)
     received = send(terms[0].astype(BF), 0)
     product, ahead, solved = [None] * below_top, [None] * below_top, [None] * below_top
+    joined = levels == core + 2 and core >= 3
     own_gram = call(top_gram, [((width, width), BF)], inverse)
-    inverse = after(inverse, own_gram)
-    for level in range(below_top):
+    inverse_later = after(inverse, own_gram)
+    if joined:
+        pack = call(
+            pack_top, [((3 * width, width), BF)], own_gram, inverse_later, coupling, level=core
+        )
+        mirror_pack = send(pack, below_top)
+        inverse_later = after(inverse, pack)
+        ends = call(top_ends, [((2 * cols, width), BF)], terms, values)
+    for level in range(core if joined else below_top):
         if at_home[level]:
-            product[level] = call(products, [pair], inverse, coupling, level=level, cost=1 if level < 2 else 1)
+            product[level] = call(products, [pair], inverse_later, coupling, level=level, cost=(6, 1, 1)[min(level, 2)])
         else:
             product[level], ahead[level] = call(
-                products_ahead, [pair, ((width + cols, width), BF)], inverse, coupling, terms, level=level
+                products_ahead, [pair, ((width + cols, width), BF)],
+                inverse_later, coupling, terms, level=level,
             )
 
     residue, change = values, None
-    for level in range(below_top):
+    for level in range(core if joined else below_top):
         below = change
-        if level == levels - 2:
+        if joined and level == core - 1:
+            change, out = call(
+                forward_last, [vec_bf, ((2 * cols, width), BF)], arrived(received), below,
+                product[level - 1], product[level], terms, values, level=level, cost=4,
+            )
+            received = send(out, below_top, True)
+        elif level == levels - 2:
             received, mirror_gram = lax.optimization_barrier((received, mirror_gram))
             change, out = call(
                 forward_top, [vec_bf, ((2 * cols, width), BF)],
@@ -219,12 +322,21 @@
         else:
             across = first_across <= level + 1 < core
             if not at_home[level]:
-                change, out = call(forward_mate, [vec_bf, vec_bf], arrived(received), residue, ahead[level])
+                change, out = call(
+                    forward_mate, [vec_bf, vec_bf], arrived(received), residue, ahead[level], cost=2
+                )
+                if joined and level == core - 2:
+                    mirror_ends = send(after(ends, out), below_top)
             elif level and not at_home[level - 1]:
                 change, out = call(
                     forward_back, [vec_bf, vec_bf], arrived(received), below,
                     product[level - 1], product[level], terms, values, level=level, cost=1,
                 )
+            elif level == 0 and not at_home[1]:
+                change, out, residue = call(
+                    forward_first, [vec_bf, vec_bf, vec_bf],
+                    residue, received, inverse, coupling, terms, values,
+                )
             elif not at_home[level + 1]:
                 change, out, residue = call(
                     forward_ahead, [vec_bf, vec_bf, vec_bf],
@@ -235,7 +347,7 @@
                     forward, [vec_bf, vec_bf], residue, received, product[level], terms, level=level
                 )
             received = send(out, level + 1, across)
-            if level == 0:
+            if level == 0 and not joined:
                 mirror_gram = send(after(own_gram, out), below_top)
             if not at_home[level]:
                 change = mate(change)
@@ -246,8 +358,7 @@
                 residue = call(
                     forward_residue, [slab], change, product[level], values, level=level, cost=0
                 )
-        solved[level] = call(solve, [vec], change, inverse, level=level)
-    top_pair = call(top_products, [pair], own_gram, mirror_gram, product[-1], cost=8)
+        solved[level] = call(solve, [vec], change, inverse, level=level, cost=6 if level == core - 1 else 1)
     leaf_prod = jnp.einsum("kwn,nm->kwm", leaf_cpl, leaf_inv, preferred_element_type=F32).astype(BF)
 
     mates = [level for level in range(core) if level % 2 == 0]
@@ -255,14 +366,50 @@
         product[level] = mate(after(product[level], out))
         solved[level] = mate(after(solved[level], out))
     blocks, mirrored = [None] * levels, [None] * levels
-    block, block_bf, deltas = call(
-        top, [vec, vec_bf, ((2, cols, width), BF)], out, received, top_pair, solved[-1]
-    )
-    blocks[levels - 2] = block
-    received = mirrored[levels - 2] = send(block_bf, levels - 2)
-    blocks[-1], mirrored[-1] = call(top_values, [vec, vec_bf], deltas, own_gram, mirror_gram)
+    if joined:
+        out_mate = mate(out)
+        mirror_pack = after(mirror_pack, out)
+        matrices = call(
+            join_top, [((2 * width + cols, width), BF)],
+            pack, mirror_pack, ends, mirror_ends, inverse, level=core,
+        )
+        matrices_mate = mate(matrices)
+        both, both_bf = ((2, cols, width), F32), ((2, cols, width), BF)
+        part, delta = call(join_own, [both, both_bf], out, out_mate, matrices, matrices_mate)
+        theirs = mate(received)
+        blocks[core], mirrored[core], delta_mirror, block_bf = call(
+            join, [vec, vec_bf, ((1, cols, width), BF), vec_bf],
+            theirs, received, part, matrices, matrices_mate, solved[core - 1], product[core - 1],
+            home=core - 1 not in mates,
+        )
+        blocks[-1], mirrored[-1] = call(
+            top_blocks, [vec, vec_bf], pack, mirror_pack, ends, mirror_ends, delta, delta_mirror
+        )
+        if core - 1 not in mates:
+            blocks[core - 1] = block_bf
+        solved_above = core - 1
+    else:
+        top_pair = call(top_products, [pair], own_gram, mirror_gram, product[-1], cost=8)
+        block, block_bf, deltas = call(
+            top, [vec, vec_bf, ((2, cols, width), BF)], out, received, top_pair, solved[-1]
+        )
+        blocks[levels - 2] = block
+        received = mirrored[levels - 2] = send(block_bf, levels - 2)
+        blocks[-1], mirrored[-1] = call(top_values, [vec, vec_bf], deltas, own_gram, mirror_gram)
+        solved_above = levels - 2
     late = [0]
-    for level in reversed(range(levels - 2)):
+    def pass_on(level, home):
+        received = send(block_bf, level, level < core)
+        if home == (level < core):
+            mirrored[level] = mate(received)
+            late.append(level)
+        else:
+            mirrored[level] = received
+        return received
+
+    if joined:
+        received = pass_on(solved_above, solved_above not in mates)
+    for level in reversed(range(solved_above)):
         home = level not in mates
         outs = [vec, vec_bf] if home else [vec_bf]
         if level + 1 >= core:
@@ -278,12 +425,7 @@
             blocks[level], block_bf = made
         else:
             block_bf = made
-        received = send(block_bf, level, level < core)
-        if home == (level < core):
-            mirrored[level] = mate(received)
-            late.append(level)
-        else:
-            mirrored[level] = received
+        received = pass_on(level, home)
     if 0 in mates:
         blocks[0] = mate(block_bf)
     early = tuple(level for level in range(levels) if level not in late)

time: 35.9 us -> 34.9 us (0.972)
  waiting for transfers between devices: 8.4 us -> 5.39 us
  starting transfers between devices: 19.3 us -> 21.2 us
    ppermute x21 -> x23, waiting for transfers between devices: 8.4 us -> 5.39 us  [exchange(): return lax.ppermute(value, ('gx', 'gy'), pairs)]
    ppermute x21 -> x23, starting transfers between devices: 19.3 us -> 21.2 us  [exchange(): return lax.ppermute(value, ('gx', 'gy'), pairs)]
    pallas_call x23 -> x20, Pallas kernels: 5.59 us -> 5.7 us  [call(): pl.pallas_call(functools.partial(body, **static), out_shape=[jax.ShapeDty...]
  transfers between devices with their start and end apart: 21 -> 23, of which waited for: 9 -> 8; matrix products, arithmetic and copies ran while one was open for 1% -> 1% of each run, Pallas kernels for 11% -> 13%
where the time goes in v4:
time: 34.9 us; the launch traced here: 34.8 us
  starting transfers between devices  21.2 us (61%)
  Pallas kernels  5.7 us (16%)
  waiting for transfers between devices  5.39 us (15%)
  matrix products  1.53 us (4%)
  between operations  0.89 us (3%)
    ppermute x23, starting transfers between devices, exchange(): return lax.ppermute(value, ('gx', 'gy'), pairs)  21.2 us
    pallas_call x20, Pallas kernels, call(): pl.pallas_call(functools.partial(body, **static), out_shape=[jax.ShapeDty...  5.7 us
    ppermute x23, waiting for transfers between devices, exchange(): return lax.ppermute(value, ('gx', 'gy'), pairs)  5.39 us
    dot_general x1, matrix products, times_t(): lax.dot_general(values, matrix, (((1,), (1,)), ((), ())), preferred_eleme...  1.04 us
  transfers between devices with their start and end apart: 23, of which 8 were waited for; matrix products, arithmetic and copies ran while one was open for 1% of the time, Pallas kernels for 13%

profile of v4, /device:TPU:0, one launch (start us, length us, event | category | flops | bytes accessed | tf_op | source)
XLA Modules:
  0.0 34.8 jit_solution(16534523025124963327)
XLA Ops:
  0.7 1.0 %fusion.6.leaf = f32[64,128]{1,0:T(8,128)S(1)} fusion(f32[128,64]{0,1:T(8,128)} %param.6, bf16[1,128,128]{2,1,0:T(8,128)(2,1)} %param.7), kind=kOutput, calls=%fused_computation.9 | convolution fusion | flops 2105344 | bytes 98304 | tf_op jit(solution)/shard_map/dot_general | solution.py:20
  1.7 0.3 convolution_bitcast_fusion.terms
  2.0 3.0 %collective-permute-start = (bf16[64,256]{1,0:T(8,128)(2,1)S(1)}, bf16[64,256]{1,0:T(8,128)(2,1)S(1)}, u32[]{:S(2)}, u32[]{:S(2)}) collective-permute-start(bf16[64,256]{1,0:T(8,128)(2,1)S(1)} %fusion.2), channel_id=1, source_target_pairs={{0,1},{1,0},{2,3},{3,2},{4,5},{5,4},{6,7},{7,6},{8,9},{9,8},{10,11... | collective-permute-start | bytes 98312 | tf_op jit(solution)/shard_map/ppermute | solution.py:31
  5.5 1.6 %collective-permute-start.9 = (bf16[768,256]{1,0:T(8,128)(2,1)S(1)}, bf16[768,256]{1,0:T(8,128)(2,1)S(1)}, u32[]{:S(2)}, u32[]{:S(2)}) collective-permute-start(bf16[768,256]{1,0:T(8,128)(2,1)S(1)} %shard_map.79.mine), channel_id=1, source_target_pairs={{0,16},{1,17},{2,18},{3,19},{4,20},{5,21},{6,22},{7,23},{8,24},{9,... | collective-permute-start | bytes 1179656 | tf_op jit(solution)/shard_map/ppermute | solution.py:31
  7.3 0.4 %shard_map.77 = (bf16[64,256]{1,0:T(8,128)(2,1)S(1)}, bf16[64,256]{1,0:T(8,128)(2,1)S(1)}, bf16[64,256]{1,0:T(8,128)(2,1)S(1)}) custom-call(f32[5,64,256]{2,1,0:T(8,128)S(1)} %bitcast.42, bf16[64,256]{1,0:T(8,128)(2,1)S(1)} %collective-permute-done.received, bf16[5,256,256]{2,1,0:T(8,128)(2,1)S(1)} %bitcast.35, bf16[4,2,256,256]{3,2,1,0:T(8,128)(2,1)S(1)} %bitcast.29, ...), custom_call_target="tpu_custom_call" | custom-call | flops 300000000 | bytes 2719744 | tf_op jit(solution)/shard_map/pallas_call | solution.py:36
  7.7 1.8 %collective-permute-start.1 = (bf16[64,256]{1,0:T(8,128)(2,1)S(1)}, bf16[64,256]{1,0:T(8,128)(2,1)S(1)}, u32[]{:S(2)}, u32[]{:S(2)}) collective-permute-start(bf16[64,256]{1,0:T(8,128)(2,1)S(1)} %get-tuple-element.32), channel_id=1, source_target_pairs={{0,10},{1,11},{2,8},{3,9},{4,14},{5,15},{6,12},{7,13},{8,2},{9,3},... | collective-permute-start | bytes 98312 | tf_op jit(solution)/shard_map/ppermute | solution.py:31
  9.6 1.6 %collective-permute-done.1 = bf16[64,256]{1,0:T(8,128)(2,1)S(1)} collective-permute-done((bf16[64,256]{1,0:T(8,128)(2,1)S(1)}, bf16[64,256]{1,0:T(8,128)(2,1)S(1)}, u32[]{:S(2)}, u32[]{:S(2)}) %collective-permute-start.1) | collective-permute-done | bytes 32800 | tf_op jit(solution)/shard_map/ppermute | solution.py:31
  11.3 3.1 %collective-permute-start.4 = (bf16[64,256]{1,0:T(8,128)(2,1)S(1)}, bf16[64,256]{1,0:T(8,128)(2,1)S(1)}, u32[]{:S(2)}, u32[]{:S(2)}) collective-permute-start(bf16[64,256]{1,0:T(8,128)(2,1)S(1)} %get-tuple-element.38), channel_id=1, source_target_pairs={{0,12},{1,13},{2,14},{3,15},{4,8},{5,9},{6,10},{7,11},{8,4},{9,5},... | collective-permute-start | bytes 98312 | tf_op jit(solution)/shard_map/ppermute | solution.py:31
  14.6 1.6 %collective-permute-start.10 = (bf16[128,256]{1,0:T(8,128)(2,1)S(1)}, bf16[128,256]{1,0:T(8,128)(2,1)S(1)}, u32[]{:S(2)}, u32[]{:S(2)}) collective-permute-start(bf16[128,256]{1,0:T(8,128)(2,1)S(1)} %shard_map.84.ends), channel_id=1, source_target_pairs={{0,16},{1,17},{2,18},{3,19},{4,20},{5,21},{6,22},{7,23},{8,24},{9,... | collective-permute-start | bytes 196616 | tf_op jit(solution)/shard_map/ppermute | solution.py:31
  16.2 0.4 %shard_map.83 = (bf16[64,256]{1,0:T(8,128)(2,1)S(1)}, bf16[128,256]{1,0:T(8,128)(2,1)S(1)}) custom-call(f32[64,256]{1,0:T(8,128)S(1)} %convert_element_type.34.received, bf16[64,256]{1,0:T(8,128)(2,1)S(1)} %collective-permute-done.5.below.delta, bf16[2,256,256]{2,1,0:T(8,128)(2,1)S(1)} %get-tuple-element.40.product_below.product, ...), custom_call_target="tpu_custom_call" | custom-call | flops 1200000000 | bytes 1277952 | tf_op jit(solution)/shard_map/pallas_call | solution.py:36
  16.6 0.3 collective-permute-start.8
  16.9 1.2 %collective-permute-start.6 = (bf16[128,256]{1,0:T(8,128)(2,1)S(1)}, bf16[128,256]{1,0:T(8,128)(2,1)S(1)}, u32[]{:S(2)}, u32[]{:S(2)}) collective-permute-start(bf16[128,256]{1,0:T(8,128)(2,1)S(1)} %get-tuple-element.41.mine), channel_id=1, source_target_pairs={{0,24},{1,25},{2,26},{3,27},{4,28},{5,29},{6,30},{7,31},{8,16},{9,... | collective-permute-start | bytes 196616 | tf_op jit(solution)/shard_map/ppermute | solution.py:31
  18.1 0.4 %collective-permute-start.13 = (bf16[2,256,256]{2,1,0:T(8,128)(2,1)S(1)}, bf16[2,256,256]{2,1,0:T(8,128)(2,1)S(1)}, u32[]{:S(2)}, u32[]{:S(2)}) collective-permute-start(bf16[2,256,256]{2,1,0:T(8,128)(2,1)S(1)} %shard_map.82.product), channel_id=1, source_target_pairs={{0,8},{1,9},{2,10},{3,11},{4,12},{5,13},{6,14},{7,15},{8,0},{9,1},... | collective-permute-start | bytes 786440 | tf_op jit(solution)/shard_map/ppermute | solution.py:31
  18.5 0.7 %collective-permute-done.10.mirror_ends = bf16[128,256]{1,0:T(8,128)(2,1)S(1)} collective-permute-done((bf16[128,256]{1,0:T(8,128)(2,1)S(1)}, bf16[128,256]{1,0:T(8,128)(2,1)S(1)}, u32[]{:S(2)}, u32[]{:S(2)}) %collective-permute-start.10) | collective-permute-done | bytes 65568 | tf_op jit(solution)/shard_map/ppermute | solution.py:31
  19.2 0.6 %shard_map.85.joined = bf16[576,256]{1,0:T(8,128)(2,1)S(1)} custom-call(bf16[768,256]{1,0:T(8,128)(2,1)S(1)} %shard_map.79.mine, bf16[768,256]{1,0:T(8,128)(2,1)S(1)} %collective-permute-done.9.mirror, bf16[128,256]{1,0:T(8,128)(2,1)S(1)} %shard_map.84.ends, bf16[128,256]{1,0:T(8,128)(2,1)S(1)} %collective-permute-done.10.mirror_ends, ...), custom_call_target="tpu_custom_call" | custom-call | flops 300000000 | bytes 1572864 | tf_op jit(solution)/shard_map/pallas_call | solution.py:36
  19.9 0.3 shard_map.87
  20.2 0.6 %collective-permute-start.12 = (f32[64,256]{1,0:T(8,128)S(1)}, f32[64,256]{1,0:T(8,128)S(1)}, u32[]{:S(2)}, u32[]{:S(2)}) collective-permute-start(f32[64,256]{1,0:T(8,128)S(1)} %shard_map.87), channel_id=1, source_target_pairs={{0,8},{1,9},{2,10},{3,11},{4,12},{5,13},{6,14},{7,15},{8,0},{9,1},... | collective-permute-start | bytes 196616 | tf_op jit(solution)/shard_map/ppermute | solution.py:31
  21.6 0.5 %collective-permute-done.7.theirs = bf16[128,256]{1,0:T(8,128)(2,1)S(1)} collective-permute-done((bf16[128,256]{1,0:T(8,128)(2,1)S(1)}, bf16[128,256]{1,0:T(8,128)(2,1)S(1)}, u32[]{:S(2)}, u32[]{:S(2)}) %collective-permute-start.7) | collective-permute-done | bytes 65568 | tf_op jit(solution)/shard_map/ppermute | solution.py:31
  22.2 0.3 shard_map.88
  22.4 2.5 %collective-permute-start.14 = (bf16[64,256]{1,0:T(8,128)(2,1)S(1)}, bf16[64,256]{1,0:T(8,128)(2,1)S(1)}, u32[]{:S(2)}, u32[]{:S(2)}) collective-permute-start(bf16[64,256]{1,0:T(8,128)(2,1)S(1)} %get-tuple-element.48), channel_id=1, source_target_pairs={{0,12},{1,13},{2,14},{3,15},{4,8},{5,9},{6,10},{7,11},{8,4},{9,5},... | collective-permute-start | bytes 98312 | tf_op jit(solution)/shard_map/ppermute | solution.py:31
  25.0 0.4 %collective-permute-start.15 = (bf16[64,256]{1,0:T(8,128)(2,1)S(1)}, bf16[64,256]{1,0:T(8,128)(2,1)S(1)}, u32[]{:S(2)}, u32[]{:S(2)}) collective-permute-start(bf16[64,256]{1,0:T(8,128)(2,1)S(1)} %get-tuple-element.48), channel_id=1, source_target_pairs={{0,8},{1,9},{2,10},{3,11},{4,12},{5,13},{6,14},{7,15},{8,0},{9,1},... | collective-permute-start | bytes 98312 | tf_op jit(solution)/shard_map/ppermute | solution.py:31
  25.3 0.3 shard_map.93
  25.9 0.4 %collective-permute-start.18 = (f32[64,256]{1,0:T(8,128)S(1)}, f32[64,256]{1,0:T(8,128)S(1)}, u32[]{:S(2)}, u32[]{:S(2)}) collective-permute-start(f32[64,256]{1,0:T(8,128)S(1)} %shard_map.93), channel_id=1, source_target_pairs={{0,8},{1,9},{2,10},{3,11},{4,12},{5,13},{6,14},{7,15},{8,0},{9,1},... | collective-permute-start | bytes 196616 | tf_op jit(solution)/shard_map/ppermute | solution.py:31
  26.2 0.3 shard_map.91.solved
  27.0 1.6 %collective-permute-start.16 = (bf16[64,256]{1,0:T(8,128)(2,1)S(1)}, bf16[64,256]{1,0:T(8,128)(2,1)S(1)}, u32[]{:S(2)}, u32[]{:S(2)}) collective-permute-start(bf16[64,256]{1,0:T(8,128)(2,1)S(1)} %get-tuple-element.53), channel_id=1, source_target_pairs={{0,10},{1,11},{2,8},{3,9},{4,14},{5,15},{6,12},{7,13},{8,2},{9,3},... | collective-permute-start | bytes 98312 | tf_op jit(solution)/shard_map/ppermute | solution.py:31
  28.6 0.4 %collective-permute-start.17 = (bf16[64,256]{1,0:T(8,128)(2,1)S(1)}, bf16[64,256]{1,0:T(8,128)(2,1)S(1)}, u32[]{:S(2)}, u32[]{:S(2)}) collective-permute-start(bf16[64,256]{1,0:T(8,128)(2,1)S(1)} %get-tuple-element.53), channel_id=1, source_target_pairs={{0,8},{1,9},{2,10},{3,11},{4,12},{5,13},{6,14},{7,15},{8,0},{9,1},... | collective-permute-start | bytes 98312 | tf_op jit(solution)/shard_map/ppermute | solution.py:31
  29.2 1.1 %collective-permute-done.16 = bf16[64,256]{1,0:T(8,128)(2,1)S(1)} collective-permute-done((bf16[64,256]{1,0:T(8,128)(2,1)S(1)}, bf16[64,256]{1,0:T(8,128)(2,1)S(1)}, u32[]{:S(2)}, u32[]{:S(2)}) %collective-permute-start.16) | collective-permute-done | bytes 32800 | tf_op jit(solution)/shard_map/ppermute | solution.py:31
  30.6 1.4 %collective-permute-start.20 = (bf16[64,256]{1,0:T(8,128)(2,1)S(1)}, bf16[64,256]{1,0:T(8,128)(2,1)S(1)}, u32[]{:S(2)}, u32[]{:S(2)}) collective-permute-start(bf16[64,256]{1,0:T(8,128)(2,1)S(1)} %shard_map.95), channel_id=1, source_target_pairs={{0,9},{1,8},{2,11},{3,10},{4,13},{5,12},{6,15},{7,14},{8,1},{9,0},... | collective-permute-start | bytes 98312 | tf_op jit(solution)/shard_map/ppermute | solution.py:31
  32.2 0.3 collective-permute-start.21
  32.5 0.4 %shard_map.89 = (f32[64,256]{1,0:T(8,128)S(1)}, bf16[64,256]{1,0:T(8,128)(2,1)S(1)}) custom-call(bf16[768,256]{1,0:T(8,128)(2,1)S(1)} %shard_map.79.mine, bf16[768,256]{1,0:T(8,128)(2,1)S(1)} %collective-permute-done.9.mirror, bf16[128,256]{1,0:T(8,128)(2,1)S(1)} %shard_map.84.ends, bf16[128,256]{1,0:T(8,128)(2,1)S(1)} %collective-permute-done.10.mirror_ends, ...), custom_call_target="tpu_custom_call" | custom-call | flops 300000000 | bytes 1015808 | tf_op jit(solution)/shard_map/pallas_call | solution.py:36
  33.0 0.9 %collective-permute-done.20 = bf16[64,256]{1,0:T(8,128)(2,1)S(1)} collective-permute-done((bf16[64,256]{1,0:T(8,128)(2,1)S(1)}, bf16[64,256]{1,0:T(8,128)(2,1)S(1)}, u32[]{:S(2)}, u32[]{:S(2)}) %collective-permute-start.20) | collective-permute-done | bytes 32800 | tf_op jit(solution)/shard_map/ppermute | solution.py:31
  34.0 0.8 %shard_map.96 = (f32[64,128]{1,0:T(8,128)}, f32[5,64,256]{2,1,0:T(8,128)}) custom-call(f32[64,128]{1,0:T(8,128)S(1)} %shard_map.90.part, bf16[5,256,128]{2,1,0:T(8,128)(2,1)S(1)} %convolution_convert_fusion.leaf_products, f32[64,256]{1,0:T(8,128)S(1)} %convert_element_type.37.refs_0_, bf16[64,256]{1,0:T(8,128)(2,1)S(1)} %collective-permute-done.21.refs_1_, ...), custom_call_target="tpu_custom_call" | custom-call | flops 300000000 | bytes 720896 | tf_op jit(solution)/shard_map/pallas_call | solution.py:36
  (53 shorter events, 3.7 us)
Async XLA Ops:
  0.6 1.1 %copy-start = (bf16[1,5,256,128]{3,2,1,0:T(8,128)(2,1)S(1)}, bf16[1,5,256,128]{3,2,1,0:T(8,128)(2,1)}, u32[]{:S(2)}) copy-start(bf16[1,5,256,128]{3,2,1,0:T(8,128)(2,1)} %param.8) | copy-start | bytes 983044
  0.6 4.3 %copy-start.2 = (bf16[1,5,256,256]{3,2,1,0:T(8,128)(2,1)S(1)}, bf16[1,5,256,256]{3,2,1,0:T(8,128)(2,1)}, u32[]{:S(2)}) copy-start(bf16[1,5,256,256]{3,2,1,0:T(8,128)(2,1)} %param.10) | copy-start | bytes 1966084
  0.7 4.6 %copy-start.1 = (bf16[1,4,1,2,256,256]{5,4,3,2,1,0:T(8,128)(2,1)S(1)}, bf16[1,4,1,2,256,256]{5,4,3,2,1,0:T(8,128)(2,1)}, u32[]{:S(2)}) copy-start(bf16[1,4,1,2,256,256]{5,4,3,2,1,0:T(8,128)(2,1)} %param.11) | copy-start | bytes 3145732
  2.0 5.3 %collective-permute-start = (bf16[64,256]{1,0:T(8,128)(2,1)S(1)}, bf16[64,256]{1,0:T(8,128)(2,1)S(1)}, u32[]{:S(2)}, u32[]{:S(2)}) collective-permute-start(bf16[64,256]{1,0:T(8,128)(2,1)S(1)} %fusion.2), channel_id=1, source_target_pairs={{0,1},{1,0},{2,3},{3,2},{4,5},{5,4},{6,7},{7,6},{8,9},{9,8},{10,11... | collective-permute-start | bytes 98312 | tf_op jit(solution)/shard_map/ppermute | solution.py:31
  5.5 1.8 %copy-start.3 = (f32[1,5,256,64]{2,3,1,0:T(8,128)S(1)}, f32[1,5,256,64]{2,3,1,0:T(8,128)}, u32[]{:S(2)}) copy-start(f32[1,5,256,64]{2,3,1,0:T(8,128)} %param.9) | copy-start | bytes 983044
  5.5 13.0 %collective-permute-start.9 = (bf16[768,256]{1,0:T(8,128)(2,1)S(1)}, bf16[768,256]{1,0:T(8,128)(2,1)S(1)}, u32[]{:S(2)}, u32[]{:S(2)}) collective-permute-start(bf16[768,256]{1,0:T(8,128)(2,1)S(1)} %shard_map.79.mine), channel_id=1, source_target_pairs={{0,16},{1,17},{2,18},{3,19},{4,20},{5,21},{6,22},{7,23},{8,24},{9,... | collective-permute-start | bytes 1179656 | tf_op jit(solution)/shard_map/ppermute | solution.py:31
  7.7 3.5 %collective-permute-start.3 = (bf16[320,256]{1,0:T(8,128)(2,1)S(1)}, bf16[320,256]{1,0:T(8,128)(2,1)S(1)}, u32[]{:S(2)}, u32[]{:S(2)}) collective-permute-start(bf16[320,256]{1,0:T(8,128)(2,1)S(1)} %get-tuple-element.37), channel_id=1, source_target_pairs={{0,8},{1,9},{2,10},{3,11},{4,12},{5,13},{6,14},{7,15},{8,0},{9,1},... | collective-permute-start | bytes 491528 | tf_op jit(solution)/shard_map/ppermute | solution.py:31
  7.7 3.4 %collective-permute-start.1 = (bf16[64,256]{1,0:T(8,128)(2,1)S(1)}, bf16[64,256]{1,0:T(8,128)(2,1)S(1)}, u32[]{:S(2)}, u32[]{:S(2)}) collective-permute-start(bf16[64,256]{1,0:T(8,128)(2,1)S(1)} %get-tuple-element.32), channel_id=1, source_target_pairs={{0,10},{1,11},{2,8},{3,9},{4,14},{5,15},{6,12},{7,13},{8,2},{9,3},... | collective-permute-start | bytes 98312 | tf_op jit(solution)/shard_map/ppermute | solution.py:31
  9.5 1.6 %collective-permute-start.2 = (bf16[64,256]{1,0:T(8,128)(2,1)S(1)}, bf16[64,256]{1,0:T(8,128)(2,1)S(1)}, u32[]{:S(2)}, u32[]{:S(2)}) collective-permute-start(bf16[64,256]{1,0:T(8,128)(2,1)S(1)} %get-tuple-element.33), channel_id=1, source_target_pairs={{0,8},{1,9},{2,10},{3,11},{4,12},{5,13},{6,14},{7,15},{8,0},{9,1},... | collective-permute-start | bytes 98312 | tf_op jit(solution)/shard_map/ppermute | solution.py:31
  11.3 4.9 %collective-permute-start.4 = (bf16[64,256]{1,0:T(8,128)(2,1)S(1)}, bf16[64,256]{1,0:T(8,128)(2,1)S(1)}, u32[]{:S(2)}, u32[]{:S(2)}) collective-permute-start(bf16[64,256]{1,0:T(8,128)(2,1)S(1)} %get-tuple-element.38), channel_id=1, source_target_pairs={{0,12},{1,13},{2,14},{3,15},{4,8},{5,9},{6,10},{7,11},{8,4},{9,5},... | collective-permute-start | bytes 98312 | tf_op jit(solution)/shard_map/ppermute | solution.py:31
  14.4 1.8 %collective-permute-start.5 = (bf16[64,256]{1,0:T(8,128)(2,1)S(1)}, bf16[64,256]{1,0:T(8,128)(2,1)S(1)}, u32[]{:S(2)}, u32[]{:S(2)}) collective-permute-start(bf16[64,256]{1,0:T(8,128)(2,1)S(1)} %get-tuple-element.39), channel_id=1, source_target_pairs={{0,8},{1,9},{2,10},{3,11},{4,12},{5,13},{6,14},{7,15},{8,0},{9,1},... | collective-permute-start | bytes 98312 | tf_op jit(solution)/shard_map/ppermute | solution.py:31
  14.6 4.6 %collective-permute-start.10 = (bf16[128,256]{1,0:T(8,128)(2,1)S(1)}, bf16[128,256]{1,0:T(8,128)(2,1)S(1)}, u32[]{:S(2)}, u32[]{:S(2)}) collective-permute-start(bf16[128,256]{1,0:T(8,128)(2,1)S(1)} %shard_map.84.ends), channel_id=1, source_target_pairs={{0,16},{1,17},{2,18},{3,19},{4,20},{5,21},{6,22},{7,23},{8,24},{9,... | collective-permute-start | bytes 196616 | tf_op jit(solution)/shard_map/ppermute | solution.py:31
  16.6 4.7 %collective-permute-start.8 = (bf16[128,256]{1,0:T(8,128)(2,1)S(1)}, bf16[128,256]{1,0:T(8,128)(2,1)S(1)}, u32[]{:S(2)}, u32[]{:S(2)}) collective-permute-start(bf16[128,256]{1,0:T(8,128)(2,1)S(1)} %get-tuple-element.41.mine), channel_id=1, source_target_pairs={{0,8},{1,9},{2,10},{3,11},{4,12},{5,13},{6,14},{7,15},{8,0},{9,1},... | collective-permute-start | bytes 196616 | tf_op jit(solution)/shard_map/ppermute | solution.py:31
  16.9 4.0 %collective-permute-start.6 = (bf16[128,256]{1,0:T(8,128)(2,1)S(1)}, bf16[128,256]{1,0:T(8,128)(2,1)S(1)}, u32[]{:S(2)}, u32[]{:S(2)}) collective-permute-start(bf16[128,256]{1,0:T(8,128)(2,1)S(1)} %get-tuple-element.41.mine), channel_id=1, source_target_pairs={{0,24},{1,25},{2,26},{3,27},{4,28},{5,29},{6,30},{7,31},{8,16},{9,... | collective-permute-start | bytes 196616 | tf_op jit(solution)/shard_map/ppermute | solution.py:31
  18.1 4.1 %collective-permute-start.13 = (bf16[2,256,256]{2,1,0:T(8,128)(2,1)S(1)}, bf16[2,256,256]{2,1,0:T(8,128)(2,1)S(1)}, u32[]{:S(2)}, u32[]{:S(2)}) collective-permute-start(bf16[2,256,256]{2,1,0:T(8,128)(2,1)S(1)} %shard_map.82.product), channel_id=1, source_target_pairs={{0,8},{1,9},{2,10},{3,11},{4,12},{5,13},{6,14},{7,15},{8,0},{9,1},... | collective-permute-start | bytes 786440 | tf_op jit(solution)/shard_map/ppermute | solution.py:31
  19.8 1.6 %collective-permute-start.11 = (bf16[576,256]{1,0:T(8,128)(2,1)S(1)}, bf16[576,256]{1,0:T(8,128)(2,1)S(1)}, u32[]{:S(2)}, u32[]{:S(2)}) collective-permute-start(bf16[576,256]{1,0:T(8,128)(2,1)S(1)} %shard_map.85.joined), channel_id=1, source_target_pairs={{0,8},{1,9},{2,10},{3,11},{4,12},{5,13},{6,14},{7,15},{8,0},{9,1},... | collective-permute-start | bytes 884744 | tf_op jit(solution)/shard_map/ppermute | solution.py:31
  20.2 1.5 %collective-permute-start.12 = (f32[64,256]{1,0:T(8,128)S(1)}, f32[64,256]{1,0:T(8,128)S(1)}, u32[]{:S(2)}, u32[]{:S(2)}) collective-permute-start(f32[64,256]{1,0:T(8,128)S(1)} %shard_map.87), channel_id=1, source_target_pairs={{0,8},{1,9},{2,10},{3,11},{4,12},{5,13},{6,14},{7,15},{8,0},{9,1},... | collective-permute-start | bytes 196616 | tf_op jit(solution)/shard_map/ppermute | solution.py:31
  20.9 1.3 %collective-permute-start.7 = (bf16[128,256]{1,0:T(8,128)(2,1)S(1)}, bf16[128,256]{1,0:T(8,128)(2,1)S(1)}, u32[]{:S(2)}, u32[]{:S(2)}) collective-permute-start(bf16[128,256]{1,0:T(8,128)(2,1)S(1)} %collective-permute-done.6.across), channel_id=1, source_target_pairs={{0,8},{1,9},{2,10},{3,11},{4,12},{5,13},{6,14},{7,15},{8,0},{9,1},... | collective-permute-start | bytes 196616 | tf_op jit(solution)/shard_map/ppermute | solution.py:31
  22.4 4.3 %collective-permute-start.14 = (bf16[64,256]{1,0:T(8,128)(2,1)S(1)}, bf16[64,256]{1,0:T(8,128)(2,1)S(1)}, u32[]{:S(2)}, u32[]{:S(2)}) collective-permute-start(bf16[64,256]{1,0:T(8,128)(2,1)S(1)} %get-tuple-element.48), channel_id=1, source_target_pairs={{0,12},{1,13},{2,14},{3,15},{4,8},{5,9},{6,10},{7,11},{8,4},{9,5},... | collective-permute-start | bytes 98312 | tf_op jit(solution)/shard_map/ppermute | solution.py:31
  25.0 1.8 %collective-permute-start.15 = (bf16[64,256]{1,0:T(8,128)(2,1)S(1)}, bf16[64,256]{1,0:T(8,128)(2,1)S(1)}, u32[]{:S(2)}, u32[]{:S(2)}) collective-permute-start(bf16[64,256]{1,0:T(8,128)(2,1)S(1)} %get-tuple-element.48), channel_id=1, source_target_pairs={{0,8},{1,9},{2,10},{3,11},{4,12},{5,13},{6,14},{7,15},{8,0},{9,1},... | collective-permute-start | bytes 98312 | tf_op jit(solution)/shard_map/ppermute | solution.py:31
  25.6 4.7 %collective-permute-start.19 = (bf16[2,256,256]{2,1,0:T(8,128)(2,1)S(1)}, bf16[2,256,256]{2,1,0:T(8,128)(2,1)S(1)}, u32[]{:S(2)}, u32[]{:S(2)}) collective-permute-start(bf16[2,256,256]{2,1,0:T(8,128)(2,1)S(1)} %shard_map.94), channel_id=1, source_target_pairs={{0,8},{1,9},{2,10},{3,11},{4,12},{5,13},{6,14},{7,15},{8,0},{9,1},... | collective-permute-start | bytes 786440 | tf_op jit(solution)/shard_map/ppermute | solution.py:31
  25.9 4.5 %collective-permute-start.18 = (f32[64,256]{1,0:T(8,128)S(1)}, f32[64,256]{1,0:T(8,128)S(1)}, u32[]{:S(2)}, u32[]{:S(2)}) collective-permute-start(f32[64,256]{1,0:T(8,128)S(1)} %shard_map.93), channel_id=1, source_target_pairs={{0,8},{1,9},{2,10},{3,11},{4,12},{5,13},{6,14},{7,15},{8,0},{9,1},... | collective-permute-start | bytes 196616 | tf_op jit(solution)/shard_map/ppermute | solution.py:31
  26.8 2.2 %copy-start.4 = (bf16[1,128,128]{2,1,0:T(8,128)(2,1)S(1)}, bf16[1,128,128]{2,1,0:T(8,128)(2,1)}, u32[]{:S(2)}) copy-start(bf16[1,128,128]{2,1,0:T(8,128)(2,1)} %param.7) | copy-start | bytes 98308
  27.0 3.4 %collective-permute-start.16 = (bf16[64,256]{1,0:T(8,128)(2,1)S(1)}, bf16[64,256]{1,0:T(8,128)(2,1)S(1)}, u32[]{:S(2)}, u32[]{:S(2)}) collective-permute-start(bf16[64,256]{1,0:T(8,128)(2,1)S(1)} %get-tuple-element.53), channel_id=1, source_target_pairs={{0,10},{1,11},{2,8},{3,9},{4,14},{5,15},{6,12},{7,13},{8,2},{9,3},... | collective-permute-start | bytes 98312 | tf_op jit(solution)/shard_map/ppermute | solution.py:31
  28.6 1.8 %collective-permute-start.17 = (bf16[64,256]{1,0:T(8,128)(2,1)S(1)}, bf16[64,256]{1,0:T(8,128)(2,1)S(1)}, u32[]{:S(2)}, u32[]{:S(2)}) collective-permute-start(bf16[64,256]{1,0:T(8,128)(2,1)S(1)} %get-tuple-element.53), channel_id=1, source_target_pairs={{0,8},{1,9},{2,10},{3,11},{4,12},{5,13},{6,14},{7,15},{8,0},{9,1},... | collective-permute-start | bytes 98312 | tf_op jit(solution)/shard_map/ppermute | solution.py:31
  30.6 3.4 %collective-permute-start.20 = (bf16[64,256]{1,0:T(8,128)(2,1)S(1)}, bf16[64,256]{1,0:T(8,128)(2,1)S(1)}, u32[]{:S(2)}, u32[]{:S(2)}) collective-permute-start(bf16[64,256]{1,0:T(8,128)(2,1)S(1)} %shard_map.95), channel_id=1, source_target_pairs={{0,9},{1,8},{2,11},{3,10},{4,13},{5,12},{6,15},{7,14},{8,1},{9,0},... | collective-permute-start | bytes 98312 | tf_op jit(solution)/shard_map/ppermute | solution.py:31
  32.0 2.0 %collective-permute-start.22 = (bf16[64,256]{1,0:T(8,128)(2,1)S(1)}, bf16[64,256]{1,0:T(8,128)(2,1)S(1)}, u32[]{:S(2)}, u32[]{:S(2)}) collective-permute-start(bf16[64,256]{1,0:T(8,128)(2,1)S(1)} %shard_map.95), channel_id=1, source_target_pairs={{0,8},{1,9},{2,10},{3,11},{4,12},{5,13},{6,14},{7,15},{8,0},{9,1},... | collective-permute-start | bytes 98312 | tf_op jit(solution)/shard_map/ppermute | solution.py:31
  32.2 1.8 %collective-permute-start.21 = (bf16[64,256]{1,0:T(8,128)(2,1)S(1)}, bf16[64,256]{1,0:T(8,128)(2,1)S(1)}, u32[]{:S(2)}, u32[]{:S(2)}) collective-permute-start(bf16[64,256]{1,0:T(8,128)(2,1)S(1)} %collective-permute-done.16), channel_id=1, source_target_pairs={{0,8},{1,9},{2,10},{3,11},{4,12},{5,13},{6,14},{7,15},{8,0},{9,1},... | collective-permute-start | bytes 98312 | tf_op jit(solution)/shard_map/ppermute | solution.py:31

commit v5 on v4

--- a/solution.py
+++ b/solution.py
@@ -138,7 +138,7 @@
     out[cols:] = terms[terms.shape[0] - 1].astype(BF)
 
 
-def join_top(mine, mirror, ends, mirror_ends, inverse, out, *, level):
+def join_top(mine, mirror, ends, mirror_ends, inverse, sent, out, *, level):
     width = inverse.shape[1]
     gram_mine, gram_mirror = mine[:width], mirror[:width]
     own, other = mine[width : 2 * width], mine[2 * width : 3 * width]
@@ -149,7 +149,9 @@
     out[:width] = (gram(matrix, matrix) + gram(own, first) + gram(other, second)).astype(BF)
     out[width : 2 * width] = (gram(mirror_other, first) + gram(mirror_own, second)).astype(BF)
     right, mirror_right = top_rights(ends, mirror_ends)
-    out[2 * width :] = (-times(right, first) - times(mirror_right, second)).astype(BF)
+    cols = right.shape[0]
+    out[2 * width : 2 * width + cols] = (-times(right, first) - times(mirror_right, second)).astype(BF)
+    out[2 * width + cols :] = sent[...]
 
 
 def top_rights(mine, mirror):
@@ -159,12 +161,13 @@
     return right.astype(BF), mirror_right.astype(BF)
 
 
-def join_own(mine, mate, joined, joined_mate, out, delta):
+def join_own(joined, joined_mate, out, delta):
     rows, width = out.shape[1], joined.shape[1]
+    mine, mate = joined[2 * width + rows :], joined_mate[2 * width + rows :]
     for at, (a, b, matrices) in enumerate(((mine, mate, joined), (mate, mine, joined_mate))):
         change = (a[rows:].astype(F32) - b[:rows].astype(F32)).astype(BF)
         delta[at] = change
-        out[at] = times(change, matrices[:width]) + matrices[2 * width :].astype(F32)
+        out[at] = times(change, matrices[:width]) + matrices[2 * width : 2 * width + rows].astype(F32)
 
 
 def join(theirs, across, part, joined, joined_mate, solved, product, block, block_mate, delta, below, *, home):
@@ -296,7 +299,7 @@
         ends = call(top_ends, [((2 * cols, width), BF)], terms, values)
     for level in range(core if joined else below_top):
         if at_home[level]:
-            product[level] = call(products, [pair], inverse_later, coupling, level=level, cost=(6, 1, 1)[min(level, 2)])
+            product[level] = call(products, [pair], inverse_later, coupling, level=level, cost=(8, 1, 1)[min(level, 2)])
         else:
             product[level], ahead[level] = call(
                 products_ahead, [pair, ((width + cols, width), BF)],
@@ -322,6 +325,11 @@
         else:
             across = first_across <= level + 1 < core
             if not at_home[level]:
+                if joined and level == core - 2:
+                    sent, product[level + 1], ends = lax.optimization_barrier(
+                        (ahead[level], product[level + 1], ends)
+                    )
+                    ahead[level] = sent
                 change, out = call(
                     forward_mate, [vec_bf, vec_bf], arrived(received), residue, ahead[level], cost=2
                 )
@@ -358,7 +366,7 @@
                 residue = call(
                     forward_residue, [slab], change, product[level], values, level=level, cost=0
                 )
-        solved[level] = call(solve, [vec], change, inverse, level=level, cost=6 if level == core - 1 else 1)
+        solved[level] = call(solve, [vec], change, inverse, level=level, cost=8 if level == core - 1 else 1)
     leaf_prod = jnp.einsum("kwn,nm->kwm", leaf_cpl, leaf_inv, preferred_element_type=F32).astype(BF)
 
     mates = [level for level in range(core) if level % 2 == 0]
@@ -367,15 +375,14 @@
         solved[level] = mate(after(solved[level], out))
     blocks, mirrored = [None] * levels, [None] * levels
     if joined:
-        out_mate = mate(out)
         mirror_pack = after(mirror_pack, out)
         matrices = call(
-            join_top, [((2 * width + cols, width), BF)],
-            pack, mirror_pack, ends, mirror_ends, inverse, level=core,
+            join_top, [((2 * width + 3 * cols, width), BF)],
+            pack, mirror_pack, ends, mirror_ends, inverse, out, level=core, cost=1,
         )
         matrices_mate = mate(matrices)
         both, both_bf = ((2, cols, width), F32), ((2, cols, width), BF)
-        part, delta = call(join_own, [both, both_bf], out, out_mate, matrices, matrices_mate)
+        part, delta = call(join_own, [both, both_bf], matrices, matrices_mate)
         theirs = mate(received)
         blocks[core], mirrored[core], delta_mirror, block_bf = call(
             join, [vec, vec_bf, ((1, cols, width), BF), vec_bf],

time: 34.9 us -> 34.5 us (0.989)
  starting transfers between devices: 21.2 us -> 20.3 us
  waiting for transfers between devices: 5.39 us -> 5.83 us
    ppermute x23 -> x22, starting transfers between devices: 21.2 us -> 20.3 us  [exchange(): return lax.ppermute(value, ('gx', 'gy'), pairs)]
    ppermute x23 -> x22, waiting for transfers between devices: 5.39 us -> 5.83 us  [exchange(): return lax.ppermute(value, ('gx', 'gy'), pairs)]
  transfers between devices with their start and end apart: 23 -> 22, of which waited for: 8 -> 8; matrix products, arithmetic and copies ran while one was open for 1% -> 1% of each run, Pallas kernels for 13% -> 13%
where the time goes in v5:
time: 34.5 us; the launch traced here: 34.3 us
  starting transfers between devices  20.3 us (59%)
  waiting for transfers between devices  5.83 us (17%)
  Pallas kernels  5.71 us (17%)
  matrix products  1.53 us (4%)
  between operations  0.88 us (3%)
    ppermute x22, starting transfers between devices, exchange(): return lax.ppermute(value, ('gx', 'gy'), pairs)  20.3 us
    ppermute x22, waiting for transfers between devices, exchange(): return lax.ppermute(value, ('gx', 'gy'), pairs)  5.83 us
    pallas_call x20, Pallas kernels, call(): pl.pallas_call(functools.partial(body, **static), out_shape=[jax.ShapeDty...  5.71 us
    dot_general x1, matrix products, times_t(): lax.dot_general(values, matrix, (((1,), (1,)), ((), ())), preferred_eleme...  1.04 us
  transfers between devices with their start and end apart: 22, of which 8 were waited for; matrix products, arithmetic and copies ran while one was open for 1% of the time, Pallas kernels for 13%

profile of v5, /device:TPU:0, one launch (start us, length us, event | category | flops | bytes accessed | tf_op | source)
XLA Modules:
  0.0 34.3 jit_solution(9815260502704841087)
XLA Ops:
  0.7 1.0 %fusion.6.leaf = f32[64,128]{1,0:T(8,128)S(1)} fusion(f32[128,64]{0,1:T(8,128)} %param.6, bf16[1,128,128]{2,1,0:T(8,128)(2,1)} %param.7), kind=kOutput, calls=%fused_computation.9 | convolution fusion | flops 2105344 | bytes 98304 | tf_op jit(solution)/shard_map/dot_general | solution.py:20
  1.7 0.3 convolution_bitcast_fusion.terms
  2.0 3.0 %collective-permute-start = (bf16[64,256]{1,0:T(8,128)(2,1)S(1)}, bf16[64,256]{1,0:T(8,128)(2,1)S(1)}, u32[]{:S(2)}, u32[]{:S(2)}) collective-permute-start(bf16[64,256]{1,0:T(8,128)(2,1)S(1)} %fusion.2), channel_id=1, source_target_pairs={{0,1},{1,0},{2,3},{3,2},{4,5},{5,4},{6,7},{7,6},{8,9},{9,8},{10,11... | collective-permute-start | bytes 98312 | tf_op jit(solution)/shard_map/ppermute | solution.py:31
  5.5 1.6 %collective-permute-start.8 = (bf16[768,256]{1,0:T(8,128)(2,1)S(1)}, bf16[768,256]{1,0:T(8,128)(2,1)S(1)}, u32[]{:S(2)}, u32[]{:S(2)}) collective-permute-start(bf16[768,256]{1,0:T(8,128)(2,1)S(1)} %shard_map.79.mine), channel_id=1, source_target_pairs={{0,16},{1,17},{2,18},{3,19},{4,20},{5,21},{6,22},{7,23},{8,24},{9,... | collective-permute-start | bytes 1179656 | tf_op jit(solution)/shard_map/ppermute | solution.py:31
  7.3 0.4 %shard_map.77 = (bf16[64,256]{1,0:T(8,128)(2,1)S(1)}, bf16[64,256]{1,0:T(8,128)(2,1)S(1)}, bf16[64,256]{1,0:T(8,128)(2,1)S(1)}) custom-call(f32[5,64,256]{2,1,0:T(8,128)S(1)} %bitcast.42, bf16[64,256]{1,0:T(8,128)(2,1)S(1)} %collective-permute-done.received, bf16[5,256,256]{2,1,0:T(8,128)(2,1)S(1)} %bitcast.35, bf16[4,2,256,256]{3,2,1,0:T(8,128)(2,1)S(1)} %bitcast.29, ...), custom_call_target="tpu_custom_call" | custom-call | flops 300000000 | bytes 2719744 | tf_op jit(solution)/shard_map/pallas_call | solution.py:36
  7.7 1.8 %collective-permute-start.1 = (bf16[64,256]{1,0:T(8,128)(2,1)S(1)}, bf16[64,256]{1,0:T(8,128)(2,1)S(1)}, u32[]{:S(2)}, u32[]{:S(2)}) collective-permute-start(bf16[64,256]{1,0:T(8,128)(2,1)S(1)} %get-tuple-element.35), channel_id=1, source_target_pairs={{0,10},{1,11},{2,8},{3,9},{4,14},{5,15},{6,12},{7,13},{8,2},{9,3},... | collective-permute-start | bytes 98312 | tf_op jit(solution)/shard_map/ppermute | solution.py:31
  9.8 1.3 %collective-permute-done.1 = bf16[64,256]{1,0:T(8,128)(2,1)S(1)} collective-permute-done((bf16[64,256]{1,0:T(8,128)(2,1)S(1)}, bf16[64,256]{1,0:T(8,128)(2,1)S(1)}, u32[]{:S(2)}, u32[]{:S(2)}) %collective-permute-start.1) | collective-permute-done | bytes 32800 | tf_op jit(solution)/shard_map/ppermute | solution.py:31
  11.3 3.1 %collective-permute-start.4 = (bf16[64,256]{1,0:T(8,128)(2,1)S(1)}, bf16[64,256]{1,0:T(8,128)(2,1)S(1)}, u32[]{:S(2)}, u32[]{:S(2)}) collective-permute-start(bf16[64,256]{1,0:T(8,128)(2,1)S(1)} %get-tuple-element.42), channel_id=1, source_target_pairs={{0,12},{1,13},{2,14},{3,15},{4,8},{5,9},{6,10},{7,11},{8,4},{9,5},... | collective-permute-start | bytes 98312 | tf_op jit(solution)/shard_map/ppermute | solution.py:31
  14.4 1.5 %collective-permute-start.9 = (bf16[128,256]{1,0:T(8,128)(2,1)S(1)}, bf16[128,256]{1,0:T(8,128)(2,1)S(1)}, u32[]{:S(2)}, u32[]{:S(2)}) collective-permute-start(bf16[128,256]{1,0:T(8,128)(2,1)S(1)} %shard_map.82.ends), channel_id=1, source_target_pairs={{0,16},{1,17},{2,18},{3,19},{4,20},{5,21},{6,22},{7,23},{8,24},{9,... | collective-permute-start | bytes 196616 | tf_op jit(solution)/shard_map/ppermute | solution.py:31
  16.0 0.4 %shard_map.84 = (bf16[64,256]{1,0:T(8,128)(2,1)S(1)}, bf16[128,256]{1,0:T(8,128)(2,1)S(1)}) custom-call(f32[64,256]{1,0:T(8,128)S(1)} %convert_element_type.34.received, bf16[64,256]{1,0:T(8,128)(2,1)S(1)} %collective-permute-done.5.below.delta, bf16[2,256,256]{2,1,0:T(8,128)(2,1)S(1)} %get-tuple-element.44.product_below.product, ...), custom_call_target="tpu_custom_call" | custom-call | flops 1200000000 | bytes 1277952 | tf_op jit(solution)/shard_map/pallas_call | solution.py:36
  16.4 1.6 %collective-permute-start.6 = (bf16[128,256]{1,0:T(8,128)(2,1)S(1)}, bf16[128,256]{1,0:T(8,128)(2,1)S(1)}, u32[]{:S(2)}, u32[]{:S(2)}) collective-permute-start(bf16[128,256]{1,0:T(8,128)(2,1)S(1)} %get-tuple-element.46.sent), channel_id=1, source_target_pairs={{0,24},{1,25},{2,26},{3,27},{4,28},{5,29},{6,30},{7,31},{8,16},{9,... | collective-permute-start | bytes 196616 | tf_op jit(solution)/shard_map/ppermute | solution.py:31
  18.0 0.9 %collective-permute-done.9.mirror_ends = bf16[128,256]{1,0:T(8,128)(2,1)S(1)} collective-permute-done((bf16[128,256]{1,0:T(8,128)(2,1)S(1)}, bf16[128,256]{1,0:T(8,128)(2,1)S(1)}, u32[]{:S(2)}, u32[]{:S(2)}) %collective-permute-start.9) | collective-permute-done | bytes 65568 | tf_op jit(solution)/shard_map/ppermute | solution.py:31
  18.9 0.6 %shard_map.85.joined = bf16[704,256]{1,0:T(8,128)(2,1)S(1)} custom-call(bf16[768,256]{1,0:T(8,128)(2,1)S(1)} %shard_map.79.mine, bf16[768,256]{1,0:T(8,128)(2,1)S(1)} %collective-permute-done.8.mirror, bf16[128,256]{1,0:T(8,128)(2,1)S(1)} %shard_map.82.ends, bf16[128,256]{1,0:T(8,128)(2,1)S(1)} %collective-permute-done.9.mirror_ends, ...), custom_call_target="tpu_custom_call" | custom-call | flops 300000000 | bytes 1638400 | tf_op jit(solution)/shard_map/pallas_call | solution.py:36
  19.6 0.3 shard_map.87
  19.9 0.6 %collective-permute-start.11 = (f32[64,256]{1,0:T(8,128)S(1)}, f32[64,256]{1,0:T(8,128)S(1)}, u32[]{:S(2)}, u32[]{:S(2)}) collective-permute-start(f32[64,256]{1,0:T(8,128)S(1)} %shard_map.87), channel_id=1, source_target_pairs={{0,8},{1,9},{2,10},{3,11},{4,12},{5,13},{6,14},{7,15},{8,0},{9,1},... | collective-permute-start | bytes 196616 | tf_op jit(solution)/shard_map/ppermute | solution.py:31
  20.8 0.4 %collective-permute-done.10.joined_mate = bf16[704,256]{1,0:T(8,128)(2,1)S(1)} collective-permute-done((bf16[704,256]{1,0:T(8,128)(2,1)S(1)}, bf16[704,256]{1,0:T(8,128)(2,1)S(1)}, u32[]{:S(2)}, u32[]{:S(2)}) %collective-permute-start.10) | collective-permute-done | bytes 360480 | tf_op jit(solution)/shard_map/ppermute | solution.py:31
  21.4 0.3 collective-permute-done.7.theirs
  21.7 0.3 shard_map.88
  22.0 2.4 %collective-permute-start.13 = (bf16[64,256]{1,0:T(8,128)(2,1)S(1)}, bf16[64,256]{1,0:T(8,128)(2,1)S(1)}, u32[]{:S(2)}, u32[]{:S(2)}) collective-permute-start(bf16[64,256]{1,0:T(8,128)(2,1)S(1)} %get-tuple-element.54), channel_id=1, source_target_pairs={{0,12},{1,13},{2,14},{3,15},{4,8},{5,9},{6,10},{7,11},{8,4},{9,5},... | collective-permute-start | bytes 98312 | tf_op jit(solution)/shard_map/ppermute | solution.py:31
  24.5 0.3 shard_map.93
  24.8 0.4 %collective-permute-start.18 = (bf16[2,256,256]{2,1,0:T(8,128)(2,1)S(1)}, bf16[2,256,256]{2,1,0:T(8,128)(2,1)S(1)}, u32[]{:S(2)}, u32[]{:S(2)}) collective-permute-start(bf16[2,256,256]{2,1,0:T(8,128)(2,1)S(1)} %shard_map.94), channel_id=1, source_target_pairs={{0,8},{1,9},{2,10},{3,11},{4,12},{5,13},{6,14},{7,15},{8,0},{9,1},... | collective-permute-start | bytes 786440 | tf_op jit(solution)/shard_map/ppermute | solution.py:31
  25.4 0.3 shard_map.91.solved
  25.7 0.6 %collective-permute-done.13.refs_0_ = bf16[64,256]{1,0:T(8,128)(2,1)S(1)} collective-permute-done((bf16[64,256]{1,0:T(8,128)(2,1)S(1)}, bf16[64,256]{1,0:T(8,128)(2,1)S(1)}, u32[]{:S(2)}, u32[]{:S(2)}) %collective-permute-start.13) | collective-permute-done | bytes 32800 | tf_op jit(solution)/shard_map/ppermute | solution.py:31
  26.5 1.5 %collective-permute-start.15 = (bf16[64,256]{1,0:T(8,128)(2,1)S(1)}, bf16[64,256]{1,0:T(8,128)(2,1)S(1)}, u32[]{:S(2)}, u32[]{:S(2)}) collective-permute-start(bf16[64,256]{1,0:T(8,128)(2,1)S(1)} %get-tuple-element.59), channel_id=1, source_target_pairs={{0,10},{1,11},{2,8},{3,9},{4,14},{5,15},{6,12},{7,13},{8,2},{9,3},... | collective-permute-start | bytes 98312 | tf_op jit(solution)/shard_map/ppermute | solution.py:31
  28.0 0.2 collective-permute-start.16
  28.3 0.2 convolution_convert_fusion.leaf_products
  28.5 1.4 %collective-permute-done.15 = bf16[64,256]{1,0:T(8,128)(2,1)S(1)} collective-permute-done((bf16[64,256]{1,0:T(8,128)(2,1)S(1)}, bf16[64,256]{1,0:T(8,128)(2,1)S(1)}, u32[]{:S(2)}, u32[]{:S(2)}) %collective-permute-start.15) | collective-permute-done | bytes 32800 | tf_op jit(solution)/shard_map/ppermute | solution.py:31
  30.1 1.3 %collective-permute-start.19 = (bf16[64,256]{1,0:T(8,128)(2,1)S(1)}, bf16[64,256]{1,0:T(8,128)(2,1)S(1)}, u32[]{:S(2)}, u32[]{:S(2)}) collective-permute-start(bf16[64,256]{1,0:T(8,128)(2,1)S(1)} %shard_map.95), channel_id=1, source_target_pairs={{0,9},{1,8},{2,11},{3,10},{4,13},{5,12},{6,15},{7,14},{8,1},{9,0},... | collective-permute-start | bytes 98312 | tf_op jit(solution)/shard_map/ppermute | solution.py:31
  31.4 0.3 collective-permute-start.21
  32.0 0.4 %shard_map.89 = (f32[64,256]{1,0:T(8,128)S(1)}, bf16[64,256]{1,0:T(8,128)(2,1)S(1)}) custom-call(bf16[768,256]{1,0:T(8,128)(2,1)S(1)} %shard_map.79.mine, bf16[768,256]{1,0:T(8,128)(2,1)S(1)} %collective-permute-done.8.mirror, bf16[128,256]{1,0:T(8,128)(2,1)S(1)} %shard_map.82.ends, bf16[128,256]{1,0:T(8,128)(2,1)S(1)} %collective-permute-done.9.mirror_ends, ...), custom_call_target="tpu_custom_call" | custom-call | flops 300000000 | bytes 1015808 | tf_op jit(solution)/shard_map/pallas_call | solution.py:36
  32.5 1.0 %collective-permute-done.19 = bf16[64,256]{1,0:T(8,128)(2,1)S(1)} collective-permute-done((bf16[64,256]{1,0:T(8,128)(2,1)S(1)}, bf16[64,256]{1,0:T(8,128)(2,1)S(1)}, u32[]{:S(2)}, u32[]{:S(2)}) %collective-permute-start.19) | collective-permute-done | bytes 32800 | tf_op jit(solution)/shard_map/ppermute | solution.py:31
  33.5 0.8 %shard_map.96 = (f32[64,128]{1,0:T(8,128)}, f32[5,64,256]{2,1,0:T(8,128)}) custom-call(f32[64,128]{1,0:T(8,128)S(1)} %shard_map.90.part, bf16[5,256,128]{2,1,0:T(8,128)(2,1)S(1)} %convolution_convert_fusion.leaf_products, f32[64,256]{1,0:T(8,128)S(1)} %convert_element_type.37.refs_0_, bf16[64,256]{1,0:T(8,128)(2,1)S(1)} %collective-permute-done.20.refs_1_, ...), custom_call_target="tpu_custom_call" | custom-call | flops 300000000 | bytes 720896 | tf_op jit(solution)/shard_map/pallas_call | solution.py:36
  (51 shorter events, 3.1 us)
Async XLA Ops:
  0.6 1.1 %copy-start = (bf16[1,5,256,128]{3,2,1,0:T(8,128)(2,1)S(1)}, bf16[1,5,256,128]{3,2,1,0:T(8,128)(2,1)}, u32[]{:S(2)}) copy-start(bf16[1,5,256,128]{3,2,1,0:T(8,128)(2,1)} %param.8) | copy-start | bytes 983044
  0.6 4.3 %copy-start.2 = (bf16[1,5,256,256]{3,2,1,0:T(8,128)(2,1)S(1)}, bf16[1,5,256,256]{3,2,1,0:T(8,128)(2,1)}, u32[]{:S(2)}) copy-start(bf16[1,5,256,256]{3,2,1,0:T(8,128)(2,1)} %param.10) | copy-start | bytes 1966084
  0.7 4.6 %copy-start.1 = (bf16[1,4,1,2,256,256]{5,4,3,2,1,0:T(8,128)(2,1)S(1)}, bf16[1,4,1,2,256,256]{5,4,3,2,1,0:T(8,128)(2,1)}, u32[]{:S(2)}) copy-start(bf16[1,4,1,2,256,256]{5,4,3,2,1,0:T(8,128)(2,1)} %param.11) | copy-start | bytes 3145732
  2.0 5.3 %collective-permute-start = (bf16[64,256]{1,0:T(8,128)(2,1)S(1)}, bf16[64,256]{1,0:T(8,128)(2,1)S(1)}, u32[]{:S(2)}, u32[]{:S(2)}) collective-permute-start(bf16[64,256]{1,0:T(8,128)(2,1)S(1)} %fusion.2), channel_id=1, source_target_pairs={{0,1},{1,0},{2,3},{3,2},{4,5},{5,4},{6,7},{7,6},{8,9},{9,8},{10,11... | collective-permute-start | bytes 98312 | tf_op jit(solution)/shard_map/ppermute | solution.py:31
  5.5 1.8 %copy-start.3 = (f32[1,5,256,64]{2,3,1,0:T(8,128)S(1)}, f32[1,5,256,64]{2,3,1,0:T(8,128)}, u32[]{:S(2)}) copy-start(f32[1,5,256,64]{2,3,1,0:T(8,128)} %param.9) | copy-start | bytes 983044
  5.5 12.6 %collective-permute-start.8 = (bf16[768,256]{1,0:T(8,128)(2,1)S(1)}, bf16[768,256]{1,0:T(8,128)(2,1)S(1)}, u32[]{:S(2)}, u32[]{:S(2)}) collective-permute-start(bf16[768,256]{1,0:T(8,128)(2,1)S(1)} %shard_map.79.mine), channel_id=1, source_target_pairs={{0,16},{1,17},{2,18},{3,19},{4,20},{5,21},{6,22},{7,23},{8,24},{9,... | collective-permute-start | bytes 1179656 | tf_op jit(solution)/shard_map/ppermute | solution.py:31
  7.7 3.5 %collective-permute-start.3 = (bf16[320,256]{1,0:T(8,128)(2,1)S(1)}, bf16[320,256]{1,0:T(8,128)(2,1)S(1)}, u32[]{:S(2)}, u32[]{:S(2)}) collective-permute-start(bf16[320,256]{1,0:T(8,128)(2,1)S(1)} %get-tuple-element.40), channel_id=1, source_target_pairs={{0,8},{1,9},{2,10},{3,11},{4,12},{5,13},{6,14},{7,15},{8,0},{9,1},... | collective-permute-start | bytes 491528 | tf_op jit(solution)/shard_map/ppermute | solution.py:31
  7.7 3.4 %collective-permute-start.1 = (bf16[64,256]{1,0:T(8,128)(2,1)S(1)}, bf16[64,256]{1,0:T(8,128)(2,1)S(1)}, u32[]{:S(2)}, u32[]{:S(2)}) collective-permute-start(bf16[64,256]{1,0:T(8,128)(2,1)S(1)} %get-tuple-element.35), channel_id=1, source_target_pairs={{0,10},{1,11},{2,8},{3,9},{4,14},{5,15},{6,12},{7,13},{8,2},{9,3},... | collective-permute-start | bytes 98312 | tf_op jit(solution)/shard_map/ppermute | solution.py:31
  9.5 1.6 %collective-permute-start.2 = (bf16[64,256]{1,0:T(8,128)(2,1)S(1)}, bf16[64,256]{1,0:T(8,128)(2,1)S(1)}, u32[]{:S(2)}, u32[]{:S(2)}) collective-permute-start(bf16[64,256]{1,0:T(8,128)(2,1)S(1)} %get-tuple-element.36), channel_id=1, source_target_pairs={{0,8},{1,9},{2,10},{3,11},{4,12},{5,13},{6,14},{7,15},{8,0},{9,1},... | collective-permute-start | bytes 98312 | tf_op jit(solution)/shard_map/ppermute | solution.py:31
  11.3 4.7 %collective-permute-start.4 = (bf16[64,256]{1,0:T(8,128)(2,1)S(1)}, bf16[64,256]{1,0:T(8,128)(2,1)S(1)}, u32[]{:S(2)}, u32[]{:S(2)}) collective-permute-start(bf16[64,256]{1,0:T(8,128)(2,1)S(1)} %get-tuple-element.42), channel_id=1, source_target_pairs={{0,12},{1,13},{2,14},{3,15},{4,8},{5,9},{6,10},{7,11},{8,4},{9,5},... | collective-permute-start | bytes 98312 | tf_op jit(solution)/shard_map/ppermute | solution.py:31
  14.4 1.6 %collective-permute-start.5 = (bf16[64,256]{1,0:T(8,128)(2,1)S(1)}, bf16[64,256]{1,0:T(8,128)(2,1)S(1)}, u32[]{:S(2)}, u32[]{:S(2)}) collective-permute-start(bf16[64,256]{1,0:T(8,128)(2,1)S(1)} %get-tuple-element.43), channel_id=1, source_target_pairs={{0,8},{1,9},{2,10},{3,11},{4,12},{5,13},{6,14},{7,15},{8,0},{9,1},... | collective-permute-start | bytes 98312 | tf_op jit(solution)/shard_map/ppermute | solution.py:31
  14.4 4.5 %collective-permute-start.9 = (bf16[128,256]{1,0:T(8,128)(2,1)S(1)}, bf16[128,256]{1,0:T(8,128)(2,1)S(1)}, u32[]{:S(2)}, u32[]{:S(2)}) collective-permute-start(bf16[128,256]{1,0:T(8,128)(2,1)S(1)} %shard_map.82.ends), channel_id=1, source_target_pairs={{0,16},{1,17},{2,18},{3,19},{4,20},{5,21},{6,22},{7,23},{8,24},{9,... | collective-permute-start | bytes 196616 | tf_op jit(solution)/shard_map/ppermute | solution.py:31
  16.4 4.0 %collective-permute-start.6 = (bf16[128,256]{1,0:T(8,128)(2,1)S(1)}, bf16[128,256]{1,0:T(8,128)(2,1)S(1)}, u32[]{:S(2)}, u32[]{:S(2)}) collective-permute-start(bf16[128,256]{1,0:T(8,128)(2,1)S(1)} %get-tuple-element.46.sent), channel_id=1, source_target_pairs={{0,24},{1,25},{2,26},{3,27},{4,28},{5,29},{6,30},{7,31},{8,16},{9,... | collective-permute-start | bytes 196616 | tf_op jit(solution)/shard_map/ppermute | solution.py:31
  18.0 3.7 %collective-permute-start.12 = (bf16[2,256,256]{2,1,0:T(8,128)(2,1)S(1)}, bf16[2,256,256]{2,1,0:T(8,128)(2,1)S(1)}, u32[]{:S(2)}, u32[]{:S(2)}) collective-permute-start(bf16[2,256,256]{2,1,0:T(8,128)(2,1)S(1)} %shard_map.81.product), channel_id=1, source_target_pairs={{0,8},{1,9},{2,10},{3,11},{4,12},{5,13},{6,14},{7,15},{8,0},{9,1},... | collective-permute-start | bytes 786440 | tf_op jit(solution)/shard_map/ppermute | solution.py:31
  19.5 1.7 %collective-permute-start.10 = (bf16[704,256]{1,0:T(8,128)(2,1)S(1)}, bf16[704,256]{1,0:T(8,128)(2,1)S(1)}, u32[]{:S(2)}, u32[]{:S(2)}) collective-permute-start(bf16[704,256]{1,0:T(8,128)(2,1)S(1)} %shard_map.85.joined), channel_id=1, source_target_pairs={{0,8},{1,9},{2,10},{3,11},{4,12},{5,13},{6,14},{7,15},{8,0},{9,1},... | collective-permute-start | bytes 1081352 | tf_op jit(solution)/shard_map/ppermute | solution.py:31
  19.9 1.5 %collective-permute-start.11 = (f32[64,256]{1,0:T(8,128)S(1)}, f32[64,256]{1,0:T(8,128)S(1)}, u32[]{:S(2)}, u32[]{:S(2)}) collective-permute-start(f32[64,256]{1,0:T(8,128)S(1)} %shard_map.87), channel_id=1, source_target_pairs={{0,8},{1,9},{2,10},{3,11},{4,12},{5,13},{6,14},{7,15},{8,0},{9,1},... | collective-permute-start | bytes 196616 | tf_op jit(solution)/shard_map/ppermute | solution.py:31
  20.4 1.3 %collective-permute-start.7 = (bf16[128,256]{1,0:T(8,128)(2,1)S(1)}, bf16[128,256]{1,0:T(8,128)(2,1)S(1)}, u32[]{:S(2)}, u32[]{:S(2)}) collective-permute-start(bf16[128,256]{1,0:T(8,128)(2,1)S(1)} %collective-permute-done.6.across), channel_id=1, source_target_pairs={{0,8},{1,9},{2,10},{3,11},{4,12},{5,13},{6,14},{7,15},{8,0},{9,1},... | collective-permute-start | bytes 196616 | tf_op jit(solution)/shard_map/ppermute | solution.py:31
  22.0 4.3 %collective-permute-start.13 = (bf16[64,256]{1,0:T(8,128)(2,1)S(1)}, bf16[64,256]{1,0:T(8,128)(2,1)S(1)}, u32[]{:S(2)}, u32[]{:S(2)}) collective-permute-start(bf16[64,256]{1,0:T(8,128)(2,1)S(1)} %get-tuple-element.54), channel_id=1, source_target_pairs={{0,12},{1,13},{2,14},{3,15},{4,8},{5,9},{6,10},{7,11},{8,4},{9,5},... | collective-permute-start | bytes 98312 | tf_op jit(solution)/shard_map/ppermute | solution.py:31
  24.4 1.9 %collective-permute-start.14 = (bf16[64,256]{1,0:T(8,128)(2,1)S(1)}, bf16[64,256]{1,0:T(8,128)(2,1)S(1)}, u32[]{:S(2)}, u32[]{:S(2)}) collective-permute-start(bf16[64,256]{1,0:T(8,128)(2,1)S(1)} %get-tuple-element.54), channel_id=1, source_target_pairs={{0,8},{1,9},{2,10},{3,11},{4,12},{5,13},{6,14},{7,15},{8,0},{9,1},... | collective-permute-start | bytes 98312 | tf_op jit(solution)/shard_map/ppermute | solution.py:31
  24.8 5.1 %collective-permute-start.18 = (bf16[2,256,256]{2,1,0:T(8,128)(2,1)S(1)}, bf16[2,256,256]{2,1,0:T(8,128)(2,1)S(1)}, u32[]{:S(2)}, u32[]{:S(2)}) collective-permute-start(bf16[2,256,256]{2,1,0:T(8,128)(2,1)S(1)} %shard_map.94), channel_id=1, source_target_pairs={{0,8},{1,9},{2,10},{3,11},{4,12},{5,13},{6,14},{7,15},{8,0},{9,1},... | collective-permute-start | bytes 786440 | tf_op jit(solution)/shard_map/ppermute | solution.py:31
  25.3 4.6 %collective-permute-start.17 = (f32[64,256]{1,0:T(8,128)S(1)}, f32[64,256]{1,0:T(8,128)S(1)}, u32[]{:S(2)}, u32[]{:S(2)}) collective-permute-start(f32[64,256]{1,0:T(8,128)S(1)} %shard_map.93), channel_id=1, source_target_pairs={{0,8},{1,9},{2,10},{3,11},{4,12},{5,13},{6,14},{7,15},{8,0},{9,1},... | collective-permute-start | bytes 196616 | tf_op jit(solution)/shard_map/ppermute | solution.py:31
  26.3 2.0 %copy-start.4 = (bf16[1,128,128]{2,1,0:T(8,128)(2,1)S(1)}, bf16[1,128,128]{2,1,0:T(8,128)(2,1)}, u32[]{:S(2)}) copy-start(bf16[1,128,128]{2,1,0:T(8,128)(2,1)} %param.7) | copy-start | bytes 98308
  26.5 3.4 %collective-permute-start.15 = (bf16[64,256]{1,0:T(8,128)(2,1)S(1)}, bf16[64,256]{1,0:T(8,128)(2,1)S(1)}, u32[]{:S(2)}, u32[]{:S(2)}) collective-permute-start(bf16[64,256]{1,0:T(8,128)(2,1)S(1)} %get-tuple-element.59), channel_id=1, source_target_pairs={{0,10},{1,11},{2,8},{3,9},{4,14},{5,15},{6,12},{7,13},{8,2},{9,3},... | collective-permute-start | bytes 98312 | tf_op jit(solution)/shard_map/ppermute | solution.py:31
  28.0 1.9 %collective-permute-start.16 = (bf16[64,256]{1,0:T(8,128)(2,1)S(1)}, bf16[64,256]{1,0:T(8,128)(2,1)S(1)}, u32[]{:S(2)}, u32[]{:S(2)}) collective-permute-start(bf16[64,256]{1,0:T(8,128)(2,1)S(1)} %get-tuple-element.59), channel_id=1, source_target_pairs={{0,8},{1,9},{2,10},{3,11},{4,12},{5,13},{6,14},{7,15},{8,0},{9,1},... | collective-permute-start | bytes 98312 | tf_op jit(solution)/shard_map/ppermute | solution.py:31
  30.1 3.4 %collective-permute-start.19 = (bf16[64,256]{1,0:T(8,128)(2,1)S(1)}, bf16[64,256]{1,0:T(8,128)(2,1)S(1)}, u32[]{:S(2)}, u32[]{:S(2)}) collective-permute-start(bf16[64,256]{1,0:T(8,128)(2,1)S(1)} %shard_map.95), channel_id=1, source_target_pairs={{0,9},{1,8},{2,11},{3,10},{4,13},{5,12},{6,15},{7,14},{8,1},{9,0},... | collective-permute-start | bytes 98312 | tf_op jit(solution)/shard_map/ppermute | solution.py:31
  31.4 2.1 %collective-permute-start.21 = (bf16[64,256]{1,0:T(8,128)(2,1)S(1)}, bf16[64,256]{1,0:T(8,128)(2,1)S(1)}, u32[]{:S(2)}, u32[]{:S(2)}) collective-permute-start(bf16[64,256]{1,0:T(8,128)(2,1)S(1)} %shard_map.95), channel_id=1, source_target_pairs={{0,8},{1,9},{2,10},{3,11},{4,12},{5,13},{6,14},{7,15},{8,0},{9,1},... | collective-permute-start | bytes 98312 | tf_op jit(solution)/shard_map/ppermute | solution.py:31
  31.8 1.8 %collective-permute-start.20 = (bf16[64,256]{1,0:T(8,128)(2,1)S(1)}, bf16[64,256]{1,0:T(8,128)(2,1)S(1)}, u32[]{:S(2)}, u32[]{:S(2)}) collective-permute-start(bf16[64,256]{1,0:T(8,128)(2,1)S(1)} %collective-permute-done.15), channel_id=1, source_target_pairs={{0,8},{1,9},{2,10},{3,11},{4,12},{5,13},{6,14},{7,15},{8,0},{9,1},... | collective-permute-start | bytes 98312 | tf_op jit(solution)/shard_map/ppermute | solution.py:31

commit v6 on v5

--- a/solution.py
+++ b/solution.py
@@ -124,25 +124,25 @@
     out[rows:] = (values[level + 1] - times_t(change, product[0])).astype(BF)
 
 
-def pack_top(own_gram, inverse, coupling, out, *, level):
+def pack_top(inverse, coupling, out, *, level):
     width = inverse.shape[1]
-    out[:width] = own_gram[...]
     for side in range(2):
         made = times(coupling[level, side], inverse[level]).astype(BF)
-        out[(side + 1) * width : (side + 2) * width] = made
-
-
-def top_ends(terms, values, out):
-    cols = values.shape[1]
-    out[:cols] = values[values.shape[0] - 1].astype(BF)
-    out[cols:] = terms[terms.shape[0] - 1].astype(BF)
+        out[side * width : (side + 1) * width] = made
+
+
+def top_ends(own_gram, terms, values, out):
+    width, cols = own_gram.shape[0], values.shape[1]
+    out[:width] = own_gram[...]
+    out[width : width + cols] = values[values.shape[0] - 1].astype(BF)
+    out[width + cols :] = terms[terms.shape[0] - 1].astype(BF)
 
 
 def join_top(mine, mirror, ends, mirror_ends, inverse, sent, out, *, level):
     width = inverse.shape[1]
-    gram_mine, gram_mirror = mine[:width], mirror[:width]
-    own, other = mine[width : 2 * width], mine[2 * width : 3 * width]
-    mirror_own, mirror_other = mirror[width : 2 * width], mirror[2 * width : 3 * width]
+    gram_mine, gram_mirror = ends[:width], mirror_ends[:width]
+    own, other = mine[:width], mine[width:]
+    mirror_own, mirror_other = mirror[:width], mirror[width:]
     first = times(gram_mine, own).astype(BF)
     second = times(gram_mirror, other).astype(BF)
     matrix = inverse[level]
@@ -155,9 +155,10 @@
 
 
 def top_rights(mine, mirror):
-    cols = mine.shape[0] // 2
-    right = mine[:cols].astype(F32) - mirror[cols:].astype(F32)
-    mirror_right = mirror[:cols].astype(F32) - mine[cols:].astype(F32)
+    width = mine.shape[1]
+    cols = (mine.shape[0] - width) // 2
+    right = mine[width : width + cols].astype(F32) - mirror[width + cols :].astype(F32)
+    mirror_right = mirror[width : width + cols].astype(F32) - mine[width + cols :].astype(F32)
     return right.astype(BF), mirror_right.astype(BF)
 
 
@@ -190,12 +191,12 @@
     width = out.shape[1]
     right, mirror_right = top_rights(ends, mirror_ends)
     change, other = delta[0], delta_mirror[0]
-    own = right.astype(F32) - times_t(change, mine[width : 2 * width])
-    own = own - times_t(other, mirror[2 * width : 3 * width])
-    theirs = mirror_right.astype(F32) - times_t(other, mirror[width : 2 * width])
-    theirs = theirs - times_t(change, mine[2 * width : 3 * width])
-    out[...] = times(own.astype(BF), mine[:width])
-    mirrored[...] = times(theirs.astype(BF), mirror[:width]).astype(BF)
+    own = right.astype(F32) - times_t(change, mine[:width])
+    own = own - times_t(other, mirror[width:])
+    theirs = mirror_right.astype(F32) - times_t(other, mirror[:width])
+    theirs = theirs - times_t(change, mine[width:])
+    out[...] = times(own.astype(BF), ends[:width])
+    mirrored[...] = times(theirs.astype(BF), mirror_ends[:width]).astype(BF)
 
 
 def solve(delta, inverse, solved, *, level):
@@ -292,11 +293,11 @@
     inverse_later = after(inverse, own_gram)
     if joined:
         pack = call(
-            pack_top, [((3 * width, width), BF)], own_gram, inverse_later, coupling, level=core
+            pack_top, [((2 * width, width), BF)], inverse_later, coupling, level=core
         )
         mirror_pack = send(pack, below_top)
         inverse_later = after(inverse, pack)
-        ends = call(top_ends, [((2 * cols, width), BF)], terms, values)
+        ends = call(top_ends, [((width + 2 * cols, width), BF)], own_gram, terms, values, cost=0)
     for level in range(core if joined else below_top):
         if at_home[level]:
             product[level] = call(products, [pair], inverse_later, coupling, level=level, cost=(8, 1, 1)[min(level, 2)])
@@ -310,6 +311,7 @@
     for level in range(core if joined else below_top):
         below = change
         if joined and level == core - 1:
+            below, mirror_pack = lax.optimization_barrier((below, mirror_pack))
             change, out = call(
                 forward_last, [vec_bf, ((2 * cols, width), BF)], arrived(received), below,
                 product[level - 1], product[level], terms, values, level=level, cost=4,
@@ -326,15 +328,10 @@
             across = first_across <= level + 1 < core
             if not at_home[level]:
                 if joined and level == core - 2:
-                    sent, product[level + 1], ends = lax.optimization_barrier(
-                        (ahead[level], product[level + 1], ends)
-                    )
-                    ahead[level] = sent
+                    ahead[level], ends = lax.optimization_barrier((ahead[level], ends))
                 change, out = call(
                     forward_mate, [vec_bf, vec_bf], arrived(received), residue, ahead[level], cost=2
                 )
-                if joined and level == core - 2:
-                    mirror_ends = send(after(ends, out), below_top)
             elif level and not at_home[level - 1]:
                 change, out = call(
                     forward_back, [vec_bf, vec_bf], arrived(received), below,
@@ -343,7 +340,7 @@
             elif level == 0 and not at_home[1]:
                 change, out, residue = call(
                     forward_first, [vec_bf, vec_bf, vec_bf],
-                    residue, received, inverse, coupling, terms, values,
+                    residue, received, inverse, coupling, terms, values, cost=0,
                 )
             elif not at_home[level + 1]:
                 change, out, residue = call(
@@ -355,8 +352,11 @@
                     forward, [vec_bf, vec_bf], residue, received, product[level], terms, level=level
                 )
             received = send(out, level + 1, across)
-            if level == 0 and not joined:
-                mirror_gram = send(after(own_gram, out), below_top)
+            if level == 0:
+                if joined:
+                    mirror_ends = send(after(ends, out), below_top)
+                else:
+                    mirror_gram = send(after(own_gram, out), below_top)
             if not at_home[level]:
                 change = mate(change)
             elif not at_home[level + 1]:
@@ -375,7 +375,7 @@
         solved[level] = mate(after(solved[level], out))
     blocks, mirrored = [None] * levels, [None] * levels
     if joined:
-        mirror_pack = after(mirror_pack, out)
+        mirror_ends = after(mirror_ends, out)
         matrices = call(
             join_top, [((2 * width + 3 * cols, width), BF)],
             pack, mirror_pack, ends, mirror_ends, inverse, out, level=core, cost=1,

time: 34.5 us -> 34.4 us (level)
  waiting for transfers between devices: 5.83 us -> 5.31 us
  starting transfers between devices: 20.3 us -> 20.7 us
    ppermute x22, waiting for transfers between devices: 5.83 us -> 5.31 us  [exchange(): return lax.ppermute(value, ('gx', 'gy'), pairs)]
    ppermute x22, starting transfers between devices: 20.3 us -> 20.7 us  [exchange(): return lax.ppermute(value, ('gx', 'gy'), pairs)]
  transfers between devices with their start and end apart: 22 -> 22, of which waited for: 8 -> 6; matrix products, arithmetic and copies ran while one was open for 1% -> 1% of each run, Pallas kernels for 13% -> 13%
where the time goes in v6:
time: 34.4 us; the launch traced here: 34.2 us
  starting transfers between devices  20.7 us (60%)
  Pallas kernels  5.71 us (17%)
  waiting for transfers between devices  5.31 us (15%)
  matrix products  1.52 us (4%)
  between operations  0.89 us (3%)
    ppermute x22, starting transfers between devices, exchange(): return lax.ppermute(value, ('gx', 'gy'), pairs)  20.7 us
    pallas_call x20, Pallas kernels, call(): pl.pallas_call(functools.partial(body, **static), out_shape=[jax.ShapeDty...  5.71 us
    ppermute x22, waiting for transfers between devices, exchange(): return lax.ppermute(value, ('gx', 'gy'), pairs)  5.31 us
    dot_general x1, matrix products, times_t(): lax.dot_general(values, matrix, (((1,), (1,)), ((), ())), preferred_eleme...  1.04 us
  transfers between devices with their start and end apart: 22, of which 6 were waited for; matrix products, arithmetic and copies ran while one was open for 1% of the time, Pallas kernels for 13%

profile of v6, /device:TPU:0, one launch (start us, length us, event | category | flops | bytes accessed | tf_op | source)
XLA Modules:
  0.0 34.2 jit_solution(12020404934198258230)
XLA Ops:
  0.7 1.0 %fusion.6.leaf = f32[64,128]{1,0:T(8,128)S(1)} fusion(f32[128,64]{0,1:T(8,128)} %param.6, bf16[1,128,128]{2,1,0:T(8,128)(2,1)} %param.7), kind=kOutput, calls=%fused_computation.9 | convolution fusion | flops 2105344 | bytes 98304 | tf_op jit(solution)/shard_map/dot_general | solution.py:20
  1.7 0.3 convolution_bitcast_fusion.terms
  2.0 3.0 %collective-permute-start = (bf16[64,256]{1,0:T(8,128)(2,1)S(1)}, bf16[64,256]{1,0:T(8,128)(2,1)S(1)}, u32[]{:S(2)}, u32[]{:S(2)}) collective-permute-start(bf16[64,256]{1,0:T(8,128)(2,1)S(1)} %fusion.2), channel_id=1, source_target_pairs={{0,1},{1,0},{2,3},{3,2},{4,5},{5,4},{6,7},{7,6},{8,9},{9,8},{10,11... | collective-permute-start | bytes 98312 | tf_op jit(solution)/shard_map/ppermute | solution.py:31
  5.2 0.2 shard_map.79.mine
  5.5 1.6 %collective-permute-start.6 = (bf16[512,256]{1,0:T(8,128)(2,1)S(1)}, bf16[512,256]{1,0:T(8,128)(2,1)S(1)}, u32[]{:S(2)}, u32[]{:S(2)}) collective-permute-start(bf16[512,256]{1,0:T(8,128)(2,1)S(1)} %shard_map.79.mine), channel_id=1, source_target_pairs={{0,16},{1,17},{2,18},{3,19},{4,20},{5,21},{6,22},{7,23},{8,24},{9,... | collective-permute-start | bytes 786440 | tf_op jit(solution)/shard_map/ppermute | solution.py:31
  7.3 0.4 %shard_map.77 = (bf16[64,256]{1,0:T(8,128)(2,1)S(1)}, bf16[64,256]{1,0:T(8,128)(2,1)S(1)}, bf16[64,256]{1,0:T(8,128)(2,1)S(1)}) custom-call(f32[5,64,256]{2,1,0:T(8,128)S(1)} %bitcast.42, bf16[64,256]{1,0:T(8,128)(2,1)S(1)} %collective-permute-done.received, bf16[5,256,256]{2,1,0:T(8,128)(2,1)S(1)} %bitcast.35, bf16[4,2,256,256]{3,2,1,0:T(8,128)(2,1)S(1)} %bitcast.29, ...), custom_call_target="tpu_custom_call" | custom-call | bytes 2719744 | tf_op jit(solution)/shard_map/pallas_call | solution.py:36
  7.7 1.8 %collective-permute-start.1 = (bf16[64,256]{1,0:T(8,128)(2,1)S(1)}, bf16[64,256]{1,0:T(8,128)(2,1)S(1)}, u32[]{:S(2)}, u32[]{:S(2)}) collective-permute-start(bf16[64,256]{1,0:T(8,128)(2,1)S(1)} %get-tuple-element.36), channel_id=1, source_target_pairs={{0,10},{1,11},{2,8},{3,9},{4,14},{5,15},{6,12},{7,13},{8,2},{9,3},... | collective-permute-start | bytes 98312 | tf_op jit(solution)/shard_map/ppermute | solution.py:31
  9.6 1.6 %collective-permute-start.9 = (bf16[384,256]{1,0:T(8,128)(2,1)S(1)}, bf16[384,256]{1,0:T(8,128)(2,1)S(1)}, u32[]{:S(2)}, u32[]{:S(2)}) collective-permute-start(bf16[384,256]{1,0:T(8,128)(2,1)S(1)} %shard_map.81.ends), channel_id=1, source_target_pairs={{0,16},{1,17},{2,18},{3,19},{4,20},{5,21},{6,22},{7,23},{8,24},{9,... | collective-permute-start | bytes 589832 | tf_op jit(solution)/shard_map/ppermute | solution.py:31
  11.4 3.0 %collective-permute-start.4 = (bf16[64,256]{1,0:T(8,128)(2,1)S(1)}, bf16[64,256]{1,0:T(8,128)(2,1)S(1)}, u32[]{:S(2)}, u32[]{:S(2)}) collective-permute-start(bf16[64,256]{1,0:T(8,128)(2,1)S(1)} %get-tuple-element.43), channel_id=1, source_target_pairs={{0,12},{1,13},{2,14},{3,15},{4,8},{5,9},{6,10},{7,11},{8,4},{9,5},... | collective-permute-start | bytes 98312 | tf_op jit(solution)/shard_map/ppermute | solution.py:31
  14.6 1.4 %collective-permute-done.4 = bf16[64,256]{1,0:T(8,128)(2,1)S(1)} collective-permute-done((bf16[64,256]{1,0:T(8,128)(2,1)S(1)}, bf16[64,256]{1,0:T(8,128)(2,1)S(1)}, u32[]{:S(2)}, u32[]{:S(2)}) %collective-permute-start.4) | collective-permute-done | bytes 32800 | tf_op jit(solution)/shard_map/ppermute | solution.py:31
  16.0 0.4 %shard_map.84 = (bf16[64,256]{1,0:T(8,128)(2,1)S(1)}, bf16[128,256]{1,0:T(8,128)(2,1)S(1)}) custom-call(f32[64,256]{1,0:T(8,128)S(1)} %convert_element_type.34.received, bf16[64,256]{1,0:T(8,128)(2,1)S(1)} %collective-permute-done.5.below.delta, bf16[2,256,256]{2,1,0:T(8,128)(2,1)S(1)} %get-tuple-element.46.product_below.product, ...), custom_call_target="tpu_custom_call" | custom-call | flops 1200000000 | bytes 1277952 | tf_op jit(solution)/shard_map/pallas_call | solution.py:36
  16.4 1.6 %collective-permute-start.7 = (bf16[128,256]{1,0:T(8,128)(2,1)S(1)}, bf16[128,256]{1,0:T(8,128)(2,1)S(1)}, u32[]{:S(2)}, u32[]{:S(2)}) collective-permute-start(bf16[128,256]{1,0:T(8,128)(2,1)S(1)} %get-tuple-element.47.sent), channel_id=1, source_target_pairs={{0,24},{1,25},{2,26},{3,27},{4,28},{5,29},{6,30},{7,31},{8,16},{9,... | collective-permute-start | bytes 196616 | tf_op jit(solution)/shard_map/ppermute | solution.py:31
  18.0 0.6 %shard_map.85.joined = bf16[704,256]{1,0:T(8,128)(2,1)S(1)} custom-call(bf16[512,256]{1,0:T(8,128)(2,1)S(1)} %shard_map.79.mine, bf16[512,256]{1,0:T(8,128)(2,1)S(1)} %collective-permute-done.6.mirror, bf16[384,256]{1,0:T(8,128)(2,1)S(1)} %shard_map.81.ends, bf16[384,256]{1,0:T(8,128)(2,1)S(1)} %collective-permute-done.9.mirror_ends, ...), custom_call_target="tpu_custom_call" | custom-call | flops 300000000 | bytes 1638400 | tf_op jit(solution)/shard_map/pallas_call | solution.py:36
  18.7 0.4 %collective-permute-start.12 = (bf16[2,256,256]{2,1,0:T(8,128)(2,1)S(1)}, bf16[2,256,256]{2,1,0:T(8,128)(2,1)S(1)}, u32[]{:S(2)}, u32[]{:S(2)}) collective-permute-start(bf16[2,256,256]{2,1,0:T(8,128)(2,1)S(1)} %shard_map.83.product), channel_id=1, source_target_pairs={{0,8},{1,9},{2,10},{3,11},{4,12},{5,13},{6,14},{7,15},{8,0},{9,1},... | collective-permute-start | bytes 786440 | tf_op jit(solution)/shard_map/ppermute | solution.py:31
  19.1 0.3 shard_map.87
  19.6 0.7 %collective-permute-done.7.across = bf16[128,256]{1,0:T(8,128)(2,1)S(1)} collective-permute-done((bf16[128,256]{1,0:T(8,128)(2,1)S(1)}, bf16[128,256]{1,0:T(8,128)(2,1)S(1)}, u32[]{:S(2)}, u32[]{:S(2)}) %collective-permute-start.7) | collective-permute-done | bytes 65568 | tf_op jit(solution)/shard_map/ppermute | solution.py:31
  20.3 0.3 collective-permute-start.8
  21.1 0.5 %collective-permute-done.8.theirs = bf16[128,256]{1,0:T(8,128)(2,1)S(1)} collective-permute-done((bf16[128,256]{1,0:T(8,128)(2,1)S(1)}, bf16[128,256]{1,0:T(8,128)(2,1)S(1)}, u32[]{:S(2)}, u32[]{:S(2)}) %collective-permute-start.8) | collective-permute-done | bytes 65568 | tf_op jit(solution)/shard_map/ppermute | solution.py:31
  21.6 0.3 shard_map.88
  21.9 2.5 %collective-permute-start.13 = (bf16[64,256]{1,0:T(8,128)(2,1)S(1)}, bf16[64,256]{1,0:T(8,128)(2,1)S(1)}, u32[]{:S(2)}, u32[]{:S(2)}) collective-permute-start(bf16[64,256]{1,0:T(8,128)(2,1)S(1)} %get-tuple-element.56), channel_id=1, source_target_pairs={{0,12},{1,13},{2,14},{3,15},{4,8},{5,9},{6,10},{7,11},{8,4},{9,5},... | collective-permute-start | bytes 98312 | tf_op jit(solution)/shard_map/ppermute | solution.py:31
  24.5 0.3 shard_map.93
  24.9 0.3 shard_map.91.solved
  25.2 0.4 %collective-permute-start.17 = (f32[64,256]{1,0:T(8,128)S(1)}, f32[64,256]{1,0:T(8,128)S(1)}, u32[]{:S(2)}, u32[]{:S(2)}) collective-permute-start(f32[64,256]{1,0:T(8,128)S(1)} %shard_map.93), channel_id=1, source_target_pairs={{0,8},{1,9},{2,10},{3,11},{4,12},{5,13},{6,14},{7,15},{8,0},{9,1},... | collective-permute-start | bytes 196616 | tf_op jit(solution)/shard_map/ppermute | solution.py:31
  25.7 0.5 %collective-permute-done.13.refs_0_ = bf16[64,256]{1,0:T(8,128)(2,1)S(1)} collective-permute-done((bf16[64,256]{1,0:T(8,128)(2,1)S(1)}, bf16[64,256]{1,0:T(8,128)(2,1)S(1)}, u32[]{:S(2)}, u32[]{:S(2)}) %collective-permute-start.13) | collective-permute-done | bytes 32800 | tf_op jit(solution)/shard_map/ppermute | solution.py:31
  26.4 1.6 %collective-permute-start.15 = (bf16[64,256]{1,0:T(8,128)(2,1)S(1)}, bf16[64,256]{1,0:T(8,128)(2,1)S(1)}, u32[]{:S(2)}, u32[]{:S(2)}) collective-permute-start(bf16[64,256]{1,0:T(8,128)(2,1)S(1)} %get-tuple-element.61), channel_id=1, source_target_pairs={{0,10},{1,11},{2,8},{3,9},{4,14},{5,15},{6,12},{7,13},{8,2},{9,3},... | collective-permute-start | bytes 98312 | tf_op jit(solution)/shard_map/ppermute | solution.py:31
  28.0 0.2 collective-permute-start.16
  28.5 1.3 %collective-permute-done.15 = bf16[64,256]{1,0:T(8,128)(2,1)S(1)} collective-permute-done((bf16[64,256]{1,0:T(8,128)(2,1)S(1)}, bf16[64,256]{1,0:T(8,128)(2,1)S(1)}, u32[]{:S(2)}, u32[]{:S(2)}) %collective-permute-start.15) | collective-permute-done | bytes 32800 | tf_op jit(solution)/shard_map/ppermute | solution.py:31
  30.0 1.4 %collective-permute-start.19 = (bf16[64,256]{1,0:T(8,128)(2,1)S(1)}, bf16[64,256]{1,0:T(8,128)(2,1)S(1)}, u32[]{:S(2)}, u32[]{:S(2)}) collective-permute-start(bf16[64,256]{1,0:T(8,128)(2,1)S(1)} %shard_map.95), channel_id=1, source_target_pairs={{0,9},{1,8},{2,11},{3,10},{4,13},{5,12},{6,15},{7,14},{8,1},{9,0},... | collective-permute-start | bytes 98312 | tf_op jit(solution)/shard_map/ppermute | solution.py:31
  31.6 0.4 %collective-permute-start.20 = (bf16[64,256]{1,0:T(8,128)(2,1)S(1)}, bf16[64,256]{1,0:T(8,128)(2,1)S(1)}, u32[]{:S(2)}, u32[]{:S(2)}) collective-permute-start(bf16[64,256]{1,0:T(8,128)(2,1)S(1)} %collective-permute-done.15), channel_id=1, source_target_pairs={{0,8},{1,9},{2,10},{3,11},{4,12},{5,13},{6,14},{7,15},{8,0},{9,1},... | collective-permute-start | bytes 98312 | tf_op jit(solution)/shard_map/ppermute | solution.py:31
  32.0 0.4 %shard_map.89 = (f32[64,256]{1,0:T(8,128)S(1)}, bf16[64,256]{1,0:T(8,128)(2,1)S(1)}) custom-call(bf16[512,256]{1,0:T(8,128)(2,1)S(1)} %shard_map.79.mine, bf16[512,256]{1,0:T(8,128)(2,1)S(1)} %collective-permute-done.6.mirror, bf16[384,256]{1,0:T(8,128)(2,1)S(1)} %shard_map.81.ends, bf16[384,256]{1,0:T(8,128)(2,1)S(1)} %collective-permute-done.9.mirror_ends, ...), custom_call_target="tpu_custom_call" | custom-call | flops 300000000 | bytes 1015808 | tf_op jit(solution)/shard_map/pallas_call | solution.py:36
  32.5 0.9 %collective-permute-done.19 = bf16[64,256]{1,0:T(8,128)(2,1)S(1)} collective-permute-done((bf16[64,256]{1,0:T(8,128)(2,1)S(1)}, bf16[64,256]{1,0:T(8,128)(2,1)S(1)}, u32[]{:S(2)}, u32[]{:S(2)}) %collective-permute-start.19) | collective-permute-done | bytes 32800 | tf_op jit(solution)/shard_map/ppermute | solution.py:31
  33.4 0.8 %shard_map.96 = (f32[64,128]{1,0:T(8,128)}, f32[5,64,256]{2,1,0:T(8,128)}) custom-call(f32[64,128]{1,0:T(8,128)S(1)} %shard_map.90.part, bf16[5,256,128]{2,1,0:T(8,128)(2,1)S(1)} %convolution_convert_fusion.leaf_products, f32[64,256]{1,0:T(8,128)S(1)} %convert_element_type.37.refs_0_, bf16[64,256]{1,0:T(8,128)(2,1)S(1)} %collective-permute-done.20.refs_1_, ...), custom_call_target="tpu_custom_call" | custom-call | flops 300000000 | bytes 720896 | tf_op jit(solution)/shard_map/pallas_call | solution.py:36
  (51 shorter events, 2.9 us)
Async XLA Ops:
  0.6 1.1 %copy-start = (bf16[1,5,256,128]{3,2,1,0:T(8,128)(2,1)S(1)}, bf16[1,5,256,128]{3,2,1,0:T(8,128)(2,1)}, u32[]{:S(2)}) copy-start(bf16[1,5,256,128]{3,2,1,0:T(8,128)(2,1)} %param.8) | copy-start | bytes 983044
  0.6 4.3 %copy-start.2 = (bf16[1,5,256,256]{3,2,1,0:T(8,128)(2,1)S(1)}, bf16[1,5,256,256]{3,2,1,0:T(8,128)(2,1)}, u32[]{:S(2)}) copy-start(bf16[1,5,256,256]{3,2,1,0:T(8,128)(2,1)} %param.10) | copy-start | bytes 1966084
  0.7 4.6 %copy-start.1 = (bf16[1,4,1,2,256,256]{5,4,3,2,1,0:T(8,128)(2,1)S(1)}, bf16[1,4,1,2,256,256]{5,4,3,2,1,0:T(8,128)(2,1)}, u32[]{:S(2)}) copy-start(bf16[1,4,1,2,256,256]{5,4,3,2,1,0:T(8,128)(2,1)} %param.11) | copy-start | bytes 3145732
  2.0 5.3 %collective-permute-start = (bf16[64,256]{1,0:T(8,128)(2,1)S(1)}, bf16[64,256]{1,0:T(8,128)(2,1)S(1)}, u32[]{:S(2)}, u32[]{:S(2)}) collective-permute-start(bf16[64,256]{1,0:T(8,128)(2,1)S(1)} %fusion.2), channel_id=1, source_target_pairs={{0,1},{1,0},{2,3},{3,2},{4,5},{5,4},{6,7},{7,6},{8,9},{9,8},{10,11... | collective-permute-start | bytes 98312 | tf_op jit(solution)/shard_map/ppermute | solution.py:31
  5.5 1.8 %copy-start.3 = (f32[1,5,256,64]{2,3,1,0:T(8,128)S(1)}, f32[1,5,256,64]{2,3,1,0:T(8,128)}, u32[]{:S(2)}) copy-start(f32[1,5,256,64]{2,3,1,0:T(8,128)} %param.9) | copy-start | bytes 983044
  5.5 10.5 %collective-permute-start.6 = (bf16[512,256]{1,0:T(8,128)(2,1)S(1)}, bf16[512,256]{1,0:T(8,128)(2,1)S(1)}, u32[]{:S(2)}, u32[]{:S(2)}) collective-permute-start(bf16[512,256]{1,0:T(8,128)(2,1)S(1)} %shard_map.79.mine), channel_id=1, source_target_pairs={{0,16},{1,17},{2,18},{3,19},{4,20},{5,21},{6,22},{7,23},{8,24},{9,... | collective-permute-start | bytes 786440 | tf_op jit(solution)/shard_map/ppermute | solution.py:31
  7.7 3.5 %collective-permute-start.3 = (bf16[320,256]{1,0:T(8,128)(2,1)S(1)}, bf16[320,256]{1,0:T(8,128)(2,1)S(1)}, u32[]{:S(2)}, u32[]{:S(2)}) collective-permute-start(bf16[320,256]{1,0:T(8,128)(2,1)S(1)} %get-tuple-element.41), channel_id=1, source_target_pairs={{0,8},{1,9},{2,10},{3,11},{4,12},{5,13},{6,14},{7,15},{8,0},{9,1},... | collective-permute-start | bytes 491528 | tf_op jit(solution)/shard_map/ppermute | solution.py:31
  7.7 3.5 %collective-permute-start.1 = (bf16[64,256]{1,0:T(8,128)(2,1)S(1)}, bf16[64,256]{1,0:T(8,128)(2,1)S(1)}, u32[]{:S(2)}, u32[]{:S(2)}) collective-permute-start(bf16[64,256]{1,0:T(8,128)(2,1)S(1)} %get-tuple-element.36), channel_id=1, source_target_pairs={{0,10},{1,11},{2,8},{3,9},{4,14},{5,15},{6,12},{7,13},{8,2},{9,3},... | collective-permute-start | bytes 98312 | tf_op jit(solution)/shard_map/ppermute | solution.py:31
  9.5 1.7 %collective-permute-start.2 = (bf16[64,256]{1,0:T(8,128)(2,1)S(1)}, bf16[64,256]{1,0:T(8,128)(2,1)S(1)}, u32[]{:S(2)}, u32[]{:S(2)}) collective-permute-start(bf16[64,256]{1,0:T(8,128)(2,1)S(1)} %get-tuple-element.37), channel_id=1, source_target_pairs={{0,8},{1,9},{2,10},{3,11},{4,12},{5,13},{6,14},{7,15},{8,0},{9,1},... | collective-permute-start | bytes 98312 | tf_op jit(solution)/shard_map/ppermute | solution.py:31
  9.6 8.4 %collective-permute-start.9 = (bf16[384,256]{1,0:T(8,128)(2,1)S(1)}, bf16[384,256]{1,0:T(8,128)(2,1)S(1)}, u32[]{:S(2)}, u32[]{:S(2)}) collective-permute-start(bf16[384,256]{1,0:T(8,128)(2,1)S(1)} %shard_map.81.ends), channel_id=1, source_target_pairs={{0,16},{1,17},{2,18},{3,19},{4,20},{5,21},{6,22},{7,23},{8,24},{9,... | collective-permute-start | bytes 589832 | tf_op jit(solution)/shard_map/ppermute | solution.py:31
  11.4 4.6 %collective-permute-start.4 = (bf16[64,256]{1,0:T(8,128)(2,1)S(1)}, bf16[64,256]{1,0:T(8,128)(2,1)S(1)}, u32[]{:S(2)}, u32[]{:S(2)}) collective-permute-start(bf16[64,256]{1,0:T(8,128)(2,1)S(1)} %get-tuple-element.43), channel_id=1, source_target_pairs={{0,12},{1,13},{2,14},{3,15},{4,8},{5,9},{6,10},{7,11},{8,4},{9,5},... | collective-permute-start | bytes 98312 | tf_op jit(solution)/shard_map/ppermute | solution.py:31
  14.4 1.6 %collective-permute-start.5 = (bf16[64,256]{1,0:T(8,128)(2,1)S(1)}, bf16[64,256]{1,0:T(8,128)(2,1)S(1)}, u32[]{:S(2)}, u32[]{:S(2)}) collective-permute-start(bf16[64,256]{1,0:T(8,128)(2,1)S(1)} %get-tuple-element.44), channel_id=1, source_target_pairs={{0,8},{1,9},{2,10},{3,11},{4,12},{5,13},{6,14},{7,15},{8,0},{9,1},... | collective-permute-start | bytes 98312 | tf_op jit(solution)/shard_map/ppermute | solution.py:31
  16.4 3.9 %collective-permute-start.7 = (bf16[128,256]{1,0:T(8,128)(2,1)S(1)}, bf16[128,256]{1,0:T(8,128)(2,1)S(1)}, u32[]{:S(2)}, u32[]{:S(2)}) collective-permute-start(bf16[128,256]{1,0:T(8,128)(2,1)S(1)} %get-tuple-element.47.sent), channel_id=1, source_target_pairs={{0,24},{1,25},{2,26},{3,27},{4,28},{5,29},{6,30},{7,31},{8,16},{9,... | collective-permute-start | bytes 196616 | tf_op jit(solution)/shard_map/ppermute | solution.py:31
  18.6 2.3 %collective-permute-start.10 = (bf16[704,256]{1,0:T(8,128)(2,1)S(1)}, bf16[704,256]{1,0:T(8,128)(2,1)S(1)}, u32[]{:S(2)}, u32[]{:S(2)}) collective-permute-start(bf16[704,256]{1,0:T(8,128)(2,1)S(1)} %shard_map.85.joined), channel_id=1, source_target_pairs={{0,8},{1,9},{2,10},{3,11},{4,12},{5,13},{6,14},{7,15},{8,0},{9,1},... | collective-permute-start | bytes 1081352 | tf_op jit(solution)/shard_map/ppermute | solution.py:31
  18.7 2.9 %collective-permute-start.12 = (bf16[2,256,256]{2,1,0:T(8,128)(2,1)S(1)}, bf16[2,256,256]{2,1,0:T(8,128)(2,1)S(1)}, u32[]{:S(2)}, u32[]{:S(2)}) collective-permute-start(bf16[2,256,256]{2,1,0:T(8,128)(2,1)S(1)} %shard_map.83.product), channel_id=1, source_target_pairs={{0,8},{1,9},{2,10},{3,11},{4,12},{5,13},{6,14},{7,15},{8,0},{9,1},... | collective-permute-start | bytes 786440 | tf_op jit(solution)/shard_map/ppermute | solution.py:31
  19.5 1.6 %collective-permute-start.11 = (f32[64,256]{1,0:T(8,128)S(1)}, f32[64,256]{1,0:T(8,128)S(1)}, u32[]{:S(2)}, u32[]{:S(2)}) collective-permute-start(f32[64,256]{1,0:T(8,128)S(1)} %shard_map.87), channel_id=1, source_target_pairs={{0,8},{1,9},{2,10},{3,11},{4,12},{5,13},{6,14},{7,15},{8,0},{9,1},... | collective-permute-start | bytes 196616 | tf_op jit(solution)/shard_map/ppermute | solution.py:31
  20.3 1.3 %collective-permute-start.8 = (bf16[128,256]{1,0:T(8,128)(2,1)S(1)}, bf16[128,256]{1,0:T(8,128)(2,1)S(1)}, u32[]{:S(2)}, u32[]{:S(2)}) collective-permute-start(bf16[128,256]{1,0:T(8,128)(2,1)S(1)} %collective-permute-done.7.across), channel_id=1, source_target_pairs={{0,8},{1,9},{2,10},{3,11},{4,12},{5,13},{6,14},{7,15},{8,0},{9,1},... | collective-permute-start | bytes 196616 | tf_op jit(solution)/shard_map/ppermute | solution.py:31
  21.9 4.3 %collective-permute-start.13 = (bf16[64,256]{1,0:T(8,128)(2,1)S(1)}, bf16[64,256]{1,0:T(8,128)(2,1)S(1)}, u32[]{:S(2)}, u32[]{:S(2)}) collective-permute-start(bf16[64,256]{1,0:T(8,128)(2,1)S(1)} %get-tuple-element.56), channel_id=1, source_target_pairs={{0,12},{1,13},{2,14},{3,15},{4,8},{5,9},{6,10},{7,11},{8,4},{9,5},... | collective-permute-start | bytes 98312 | tf_op jit(solution)/shard_map/ppermute | solution.py:31
  24.4 1.8 %collective-permute-start.14 = (bf16[64,256]{1,0:T(8,128)(2,1)S(1)}, bf16[64,256]{1,0:T(8,128)(2,1)S(1)}, u32[]{:S(2)}, u32[]{:S(2)}) collective-permute-start(bf16[64,256]{1,0:T(8,128)(2,1)S(1)} %get-tuple-element.56), channel_id=1, source_target_pairs={{0,8},{1,9},{2,10},{3,11},{4,12},{5,13},{6,14},{7,15},{8,0},{9,1},... | collective-permute-start | bytes 98312 | tf_op jit(solution)/shard_map/ppermute | solution.py:31
  25.2 4.6 %collective-permute-start.17 = (f32[64,256]{1,0:T(8,128)S(1)}, f32[64,256]{1,0:T(8,128)S(1)}, u32[]{:S(2)}, u32[]{:S(2)}) collective-permute-start(f32[64,256]{1,0:T(8,128)S(1)} %shard_map.93), channel_id=1, source_target_pairs={{0,8},{1,9},{2,10},{3,11},{4,12},{5,13},{6,14},{7,15},{8,0},{9,1},... | collective-permute-start | bytes 196616 | tf_op jit(solution)/shard_map/ppermute | solution.py:31
  25.6 4.2 %collective-permute-start.18 = (bf16[2,256,256]{2,1,0:T(8,128)(2,1)S(1)}, bf16[2,256,256]{2,1,0:T(8,128)(2,1)S(1)}, u32[]{:S(2)}, u32[]{:S(2)}) collective-permute-start(bf16[2,256,256]{2,1,0:T(8,128)(2,1)S(1)} %shard_map.94), channel_id=1, source_target_pairs={{0,8},{1,9},{2,10},{3,11},{4,12},{5,13},{6,14},{7,15},{8,0},{9,1},... | collective-permute-start | bytes 786440 | tf_op jit(solution)/shard_map/ppermute | solution.py:31
  26.2 2.1 %copy-start.4 = (bf16[1,128,128]{2,1,0:T(8,128)(2,1)S(1)}, bf16[1,128,128]{2,1,0:T(8,128)(2,1)}, u32[]{:S(2)}) copy-start(bf16[1,128,128]{2,1,0:T(8,128)(2,1)} %param.7) | copy-start | bytes 98308
  26.4 3.4 %collective-permute-start.15 = (bf16[64,256]{1,0:T(8,128)(2,1)S(1)}, bf16[64,256]{1,0:T(8,128)(2,1)S(1)}, u32[]{:S(2)}, u32[]{:S(2)}) collective-permute-start(bf16[64,256]{1,0:T(8,128)(2,1)S(1)} %get-tuple-element.61), channel_id=1, source_target_pairs={{0,10},{1,11},{2,8},{3,9},{4,14},{5,15},{6,12},{7,13},{8,2},{9,3},... | collective-permute-start | bytes 98312 | tf_op jit(solution)/shard_map/ppermute | solution.py:31
  28.0 1.8 %collective-permute-start.16 = (bf16[64,256]{1,0:T(8,128)(2,1)S(1)}, bf16[64,256]{1,0:T(8,128)(2,1)S(1)}, u32[]{:S(2)}, u32[]{:S(2)}) collective-permute-start(bf16[64,256]{1,0:T(8,128)(2,1)S(1)} %get-tuple-element.61), channel_id=1, source_target_pairs={{0,8},{1,9},{2,10},{3,11},{4,12},{5,13},{6,14},{7,15},{8,0},{9,1},... | collective-permute-start | bytes 98312 | tf_op jit(solution)/shard_map/ppermute | solution.py:31
  30.0 3.4 %collective-permute-start.19 = (bf16[64,256]{1,0:T(8,128)(2,1)S(1)}, bf16[64,256]{1,0:T(8,128)(2,1)S(1)}, u32[]{:S(2)}, u32[]{:S(2)}) collective-permute-start(bf16[64,256]{1,0:T(8,128)(2,1)S(1)} %shard_map.95), channel_id=1, source_target_pairs={{0,9},{1,8},{2,11},{3,10},{4,13},{5,12},{6,15},{7,14},{8,1},{9,0},... | collective-permute-start | bytes 98312 | tf_op jit(solution)/shard_map/ppermute | solution.py:31
  31.5 2.0 %collective-permute-start.21 = (bf16[64,256]{1,0:T(8,128)(2,1)S(1)}, bf16[64,256]{1,0:T(8,128)(2,1)S(1)}, u32[]{:S(2)}, u32[]{:S(2)}) collective-permute-start(bf16[64,256]{1,0:T(8,128)(2,1)S(1)} %shard_map.95), channel_id=1, source_target_pairs={{0,8},{1,9},{2,10},{3,11},{4,12},{5,13},{6,14},{7,15},{8,0},{9,1},... | collective-permute-start | bytes 98312 | tf_op jit(solution)/shard_map/ppermute | solution.py:31
  31.6 1.8 %collective-permute-start.20 = (bf16[64,256]{1,0:T(8,128)(2,1)S(1)}, bf16[64,256]{1,0:T(8,128)(2,1)S(1)}, u32[]{:S(2)}, u32[]{:S(2)}) collective-permute-start(bf16[64,256]{1,0:T(8,128)(2,1)S(1)} %collective-permute-done.15), channel_id=1, source_target_pairs={{0,8},{1,9},{2,10},{3,11},{4,12},{5,13},{6,14},{7,15},{8,0},{9,1},... | collective-permute-start | bytes 98312 | tf_op jit(solution)/shard_map/ppermute | solution.py:31

commit v7 on v6

--- a/solution.py
+++ b/solution.py
@@ -22,6 +22,10 @@
 
 def gram(left, right):
     return lax.dot_general(left, right, (((0,), (0,)), ((), ())), preferred_element_type=F32)
+
+
+def turned(inverse, coupling):
+    return lax.dot_general(inverse, coupling, (((0,), (1,)), ((), ())), preferred_element_type=F32)
 
 
 def exchange(value, level, gy_levels, cross=False):
@@ -49,13 +53,18 @@
         out[side] = times(coupling[level, side], inverse[level]).astype(BF)
 
 
-def products_ahead(inverse, coupling, terms, out, ahead, *, level):
+def products_ahead(inverse, coupling, terms, ahead, *, level):
     rows = inverse.shape[1]
-    out[0] = times(coupling[level, 0], inverse[level]).astype(BF)
-    mirror = times(coupling[level, 1], inverse[level]).astype(BF)
-    out[1] = mirror
-    ahead[:rows] = mirror
+    ahead[:rows] = turned(inverse[level], coupling[level, 1]).astype(BF)
     ahead[rows:] = terms[level + 1].astype(BF)
+
+
+def products_last(inverse, coupling, out, out_turned, below, below_turned, *, level):
+    for side in range(2):
+        out[side] = times(coupling[level, side], inverse[level]).astype(BF)
+        below[side] = times(coupling[level - 1, side], inverse[level - 1]).astype(BF)
+        out_turned[side] = turned(inverse[level], coupling[level, side]).astype(BF)
+    below_turned[...] = turned(inverse[level - 1], coupling[level - 1, 0]).astype(BF)
 
 
 def top_gram(inverse, out):
@@ -85,7 +94,7 @@
     rows = ahead.shape[1]
     change = (residue[...].astype(F32) - received[...].astype(F32)).astype(BF)
     delta[...] = change
-    out[...] = (ahead[rows:].astype(F32) + times_t(change, ahead[:rows])).astype(BF)
+    out[...] = (ahead[rows:].astype(F32) + times(change, ahead[:rows])).astype(BF)
 
 
 def forward_back(received, below, product_below, product, terms, values, delta, out, *, level):
@@ -107,28 +116,29 @@
     out[rows:] = (values[level + 1] - times_t(change, product[0])).astype(BF)
 
 
-def forward_first(residue, received, inverse, coupling, terms, values, delta, out, ahead):
+def forward_lowest(residue, received, product, terms, values, delta, out, ahead):
     change = (residue[0] - received[...].astype(F32)).astype(BF)
     delta[...] = change
-    step = times_t(change, inverse[0]).astype(BF)
-    out[...] = (terms[1] + times_t(step, coupling[0, 1])).astype(BF)
-    ahead[...] = (values[1] - times_t(step, coupling[0, 0])).astype(BF)
+    out[...] = (terms[1] + times(change, product[1])).astype(BF)
+    ahead[...] = (values[1] - times(change, product[0])).astype(BF)
 
 
 def forward_last(received, below, product_below, product, terms, values, delta, out, *, level):
-    residue = values[level] - times_t(below[...], product_below[0])
+    residue = values[level] - times(below[...], product_below[...])
     change = (residue - received[...].astype(F32)).astype(BF)
     delta[...] = change
     rows = change.shape[0]
-    out[:rows] = (terms[level + 1] + times_t(change, product[1])).astype(BF)
-    out[rows:] = (values[level + 1] - times_t(change, product[0])).astype(BF)
-
-
-def pack_top(inverse, coupling, out, *, level):
+    out[:rows] = (terms[level + 1] + times(change, product[1])).astype(BF)
+    out[rows:] = (values[level + 1] - times(change, product[0])).astype(BF)
+
+
+def early_products(inverse, coupling, terms, pack, ahead, lowest, *, level):
     width = inverse.shape[1]
     for side in range(2):
         made = times(coupling[level, side], inverse[level]).astype(BF)
-        out[side * width : (side + 1) * width] = made
+        pack[side * width : (side + 1) * width] = made
+        lowest[side] = turned(inverse[0], coupling[0, side]).astype(BF)
+    products_ahead(inverse, coupling, terms, ahead, level=1)
 
 
 def top_ends(own_gram, terms, values, out):
@@ -162,29 +172,34 @@
     return right.astype(BF), mirror_right.astype(BF)
 
 
-def join_own(joined, joined_mate, out, delta):
-    rows, width = out.shape[1], joined.shape[1]
+def join_own(joined, joined_mate, solved, product, part, delta, folded, base, *, home):
+    rows, width = part.shape[1], joined.shape[1]
     mine, mate = joined[2 * width + rows :], joined_mate[2 * width + rows :]
     for at, (a, b, matrices) in enumerate(((mine, mate, joined), (mate, mine, joined_mate))):
         change = (a[rows:].astype(F32) - b[:rows].astype(F32)).astype(BF)
         delta[at] = change
-        out[at] = times(change, matrices[:width]) + matrices[2 * width : 2 * width + rows].astype(F32)
-
-
-def join(theirs, across, part, joined, joined_mate, solved, product, block, block_mate, delta, below, *, home):
-    rows, width = part.shape[1], joined.shape[1]
-    found = []
-    pairs = ((theirs, across, joined), (across, theirs, joined_mate))
-    for at, (a, b, matrices) in enumerate(pairs):
-        change = (a[rows:].astype(F32) - b[:rows].astype(F32)).astype(BF)
-        value = part[at] + times(change, matrices[width : 2 * width])
-        found.append(value.astype(BF))
-        if at == 0:
-            block[...] = value
-            delta[0] = change
-    block_mate[...] = found[1]
-    own, other = found if home else found[::-1]
-    below[...] = (solved[...] - times(own, product[0]) - times(other, product[1])).astype(BF)
+        part[at] = times(change, matrices[:width]) + matrices[2 * width : 2 * width + rows].astype(F32)
+    total = solved[...]
+    for side, at in enumerate((0, 1) if home else (1, 0)):
+        matrices = (joined, joined_mate)[at]
+        total = total - times(part[at].astype(BF), product[side])
+        folded[side] = times(matrices[width : 2 * width], product[side]).astype(BF)
+    base[...] = total
+
+
+def join(theirs, across, base, folded, delta, below, *, home):
+    rows = base.shape[0]
+    for at, (a, b) in enumerate(((theirs, across), (across, theirs))):
+        delta[at] = (a[rows:].astype(F32) - b[:rows].astype(F32)).astype(BF)
+    own, other = (delta[0], delta[1]) if home else (delta[1], delta[0])
+    below[...] = (base[...] - times(own, folded[0]) - times(other, folded[1])).astype(BF)
+
+
+def join_blocks(part, delta, joined, joined_mate, block, block_mate):
+    width = joined.shape[1]
+    block[...] = part[0] + times(delta[0], joined[width : 2 * width])
+    value = part[1] + times(delta[1], joined_mate[width : 2 * width])
+    block_mate[...] = value.astype(BF)
 
 
 def top_blocks(mine, mirror, ends, mirror_ends, delta, delta_mirror, out, mirrored):
@@ -288,23 +303,25 @@
     terms = jnp.einsum("kwn,rn->krw", leaf_cpl, leaf.astype(BF), preferred_element_type=F32)
     received = send(terms[0].astype(BF), 0)
     product, ahead, solved = [None] * below_top, [None] * below_top, [None] * below_top
-    joined = levels == core + 2 and core >= 3
+    joined = levels == core + 2 and core >= 3 and core % 2 == 1
     own_gram = call(top_gram, [((width, width), BF)], inverse)
     inverse_later = after(inverse, own_gram)
     if joined:
-        pack = call(
-            pack_top, [((2 * width, width), BF)], inverse_later, coupling, level=core
+        pack, ahead[1], lowest = call(
+            early_products, [((2 * width, width), BF), ((width + cols, width), BF), pair],
+            inverse_later, coupling, terms, level=core,
         )
         mirror_pack = send(pack, below_top)
         inverse_later = after(inverse, pack)
         ends = call(top_ends, [((width + 2 * cols, width), BF)], own_gram, terms, values, cost=0)
-    for level in range(core if joined else below_top):
-        if at_home[level]:
-            product[level] = call(products, [pair], inverse_later, coupling, level=level, cost=(8, 1, 1)[min(level, 2)])
-        else:
-            product[level], ahead[level] = call(
-                products_ahead, [pair, ((width + cols, width), BF)],
-                inverse_later, coupling, terms, level=level,
+    for level in range(core - 2 if joined else below_top):
+        product[level] = call(
+            products, [pair], inverse_later, coupling, level=level, cost=8 if level == 0 else 1
+        )
+    for level in range(core):
+        if not at_home[level] and ahead[level] is None:
+            ahead[level] = call(
+                products_ahead, [((width + cols, width), BF)], inverse_later, coupling, terms, level=level
             )
 
     residue, change = values, None
@@ -314,7 +331,7 @@
             below, mirror_pack = lax.optimization_barrier((below, mirror_pack))
             change, out = call(
                 forward_last, [vec_bf, ((2 * cols, width), BF)], arrived(received), below,
-                product[level - 1], product[level], terms, values, level=level, cost=4,
+                below_turned, last_turned, terms, values, level=level, cost=4,
             )
             received = send(out, below_top, True)
         elif level == levels - 2:
@@ -337,10 +354,10 @@
                     forward_back, [vec_bf, vec_bf], arrived(received), below,
                     product[level - 1], product[level], terms, values, level=level, cost=1,
                 )
-            elif level == 0 and not at_home[1]:
+            elif joined and level == 0:
                 change, out, residue = call(
-                    forward_first, [vec_bf, vec_bf, vec_bf],
-                    residue, received, inverse, coupling, terms, values, cost=0,
+                    forward_lowest, [vec_bf, vec_bf, vec_bf],
+                    residue, received, lowest, terms, values, cost=0,
                 )
             elif not at_home[level + 1]:
                 change, out, residue = call(
@@ -352,6 +369,11 @@
                     forward, [vec_bf, vec_bf], residue, received, product[level], terms, level=level
                 )
             received = send(out, level + 1, across)
+            if joined and level == core - 2:
+                product[core - 1], last_turned, product[core - 2], below_turned = call(
+                    products_last, [pair, pair, pair, ((width, width), BF)],
+                    after(inverse, out), coupling, level=core - 1, cost=1,
+                )
             if level == 0:
                 if joined:
                     mirror_ends = send(after(ends, out), below_top)
@@ -382,12 +404,17 @@
         )
         matrices_mate = mate(matrices)
         both, both_bf = ((2, cols, width), F32), ((2, cols, width), BF)
-        part, delta = call(join_own, [both, both_bf], matrices, matrices_mate)
+        at_own = core - 1 not in mates
+        part, delta, folded, base = call(
+            join_own, [both, both_bf, pair, vec],
+            matrices, matrices_mate, solved[core - 1], product[core - 1], home=at_own,
+        )
         theirs = mate(received)
-        blocks[core], mirrored[core], delta_mirror, block_bf = call(
-            join, [vec, vec_bf, ((1, cols, width), BF), vec_bf],
-            theirs, received, part, matrices, matrices_mate, solved[core - 1], product[core - 1],
-            home=core - 1 not in mates,
+        delta_mirror, block_bf = call(
+            join, [both_bf, vec_bf], theirs, received, base, folded, home=at_own
+        )
+        blocks[core], mirrored[core] = call(
+            join_blocks, [vec, vec_bf], part, delta_mirror, matrices, matrices_mate
         )
         blocks[-1], mirrored[-1] = call(
             top_blocks, [vec, vec_bf], pack, mirror_pack, ends, mirror_ends, delta, delta_mirror

time: 34.4 us -> 34.2 us (level)
  starting transfers between devices: 20.7 us -> 20.3 us
    ppermute x22, starting transfers between devices: 20.7 us -> 20.3 us  [exchange(): return lax.ppermute(value, ('gx', 'gy'), pairs)]
  transfers between devices with their start and end apart: 22 -> 22, of which waited for: 6 -> 6; matrix products, arithmetic and copies ran while one was open for 1% -> 1% of each run, Pallas kernels for 13% -> 14%
where the time goes in v7:
time: 34.2 us; the launch traced here: 34 us
  starting transfers between devices  20.3 us (59%)
  Pallas kernels  5.85 us (17%)
  waiting for transfers between devices  5.45 us (16%)
  matrix products  1.52 us (4%)
  between operations  0.88 us (3%)
    ppermute x22, starting transfers between devices, exchange(): return lax.ppermute(value, ('gx', 'gy'), pairs)  20.3 us
    pallas_call x20, Pallas kernels, call(): pl.pallas_call(functools.partial(body, **static), out_shape=[jax.ShapeDty...  5.85 us
    ppermute x22, waiting for transfers between devices, exchange(): return lax.ppermute(value, ('gx', 'gy'), pairs)  5.45 us
    dot_general x1, matrix products, times_t(): lax.dot_general(values, matrix, (((1,), (1,)), ((), ())), preferred_eleme...  1.04 us
  transfers between devices with their start and end apart: 22, of which 6 were waited for; matrix products, arithmetic and copies ran while one was open for 1% of the time, Pallas kernels for 14%

profile of v7, /device:TPU:0, one launch (start us, length us, event | category | flops | bytes accessed | tf_op | source)
XLA Modules:
  0.0 34.0 jit_solution(15418529906880543813)
XLA Ops:
  0.7 1.0 %fusion.6.leaf = f32[64,128]{1,0:T(8,128)S(1)} fusion(f32[128,64]{0,1:T(8,128)} %param.6, bf16[1,128,128]{2,1,0:T(8,128)(2,1)} %param.7), kind=kOutput, calls=%fused_computation.9 | convolution fusion | flops 2105344 | bytes 98304 | tf_op jit(solution)/shard_map/dot_general | solution.py:20
  1.7 0.3 convolution_bitcast_fusion.terms
  2.0 3.0 %collective-permute-start = (bf16[64,256]{1,0:T(8,128)(2,1)S(1)}, bf16[64,256]{1,0:T(8,128)(2,1)S(1)}, u32[]{:S(2)}, u32[]{:S(2)}) collective-permute-start(bf16[64,256]{1,0:T(8,128)(2,1)S(1)} %fusion.2), channel_id=1, source_target_pairs={{0,1},{1,0},{2,3},{3,2},{4,5},{5,4},{6,7},{7,6},{8,9},{9,8},{10,11... | collective-permute-start | bytes 98312 | tf_op jit(solution)/shard_map/ppermute | solution.py:35
  5.0 0.2 shard_map.77.own_gram
  5.2 0.3 %shard_map.78 = (bf16[512,256]{1,0:T(8,128)(2,1)S(1)}, bf16[320,256]{1,0:T(8,128)(2,1)S(1)}, bf16[2,256,256]{2,1,0:T(8,128)(2,1)S(1)}) custom-call(bf16[5,256,256]{2,1,0:T(8,128)(2,1)S(1)} %bitcast.28, bf16[4,2,256,256]{3,2,1,0:T(8,128)(2,1)S(1)} %bitcast.35, f32[5,64,256]{2,1,0:T(8,128)S(1)} %convolution_bitcast_fusion.terms), custom_call_target="tpu_custom_call" | custom-call | flops 300000000 | bytes 2031616 | tf_op jit(solution)/shard_map/pallas_call | solution.py:40
  5.6 1.6 %collective-permute-start.6 = (bf16[512,256]{1,0:T(8,128)(2,1)S(1)}, bf16[512,256]{1,0:T(8,128)(2,1)S(1)}, u32[]{:S(2)}, u32[]{:S(2)}) collective-permute-start(bf16[512,256]{1,0:T(8,128)(2,1)S(1)} %get-tuple-element.53.mine), channel_id=1, source_target_pairs={{0,16},{1,17},{2,18},{3,19},{4,20},{5,21},{6,22},{7,23},{8,24},{9,... | collective-permute-start | bytes 786440 | tf_op jit(solution)/shard_map/ppermute | solution.py:35
  7.4 1.9 %collective-permute-start.1 = (bf16[64,256]{1,0:T(8,128)(2,1)S(1)}, bf16[64,256]{1,0:T(8,128)(2,1)S(1)}, u32[]{:S(2)}, u32[]{:S(2)}) collective-permute-start(bf16[64,256]{1,0:T(8,128)(2,1)S(1)} %get-tuple-element.46), channel_id=1, source_target_pairs={{0,10},{1,11},{2,8},{3,9},{4,14},{5,15},{6,12},{7,13},{8,2},{9,3},... | collective-permute-start | bytes 98312 | tf_op jit(solution)/shard_map/ppermute | solution.py:35
  9.4 1.6 %collective-permute-start.9 = (bf16[384,256]{1,0:T(8,128)(2,1)S(1)}, bf16[384,256]{1,0:T(8,128)(2,1)S(1)}, u32[]{:S(2)}, u32[]{:S(2)}) collective-permute-start(bf16[384,256]{1,0:T(8,128)(2,1)S(1)} %shard_map.80.ends), channel_id=1, source_target_pairs={{0,16},{1,17},{2,18},{3,19},{4,20},{5,21},{6,22},{7,23},{8,24},{9,... | collective-permute-start | bytes 589832 | tf_op jit(solution)/shard_map/ppermute | solution.py:35
  11.2 3.0 %collective-permute-start.4 = (bf16[64,256]{1,0:T(8,128)(2,1)S(1)}, bf16[64,256]{1,0:T(8,128)(2,1)S(1)}, u32[]{:S(2)}, u32[]{:S(2)}) collective-permute-start(bf16[64,256]{1,0:T(8,128)(2,1)S(1)} %get-tuple-element.51), channel_id=1, source_target_pairs={{0,12},{1,13},{2,14},{3,15},{4,8},{5,9},{6,10},{7,11},{8,4},{9,5},... | collective-permute-start | bytes 98312 | tf_op jit(solution)/shard_map/ppermute | solution.py:35
  14.2 0.4 %shard_map.82 = (bf16[2,256,256]{2,1,0:T(8,128)(2,1)S(1)}, bf16[2,256,256]{2,1,0:T(8,128)(2,1)S(1)}, bf16[2,256,256]{2,1,0:T(8,128)(2,1)S(1)}, bf16[256,256]{1,0:T(8,128)(2,1)S(1)}) custom-call(bf16[5,256,256]{2,1,0:T(8,128)(2,1)S(1)} %bitcast.29, bf16[4,2,256,256]{3,2,1,0:T(8,128)(2,1)S(1)} %bitcast.36), custom_call_target="tpu_custom_call" | custom-call | flops 300000000 | bytes 1703936 | tf_op jit(solution)/shard_map/pallas_call | solution.py:40
  14.6 1.2 %collective-permute-done.4 = bf16[64,256]{1,0:T(8,128)(2,1)S(1)} collective-permute-done((bf16[64,256]{1,0:T(8,128)(2,1)S(1)}, bf16[64,256]{1,0:T(8,128)(2,1)S(1)}, u32[]{:S(2)}, u32[]{:S(2)}) %collective-permute-start.4) | collective-permute-done | bytes 32800 | tf_op jit(solution)/shard_map/ppermute | solution.py:35
  15.8 0.3 shard_map.83
  16.1 1.6 %collective-permute-start.7 = (bf16[128,256]{1,0:T(8,128)(2,1)S(1)}, bf16[128,256]{1,0:T(8,128)(2,1)S(1)}, u32[]{:S(2)}, u32[]{:S(2)}) collective-permute-start(bf16[128,256]{1,0:T(8,128)(2,1)S(1)} %get-tuple-element.58.sent), channel_id=1, source_target_pairs={{0,24},{1,25},{2,26},{3,27},{4,28},{5,29},{6,30},{7,31},{8,16},{9,... | collective-permute-start | bytes 196616 | tf_op jit(solution)/shard_map/ppermute | solution.py:35
  17.8 0.6 %shard_map.84.joined = bf16[704,256]{1,0:T(8,128)(2,1)S(1)} custom-call(bf16[512,256]{1,0:T(8,128)(2,1)S(1)} %get-tuple-element.53.mine, bf16[512,256]{1,0:T(8,128)(2,1)S(1)} %collective-permute-done.6.mirror, bf16[384,256]{1,0:T(8,128)(2,1)S(1)} %shard_map.80.ends, bf16[384,256]{1,0:T(8,128)(2,1)S(1)} %collective-permute-done.9.mirror_ends, ...), custom_call_target="tpu_custom_call" | custom-call | flops 300000000 | bytes 1638400 | tf_op jit(solution)/shard_map/pallas_call | solution.py:40
  18.4 0.5 %collective-permute-start.10 = (bf16[704,256]{1,0:T(8,128)(2,1)S(1)}, bf16[704,256]{1,0:T(8,128)(2,1)S(1)}, u32[]{:S(2)}, u32[]{:S(2)}) collective-permute-start(bf16[704,256]{1,0:T(8,128)(2,1)S(1)} %shard_map.84.joined), channel_id=1, source_target_pairs={{0,8},{1,9},{2,10},{3,11},{4,12},{5,13},{6,14},{7,15},{8,0},{9,1},... | collective-permute-start | bytes 1081352 | tf_op jit(solution)/shard_map/ppermute | solution.py:35
  18.9 0.3 shard_map.85
  19.3 0.9 %collective-permute-done.7.across = bf16[128,256]{1,0:T(8,128)(2,1)S(1)} collective-permute-done((bf16[128,256]{1,0:T(8,128)(2,1)S(1)}, bf16[128,256]{1,0:T(8,128)(2,1)S(1)}, u32[]{:S(2)}, u32[]{:S(2)}) %collective-permute-start.7) | collective-permute-done | bytes 65568 | tf_op jit(solution)/shard_map/ppermute | solution.py:35
  20.7 0.5 %shard_map.86 = (f32[2,64,256]{2,1,0:T(8,128)S(1)}, bf16[2,64,256]{2,1,0:T(8,128)(2,1)S(1)}, bf16[2,256,256]{2,1,0:T(8,128)(2,1)S(1)}, f32[64,256]{1,0:T(8,128)S(1)}) custom-call(bf16[704,256]{1,0:T(8,128)(2,1)S(1)} %shard_map.84.joined, bf16[704,256]{1,0:T(8,128)(2,1)S(1)} %collective-permute-done.10.joined_mate, ...), custom_call_target="tpu_custom_call" | custom-call | flops 300000000 | bytes 1048576 | tf_op jit(solution)/shard_map/pallas_call | solution.py:40
  21.1 0.4 %collective-permute-done.8.theirs = bf16[128,256]{1,0:T(8,128)(2,1)S(1)} collective-permute-done((bf16[128,256]{1,0:T(8,128)(2,1)S(1)}, bf16[128,256]{1,0:T(8,128)(2,1)S(1)}, u32[]{:S(2)}, u32[]{:S(2)}) %collective-permute-start.8) | collective-permute-done | bytes 65568 | tf_op jit(solution)/shard_map/ppermute | solution.py:35
  21.7 2.3 %collective-permute-start.13 = (bf16[64,256]{1,0:T(8,128)(2,1)S(1)}, bf16[64,256]{1,0:T(8,128)(2,1)S(1)}, u32[]{:S(2)}, u32[]{:S(2)}) collective-permute-start(bf16[64,256]{1,0:T(8,128)(2,1)S(1)} %get-tuple-element.69), channel_id=1, source_target_pairs={{0,12},{1,13},{2,14},{3,15},{4,8},{5,9},{6,10},{7,11},{8,4},{9,5},... | collective-permute-start | bytes 98312 | tf_op jit(solution)/shard_map/ppermute | solution.py:35
  24.2 0.3 shard_map.93
  24.5 0.3 shard_map.91.solved
  24.8 0.4 %collective-permute-start.17 = (f32[64,256]{1,0:T(8,128)S(1)}, f32[64,256]{1,0:T(8,128)S(1)}, u32[]{:S(2)}, u32[]{:S(2)}) collective-permute-start(f32[64,256]{1,0:T(8,128)S(1)} %shard_map.93), channel_id=1, source_target_pairs={{0,8},{1,9},{2,10},{3,11},{4,12},{5,13},{6,14},{7,15},{8,0},{9,1},... | collective-permute-start | bytes 196616 | tf_op jit(solution)/shard_map/ppermute | solution.py:35
  25.4 0.6 %collective-permute-done.13.refs_0_ = bf16[64,256]{1,0:T(8,128)(2,1)S(1)} collective-permute-done((bf16[64,256]{1,0:T(8,128)(2,1)S(1)}, bf16[64,256]{1,0:T(8,128)(2,1)S(1)}, u32[]{:S(2)}, u32[]{:S(2)}) %collective-permute-start.13) | collective-permute-done | bytes 32800 | tf_op jit(solution)/shard_map/ppermute | solution.py:35
  26.2 1.5 %collective-permute-start.15 = (bf16[64,256]{1,0:T(8,128)(2,1)S(1)}, bf16[64,256]{1,0:T(8,128)(2,1)S(1)}, u32[]{:S(2)}, u32[]{:S(2)}) collective-permute-start(bf16[64,256]{1,0:T(8,128)(2,1)S(1)} %get-tuple-element.76), channel_id=1, source_target_pairs={{0,10},{1,11},{2,8},{3,9},{4,14},{5,15},{6,12},{7,13},{8,2},{9,3},... | collective-permute-start | bytes 98312 | tf_op jit(solution)/shard_map/ppermute | solution.py:35
  27.7 0.2 collective-permute-start.16
  28.1 0.4 %shard_map.89 = (f32[64,256]{1,0:T(8,128)S(1)}, bf16[64,256]{1,0:T(8,128)(2,1)S(1)}) custom-call(bf16[512,256]{1,0:T(8,128)(2,1)S(1)} %get-tuple-element.53.mine, bf16[512,256]{1,0:T(8,128)(2,1)S(1)} %collective-permute-done.6.mirror, bf16[384,256]{1,0:T(8,128)(2,1)S(1)} %shard_map.80.ends, bf16[384,256]{1,0:T(8,128)(2,1)S(1)} %collective-permute-done.9.mirror_ends, ...), custom_call_target="tpu_custom_call" | custom-call | flops 300000000 | bytes 1048576 | tf_op jit(solution)/shard_map/pallas_call | solution.py:40
  28.5 1.1 %collective-permute-done.15 = bf16[64,256]{1,0:T(8,128)(2,1)S(1)} collective-permute-done((bf16[64,256]{1,0:T(8,128)(2,1)S(1)}, bf16[64,256]{1,0:T(8,128)(2,1)S(1)}, u32[]{:S(2)}, u32[]{:S(2)}) %collective-permute-start.15) | collective-permute-done | bytes 32800 | tf_op jit(solution)/shard_map/ppermute | solution.py:35
  29.8 1.3 %collective-permute-start.19 = (bf16[64,256]{1,0:T(8,128)(2,1)S(1)}, bf16[64,256]{1,0:T(8,128)(2,1)S(1)}, u32[]{:S(2)}, u32[]{:S(2)}) collective-permute-start(bf16[64,256]{1,0:T(8,128)(2,1)S(1)} %shard_map.95), channel_id=1, source_target_pairs={{0,9},{1,8},{2,11},{3,10},{4,13},{5,12},{6,15},{7,14},{8,1},{9,0},... | collective-permute-start | bytes 98312 | tf_op jit(solution)/shard_map/ppermute | solution.py:35
  31.2 0.4 %collective-permute-start.20 = (bf16[64,256]{1,0:T(8,128)(2,1)S(1)}, bf16[64,256]{1,0:T(8,128)(2,1)S(1)}, u32[]{:S(2)}, u32[]{:S(2)}) collective-permute-start(bf16[64,256]{1,0:T(8,128)(2,1)S(1)} %collective-permute-done.15), channel_id=1, source_target_pairs={{0,8},{1,9},{2,10},{3,11},{4,12},{5,13},{6,14},{7,15},{8,0},{9,1},... | collective-permute-start | bytes 98312 | tf_op jit(solution)/shard_map/ppermute | solution.py:35
  32.0 1.3 %collective-permute-done.19 = bf16[64,256]{1,0:T(8,128)(2,1)S(1)} collective-permute-done((bf16[64,256]{1,0:T(8,128)(2,1)S(1)}, bf16[64,256]{1,0:T(8,128)(2,1)S(1)}, u32[]{:S(2)}, u32[]{:S(2)}) %collective-permute-start.19) | collective-permute-done | bytes 32800 | tf_op jit(solution)/shard_map/ppermute | solution.py:35
  33.2 0.8 %shard_map.96 = (f32[64,128]{1,0:T(8,128)}, f32[5,64,256]{2,1,0:T(8,128)}) custom-call(f32[64,128]{1,0:T(8,128)S(1)} %shard_map.90.part, bf16[5,256,128]{2,1,0:T(8,128)(2,1)S(1)} %convolution_convert_fusion.leaf_products, f32[64,256]{1,0:T(8,128)S(1)} %convert_element_type.37.refs_0_, bf16[64,256]{1,0:T(8,128)(2,1)S(1)} %collective-permute-done.20.refs_1_, ...), custom_call_target="tpu_custom_call" | custom-call | flops 300000000 | bytes 720896 | tf_op jit(solution)/shard_map/pallas_call | solution.py:40
  (51 shorter events, 2.7 us)
Async XLA Ops:
  0.6 1.1 %copy-start = (bf16[1,5,256,128]{3,2,1,0:T(8,128)(2,1)S(1)}, bf16[1,5,256,128]{3,2,1,0:T(8,128)(2,1)}, u32[]{:S(2)}) copy-start(bf16[1,5,256,128]{3,2,1,0:T(8,128)(2,1)} %param.8) | copy-start | bytes 983044
  0.6 4.3 %copy-start.1 = (bf16[1,5,256,256]{3,2,1,0:T(8,128)(2,1)S(1)}, bf16[1,5,256,256]{3,2,1,0:T(8,128)(2,1)}, u32[]{:S(2)}) copy-start(bf16[1,5,256,256]{3,2,1,0:T(8,128)(2,1)} %param.10) | copy-start | bytes 1966084
  0.7 4.6 %copy-start.2 = (bf16[1,4,1,2,256,256]{5,4,3,2,1,0:T(8,128)(2,1)S(1)}, bf16[1,4,1,2,256,256]{5,4,3,2,1,0:T(8,128)(2,1)}, u32[]{:S(2)}) copy-start(bf16[1,4,1,2,256,256]{5,4,3,2,1,0:T(8,128)(2,1)} %param.11) | copy-start | bytes 3145732
  2.0 5.2 %collective-permute-start = (bf16[64,256]{1,0:T(8,128)(2,1)S(1)}, bf16[64,256]{1,0:T(8,128)(2,1)S(1)}, u32[]{:S(2)}, u32[]{:S(2)}) collective-permute-start(bf16[64,256]{1,0:T(8,128)(2,1)S(1)} %fusion.2), channel_id=1, source_target_pairs={{0,1},{1,0},{2,3},{3,2},{4,5},{5,4},{6,7},{7,6},{8,9},{9,8},{10,11... | collective-permute-start | bytes 98312 | tf_op jit(solution)/shard_map/ppermute | solution.py:35
  5.2 2.0 %copy-start.3 = (f32[1,5,256,64]{2,3,1,0:T(8,128)S(1)}, f32[1,5,256,64]{2,3,1,0:T(8,128)}, u32[]{:S(2)}) copy-start(f32[1,5,256,64]{2,3,1,0:T(8,128)} %param.9) | copy-start | bytes 983044
  5.6 10.2 %collective-permute-start.6 = (bf16[512,256]{1,0:T(8,128)(2,1)S(1)}, bf16[512,256]{1,0:T(8,128)(2,1)S(1)}, u32[]{:S(2)}, u32[]{:S(2)}) collective-permute-start(bf16[512,256]{1,0:T(8,128)(2,1)S(1)} %get-tuple-element.53.mine), channel_id=1, source_target_pairs={{0,16},{1,17},{2,18},{3,19},{4,20},{5,21},{6,22},{7,23},{8,24},{9,... | collective-permute-start | bytes 786440 | tf_op jit(solution)/shard_map/ppermute | solution.py:35
  7.4 3.7 %collective-permute-start.3 = (bf16[320,256]{1,0:T(8,128)(2,1)S(1)}, bf16[320,256]{1,0:T(8,128)(2,1)S(1)}, u32[]{:S(2)}, u32[]{:S(2)}) collective-permute-start(bf16[320,256]{1,0:T(8,128)(2,1)S(1)} %get-tuple-element.49), channel_id=1, source_target_pairs={{0,8},{1,9},{2,10},{3,11},{4,12},{5,13},{6,14},{7,15},{8,0},{9,1},... | collective-permute-start | bytes 491528 | tf_op jit(solution)/shard_map/ppermute | solution.py:35
  7.4 3.6 %collective-permute-start.1 = (bf16[64,256]{1,0:T(8,128)(2,1)S(1)}, bf16[64,256]{1,0:T(8,128)(2,1)S(1)}, u32[]{:S(2)}, u32[]{:S(2)}) collective-permute-start(bf16[64,256]{1,0:T(8,128)(2,1)S(1)} %get-tuple-element.46), channel_id=1, source_target_pairs={{0,10},{1,11},{2,8},{3,9},{4,14},{5,15},{6,12},{7,13},{8,2},{9,3},... | collective-permute-start | bytes 98312 | tf_op jit(solution)/shard_map/ppermute | solution.py:35
  9.4 1.7 %collective-permute-start.2 = (bf16[64,256]{1,0:T(8,128)(2,1)S(1)}, bf16[64,256]{1,0:T(8,128)(2,1)S(1)}, u32[]{:S(2)}, u32[]{:S(2)}) collective-permute-start(bf16[64,256]{1,0:T(8,128)(2,1)S(1)} %get-tuple-element.47), channel_id=1, source_target_pairs={{0,8},{1,9},{2,10},{3,11},{4,12},{5,13},{6,14},{7,15},{8,0},{9,1},... | collective-permute-start | bytes 98312 | tf_op jit(solution)/shard_map/ppermute | solution.py:35
  9.4 8.4 %collective-permute-start.9 = (bf16[384,256]{1,0:T(8,128)(2,1)S(1)}, bf16[384,256]{1,0:T(8,128)(2,1)S(1)}, u32[]{:S(2)}, u32[]{:S(2)}) collective-permute-start(bf16[384,256]{1,0:T(8,128)(2,1)S(1)} %shard_map.80.ends), channel_id=1, source_target_pairs={{0,16},{1,17},{2,18},{3,19},{4,20},{5,21},{6,22},{7,23},{8,24},{9,... | collective-permute-start | bytes 589832 | tf_op jit(solution)/shard_map/ppermute | solution.py:35
  11.2 4.6 %collective-permute-start.4 = (bf16[64,256]{1,0:T(8,128)(2,1)S(1)}, bf16[64,256]{1,0:T(8,128)(2,1)S(1)}, u32[]{:S(2)}, u32[]{:S(2)}) collective-permute-start(bf16[64,256]{1,0:T(8,128)(2,1)S(1)} %get-tuple-element.51), channel_id=1, source_target_pairs={{0,12},{1,13},{2,14},{3,15},{4,8},{5,9},{6,10},{7,11},{8,4},{9,5},... | collective-permute-start | bytes 98312 | tf_op jit(solution)/shard_map/ppermute | solution.py:35
  14.2 1.6 %collective-permute-start.5 = (bf16[64,256]{1,0:T(8,128)(2,1)S(1)}, bf16[64,256]{1,0:T(8,128)(2,1)S(1)}, u32[]{:S(2)}, u32[]{:S(2)}) collective-permute-start(bf16[64,256]{1,0:T(8,128)(2,1)S(1)} %get-tuple-element.52), channel_id=1, source_target_pairs={{0,8},{1,9},{2,10},{3,11},{4,12},{5,13},{6,14},{7,15},{8,0},{9,1},... | collective-permute-start | bytes 98312 | tf_op jit(solution)/shard_map/ppermute | solution.py:35
  16.1 4.1 %collective-permute-start.7 = (bf16[128,256]{1,0:T(8,128)(2,1)S(1)}, bf16[128,256]{1,0:T(8,128)(2,1)S(1)}, u32[]{:S(2)}, u32[]{:S(2)}) collective-permute-start(bf16[128,256]{1,0:T(8,128)(2,1)S(1)} %get-tuple-element.58.sent), channel_id=1, source_target_pairs={{0,24},{1,25},{2,26},{3,27},{4,28},{5,29},{6,30},{7,31},{8,16},{9,... | collective-permute-start | bytes 196616 | tf_op jit(solution)/shard_map/ppermute | solution.py:35
  17.8 2.9 %collective-permute-start.12 = (bf16[2,256,256]{2,1,0:T(8,128)(2,1)S(1)}, bf16[2,256,256]{2,1,0:T(8,128)(2,1)S(1)}, u32[]{:S(2)}, u32[]{:S(2)}) collective-permute-start(bf16[2,256,256]{2,1,0:T(8,128)(2,1)S(1)} %get-tuple-element.66), channel_id=1, source_target_pairs={{0,8},{1,9},{2,10},{3,11},{4,12},{5,13},{6,14},{7,15},{8,0},{9,1},... | collective-permute-start | bytes 786440 | tf_op jit(solution)/shard_map/ppermute | solution.py:35
  18.4 2.2 %collective-permute-start.10 = (bf16[704,256]{1,0:T(8,128)(2,1)S(1)}, bf16[704,256]{1,0:T(8,128)(2,1)S(1)}, u32[]{:S(2)}, u32[]{:S(2)}) collective-permute-start(bf16[704,256]{1,0:T(8,128)(2,1)S(1)} %shard_map.84.joined), channel_id=1, source_target_pairs={{0,8},{1,9},{2,10},{3,11},{4,12},{5,13},{6,14},{7,15},{8,0},{9,1},... | collective-permute-start | bytes 1081352 | tf_op jit(solution)/shard_map/ppermute | solution.py:35
  19.2 1.4 %collective-permute-start.11 = (f32[64,256]{1,0:T(8,128)S(1)}, f32[64,256]{1,0:T(8,128)S(1)}, u32[]{:S(2)}, u32[]{:S(2)}) collective-permute-start(f32[64,256]{1,0:T(8,128)S(1)} %shard_map.85), channel_id=1, source_target_pairs={{0,8},{1,9},{2,10},{3,11},{4,12},{5,13},{6,14},{7,15},{8,0},{9,1},... | collective-permute-start | bytes 196616 | tf_op jit(solution)/shard_map/ppermute | solution.py:35
  20.3 1.3 %collective-permute-start.8 = (bf16[128,256]{1,0:T(8,128)(2,1)S(1)}, bf16[128,256]{1,0:T(8,128)(2,1)S(1)}, u32[]{:S(2)}, u32[]{:S(2)}) collective-permute-start(bf16[128,256]{1,0:T(8,128)(2,1)S(1)} %collective-permute-done.7.across), channel_id=1, source_target_pairs={{0,8},{1,9},{2,10},{3,11},{4,12},{5,13},{6,14},{7,15},{8,0},{9,1},... | collective-permute-start | bytes 196616 | tf_op jit(solution)/shard_map/ppermute | solution.py:35
  21.7 4.3 %collective-permute-start.13 = (bf16[64,256]{1,0:T(8,128)(2,1)S(1)}, bf16[64,256]{1,0:T(8,128)(2,1)S(1)}, u32[]{:S(2)}, u32[]{:S(2)}) collective-permute-start(bf16[64,256]{1,0:T(8,128)(2,1)S(1)} %get-tuple-element.69), channel_id=1, source_target_pairs={{0,12},{1,13},{2,14},{3,15},{4,8},{5,9},{6,10},{7,11},{8,4},{9,5},... | collective-permute-start | bytes 98312 | tf_op jit(solution)/shard_map/ppermute | solution.py:35
  24.0 2.0 %collective-permute-start.14 = (bf16[64,256]{1,0:T(8,128)(2,1)S(1)}, bf16[64,256]{1,0:T(8,128)(2,1)S(1)}, u32[]{:S(2)}, u32[]{:S(2)}) collective-permute-start(bf16[64,256]{1,0:T(8,128)(2,1)S(1)} %get-tuple-element.69), channel_id=1, source_target_pairs={{0,8},{1,9},{2,10},{3,11},{4,12},{5,13},{6,14},{7,15},{8,0},{9,1},... | collective-permute-start | bytes 98312 | tf_op jit(solution)/shard_map/ppermute | solution.py:35
  24.8 4.8 %collective-permute-start.17 = (f32[64,256]{1,0:T(8,128)S(1)}, f32[64,256]{1,0:T(8,128)S(1)}, u32[]{:S(2)}, u32[]{:S(2)}) collective-permute-start(f32[64,256]{1,0:T(8,128)S(1)} %shard_map.93), channel_id=1, source_target_pairs={{0,8},{1,9},{2,10},{3,11},{4,12},{5,13},{6,14},{7,15},{8,0},{9,1},... | collective-permute-start | bytes 196616 | tf_op jit(solution)/shard_map/ppermute | solution.py:35
  25.2 4.4 %collective-permute-start.18 = (bf16[2,256,256]{2,1,0:T(8,128)(2,1)S(1)}, bf16[2,256,256]{2,1,0:T(8,128)(2,1)S(1)}, u32[]{:S(2)}, u32[]{:S(2)}) collective-permute-start(bf16[2,256,256]{2,1,0:T(8,128)(2,1)S(1)} %shard_map.94), channel_id=1, source_target_pairs={{0,8},{1,9},{2,10},{3,11},{4,12},{5,13},{6,14},{7,15},{8,0},{9,1},... | collective-permute-start | bytes 786440 | tf_op jit(solution)/shard_map/ppermute | solution.py:35
  26.0 1.9 %copy-start.4 = (bf16[1,128,128]{2,1,0:T(8,128)(2,1)S(1)}, bf16[1,128,128]{2,1,0:T(8,128)(2,1)}, u32[]{:S(2)}) copy-start(bf16[1,128,128]{2,1,0:T(8,128)(2,1)} %param.7) | copy-start | bytes 98308
  26.2 3.4 %collective-permute-start.15 = (bf16[64,256]{1,0:T(8,128)(2,1)S(1)}, bf16[64,256]{1,0:T(8,128)(2,1)S(1)}, u32[]{:S(2)}, u32[]{:S(2)}) collective-permute-start(bf16[64,256]{1,0:T(8,128)(2,1)S(1)} %get-tuple-element.76), channel_id=1, source_target_pairs={{0,10},{1,11},{2,8},{3,9},{4,14},{5,15},{6,12},{7,13},{8,2},{9,3},... | collective-permute-start | bytes 98312 | tf_op jit(solution)/shard_map/ppermute | solution.py:35
  27.7 2.0 %collective-permute-start.16 = (bf16[64,256]{1,0:T(8,128)(2,1)S(1)}, bf16[64,256]{1,0:T(8,128)(2,1)S(1)}, u32[]{:S(2)}, u32[]{:S(2)}) collective-permute-start(bf16[64,256]{1,0:T(8,128)(2,1)S(1)} %get-tuple-element.76), channel_id=1, source_target_pairs={{0,8},{1,9},{2,10},{3,11},{4,12},{5,13},{6,14},{7,15},{8,0},{9,1},... | collective-permute-start | bytes 98312 | tf_op jit(solution)/shard_map/ppermute | solution.py:35
  29.8 3.4 %collective-permute-start.19 = (bf16[64,256]{1,0:T(8,128)(2,1)S(1)}, bf16[64,256]{1,0:T(8,128)(2,1)S(1)}, u32[]{:S(2)}, u32[]{:S(2)}) collective-permute-start(bf16[64,256]{1,0:T(8,128)(2,1)S(1)} %shard_map.95), channel_id=1, source_target_pairs={{0,9},{1,8},{2,11},{3,10},{4,13},{5,12},{6,15},{7,14},{8,1},{9,0},... | collective-permute-start | bytes 98312 | tf_op jit(solution)/shard_map/ppermute | solution.py:35
  31.1 2.1 %collective-permute-start.21 = (bf16[64,256]{1,0:T(8,128)(2,1)S(1)}, bf16[64,256]{1,0:T(8,128)(2,1)S(1)}, u32[]{:S(2)}, u32[]{:S(2)}) collective-permute-start(bf16[64,256]{1,0:T(8,128)(2,1)S(1)} %shard_map.95), channel_id=1, source_target_pairs={{0,8},{1,9},{2,10},{3,11},{4,12},{5,13},{6,14},{7,15},{8,0},{9,1},... | collective-permute-start | bytes 98312 | tf_op jit(solution)/shard_map/ppermute | solution.py:35
  31.2 2.0 %collective-permute-start.20 = (bf16[64,256]{1,0:T(8,128)(2,1)S(1)}, bf16[64,256]{1,0:T(8,128)(2,1)S(1)}, u32[]{:S(2)}, u32[]{:S(2)}) collective-permute-start(bf16[64,256]{1,0:T(8,128)(2,1)S(1)} %collective-permute-done.15), channel_id=1, source_target_pairs={{0,8},{1,9},{2,10},{3,11},{4,12},{5,13},{6,14},{7,15},{8,0},{9,1},... | collective-permute-start | bytes 98312 | tf_op jit(solution)/shard_map/ppermute | solution.py:35

commit v8 on v7

--- a/solution.py
+++ b/solution.py
@@ -59,12 +59,17 @@
     ahead[rows:] = terms[level + 1].astype(BF)
 
 
-def products_last(inverse, coupling, out, out_turned, below, below_turned, *, level):
+def products_last(inverse, coupling, terms, values, out, out_turned, below, below_turned, folded, fixed, *, level):
     for side in range(2):
         out[side] = times(coupling[level, side], inverse[level]).astype(BF)
         below[side] = times(coupling[level - 1, side], inverse[level - 1]).astype(BF)
         out_turned[side] = turned(inverse[level], coupling[level, side]).astype(BF)
     below_turned[...] = turned(inverse[level - 1], coupling[level - 1, 0]).astype(BF)
+    for side in range(2):
+        folded[side] = times(below_turned[...], out_turned[side]).astype(BF)
+    right = values[level].astype(BF)
+    fixed[0] = values[level + 1] - times(right, out_turned[0])
+    fixed[1] = terms[level + 1] + times(right, out_turned[1])
 
 
 def top_gram(inverse, out):
@@ -123,13 +128,17 @@
     ahead[...] = (values[1] - times(change, product[0])).astype(BF)
 
 
-def forward_last(received, below, product_below, product, terms, values, delta, out, *, level):
-    residue = values[level] - times(below[...], product_below[...])
+def forward_last(received, below, folded, product, fixed, out):
+    rows, arrived = received.shape[0], received[...].astype(BF)
+    out[:rows] = (fixed[1] - times(below[...], folded[1]) - times(arrived, product[1])).astype(BF)
+    out[rows:] = (fixed[0] + times(below[...], folded[0]) + times(arrived, product[0])).astype(BF)
+
+
+def solve_last(received, below, below_turned, inverse, values, solved, *, level):
+    residue = values[level] - times(below[...], below_turned[...])
     change = (residue - received[...].astype(F32)).astype(BF)
-    delta[...] = change
-    rows = change.shape[0]
-    out[:rows] = (terms[level + 1] + times(change, product[1])).astype(BF)
-    out[rows:] = (values[level + 1] - times(change, product[0])).astype(BF)
+    step = times_t(change, inverse[level]).astype(BF)
+    solved[...] = times(step, inverse[level])
 
 
 def early_products(inverse, coupling, terms, pack, ahead, lowest, *, level):
@@ -329,9 +338,10 @@
         below = change
         if joined and level == core - 1:
             below, mirror_pack = lax.optimization_barrier((below, mirror_pack))
-            change, out = call(
-                forward_last, [vec_bf, ((2 * cols, width), BF)], arrived(received), below,
-                below_turned, last_turned, terms, values, level=level, cost=4,
+            last = arrived(received)
+            out = call(
+                forward_last, [((2 * cols, width), BF)],
+                last, below, folded, last_turned, fixed, cost=4,
             )
             received = send(out, below_top, True)
         elif level == levels - 2:
@@ -347,7 +357,7 @@
                 if joined and level == core - 2:
                     ahead[level], ends = lax.optimization_barrier((ahead[level], ends))
                 change, out = call(
-                    forward_mate, [vec_bf, vec_bf], arrived(received), residue, ahead[level], cost=2
+                    forward_mate, [vec_bf, vec_bf], received, residue, ahead[level], cost=2
                 )
             elif level and not at_home[level - 1]:
                 change, out = call(
@@ -370,9 +380,10 @@
                 )
             received = send(out, level + 1, across)
             if joined and level == core - 2:
-                product[core - 1], last_turned, product[core - 2], below_turned = call(
-                    products_last, [pair, pair, pair, ((width, width), BF)],
-                    after(inverse, out), coupling, level=core - 1, cost=1,
+                product[core - 1], last_turned, product[core - 2], below_turned, folded, fixed = call(
+                    products_last,
+                    [pair, pair, pair, ((width, width), BF), pair, ((2, cols, width), F32)],
+                    after(inverse, out), coupling, terms, values, level=core - 1, cost=1,
                 )
             if level == 0:
                 if joined:
@@ -388,7 +399,12 @@
                 residue = call(
                     forward_residue, [slab], change, product[level], values, level=level, cost=0
                 )
-        solved[level] = call(solve, [vec], change, inverse, level=level, cost=8 if level == core - 1 else 1)
+        if joined and level == core - 1:
+            solved[level] = call(
+                solve_last, [vec], last, below, below_turned, inverse, values, level=level, cost=8
+            )
+        else:
+            solved[level] = call(solve, [vec], change, inverse, level=level)
     leaf_prod = jnp.einsum("kwn,nm->kwm", leaf_cpl, leaf_inv, preferred_element_type=F32).astype(BF)
 
     mates = [level for level in range(core) if level % 2 == 0]
@@ -454,7 +470,7 @@
             known = mate(block_bf)
             if home:
                 blocks[level + 1] = known
-            made = call(back_both, outs, arrived(received), known, solved[level], product[level])
+            made = call(back_both, outs, received, known, solved[level], product[level])
         if home:
             blocks[level], block_bf = made
         else:
@@ -467,7 +483,6 @@
         leaf_part, [((cols, size), F32)],
         leaf, leaf_inv, leaf_prod, *[mirrored[level] for level in early], early=early,
     )
-    mirrored[0] = arrived(mirrored[0])
     leaf_solution, stacked = call(
         finish, [((cols, size), F32), ((levels, cols, width), F32)],
         part, leaf_prod, *[mirrored[level] for level in late], *blocks, late=tuple(late),

time: 34.2 us -> 34 us (level)
  transfers between devices with their start and end apart: 22 -> 22, of which waited for: 6 -> 6; matrix products, arithmetic and copies ran while one was open for 1% -> 1% of each run, Pallas kernels for 14% -> 15%
where the time goes in v8:
time: 34 us; the launch traced here: 33.8 us
  starting transfers between devices  20.3 us (60%)
  Pallas kernels  6.04 us (18%)
  waiting for transfers between devices  5.13 us (15%)
  matrix products  1.52 us (4%)
  between operations  0.83 us (2%)
    ppermute x22, starting transfers between devices, exchange(): return lax.ppermute(value, ('gx', 'gy'), pairs)  20.3 us
    pallas_call x20, Pallas kernels, call(): pl.pallas_call(functools.partial(body, **static), out_shape=[jax.ShapeDty...  6.04 us
    ppermute x22, waiting for transfers between devices, exchange(): return lax.ppermute(value, ('gx', 'gy'), pairs)  5.13 us
    dot_general x1, matrix products, times_t(): lax.dot_general(values, matrix, (((1,), (1,)), ((), ())), preferred_eleme...  1.04 us
  transfers between devices with their start and end apart: 22, of which 6 were waited for; matrix products, arithmetic and copies ran while one was open for 1% of the time, Pallas kernels for 15%

profile of v8, /device:TPU:0, one launch (start us, length us, event | category | flops | bytes accessed | tf_op | source)
XLA Modules:
  0.0 33.8 jit_solution(9426594756165257318)
XLA Ops:
  0.7 1.0 %fusion.6.leaf = f32[64,128]{1,0:T(8,128)S(1)} fusion(f32[128,64]{0,1:T(8,128)} %param.6, bf16[1,128,128]{2,1,0:T(8,128)(2,1)} %param.7), kind=kOutput, calls=%fused_computation.9 | convolution fusion | flops 2105344 | bytes 98304 | tf_op jit(solution)/shard_map/dot_general | solution.py:20
  1.7 0.3 convolution_bitcast_fusion.terms
  2.0 3.0 %collective-permute-start = (bf16[64,256]{1,0:T(8,128)(2,1)S(1)}, bf16[64,256]{1,0:T(8,128)(2,1)S(1)}, u32[]{:S(2)}, u32[]{:S(2)}) collective-permute-start(bf16[64,256]{1,0:T(8,128)(2,1)S(1)} %fusion.2), channel_id=1, source_target_pairs={{0,1},{1,0},{2,3},{3,2},{4,5},{5,4},{6,7},{7,6},{8,9},{9,8},{10,11... | collective-permute-start | bytes 98312 | tf_op jit(solution)/shard_map/ppermute | solution.py:35
  5.0 0.2 shard_map.77.own_gram
  5.2 0.3 %shard_map.78 = (bf16[512,256]{1,0:T(8,128)(2,1)S(1)}, bf16[320,256]{1,0:T(8,128)(2,1)S(1)}, bf16[2,256,256]{2,1,0:T(8,128)(2,1)S(1)}) custom-call(bf16[5,256,256]{2,1,0:T(8,128)(2,1)S(1)} %bitcast.28, bf16[4,2,256,256]{3,2,1,0:T(8,128)(2,1)S(1)} %bitcast.40, f32[5,64,256]{2,1,0:T(8,128)S(1)} %convolution_bitcast_fusion.terms), custom_call_target="tpu_custom_call" | custom-call | flops 300000000 | bytes 2031616 | tf_op jit(solution)/shard_map/pallas_call | solution.py:40
  5.6 1.6 %collective-permute-start.6 = (bf16[512,256]{1,0:T(8,128)(2,1)S(1)}, bf16[512,256]{1,0:T(8,128)(2,1)S(1)}, u32[]{:S(2)}, u32[]{:S(2)}) collective-permute-start(bf16[512,256]{1,0:T(8,128)(2,1)S(1)} %get-tuple-element.53.mine), channel_id=1, source_target_pairs={{0,16},{1,17},{2,18},{3,19},{4,20},{5,21},{6,22},{7,23},{8,24},{9,... | collective-permute-start | bytes 786440 | tf_op jit(solution)/shard_map/ppermute | solution.py:35
  7.4 1.9 %collective-permute-start.1 = (bf16[64,256]{1,0:T(8,128)(2,1)S(1)}, bf16[64,256]{1,0:T(8,128)(2,1)S(1)}, u32[]{:S(2)}, u32[]{:S(2)}) collective-permute-start(bf16[64,256]{1,0:T(8,128)(2,1)S(1)} %get-tuple-element.46), channel_id=1, source_target_pairs={{0,10},{1,11},{2,8},{3,9},{4,14},{5,15},{6,12},{7,13},{8,2},{9,3},... | collective-permute-start | bytes 98312 | tf_op jit(solution)/shard_map/ppermute | solution.py:35
  9.4 1.6 %collective-permute-start.9 = (bf16[384,256]{1,0:T(8,128)(2,1)S(1)}, bf16[384,256]{1,0:T(8,128)(2,1)S(1)}, u32[]{:S(2)}, u32[]{:S(2)}) collective-permute-start(bf16[384,256]{1,0:T(8,128)(2,1)S(1)} %shard_map.80.ends), channel_id=1, source_target_pairs={{0,16},{1,17},{2,18},{3,19},{4,20},{5,21},{6,22},{7,23},{8,24},{9,... | collective-permute-start | bytes 589832 | tf_op jit(solution)/shard_map/ppermute | solution.py:35
  11.2 3.0 %collective-permute-start.4 = (bf16[64,256]{1,0:T(8,128)(2,1)S(1)}, bf16[64,256]{1,0:T(8,128)(2,1)S(1)}, u32[]{:S(2)}, u32[]{:S(2)}) collective-permute-start(bf16[64,256]{1,0:T(8,128)(2,1)S(1)} %get-tuple-element.51), channel_id=1, source_target_pairs={{0,12},{1,13},{2,14},{3,15},{4,8},{5,9},{6,10},{7,11},{8,4},{9,5},... | collective-permute-start | bytes 98312 | tf_op jit(solution)/shard_map/ppermute | solution.py:35
  14.2 0.6 %shard_map.82 = (bf16[2,256,256]{2,1,0:T(8,128)(2,1)S(1)}, bf16[2,256,256]{2,1,0:T(8,128)(2,1)S(1)}, bf16[2,256,256]{2,1,0:T(8,128)(2,1)S(1)}, bf16[256,256]{1,0...) custom-call(bf16[5,256,256]{2,1,0:T(8,128)(2,1)S(1)} %bitcast.29, ...), custom_call_target="tpu_custom_call" | custom-call | flops 300000000 | bytes 2359296 | tf_op jit(solution)/shard_map/pallas_call | solution.py:40
  14.8 1.0 %collective-permute-done.4 = bf16[64,256]{1,0:T(8,128)(2,1)S(1)} collective-permute-done((bf16[64,256]{1,0:T(8,128)(2,1)S(1)}, bf16[64,256]{1,0:T(8,128)(2,1)S(1)}, u32[]{:S(2)}, u32[]{:S(2)}) %collective-permute-start.4) | collective-permute-done | bytes 32800 | tf_op jit(solution)/shard_map/ppermute | solution.py:35
  16.0 1.6 %collective-permute-start.7 = (bf16[128,256]{1,0:T(8,128)(2,1)S(1)}, bf16[128,256]{1,0:T(8,128)(2,1)S(1)}, u32[]{:S(2)}, u32[]{:S(2)}) collective-permute-start(bf16[128,256]{1,0:T(8,128)(2,1)S(1)} %shard_map.83.sent), channel_id=1, source_target_pairs={{0,24},{1,25},{2,26},{3,27},{4,28},{5,29},{6,30},{7,31},{8,16},{9,... | collective-permute-start | bytes 196616 | tf_op jit(solution)/shard_map/ppermute | solution.py:35
  17.7 0.6 %shard_map.84.joined = bf16[704,256]{1,0:T(8,128)(2,1)S(1)} custom-call(bf16[512,256]{1,0:T(8,128)(2,1)S(1)} %get-tuple-element.53.mine, bf16[512,256]{1,0:T(8,128)(2,1)S(1)} %collective-permute-done.6.mirror, bf16[384,256]{1,0:T(8,128)(2,1)S(1)} %shard_map.80.ends, bf16[384,256]{1,0:T(8,128)(2,1)S(1)} %collective-permute-done.9.mirror_ends, ...), custom_call_target="tpu_custom_call" | custom-call | flops 300000000 | bytes 1638400 | tf_op jit(solution)/shard_map/pallas_call | solution.py:40
  18.3 0.5 %collective-permute-start.10 = (bf16[704,256]{1,0:T(8,128)(2,1)S(1)}, bf16[704,256]{1,0:T(8,128)(2,1)S(1)}, u32[]{:S(2)}, u32[]{:S(2)}) collective-permute-start(bf16[704,256]{1,0:T(8,128)(2,1)S(1)} %shard_map.84.joined), channel_id=1, source_target_pairs={{0,8},{1,9},{2,10},{3,11},{4,12},{5,13},{6,14},{7,15},{8,0},{9,1},... | collective-permute-start | bytes 1081352 | tf_op jit(solution)/shard_map/ppermute | solution.py:35
  18.8 0.4 %shard_map.85 = f32[64,256]{1,0:T(8,128)S(1)} custom-call(f32[64,256]{1,0:T(8,128)S(1)} %convert_element_type.21.received, bf16[64,256]{1,0:T(8,128)(2,1)S(1)} %collective-permute-done.5.below.delta, bf16[256,256]{1,0:T(8,128)(2,1)S(1)} %get-tuple-element.63.below_turned, bf16[5,256,256]{2,1,0:T(8,128)(2,1)S(1)} %bitcast.31, f32[5,64,256]{2,1,0:T(8,128)S(1)} %bitcast.39), custom_call_target="tpu_custom_call" | custom-call | flops 2400000000 | bytes 1212416 | tf_op jit(solution)/shard_map/pallas_call | solution.py:40
  19.3 0.8 %collective-permute-done.7.across = bf16[128,256]{1,0:T(8,128)(2,1)S(1)} collective-permute-done((bf16[128,256]{1,0:T(8,128)(2,1)S(1)}, bf16[128,256]{1,0:T(8,128)(2,1)S(1)}, u32[]{:S(2)}, u32[]{:S(2)}) %collective-permute-start.7) | collective-permute-done | bytes 65568 | tf_op jit(solution)/shard_map/ppermute | solution.py:35
  20.5 0.5 %shard_map.86 = (f32[2,64,256]{2,1,0:T(8,128)S(1)}, bf16[2,64,256]{2,1,0:T(8,128)(2,1)S(1)}, bf16[2,256,256]{2,1,0:T(8,128)(2,1)S(1)}, f32[64,256]{1,0:T(8,128)S(1)}) custom-call(bf16[704,256]{1,0:T(8,128)(2,1)S(1)} %shard_map.84.joined, bf16[704,256]{1,0:T(8,128)(2,1)S(1)} %collective-permute-done.10.joined_mate, ...), custom_call_target="tpu_custom_call" | custom-call | flops 300000000 | bytes 1048576 | tf_op jit(solution)/shard_map/pallas_call | solution.py:40
  21.0 0.4 %collective-permute-done.8.theirs = bf16[128,256]{1,0:T(8,128)(2,1)S(1)} collective-permute-done((bf16[128,256]{1,0:T(8,128)(2,1)S(1)}, bf16[128,256]{1,0:T(8,128)(2,1)S(1)}, u32[]{:S(2)}, u32[]{:S(2)}) %collective-permute-start.8) | collective-permute-done | bytes 65568 | tf_op jit(solution)/shard_map/ppermute | solution.py:35
  21.6 2.3 %collective-permute-start.13 = (bf16[64,256]{1,0:T(8,128)(2,1)S(1)}, bf16[64,256]{1,0:T(8,128)(2,1)S(1)}, u32[]{:S(2)}, u32[]{:S(2)}) collective-permute-start(bf16[64,256]{1,0:T(8,128)(2,1)S(1)} %get-tuple-element.69), channel_id=1, source_target_pairs={{0,12},{1,13},{2,14},{3,15},{4,8},{5,9},{6,10},{7,11},{8,4},{9,5},... | collective-permute-start | bytes 98312 | tf_op jit(solution)/shard_map/ppermute | solution.py:35
  24.1 0.3 shard_map.93
  24.4 0.3 shard_map.91.solved
  24.7 0.4 %collective-permute-start.17 = (f32[64,256]{1,0:T(8,128)S(1)}, f32[64,256]{1,0:T(8,128)S(1)}, u32[]{:S(2)}, u32[]{:S(2)}) collective-permute-start(f32[64,256]{1,0:T(8,128)S(1)} %shard_map.93), channel_id=1, source_target_pairs={{0,8},{1,9},{2,10},{3,11},{4,12},{5,13},{6,14},{7,15},{8,0},{9,1},... | collective-permute-start | bytes 196616 | tf_op jit(solution)/shard_map/ppermute | solution.py:35
  25.3 0.6 %collective-permute-done.13.refs_0_.received = bf16[64,256]{1,0:T(8,128)(2,1)S(1)} collective-permute-done((bf16[64,256]{1,0:T(8,128)(2,1)S(1)}, bf16[64,256]{1,0:T(8,128)(2,1)S(1)}, u32[]{:S(2)}, u32[]{:S(2)}) %collective-permute-start.13) | collective-permute-done | bytes 32800 | tf_op jit(solution)/shard_map/ppermute | solution.py:35
  26.1 1.5 %collective-permute-start.15 = (bf16[64,256]{1,0:T(8,128)(2,1)S(1)}, bf16[64,256]{1,0:T(8,128)(2,1)S(1)}, u32[]{:S(2)}, u32[]{:S(2)}) collective-permute-start(bf16[64,256]{1,0:T(8,128)(2,1)S(1)} %get-tuple-element.76), channel_id=1, source_target_pairs={{0,10},{1,11},{2,8},{3,9},{4,14},{5,15},{6,12},{7,13},{8,2},{9,3},... | collective-permute-start | bytes 98312 | tf_op jit(solution)/shard_map/ppermute | solution.py:35
  27.5 0.2 collective-permute-start.16
  27.8 0.2 convolution_convert_fusion.leaf_products
  28.0 0.4 %shard_map.89 = (f32[64,256]{1,0:T(8,128)S(1)}, bf16[64,256]{1,0:T(8,128)(2,1)S(1)}) custom-call(bf16[512,256]{1,0:T(8,128)(2,1)S(1)} %get-tuple-element.53.mine, bf16[512,256]{1,0:T(8,128)(2,1)S(1)} %collective-permute-done.6.mirror, bf16[384,256]{1,0:T(8,128)(2,1)S(1)} %shard_map.80.ends, bf16[384,256]{1,0:T(8,128)(2,1)S(1)} %collective-permute-done.9.mirror_ends, ...), custom_call_target="tpu_custom_call" | custom-call | flops 300000000 | bytes 1048576 | tf_op jit(solution)/shard_map/pallas_call | solution.py:40
  28.4 1.0 %collective-permute-done.15.received = bf16[64,256]{1,0:T(8,128)(2,1)S(1)} collective-permute-done((bf16[64,256]{1,0:T(8,128)(2,1)S(1)}, bf16[64,256]{1,0:T(8,128)(2,1)S(1)}, u32[]{:S(2)}, u32[]{:S(2)}) %collective-permute-start.15) | collective-permute-done | bytes 32800 | tf_op jit(solution)/shard_map/ppermute | solution.py:35
  29.6 1.3 %collective-permute-start.19 = (bf16[64,256]{1,0:T(8,128)(2,1)S(1)}, bf16[64,256]{1,0:T(8,128)(2,1)S(1)}, u32[]{:S(2)}, u32[]{:S(2)}) collective-permute-start(bf16[64,256]{1,0:T(8,128)(2,1)S(1)} %shard_map.95), channel_id=1, source_target_pairs={{0,9},{1,8},{2,11},{3,10},{4,13},{5,12},{6,15},{7,14},{8,1},{9,0},... | collective-permute-start | bytes 98312 | tf_op jit(solution)/shard_map/ppermute | solution.py:35
  31.1 0.4 %collective-permute-start.20 = (bf16[64,256]{1,0:T(8,128)(2,1)S(1)}, bf16[64,256]{1,0:T(8,128)(2,1)S(1)}, u32[]{:S(2)}, u32[]{:S(2)}) collective-permute-start(bf16[64,256]{1,0:T(8,128)(2,1)S(1)} %collective-permute-done.15.received), channel_id=1, source_target_pairs={{0,8},{1,9},{2,10},{3,11},{4,12},{5,13},{6,14},{7,15},{8,0},{9,1},... | collective-permute-start | bytes 98312 | tf_op jit(solution)/shard_map/ppermute | solution.py:35
  31.8 1.3 %collective-permute-done.19.refs_0_ = bf16[64,256]{1,0:T(8,128)(2,1)S(1)} collective-permute-done((bf16[64,256]{1,0:T(8,128)(2,1)S(1)}, bf16[64,256]{1,0:T(8,128)(2,1)S(1)}, u32[]{:S(2)}, u32[]{:S(2)}) %collective-permute-start.19) | collective-permute-done | bytes 32800 | tf_op jit(solution)/shard_map/ppermute | solution.py:35
  33.1 0.8 %shard_map.96 = (f32[64,128]{1,0:T(8,128)}, f32[5,64,256]{2,1,0:T(8,128)}) custom-call(f32[64,128]{1,0:T(8,128)S(1)} %shard_map.90.part, bf16[5,256,128]{2,1,0:T(8,128)(2,1)S(1)} %convolution_convert_fusion.leaf_products, bf16[64,256]{1,0:T(8,128)(2,1)S(1)} %collective-permute-done.19.refs_0_, bf16[64,256]{1,0:T(8,128)(2,1)S(1)} %collective-permute-done.20.refs_1_, ...), custom_call_target="tpu_custom_call" | custom-call | flops 300000000 | bytes 688128 | tf_op jit(solution)/shard_map/pallas_call | solution.py:40
  (47 shorter events, 2.6 us)
Async XLA Ops:
  0.6 1.1 %copy-start = (bf16[1,5,256,128]{3,2,1,0:T(8,128)(2,1)S(1)}, bf16[1,5,256,128]{3,2,1,0:T(8,128)(2,1)}, u32[]{:S(2)}) copy-start(bf16[1,5,256,128]{3,2,1,0:T(8,128)(2,1)} %param.8) | copy-start | bytes 983044
  0.6 4.3 %copy-start.1 = (bf16[1,5,256,256]{3,2,1,0:T(8,128)(2,1)S(1)}, bf16[1,5,256,256]{3,2,1,0:T(8,128)(2,1)}, u32[]{:S(2)}) copy-start(bf16[1,5,256,256]{3,2,1,0:T(8,128)(2,1)} %param.10) | copy-start | bytes 1966084
  0.7 4.6 %copy-start.3 = (bf16[1,4,1,2,256,256]{5,4,3,2,1,0:T(8,128)(2,1)S(1)}, bf16[1,4,1,2,256,256]{5,4,3,2,1,0:T(8,128)(2,1)}, u32[]{:S(2)}) copy-start(bf16[1,4,1,2,256,256]{5,4,3,2,1,0:T(8,128)(2,1)} %param.11) | copy-start | bytes 3145732
  2.0 5.2 %collective-permute-start = (bf16[64,256]{1,0:T(8,128)(2,1)S(1)}, bf16[64,256]{1,0:T(8,128)(2,1)S(1)}, u32[]{:S(2)}, u32[]{:S(2)}) collective-permute-start(bf16[64,256]{1,0:T(8,128)(2,1)S(1)} %fusion.2), channel_id=1, source_target_pairs={{0,1},{1,0},{2,3},{3,2},{4,5},{5,4},{6,7},{7,6},{8,9},{9,8},{10,11... | collective-permute-start | bytes 98312 | tf_op jit(solution)/shard_map/ppermute | solution.py:35
  5.2 2.0 %copy-start.2 = (f32[1,5,256,64]{2,3,1,0:T(8,128)S(1)}, f32[1,5,256,64]{2,3,1,0:T(8,128)}, u32[]{:S(2)}) copy-start(f32[1,5,256,64]{2,3,1,0:T(8,128)} %param.9) | copy-start | bytes 983044
  5.6 10.2 %collective-permute-start.6 = (bf16[512,256]{1,0:T(8,128)(2,1)S(1)}, bf16[512,256]{1,0:T(8,128)(2,1)S(1)}, u32[]{:S(2)}, u32[]{:S(2)}) collective-permute-start(bf16[512,256]{1,0:T(8,128)(2,1)S(1)} %get-tuple-element.53.mine), channel_id=1, source_target_pairs={{0,16},{1,17},{2,18},{3,19},{4,20},{5,21},{6,22},{7,23},{8,24},{9,... | collective-permute-start | bytes 786440 | tf_op jit(solution)/shard_map/ppermute | solution.py:35
  7.4 3.7 %collective-permute-start.3 = (bf16[320,256]{1,0:T(8,128)(2,1)S(1)}, bf16[320,256]{1,0:T(8,128)(2,1)S(1)}, u32[]{:S(2)}, u32[]{:S(2)}) collective-permute-start(bf16[320,256]{1,0:T(8,128)(2,1)S(1)} %get-tuple-element.49), channel_id=1, source_target_pairs={{0,8},{1,9},{2,10},{3,11},{4,12},{5,13},{6,14},{7,15},{8,0},{9,1},... | collective-permute-start | bytes 491528 | tf_op jit(solution)/shard_map/ppermute | solution.py:35
  7.4 3.6 %collective-permute-start.1 = (bf16[64,256]{1,0:T(8,128)(2,1)S(1)}, bf16[64,256]{1,0:T(8,128)(2,1)S(1)}, u32[]{:S(2)}, u32[]{:S(2)}) collective-permute-start(bf16[64,256]{1,0:T(8,128)(2,1)S(1)} %get-tuple-element.46), channel_id=1, source_target_pairs={{0,10},{1,11},{2,8},{3,9},{4,14},{5,15},{6,12},{7,13},{8,2},{9,3},... | collective-permute-start | bytes 98312 | tf_op jit(solution)/shard_map/ppermute | solution.py:35
  9.4 1.7 %collective-permute-start.2 = (bf16[64,256]{1,0:T(8,128)(2,1)S(1)}, bf16[64,256]{1,0:T(8,128)(2,1)S(1)}, u32[]{:S(2)}, u32[]{:S(2)}) collective-permute-start(bf16[64,256]{1,0:T(8,128)(2,1)S(1)} %get-tuple-element.47), channel_id=1, source_target_pairs={{0,8},{1,9},{2,10},{3,11},{4,12},{5,13},{6,14},{7,15},{8,0},{9,1},... | collective-permute-start | bytes 98312 | tf_op jit(solution)/shard_map/ppermute | solution.py:35
  9.4 8.3 %collective-permute-start.9 = (bf16[384,256]{1,0:T(8,128)(2,1)S(1)}, bf16[384,256]{1,0:T(8,128)(2,1)S(1)}, u32[]{:S(2)}, u32[]{:S(2)}) collective-permute-start(bf16[384,256]{1,0:T(8,128)(2,1)S(1)} %shard_map.80.ends), channel_id=1, source_target_pairs={{0,16},{1,17},{2,18},{3,19},{4,20},{5,21},{6,22},{7,23},{8,24},{9,... | collective-permute-start | bytes 589832 | tf_op jit(solution)/shard_map/ppermute | solution.py:35
  11.2 4.6 %collective-permute-start.4 = (bf16[64,256]{1,0:T(8,128)(2,1)S(1)}, bf16[64,256]{1,0:T(8,128)(2,1)S(1)}, u32[]{:S(2)}, u32[]{:S(2)}) collective-permute-start(bf16[64,256]{1,0:T(8,128)(2,1)S(1)} %get-tuple-element.51), channel_id=1, source_target_pairs={{0,12},{1,13},{2,14},{3,15},{4,8},{5,9},{6,10},{7,11},{8,4},{9,5},... | collective-permute-start | bytes 98312 | tf_op jit(solution)/shard_map/ppermute | solution.py:35
  14.2 1.6 %collective-permute-start.5 = (bf16[64,256]{1,0:T(8,128)(2,1)S(1)}, bf16[64,256]{1,0:T(8,128)(2,1)S(1)}, u32[]{:S(2)}, u32[]{:S(2)}) collective-permute-start(bf16[64,256]{1,0:T(8,128)(2,1)S(1)} %get-tuple-element.52), channel_id=1, source_target_pairs={{0,8},{1,9},{2,10},{3,11},{4,12},{5,13},{6,14},{7,15},{8,0},{9,1},... | collective-permute-start | bytes 98312 | tf_op jit(solution)/shard_map/ppermute | solution.py:35
  16.0 4.1 %collective-permute-start.7 = (bf16[128,256]{1,0:T(8,128)(2,1)S(1)}, bf16[128,256]{1,0:T(8,128)(2,1)S(1)}, u32[]{:S(2)}, u32[]{:S(2)}) collective-permute-start(bf16[128,256]{1,0:T(8,128)(2,1)S(1)} %shard_map.83.sent), channel_id=1, source_target_pairs={{0,24},{1,25},{2,26},{3,27},{4,28},{5,29},{6,30},{7,31},{8,16},{9,... | collective-permute-start | bytes 196616 | tf_op jit(solution)/shard_map/ppermute | solution.py:35
  17.6 2.9 %collective-permute-start.12 = (bf16[2,256,256]{2,1,0:T(8,128)(2,1)S(1)}, bf16[2,256,256]{2,1,0:T(8,128)(2,1)S(1)}, u32[]{:S(2)}, u32[]{:S(2)}) collective-permute-start(bf16[2,256,256]{2,1,0:T(8,128)(2,1)S(1)} %get-tuple-element.66), channel_id=1, source_target_pairs={{0,8},{1,9},{2,10},{3,11},{4,12},{5,13},{6,14},{7,15},{8,0},{9,1},... | collective-permute-start | bytes 786440 | tf_op jit(solution)/shard_map/ppermute | solution.py:35
  18.3 2.2 %collective-permute-start.10 = (bf16[704,256]{1,0:T(8,128)(2,1)S(1)}, bf16[704,256]{1,0:T(8,128)(2,1)S(1)}, u32[]{:S(2)}, u32[]{:S(2)}) collective-permute-start(bf16[704,256]{1,0:T(8,128)(2,1)S(1)} %shard_map.84.joined), channel_id=1, source_target_pairs={{0,8},{1,9},{2,10},{3,11},{4,12},{5,13},{6,14},{7,15},{8,0},{9,1},... | collective-permute-start | bytes 1081352 | tf_op jit(solution)/shard_map/ppermute | solution.py:35
  19.2 1.3 %collective-permute-start.11 = (f32[64,256]{1,0:T(8,128)S(1)}, f32[64,256]{1,0:T(8,128)S(1)}, u32[]{:S(2)}, u32[]{:S(2)}) collective-permute-start(f32[64,256]{1,0:T(8,128)S(1)} %shard_map.85), channel_id=1, source_target_pairs={{0,8},{1,9},{2,10},{3,11},{4,12},{5,13},{6,14},{7,15},{8,0},{9,1},... | collective-permute-start | bytes 196616 | tf_op jit(solution)/shard_map/ppermute | solution.py:35
  20.1 1.3 %collective-permute-start.8 = (bf16[128,256]{1,0:T(8,128)(2,1)S(1)}, bf16[128,256]{1,0:T(8,128)(2,1)S(1)}, u32[]{:S(2)}, u32[]{:S(2)}) collective-permute-start(bf16[128,256]{1,0:T(8,128)(2,1)S(1)} %collective-permute-done.7.across), channel_id=1, source_target_pairs={{0,8},{1,9},{2,10},{3,11},{4,12},{5,13},{6,14},{7,15},{8,0},{9,1},... | collective-permute-start | bytes 196616 | tf_op jit(solution)/shard_map/ppermute | solution.py:35
  21.6 4.3 %collective-permute-start.13 = (bf16[64,256]{1,0:T(8,128)(2,1)S(1)}, bf16[64,256]{1,0:T(8,128)(2,1)S(1)}, u32[]{:S(2)}, u32[]{:S(2)}) collective-permute-start(bf16[64,256]{1,0:T(8,128)(2,1)S(1)} %get-tuple-element.69), channel_id=1, source_target_pairs={{0,12},{1,13},{2,14},{3,15},{4,8},{5,9},{6,10},{7,11},{8,4},{9,5},... | collective-permute-start | bytes 98312 | tf_op jit(solution)/shard_map/ppermute | solution.py:35
  23.9 2.0 %collective-permute-start.14 = (bf16[64,256]{1,0:T(8,128)(2,1)S(1)}, bf16[64,256]{1,0:T(8,128)(2,1)S(1)}, u32[]{:S(2)}, u32[]{:S(2)}) collective-permute-start(bf16[64,256]{1,0:T(8,128)(2,1)S(1)} %get-tuple-element.69), channel_id=1, source_target_pairs={{0,8},{1,9},{2,10},{3,11},{4,12},{5,13},{6,14},{7,15},{8,0},{9,1},... | collective-permute-start | bytes 98312 | tf_op jit(solution)/shard_map/ppermute | solution.py:35
  24.7 3.7 %collective-permute-start.17 = (f32[64,256]{1,0:T(8,128)S(1)}, f32[64,256]{1,0:T(8,128)S(1)}, u32[]{:S(2)}, u32[]{:S(2)}) collective-permute-start(f32[64,256]{1,0:T(8,128)S(1)} %shard_map.93), channel_id=1, source_target_pairs={{0,8},{1,9},{2,10},{3,11},{4,12},{5,13},{6,14},{7,15},{8,0},{9,1},... | collective-permute-start | bytes 196616 | tf_op jit(solution)/shard_map/ppermute | solution.py:35
  25.1 3.3 %collective-permute-start.18 = (bf16[2,256,256]{2,1,0:T(8,128)(2,1)S(1)}, bf16[2,256,256]{2,1,0:T(8,128)(2,1)S(1)}, u32[]{:S(2)}, u32[]{:S(2)}) collective-permute-start(bf16[2,256,256]{2,1,0:T(8,128)(2,1)S(1)} %shard_map.94), channel_id=1, source_target_pairs={{0,8},{1,9},{2,10},{3,11},{4,12},{5,13},{6,14},{7,15},{8,0},{9,1},... | collective-permute-start | bytes 786440 | tf_op jit(solution)/shard_map/ppermute | solution.py:35
  25.9 1.9 %copy-start.4 = (bf16[1,128,128]{2,1,0:T(8,128)(2,1)S(1)}, bf16[1,128,128]{2,1,0:T(8,128)(2,1)}, u32[]{:S(2)}) copy-start(bf16[1,128,128]{2,1,0:T(8,128)(2,1)} %param.7) | copy-start | bytes 98308
  26.1 3.4 %collective-permute-start.15 = (bf16[64,256]{1,0:T(8,128)(2,1)S(1)}, bf16[64,256]{1,0:T(8,128)(2,1)S(1)}, u32[]{:S(2)}, u32[]{:S(2)}) collective-permute-start(bf16[64,256]{1,0:T(8,128)(2,1)S(1)} %get-tuple-element.76), channel_id=1, source_target_pairs={{0,10},{1,11},{2,8},{3,9},{4,14},{5,15},{6,12},{7,13},{8,2},{9,3},... | collective-permute-start | bytes 98312 | tf_op jit(solution)/shard_map/ppermute | solution.py:35
  27.5 1.9 %collective-permute-start.16 = (bf16[64,256]{1,0:T(8,128)(2,1)S(1)}, bf16[64,256]{1,0:T(8,128)(2,1)S(1)}, u32[]{:S(2)}, u32[]{:S(2)}) collective-permute-start(bf16[64,256]{1,0:T(8,128)(2,1)S(1)} %get-tuple-element.76), channel_id=1, source_target_pairs={{0,8},{1,9},{2,10},{3,11},{4,12},{5,13},{6,14},{7,15},{8,0},{9,1},... | collective-permute-start | bytes 98312 | tf_op jit(solution)/shard_map/ppermute | solution.py:35
  29.6 3.4 %collective-permute-start.19 = (bf16[64,256]{1,0:T(8,128)(2,1)S(1)}, bf16[64,256]{1,0:T(8,128)(2,1)S(1)}, u32[]{:S(2)}, u32[]{:S(2)}) collective-permute-start(bf16[64,256]{1,0:T(8,128)(2,1)S(1)} %shard_map.95), channel_id=1, source_target_pairs={{0,9},{1,8},{2,11},{3,10},{4,13},{5,12},{6,15},{7,14},{8,1},{9,0},... | collective-permute-start | bytes 98312 | tf_op jit(solution)/shard_map/ppermute | solution.py:35
  30.9 2.1 %collective-permute-start.21 = (bf16[64,256]{1,0:T(8,128)(2,1)S(1)}, bf16[64,256]{1,0:T(8,128)(2,1)S(1)}, u32[]{:S(2)}, u32[]{:S(2)}) collective-permute-start(bf16[64,256]{1,0:T(8,128)(2,1)S(1)} %shard_map.95), channel_id=1, source_target_pairs={{0,8},{1,9},{2,10},{3,11},{4,12},{5,13},{6,14},{7,15},{8,0},{9,1},... | collective-permute-start | bytes 98312 | tf_op jit(solution)/shard_map/ppermute | solution.py:35
  31.1 2.0 %collective-permute-start.20 = (bf16[64,256]{1,0:T(8,128)(2,1)S(1)}, bf16[64,256]{1,0:T(8,128)(2,1)S(1)}, u32[]{:S(2)}, u32[]{:S(2)}) collective-permute-start(bf16[64,256]{1,0:T(8,128)(2,1)S(1)} %collective-permute-done.15.received), channel_id=1, source_target_pairs={{0,8},{1,9},{2,10},{3,11},{4,12},{5,13},{6,14},{7,15},{8,0},{9,1},... | collective-permute-start | bytes 98312 | tf_op jit(solution)/shard_map/ppermute | solution.py:35

commit v9 on v8

--- a/solution.py
+++ b/solution.py
@@ -102,11 +102,13 @@
     out[...] = (ahead[rows:].astype(F32) + times(change, ahead[:rows])).astype(BF)
 
 
-def forward_back(received, below, product_below, product, terms, values, delta, out, *, level):
+def forward_back(received, below, product_below, product, terms, values, delta, out, *ahead, level):
     residue = values[level] - times_t(below[...], product_below[0])
     change = (residue - received[...].astype(F32)).astype(BF)
     delta[...] = change
     out[...] = (terms[level + 1] + times_t(change, product[1])).astype(BF)
+    for above in ahead:
+        above[...] = (values[level + 1] - times_t(change, product[0])).astype(BF)
 
 
 def forward_residue(delta, product, values, residue, *, level):
@@ -360,10 +362,11 @@
                     forward_mate, [vec_bf, vec_bf], received, residue, ahead[level], cost=2
                 )
             elif level and not at_home[level - 1]:
-                change, out = call(
-                    forward_back, [vec_bf, vec_bf], arrived(received), below,
-                    product[level - 1], product[level], terms, values, level=level, cost=1,
-                )
+                change, out, *above = call(
+                    forward_back, [vec_bf, vec_bf] + ([] if at_home[level + 1] else [vec_bf]),
+                    arrived(received), below, product[level - 1], product[level], terms, values, level=level,
+                )
+                residue = above[0] if above else None
             elif joined and level == 0:
                 change, out, residue = call(
                     forward_lowest, [vec_bf, vec_bf, vec_bf],

time: 34 us -> 34 us (level)
  no operation moved by 1% of the time
where the time goes in v9:
time: 34 us; the launch traced here: 33.8 us
  starting transfers between devices  20.3 us (60%)
  Pallas kernels  6.04 us (18%)
  waiting for transfers between devices  5.13 us (15%)
  matrix products  1.52 us (4%)
  between operations  0.83 us (2%)
    ppermute x22, starting transfers between devices, exchange(): return lax.ppermute(value, ('gx', 'gy'), pairs)  20.3 us
    pallas_call x20, Pallas kernels, call(): pl.pallas_call(functools.partial(body, **static), out_shape=[jax.ShapeDty...  6.04 us
    ppermute x22, waiting for transfers between devices, exchange(): return lax.ppermute(value, ('gx', 'gy'), pairs)  5.13 us
    dot_general x1, matrix products, times_t(): lax.dot_general(values, matrix, (((1,), (1,)), ((), ())), preferred_eleme...  1.04 us
  transfers between devices with their start and end apart: 22, of which 6 were waited for; matrix products, arithmetic and copies ran while one was open for 1% of the time, Pallas kernels for 15%

profile of v9, /device:TPU:0, one launch (start us, length us, event | category | flops | bytes accessed | tf_op | source)
XLA Modules:
  0.0 33.8 jit_solution(9426594756165257318)
XLA Ops:
  0.7 1.0 %fusion.6.leaf = f32[64,128]{1,0:T(8,128)S(1)} fusion(f32[128,64]{0,1:T(8,128)} %param.6, bf16[1,128,128]{2,1,0:T(8,128)(2,1)} %param.7), kind=kOutput, calls=%fused_computation.9 | convolution fusion | flops 2105344 | bytes 98304 | tf_op jit(solution)/shard_map/dot_general | solution.py:20
  1.7 0.3 convolution_bitcast_fusion.terms
  2.0 3.0 %collective-permute-start = (bf16[64,256]{1,0:T(8,128)(2,1)S(1)}, bf16[64,256]{1,0:T(8,128)(2,1)S(1)}, u32[]{:S(2)}, u32[]{:S(2)}) collective-permute-start(bf16[64,256]{1,0:T(8,128)(2,1)S(1)} %fusion.2), channel_id=1, source_target_pairs={{0,1},{1,0},{2,3},{3,2},{4,5},{5,4},{6,7},{7,6},{8,9},{9,8},{10,11... | collective-permute-start | bytes 98312 | tf_op jit(solution)/shard_map/ppermute | solution.py:35
  5.0 0.2 shard_map.77.own_gram
  5.2 0.3 %shard_map.78 = (bf16[512,256]{1,0:T(8,128)(2,1)S(1)}, bf16[320,256]{1,0:T(8,128)(2,1)S(1)}, bf16[2,256,256]{2,1,0:T(8,128)(2,1)S(1)}) custom-call(bf16[5,256,256]{2,1,0:T(8,128)(2,1)S(1)} %bitcast.28, bf16[4,2,256,256]{3,2,1,0:T(8,128)(2,1)S(1)} %bitcast.40, f32[5,64,256]{2,1,0:T(8,128)S(1)} %convolution_bitcast_fusion.terms), custom_call_target="tpu_custom_call" | custom-call | flops 300000000 | bytes 2031616 | tf_op jit(solution)/shard_map/pallas_call | solution.py:40
  5.6 1.6 %collective-permute-start.6 = (bf16[512,256]{1,0:T(8,128)(2,1)S(1)}, bf16[512,256]{1,0:T(8,128)(2,1)S(1)}, u32[]{:S(2)}, u32[]{:S(2)}) collective-permute-start(bf16[512,256]{1,0:T(8,128)(2,1)S(1)} %get-tuple-element.53.mine), channel_id=1, source_target_pairs={{0,16},{1,17},{2,18},{3,19},{4,20},{5,21},{6,22},{7,23},{8,24},{9,... | collective-permute-start | bytes 786440 | tf_op jit(solution)/shard_map/ppermute | solution.py:35
  7.4 1.9 %collective-permute-start.1 = (bf16[64,256]{1,0:T(8,128)(2,1)S(1)}, bf16[64,256]{1,0:T(8,128)(2,1)S(1)}, u32[]{:S(2)}, u32[]{:S(2)}) collective-permute-start(bf16[64,256]{1,0:T(8,128)(2,1)S(1)} %get-tuple-element.46), channel_id=1, source_target_pairs={{0,10},{1,11},{2,8},{3,9},{4,14},{5,15},{6,12},{7,13},{8,2},{9,3},... | collective-permute-start | bytes 98312 | tf_op jit(solution)/shard_map/ppermute | solution.py:35
  9.4 1.6 %collective-permute-start.9 = (bf16[384,256]{1,0:T(8,128)(2,1)S(1)}, bf16[384,256]{1,0:T(8,128)(2,1)S(1)}, u32[]{:S(2)}, u32[]{:S(2)}) collective-permute-start(bf16[384,256]{1,0:T(8,128)(2,1)S(1)} %shard_map.80.ends), channel_id=1, source_target_pairs={{0,16},{1,17},{2,18},{3,19},{4,20},{5,21},{6,22},{7,23},{8,24},{9,... | collective-permute-start | bytes 589832 | tf_op jit(solution)/shard_map/ppermute | solution.py:35
  11.2 3.0 %collective-permute-start.4 = (bf16[64,256]{1,0:T(8,128)(2,1)S(1)}, bf16[64,256]{1,0:T(8,128)(2,1)S(1)}, u32[]{:S(2)}, u32[]{:S(2)}) collective-permute-start(bf16[64,256]{1,0:T(8,128)(2,1)S(1)} %get-tuple-element.51), channel_id=1, source_target_pairs={{0,12},{1,13},{2,14},{3,15},{4,8},{5,9},{6,10},{7,11},{8,4},{9,5},... | collective-permute-start | bytes 98312 | tf_op jit(solution)/shard_map/ppermute | solution.py:35
  14.2 0.6 %shard_map.82 = (bf16[2,256,256]{2,1,0:T(8,128)(2,1)S(1)}, bf16[2,256,256]{2,1,0:T(8,128)(2,1)S(1)}, bf16[2,256,256]{2,1,0:T(8,128)(2,1)S(1)}, bf16[256,256]{1,0...) custom-call(bf16[5,256,256]{2,1,0:T(8,128)(2,1)S(1)} %bitcast.29, ...), custom_call_target="tpu_custom_call" | custom-call | flops 300000000 | bytes 2359296 | tf_op jit(solution)/shard_map/pallas_call | solution.py:40
  14.8 1.0 %collective-permute-done.4 = bf16[64,256]{1,0:T(8,128)(2,1)S(1)} collective-permute-done((bf16[64,256]{1,0:T(8,128)(2,1)S(1)}, bf16[64,256]{1,0:T(8,128)(2,1)S(1)}, u32[]{:S(2)}, u32[]{:S(2)}) %collective-permute-start.4) | collective-permute-done | bytes 32800 | tf_op jit(solution)/shard_map/ppermute | solution.py:35
  16.0 1.6 %collective-permute-start.7 = (bf16[128,256]{1,0:T(8,128)(2,1)S(1)}, bf16[128,256]{1,0:T(8,128)(2,1)S(1)}, u32[]{:S(2)}, u32[]{:S(2)}) collective-permute-start(bf16[128,256]{1,0:T(8,128)(2,1)S(1)} %shard_map.83.sent), channel_id=1, source_target_pairs={{0,24},{1,25},{2,26},{3,27},{4,28},{5,29},{6,30},{7,31},{8,16},{9,... | collective-permute-start | bytes 196616 | tf_op jit(solution)/shard_map/ppermute | solution.py:35
  17.7 0.6 %shard_map.84.joined = bf16[704,256]{1,0:T(8,128)(2,1)S(1)} custom-call(bf16[512,256]{1,0:T(8,128)(2,1)S(1)} %get-tuple-element.53.mine, bf16[512,256]{1,0:T(8,128)(2,1)S(1)} %collective-permute-done.6.mirror, bf16[384,256]{1,0:T(8,128)(2,1)S(1)} %shard_map.80.ends, bf16[384,256]{1,0:T(8,128)(2,1)S(1)} %collective-permute-done.9.mirror_ends, ...), custom_call_target="tpu_custom_call" | custom-call | flops 300000000 | bytes 1638400 | tf_op jit(solution)/shard_map/pallas_call | solution.py:40
  18.3 0.5 %collective-permute-start.10 = (bf16[704,256]{1,0:T(8,128)(2,1)S(1)}, bf16[704,256]{1,0:T(8,128)(2,1)S(1)}, u32[]{:S(2)}, u32[]{:S(2)}) collective-permute-start(bf16[704,256]{1,0:T(8,128)(2,1)S(1)} %shard_map.84.joined), channel_id=1, source_target_pairs={{0,8},{1,9},{2,10},{3,11},{4,12},{5,13},{6,14},{7,15},{8,0},{9,1},... | collective-permute-start | bytes 1081352 | tf_op jit(solution)/shard_map/ppermute | solution.py:35
  18.8 0.4 %shard_map.85 = f32[64,256]{1,0:T(8,128)S(1)} custom-call(f32[64,256]{1,0:T(8,128)S(1)} %convert_element_type.21.received, bf16[64,256]{1,0:T(8,128)(2,1)S(1)} %collective-permute-done.5.below.delta, bf16[256,256]{1,0:T(8,128)(2,1)S(1)} %get-tuple-element.63.below_turned, bf16[5,256,256]{2,1,0:T(8,128)(2,1)S(1)} %bitcast.31, f32[5,64,256]{2,1,0:T(8,128)S(1)} %bitcast.39), custom_call_target="tpu_custom_call" | custom-call | flops 2400000000 | bytes 1212416 | tf_op jit(solution)/shard_map/pallas_call | solution.py:40
  19.3 0.8 %collective-permute-done.7.across = bf16[128,256]{1,0:T(8,128)(2,1)S(1)} collective-permute-done((bf16[128,256]{1,0:T(8,128)(2,1)S(1)}, bf16[128,256]{1,0:T(8,128)(2,1)S(1)}, u32[]{:S(2)}, u32[]{:S(2)}) %collective-permute-start.7) | collective-permute-done | bytes 65568 | tf_op jit(solution)/shard_map/ppermute | solution.py:35
  20.5 0.5 %shard_map.86 = (f32[2,64,256]{2,1,0:T(8,128)S(1)}, bf16[2,64,256]{2,1,0:T(8,128)(2,1)S(1)}, bf16[2,256,256]{2,1,0:T(8,128)(2,1)S(1)}, f32[64,256]{1,0:T(8,128)S(1)}) custom-call(bf16[704,256]{1,0:T(8,128)(2,1)S(1)} %shard_map.84.joined, bf16[704,256]{1,0:T(8,128)(2,1)S(1)} %collective-permute-done.10.joined_mate, ...), custom_call_target="tpu_custom_call" | custom-call | flops 300000000 | bytes 1048576 | tf_op jit(solution)/shard_map/pallas_call | solution.py:40
  21.0 0.4 %collective-permute-done.8.theirs = bf16[128,256]{1,0:T(8,128)(2,1)S(1)} collective-permute-done((bf16[128,256]{1,0:T(8,128)(2,1)S(1)}, bf16[128,256]{1,0:T(8,128)(2,1)S(1)}, u32[]{:S(2)}, u32[]{:S(2)}) %collective-permute-start.8) | collective-permute-done | bytes 65568 | tf_op jit(solution)/shard_map/ppermute | solution.py:35
  21.6 2.3 %collective-permute-start.13 = (bf16[64,256]{1,0:T(8,128)(2,1)S(1)}, bf16[64,256]{1,0:T(8,128)(2,1)S(1)}, u32[]{:S(2)}, u32[]{:S(2)}) collective-permute-start(bf16[64,256]{1,0:T(8,128)(2,1)S(1)} %get-tuple-element.69), channel_id=1, source_target_pairs={{0,12},{1,13},{2,14},{3,15},{4,8},{5,9},{6,10},{7,11},{8,4},{9,5},... | collective-permute-start | bytes 98312 | tf_op jit(solution)/shard_map/ppermute | solution.py:35
  24.1 0.3 shard_map.93
  24.4 0.3 shard_map.91.solved
  24.7 0.4 %collective-permute-start.17 = (f32[64,256]{1,0:T(8,128)S(1)}, f32[64,256]{1,0:T(8,128)S(1)}, u32[]{:S(2)}, u32[]{:S(2)}) collective-permute-start(f32[64,256]{1,0:T(8,128)S(1)} %shard_map.93), channel_id=1, source_target_pairs={{0,8},{1,9},{2,10},{3,11},{4,12},{5,13},{6,14},{7,15},{8,0},{9,1},... | collective-permute-start | bytes 196616 | tf_op jit(solution)/shard_map/ppermute | solution.py:35
  25.3 0.6 %collective-permute-done.13.refs_0_.received = bf16[64,256]{1,0:T(8,128)(2,1)S(1)} collective-permute-done((bf16[64,256]{1,0:T(8,128)(2,1)S(1)}, bf16[64,256]{1,0:T(8,128)(2,1)S(1)}, u32[]{:S(2)}, u32[]{:S(2)}) %collective-permute-start.13) | collective-permute-done | bytes 32800 | tf_op jit(solution)/shard_map/ppermute | solution.py:35
  26.1 1.5 %collective-permute-start.15 = (bf16[64,256]{1,0:T(8,128)(2,1)S(1)}, bf16[64,256]{1,0:T(8,128)(2,1)S(1)}, u32[]{:S(2)}, u32[]{:S(2)}) collective-permute-start(bf16[64,256]{1,0:T(8,128)(2,1)S(1)} %get-tuple-element.76), channel_id=1, source_target_pairs={{0,10},{1,11},{2,8},{3,9},{4,14},{5,15},{6,12},{7,13},{8,2},{9,3},... | collective-permute-start | bytes 98312 | tf_op jit(solution)/shard_map/ppermute | solution.py:35
  27.5 0.2 collective-permute-start.16
  27.8 0.2 convolution_convert_fusion.leaf_products
  28.0 0.4 %shard_map.89 = (f32[64,256]{1,0:T(8,128)S(1)}, bf16[64,256]{1,0:T(8,128)(2,1)S(1)}) custom-call(bf16[512,256]{1,0:T(8,128)(2,1)S(1)} %get-tuple-element.53.mine, bf16[512,256]{1,0:T(8,128)(2,1)S(1)} %collective-permute-done.6.mirror, bf16[384,256]{1,0:T(8,128)(2,1)S(1)} %shard_map.80.ends, bf16[384,256]{1,0:T(8,128)(2,1)S(1)} %collective-permute-done.9.mirror_ends, ...), custom_call_target="tpu_custom_call" | custom-call | flops 300000000 | bytes 1048576 | tf_op jit(solution)/shard_map/pallas_call | solution.py:40
  28.4 1.0 %collective-permute-done.15.received = bf16[64,256]{1,0:T(8,128)(2,1)S(1)} collective-permute-done((bf16[64,256]{1,0:T(8,128)(2,1)S(1)}, bf16[64,256]{1,0:T(8,128)(2,1)S(1)}, u32[]{:S(2)}, u32[]{:S(2)}) %collective-permute-start.15) | collective-permute-done | bytes 32800 | tf_op jit(solution)/shard_map/ppermute | solution.py:35
  29.6 1.3 %collective-permute-start.19 = (bf16[64,256]{1,0:T(8,128)(2,1)S(1)}, bf16[64,256]{1,0:T(8,128)(2,1)S(1)}, u32[]{:S(2)}, u32[]{:S(2)}) collective-permute-start(bf16[64,256]{1,0:T(8,128)(2,1)S(1)} %shard_map.95), channel_id=1, source_target_pairs={{0,9},{1,8},{2,11},{3,10},{4,13},{5,12},{6,15},{7,14},{8,1},{9,0},... | collective-permute-start | bytes 98312 | tf_op jit(solution)/shard_map/ppermute | solution.py:35
  31.1 0.4 %collective-permute-start.20 = (bf16[64,256]{1,0:T(8,128)(2,1)S(1)}, bf16[64,256]{1,0:T(8,128)(2,1)S(1)}, u32[]{:S(2)}, u32[]{:S(2)}) collective-permute-start(bf16[64,256]{1,0:T(8,128)(2,1)S(1)} %collective-permute-done.15.received), channel_id=1, source_target_pairs={{0,8},{1,9},{2,10},{3,11},{4,12},{5,13},{6,14},{7,15},{8,0},{9,1},... | collective-permute-start | bytes 98312 | tf_op jit(solution)/shard_map/ppermute | solution.py:35
  31.8 1.3 %collective-permute-done.19.refs_0_ = bf16[64,256]{1,0:T(8,128)(2,1)S(1)} collective-permute-done((bf16[64,256]{1,0:T(8,128)(2,1)S(1)}, bf16[64,256]{1,0:T(8,128)(2,1)S(1)}, u32[]{:S(2)}, u32[]{:S(2)}) %collective-permute-start.19) | collective-permute-done | bytes 32800 | tf_op jit(solution)/shard_map/ppermute | solution.py:35
  33.1 0.8 %shard_map.96 = (f32[64,128]{1,0:T(8,128)}, f32[5,64,256]{2,1,0:T(8,128)}) custom-call(f32[64,128]{1,0:T(8,128)S(1)} %shard_map.90.part, bf16[5,256,128]{2,1,0:T(8,128)(2,1)S(1)} %convolution_convert_fusion.leaf_products, bf16[64,256]{1,0:T(8,128)(2,1)S(1)} %collective-permute-done.19.refs_0_, bf16[64,256]{1,0:T(8,128)(2,1)S(1)} %collective-permute-done.20.refs_1_, ...), custom_call_target="tpu_custom_call" | custom-call | flops 300000000 | bytes 688128 | tf_op jit(solution)/shard_map/pallas_call | solution.py:40
  (47 shorter events, 2.6 us)
Async XLA Ops:
  0.6 1.1 %copy-start = (bf16[1,5,256,128]{3,2,1,0:T(8,128)(2,1)S(1)}, bf16[1,5,256,128]{3,2,1,0:T(8,128)(2,1)}, u32[]{:S(2)}) copy-start(bf16[1,5,256,128]{3,2,1,0:T(8,128)(2,1)} %param.8) | copy-start | bytes 983044
  0.6 4.3 %copy-start.1 = (bf16[1,5,256,256]{3,2,1,0:T(8,128)(2,1)S(1)}, bf16[1,5,256,256]{3,2,1,0:T(8,128)(2,1)}, u32[]{:S(2)}) copy-start(bf16[1,5,256,256]{3,2,1,0:T(8,128)(2,1)} %param.10) | copy-start | bytes 1966084
  0.7 4.6 %copy-start.3 = (bf16[1,4,1,2,256,256]{5,4,3,2,1,0:T(8,128)(2,1)S(1)}, bf16[1,4,1,2,256,256]{5,4,3,2,1,0:T(8,128)(2,1)}, u32[]{:S(2)}) copy-start(bf16[1,4,1,2,256,256]{5,4,3,2,1,0:T(8,128)(2,1)} %param.11) | copy-start | bytes 3145732
  2.0 5.2 %collective-permute-start = (bf16[64,256]{1,0:T(8,128)(2,1)S(1)}, bf16[64,256]{1,0:T(8,128)(2,1)S(1)}, u32[]{:S(2)}, u32[]{:S(2)}) collective-permute-start(bf16[64,256]{1,0:T(8,128)(2,1)S(1)} %fusion.2), channel_id=1, source_target_pairs={{0,1},{1,0},{2,3},{3,2},{4,5},{5,4},{6,7},{7,6},{8,9},{9,8},{10,11... | collective-permute-start | bytes 98312 | tf_op jit(solution)/shard_map/ppermute | solution.py:35
  5.2 2.0 %copy-start.2 = (f32[1,5,256,64]{2,3,1,0:T(8,128)S(1)}, f32[1,5,256,64]{2,3,1,0:T(8,128)}, u32[]{:S(2)}) copy-start(f32[1,5,256,64]{2,3,1,0:T(8,128)} %param.9) | copy-start | bytes 983044
  5.6 10.2 %collective-permute-start.6 = (bf16[512,256]{1,0:T(8,128)(2,1)S(1)}, bf16[512,256]{1,0:T(8,128)(2,1)S(1)}, u32[]{:S(2)}, u32[]{:S(2)}) collective-permute-start(bf16[512,256]{1,0:T(8,128)(2,1)S(1)} %get-tuple-element.53.mine), channel_id=1, source_target_pairs={{0,16},{1,17},{2,18},{3,19},{4,20},{5,21},{6,22},{7,23},{8,24},{9,... | collective-permute-start | bytes 786440 | tf_op jit(solution)/shard_map/ppermute | solution.py:35
  7.4 3.7 %collective-permute-start.3 = (bf16[320,256]{1,0:T(8,128)(2,1)S(1)}, bf16[320,256]{1,0:T(8,128)(2,1)S(1)}, u32[]{:S(2)}, u32[]{:S(2)}) collective-permute-start(bf16[320,256]{1,0:T(8,128)(2,1)S(1)} %get-tuple-element.49), channel_id=1, source_target_pairs={{0,8},{1,9},{2,10},{3,11},{4,12},{5,13},{6,14},{7,15},{8,0},{9,1},... | collective-permute-start | bytes 491528 | tf_op jit(solution)/shard_map/ppermute | solution.py:35
  7.4 3.6 %collective-permute-start.1 = (bf16[64,256]{1,0:T(8,128)(2,1)S(1)}, bf16[64,256]{1,0:T(8,128)(2,1)S(1)}, u32[]{:S(2)}, u32[]{:S(2)}) collective-permute-start(bf16[64,256]{1,0:T(8,128)(2,1)S(1)} %get-tuple-element.46), channel_id=1, source_target_pairs={{0,10},{1,11},{2,8},{3,9},{4,14},{5,15},{6,12},{7,13},{8,2},{9,3},... | collective-permute-start | bytes 98312 | tf_op jit(solution)/shard_map/ppermute | solution.py:35
  9.4 1.7 %collective-permute-start.2 = (bf16[64,256]{1,0:T(8,128)(2,1)S(1)}, bf16[64,256]{1,0:T(8,128)(2,1)S(1)}, u32[]{:S(2)}, u32[]{:S(2)}) collective-permute-start(bf16[64,256]{1,0:T(8,128)(2,1)S(1)} %get-tuple-element.47), channel_id=1, source_target_pairs={{0,8},{1,9},{2,10},{3,11},{4,12},{5,13},{6,14},{7,15},{8,0},{9,1},... | collective-permute-start | bytes 98312 | tf_op jit(solution)/shard_map/ppermute | solution.py:35
  9.4 8.3 %collective-permute-start.9 = (bf16[384,256]{1,0:T(8,128)(2,1)S(1)}, bf16[384,256]{1,0:T(8,128)(2,1)S(1)}, u32[]{:S(2)}, u32[]{:S(2)}) collective-permute-start(bf16[384,256]{1,0:T(8,128)(2,1)S(1)} %shard_map.80.ends), channel_id=1, source_target_pairs={{0,16},{1,17},{2,18},{3,19},{4,20},{5,21},{6,22},{7,23},{8,24},{9,... | collective-permute-start | bytes 589832 | tf_op jit(solution)/shard_map/ppermute | solution.py:35
  11.2 4.6 %collective-permute-start.4 = (bf16[64,256]{1,0:T(8,128)(2,1)S(1)}, bf16[64,256]{1,0:T(8,128)(2,1)S(1)}, u32[]{:S(2)}, u32[]{:S(2)}) collective-permute-start(bf16[64,256]{1,0:T(8,128)(2,1)S(1)} %get-tuple-element.51), channel_id=1, source_target_pairs={{0,12},{1,13},{2,14},{3,15},{4,8},{5,9},{6,10},{7,11},{8,4},{9,5},... | collective-permute-start | bytes 98312 | tf_op jit(solution)/shard_map/ppermute | solution.py:35
  14.2 1.6 %collective-permute-start.5 = (bf16[64,256]{1,0:T(8,128)(2,1)S(1)}, bf16[64,256]{1,0:T(8,128)(2,1)S(1)}, u32[]{:S(2)}, u32[]{:S(2)}) collective-permute-start(bf16[64,256]{1,0:T(8,128)(2,1)S(1)} %get-tuple-element.52), channel_id=1, source_target_pairs={{0,8},{1,9},{2,10},{3,11},{4,12},{5,13},{6,14},{7,15},{8,0},{9,1},... | collective-permute-start | bytes 98312 | tf_op jit(solution)/shard_map/ppermute | solution.py:35
  16.0 4.1 %collective-permute-start.7 = (bf16[128,256]{1,0:T(8,128)(2,1)S(1)}, bf16[128,256]{1,0:T(8,128)(2,1)S(1)}, u32[]{:S(2)}, u32[]{:S(2)}) collective-permute-start(bf16[128,256]{1,0:T(8,128)(2,1)S(1)} %shard_map.83.sent), channel_id=1, source_target_pairs={{0,24},{1,25},{2,26},{3,27},{4,28},{5,29},{6,30},{7,31},{8,16},{9,... | collective-permute-start | bytes 196616 | tf_op jit(solution)/shard_map/ppermute | solution.py:35
  17.6 2.9 %collective-permute-start.12 = (bf16[2,256,256]{2,1,0:T(8,128)(2,1)S(1)}, bf16[2,256,256]{2,1,0:T(8,128)(2,1)S(1)}, u32[]{:S(2)}, u32[]{:S(2)}) collective-permute-start(bf16[2,256,256]{2,1,0:T(8,128)(2,1)S(1)} %get-tuple-element.66), channel_id=1, source_target_pairs={{0,8},{1,9},{2,10},{3,11},{4,12},{5,13},{6,14},{7,15},{8,0},{9,1},... | collective-permute-start | bytes 786440 | tf_op jit(solution)/shard_map/ppermute | solution.py:35
  18.3 2.2 %collective-permute-start.10 = (bf16[704,256]{1,0:T(8,128)(2,1)S(1)}, bf16[704,256]{1,0:T(8,128)(2,1)S(1)}, u32[]{:S(2)}, u32[]{:S(2)}) collective-permute-start(bf16[704,256]{1,0:T(8,128)(2,1)S(1)} %shard_map.84.joined), channel_id=1, source_target_pairs={{0,8},{1,9},{2,10},{3,11},{4,12},{5,13},{6,14},{7,15},{8,0},{9,1},... | collective-permute-start | bytes 1081352 | tf_op jit(solution)/shard_map/ppermute | solution.py:35
  19.2 1.3 %collective-permute-start.11 = (f32[64,256]{1,0:T(8,128)S(1)}, f32[64,256]{1,0:T(8,128)S(1)}, u32[]{:S(2)}, u32[]{:S(2)}) collective-permute-start(f32[64,256]{1,0:T(8,128)S(1)} %shard_map.85), channel_id=1, source_target_pairs={{0,8},{1,9},{2,10},{3,11},{4,12},{5,13},{6,14},{7,15},{8,0},{9,1},... | collective-permute-start | bytes 196616 | tf_op jit(solution)/shard_map/ppermute | solution.py:35
  20.1 1.3 %collective-permute-start.8 = (bf16[128,256]{1,0:T(8,128)(2,1)S(1)}, bf16[128,256]{1,0:T(8,128)(2,1)S(1)}, u32[]{:S(2)}, u32[]{:S(2)}) collective-permute-start(bf16[128,256]{1,0:T(8,128)(2,1)S(1)} %collective-permute-done.7.across), channel_id=1, source_target_pairs={{0,8},{1,9},{2,10},{3,11},{4,12},{5,13},{6,14},{7,15},{8,0},{9,1},... | collective-permute-start | bytes 196616 | tf_op jit(solution)/shard_map/ppermute | solution.py:35
  21.6 4.3 %collective-permute-start.13 = (bf16[64,256]{1,0:T(8,128)(2,1)S(1)}, bf16[64,256]{1,0:T(8,128)(2,1)S(1)}, u32[]{:S(2)}, u32[]{:S(2)}) collective-permute-start(bf16[64,256]{1,0:T(8,128)(2,1)S(1)} %get-tuple-element.69), channel_id=1, source_target_pairs={{0,12},{1,13},{2,14},{3,15},{4,8},{5,9},{6,10},{7,11},{8,4},{9,5},... | collective-permute-start | bytes 98312 | tf_op jit(solution)/shard_map/ppermute | solution.py:35
  23.9 2.0 %collective-permute-start.14 = (bf16[64,256]{1,0:T(8,128)(2,1)S(1)}, bf16[64,256]{1,0:T(8,128)(2,1)S(1)}, u32[]{:S(2)}, u32[]{:S(2)}) collective-permute-start(bf16[64,256]{1,0:T(8,128)(2,1)S(1)} %get-tuple-element.69), channel_id=1, source_target_pairs={{0,8},{1,9},{2,10},{3,11},{4,12},{5,13},{6,14},{7,15},{8,0},{9,1},... | collective-permute-start | bytes 98312 | tf_op jit(solution)/shard_map/ppermute | solution.py:35
  24.7 3.7 %collective-permute-start.17 = (f32[64,256]{1,0:T(8,128)S(1)}, f32[64,256]{1,0:T(8,128)S(1)}, u32[]{:S(2)}, u32[]{:S(2)}) collective-permute-start(f32[64,256]{1,0:T(8,128)S(1)} %shard_map.93), channel_id=1, source_target_pairs={{0,8},{1,9},{2,10},{3,11},{4,12},{5,13},{6,14},{7,15},{8,0},{9,1},... | collective-permute-start | bytes 196616 | tf_op jit(solution)/shard_map/ppermute | solution.py:35
  25.1 3.3 %collective-permute-start.18 = (bf16[2,256,256]{2,1,0:T(8,128)(2,1)S(1)}, bf16[2,256,256]{2,1,0:T(8,128)(2,1)S(1)}, u32[]{:S(2)}, u32[]{:S(2)}) collective-permute-start(bf16[2,256,256]{2,1,0:T(8,128)(2,1)S(1)} %shard_map.94), channel_id=1, source_target_pairs={{0,8},{1,9},{2,10},{3,11},{4,12},{5,13},{6,14},{7,15},{8,0},{9,1},... | collective-permute-start | bytes 786440 | tf_op jit(solution)/shard_map/ppermute | solution.py:35
  25.9 1.9 %copy-start.4 = (bf16[1,128,128]{2,1,0:T(8,128)(2,1)S(1)}, bf16[1,128,128]{2,1,0:T(8,128)(2,1)}, u32[]{:S(2)}) copy-start(bf16[1,128,128]{2,1,0:T(8,128)(2,1)} %param.7) | copy-start | bytes 98308
  26.1 3.4 %collective-permute-start.15 = (bf16[64,256]{1,0:T(8,128)(2,1)S(1)}, bf16[64,256]{1,0:T(8,128)(2,1)S(1)}, u32[]{:S(2)}, u32[]{:S(2)}) collective-permute-start(bf16[64,256]{1,0:T(8,128)(2,1)S(1)} %get-tuple-element.76), channel_id=1, source_target_pairs={{0,10},{1,11},{2,8},{3,9},{4,14},{5,15},{6,12},{7,13},{8,2},{9,3},... | collective-permute-start | bytes 98312 | tf_op jit(solution)/shard_map/ppermute | solution.py:35
  27.5 1.9 %collective-permute-start.16 = (bf16[64,256]{1,0:T(8,128)(2,1)S(1)}, bf16[64,256]{1,0:T(8,128)(2,1)S(1)}, u32[]{:S(2)}, u32[]{:S(2)}) collective-permute-start(bf16[64,256]{1,0:T(8,128)(2,1)S(1)} %get-tuple-element.76), channel_id=1, source_target_pairs={{0,8},{1,9},{2,10},{3,11},{4,12},{5,13},{6,14},{7,15},{8,0},{9,1},... | collective-permute-start | bytes 98312 | tf_op jit(solution)/shard_map/ppermute | solution.py:35
  29.6 3.4 %collective-permute-start.19 = (bf16[64,256]{1,0:T(8,128)(2,1)S(1)}, bf16[64,256]{1,0:T(8,128)(2,1)S(1)}, u32[]{:S(2)}, u32[]{:S(2)}) collective-permute-start(bf16[64,256]{1,0:T(8,128)(2,1)S(1)} %shard_map.95), channel_id=1, source_target_pairs={{0,9},{1,8},{2,11},{3,10},{4,13},{5,12},{6,15},{7,14},{8,1},{9,0},... | collective-permute-start | bytes 98312 | tf_op jit(solution)/shard_map/ppermute | solution.py:35
  30.9 2.1 %collective-permute-start.21 = (bf16[64,256]{1,0:T(8,128)(2,1)S(1)}, bf16[64,256]{1,0:T(8,128)(2,1)S(1)}, u32[]{:S(2)}, u32[]{:S(2)}) collective-permute-start(bf16[64,256]{1,0:T(8,128)(2,1)S(1)} %shard_map.95), channel_id=1, source_target_pairs={{0,8},{1,9},{2,10},{3,11},{4,12},{5,13},{6,14},{7,15},{8,0},{9,1},... | collective-permute-start | bytes 98312 | tf_op jit(solution)/shard_map/ppermute | solution.py:35
  31.1 2.0 %collective-permute-start.20 = (bf16[64,256]{1,0:T(8,128)(2,1)S(1)}, bf16[64,256]{1,0:T(8,128)(2,1)S(1)}, u32[]{:S(2)}, u32[]{:S(2)}) collective-permute-start(bf16[64,256]{1,0:T(8,128)(2,1)S(1)} %collective-permute-done.15.received), channel_id=1, source_target_pairs={{0,8},{1,9},{2,10},{3,11},{4,12},{5,13},{6,14},{7,15},{8,0},{9,1},... | collective-permute-start | bytes 98312 | tf_op jit(solution)/shard_map/ppermute | solution.py:35

commit v10 on v9

--- a/solution.py
+++ b/solution.py
@@ -143,12 +143,13 @@
     solved[...] = times(step, inverse[level])
 
 
-def early_products(inverse, coupling, terms, pack, ahead, lowest, *, level):
+def early_products(inverse, coupling, terms, pack, ahead, lowest, lowest_turned, *, level):
     width = inverse.shape[1]
     for side in range(2):
         made = times(coupling[level, side], inverse[level]).astype(BF)
         pack[side * width : (side + 1) * width] = made
-        lowest[side] = turned(inverse[0], coupling[0, side]).astype(BF)
+        lowest[side] = times(coupling[0, side], inverse[0]).astype(BF)
+        lowest_turned[side] = turned(inverse[0], coupling[0, side]).astype(BF)
     products_ahead(inverse, coupling, terms, ahead, level=1)
 
 
@@ -183,7 +184,7 @@
     return right.astype(BF), mirror_right.astype(BF)
 
 
-def join_own(joined, joined_mate, solved, product, part, delta, folded, base, *, home):
+def join_own(joined, joined_mate, solved, product, across, part, delta, folded, base, *, home):
     rows, width = part.shape[1], joined.shape[1]
     mine, mate = joined[2 * width + rows :], joined_mate[2 * width + rows :]
     for at, (a, b, matrices) in enumerate(((mine, mate, joined), (mate, mine, joined_mate))):
@@ -195,19 +196,21 @@
         matrices = (joined, joined_mate)[at]
         total = total - times(part[at].astype(BF), product[side])
         folded[side] = times(matrices[width : 2 * width], product[side]).astype(BF)
-    base[...] = total
-
-
-def join(theirs, across, base, folded, delta, below, *, home):
+    first, second = (0, 1) if home else (1, 0)
+    base[...] = total + times(across[:rows], folded[first]) - times(across[rows:], folded[second])
+
+
+def join(theirs, base, folded, below, *, home):
     rows = base.shape[0]
+    first, second = (0, 1) if home else (1, 0)
+    total = base[...] - times(theirs[rows:], folded[first]) + times(theirs[:rows], folded[second])
+    below[...] = total.astype(BF)
+
+
+def join_blocks(theirs, across, part, joined, joined_mate, delta, block, block_mate):
+    rows, width = block.shape
     for at, (a, b) in enumerate(((theirs, across), (across, theirs))):
         delta[at] = (a[rows:].astype(F32) - b[:rows].astype(F32)).astype(BF)
-    own, other = (delta[0], delta[1]) if home else (delta[1], delta[0])
-    below[...] = (base[...] - times(own, folded[0]) - times(other, folded[1])).astype(BF)
-
-
-def join_blocks(part, delta, joined, joined_mate, block, block_mate):
-    width = joined.shape[1]
     block[...] = part[0] + times(delta[0], joined[width : 2 * width])
     value = part[1] + times(delta[1], joined_mate[width : 2 * width])
     block_mate[...] = value.astype(BF)
@@ -318,16 +321,16 @@
     own_gram = call(top_gram, [((width, width), BF)], inverse)
     inverse_later = after(inverse, own_gram)
     if joined:
-        pack, ahead[1], lowest = call(
-            early_products, [((2 * width, width), BF), ((width + cols, width), BF), pair],
+        pack, ahead[1], product[0], lowest = call(
+            early_products, [((2 * width, width), BF), ((width + cols, width), BF), pair, pair],
             inverse_later, coupling, terms, level=core,
         )
         mirror_pack = send(pack, below_top)
         inverse_later = after(inverse, pack)
         ends = call(top_ends, [((width + 2 * cols, width), BF)], own_gram, terms, values, cost=0)
-    for level in range(core - 2 if joined else below_top):
+    for level in range(1 if joined else 0, core - 2 if joined else below_top):
         product[level] = call(
-            products, [pair], inverse_later, coupling, level=level, cost=8 if level == 0 else 1
+            products, [pair], inverse_later, coupling, level=level
         )
     for level in range(core):
         if not at_home[level] and ahead[level] is None:
@@ -404,7 +407,7 @@
                 )
         if joined and level == core - 1:
             solved[level] = call(
-                solve_last, [vec], last, below, below_turned, inverse, values, level=level, cost=8
+                solve_last, [vec], last, below, below_turned, inverse, values, level=level, cost=12
             )
         else:
             solved[level] = call(solve, [vec], change, inverse, level=level)
@@ -426,14 +429,12 @@
         at_own = core - 1 not in mates
         part, delta, folded, base = call(
             join_own, [both, both_bf, pair, vec],
-            matrices, matrices_mate, solved[core - 1], product[core - 1], home=at_own,
+            matrices, matrices_mate, solved[core - 1], product[core - 1], received, home=at_own, cost=9,
         )
         theirs = mate(received)
-        delta_mirror, block_bf = call(
-            join, [both_bf, vec_bf], theirs, received, base, folded, home=at_own
-        )
-        blocks[core], mirrored[core] = call(
-            join_blocks, [vec, vec_bf], part, delta_mirror, matrices, matrices_mate
+        block_bf = call(join, [vec_bf], theirs, base, folded, home=at_own)
+        delta_mirror, blocks[core], mirrored[core] = call(
+            join_blocks, [both_bf, vec, vec_bf], theirs, received, part, matrices, matrices_mate
         )
         blocks[-1], mirrored[-1] = call(
             top_blocks, [vec, vec_bf], pack, mirror_pack, ends, mirror_ends, delta, delta_mirror

time: 34 us -> 33.9 us (level)
    ppermute x22, waiting for transfers between devices: 5.13 us -> 4.79 us  [exchange(): return lax.ppermute(value, ('gx', 'gy'), pairs)]
    pallas_call x20 -> x19, Pallas kernels: 6.04 us -> 6.04 us  [call(): pl.pallas_call(functools.partial(body, **static), out_shape=[jax.ShapeDty...]
  transfers between devices with their start and end apart: 22 -> 22, of which waited for: 6 -> 7; matrix products, arithmetic and copies ran while one was open for 1% -> 1% of each run, Pallas kernels for 15% -> 15%
where the time goes in v10:
time: 33.9 us; the launch traced here: 33.7 us
  starting transfers between devices  20.5 us (60%)
  Pallas kernels  6.04 us (18%)
  waiting for transfers between devices  4.79 us (14%)
  matrix products  1.52 us (4%)
  between operations  0.81 us (2%)
    ppermute x22, starting transfers between devices, exchange(): return lax.ppermute(value, ('gx', 'gy'), pairs)  20.5 us
    pallas_call x19, Pallas kernels, call(): pl.pallas_call(functools.partial(body, **static), out_shape=[jax.ShapeDty...  6.04 us
    ppermute x22, waiting for transfers between devices, exchange(): return lax.ppermute(value, ('gx', 'gy'), pairs)  4.79 us
    dot_general x1, matrix products, times_t(): lax.dot_general(values, matrix, (((1,), (1,)), ((), ())), preferred_eleme...  1.04 us
  transfers between devices with their start and end apart: 22, of which 7 were waited for; matrix products, arithmetic and copies ran while one was open for 1% of the time, Pallas kernels for 15%

profile of v10, /device:TPU:0, one launch (start us, length us, event | category | flops | bytes accessed | tf_op | source)
XLA Modules:
  0.0 33.7 jit_solution(12626053764303554786)
XLA Ops:
  0.7 1.0 %fusion.6.leaf = f32[64,128]{1,0:T(8,128)S(1)} fusion(f32[128,64]{0,1:T(8,128)} %param.6, bf16[1,128,128]{2,1,0:T(8,128)(2,1)} %param.7), kind=kOutput, calls=%fused_computation.9 | convolution fusion | flops 2105344 | bytes 98304 | tf_op jit(solution)/shard_map/dot_general | solution.py:20
  1.7 0.3 convolution_bitcast_fusion.terms
  2.0 3.0 %collective-permute-start = (bf16[64,256]{1,0:T(8,128)(2,1)S(1)}, bf16[64,256]{1,0:T(8,128)(2,1)S(1)}, u32[]{:S(2)}, u32[]{:S(2)}) collective-permute-start(bf16[64,256]{1,0:T(8,128)(2,1)S(1)} %fusion.2), channel_id=1, source_target_pairs={{0,1},{1,0},{2,3},{3,2},{4,5},{5,4},{6,7},{7,6},{8,9},{9,8},{10,11... | collective-permute-start | bytes 98312 | tf_op jit(solution)/shard_map/ppermute | solution.py:35
  5.0 0.2 shard_map.77.own_gram
  5.2 0.4 %shard_map.78 = (bf16[512,256]{1,0:T(8,128)(2,1)S(1)}, bf16[320,256]{1,0:T(8,128)(2,1)S(1)}, bf16[2,256,256]{2,1,0:T(8,128)(2,1)S(1)}, bf16[2,256,256]{2,1,0:T(8,128)(2,1)S(1)}) custom-call(bf16[5,256,256]{2,1,0:T(8,128)(2,1)S(1)} %bitcast.28, bf16[4,2,256,256]{3,2,1,0:T(8,128)(2,1)S(1)} %bitcast.39, f32[5,64,256]{2,1,0:T(8,128)S(1)} %convolution_bitcast_fusion.terms), custom_call_target="tpu_custom_call" | custom-call | flops 300000000 | bytes 2031616 | tf_op jit(solution)/shard_map/pallas_call | solution.py:40
  5.7 1.6 %collective-permute-start.6 = (bf16[512,256]{1,0:T(8,128)(2,1)S(1)}, bf16[512,256]{1,0:T(8,128)(2,1)S(1)}, u32[]{:S(2)}, u32[]{:S(2)}) collective-permute-start(bf16[512,256]{1,0:T(8,128)(2,1)S(1)} %get-tuple-element.52.mine), channel_id=1, source_target_pairs={{0,16},{1,17},{2,18},{3,19},{4,20},{5,21},{6,22},{7,23},{8,24},{9,... | collective-permute-start | bytes 786440 | tf_op jit(solution)/shard_map/ppermute | solution.py:35
  7.5 1.8 %collective-permute-start.1 = (bf16[64,256]{1,0:T(8,128)(2,1)S(1)}, bf16[64,256]{1,0:T(8,128)(2,1)S(1)}, u32[]{:S(2)}, u32[]{:S(2)}) collective-permute-start(bf16[64,256]{1,0:T(8,128)(2,1)S(1)} %get-tuple-element.45), channel_id=1, source_target_pairs={{0,10},{1,11},{2,8},{3,9},{4,14},{5,15},{6,12},{7,13},{8,2},{9,3},... | collective-permute-start | bytes 98312 | tf_op jit(solution)/shard_map/ppermute | solution.py:35
  9.4 1.6 %collective-permute-start.9 = (bf16[384,256]{1,0:T(8,128)(2,1)S(1)}, bf16[384,256]{1,0:T(8,128)(2,1)S(1)}, u32[]{:S(2)}, u32[]{:S(2)}) collective-permute-start(bf16[384,256]{1,0:T(8,128)(2,1)S(1)} %shard_map.80.ends), channel_id=1, source_target_pairs={{0,16},{1,17},{2,18},{3,19},{4,20},{5,21},{6,22},{7,23},{8,24},{9,... | collective-permute-start | bytes 589832 | tf_op jit(solution)/shard_map/ppermute | solution.py:35
  11.2 3.0 %collective-permute-start.4 = (bf16[64,256]{1,0:T(8,128)(2,1)S(1)}, bf16[64,256]{1,0:T(8,128)(2,1)S(1)}, u32[]{:S(2)}, u32[]{:S(2)}) collective-permute-start(bf16[64,256]{1,0:T(8,128)(2,1)S(1)} %get-tuple-element.50), channel_id=1, source_target_pairs={{0,12},{1,13},{2,14},{3,15},{4,8},{5,9},{6,10},{7,11},{8,4},{9,5},... | collective-permute-start | bytes 98312 | tf_op jit(solution)/shard_map/ppermute | solution.py:35
  14.2 0.6 %shard_map.82 = (bf16[2,256,256]{2,1,0:T(8,128)(2,1)S(1)}, bf16[2,256,256]{2,1,0:T(8,128)(2,1)S(1)}, bf16[2,256,256]{2,1,0:T(8,128)(2,1)S(1)}, bf16[256,256]{1,0...) custom-call(bf16[5,256,256]{2,1,0:T(8,128)(2,1)S(1)} %bitcast.29, ...), custom_call_target="tpu_custom_call" | custom-call | flops 300000000 | bytes 2359296 | tf_op jit(solution)/shard_map/pallas_call | solution.py:40
  14.8 1.0 %collective-permute-done.4 = bf16[64,256]{1,0:T(8,128)(2,1)S(1)} collective-permute-done((bf16[64,256]{1,0:T(8,128)(2,1)S(1)}, bf16[64,256]{1,0:T(8,128)(2,1)S(1)}, u32[]{:S(2)}, u32[]{:S(2)}) %collective-permute-start.4) | collective-permute-done | bytes 32800 | tf_op jit(solution)/shard_map/ppermute | solution.py:35
  16.0 1.6 %collective-permute-start.7 = (bf16[128,256]{1,0:T(8,128)(2,1)S(1)}, bf16[128,256]{1,0:T(8,128)(2,1)S(1)}, u32[]{:S(2)}, u32[]{:S(2)}) collective-permute-start(bf16[128,256]{1,0:T(8,128)(2,1)S(1)} %shard_map.83.sent), channel_id=1, source_target_pairs={{0,24},{1,25},{2,26},{3,27},{4,28},{5,29},{6,30},{7,31},{8,16},{9,... | collective-permute-start | bytes 196616 | tf_op jit(solution)/shard_map/ppermute | solution.py:35
  17.7 0.6 %shard_map.84.joined = bf16[704,256]{1,0:T(8,128)(2,1)S(1)} custom-call(bf16[512,256]{1,0:T(8,128)(2,1)S(1)} %get-tuple-element.52.mine, bf16[512,256]{1,0:T(8,128)(2,1)S(1)} %collective-permute-done.6.mirror, bf16[384,256]{1,0:T(8,128)(2,1)S(1)} %shard_map.80.ends, bf16[384,256]{1,0:T(8,128)(2,1)S(1)} %collective-permute-done.9.mirror_ends, ...), custom_call_target="tpu_custom_call" | custom-call | flops 300000000 | bytes 1638400 | tf_op jit(solution)/shard_map/pallas_call | solution.py:40
  18.3 0.5 %collective-permute-start.10 = (bf16[704,256]{1,0:T(8,128)(2,1)S(1)}, bf16[704,256]{1,0:T(8,128)(2,1)S(1)}, u32[]{:S(2)}, u32[]{:S(2)}) collective-permute-start(bf16[704,256]{1,0:T(8,128)(2,1)S(1)} %shard_map.84.joined), channel_id=1, source_target_pairs={{0,8},{1,9},{2,10},{3,11},{4,12},{5,13},{6,14},{7,15},{8,0},{9,1},... | collective-permute-start | bytes 1081352 | tf_op jit(solution)/shard_map/ppermute | solution.py:35
  18.8 0.4 %shard_map.85 = f32[64,256]{1,0:T(8,128)S(1)} custom-call(f32[64,256]{1,0:T(8,128)S(1)} %convert_element_type.21.received, bf16[64,256]{1,0:T(8,128)(2,1)S(1)} %collective-permute-done.5.below.delta, bf16[256,256]{1,0:T(8,128)(2,1)S(1)} %get-tuple-element.62.below_turned, bf16[5,256,256]{2,1,0:T(8,128)(2,1)S(1)} %bitcast.31, f32[5,64,256]{2,1,0:T(8,128)S(1)} %bitcast.38), custom_call_target="tpu_custom_call" | custom-call | flops 3600000000 | bytes 1212416 | tf_op jit(solution)/shard_map/pallas_call | solution.py:40
  19.3 0.7 %collective-permute-done.7.across = bf16[128,256]{1,0:T(8,128)(2,1)S(1)} collective-permute-done((bf16[128,256]{1,0:T(8,128)(2,1)S(1)}, bf16[128,256]{1,0:T(8,128)(2,1)S(1)}, u32[]{:S(2)}, u32[]{:S(2)}) %collective-permute-start.7) | collective-permute-done | bytes 65568 | tf_op jit(solution)/shard_map/ppermute | solution.py:35
  20.3 0.2 collective-permute-done.11.solved
  20.5 0.6 %shard_map.86 = (f32[2,64,256]{2,1,0:T(8,128)S(1)}, bf16[2,64,256]{2,1,0:T(8,128)(2,1)S(1)}, bf16[2,256,256]{2,1,0:T(8,128)(2,1)S(1)}, f32[64,256]{1,0:T(8,128)S(1)}) custom-call(bf16[704,256]{1,0:T(8,128)(2,1)S(1)} %shard_map.84.joined, bf16[704,256]{1,0:T(8,128)(2,1)S(1)} %collective-permute-done.10.joined_mate, ...), custom_call_target="tpu_custom_call" | custom-call | flops 2700000000 | bytes 1114112 | tf_op jit(solution)/shard_map/pallas_call | solution.py:40
  21.5 2.4 %collective-permute-start.13 = (bf16[64,256]{1,0:T(8,128)(2,1)S(1)}, bf16[64,256]{1,0:T(8,128)(2,1)S(1)}, u32[]{:S(2)}, u32[]{:S(2)}) collective-permute-start(bf16[64,256]{1,0:T(8,128)(2,1)S(1)} %shard_map.87), channel_id=1, source_target_pairs={{0,12},{1,13},{2,14},{3,15},{4,8},{5,9},{6,10},{7,11},{8,4},{9,5},... | collective-permute-start | bytes 98312 | tf_op jit(solution)/shard_map/ppermute | solution.py:35
  24.1 0.3 shard_map.93
  24.4 0.3 shard_map.91.solved
  24.7 0.4 %collective-permute-start.17 = (f32[64,256]{1,0:T(8,128)S(1)}, f32[64,256]{1,0:T(8,128)S(1)}, u32[]{:S(2)}, u32[]{:S(2)}) collective-permute-start(f32[64,256]{1,0:T(8,128)S(1)} %shard_map.93), channel_id=1, source_target_pairs={{0,8},{1,9},{2,10},{3,11},{4,12},{5,13},{6,14},{7,15},{8,0},{9,1},... | collective-permute-start | bytes 196616 | tf_op jit(solution)/shard_map/ppermute | solution.py:35
  25.3 0.5 %collective-permute-done.13.refs_0_.received = bf16[64,256]{1,0:T(8,128)(2,1)S(1)} collective-permute-done((bf16[64,256]{1,0:T(8,128)(2,1)S(1)}, bf16[64,256]{1,0:T(8,128)(2,1)S(1)}, u32[]{:S(2)}, u32[]{:S(2)}) %collective-permute-start.13) | collective-permute-done | bytes 32800 | tf_op jit(solution)/shard_map/ppermute | solution.py:35
  26.0 1.6 %collective-permute-start.15 = (bf16[64,256]{1,0:T(8,128)(2,1)S(1)}, bf16[64,256]{1,0:T(8,128)(2,1)S(1)}, u32[]{:S(2)}, u32[]{:S(2)}) collective-permute-start(bf16[64,256]{1,0:T(8,128)(2,1)S(1)} %get-tuple-element.74), channel_id=1, source_target_pairs={{0,10},{1,11},{2,8},{3,9},{4,14},{5,15},{6,12},{7,13},{8,2},{9,3},... | collective-permute-start | bytes 98312 | tf_op jit(solution)/shard_map/ppermute | solution.py:35
  27.5 0.2 collective-permute-start.16
  27.8 0.2 convolution_convert_fusion.leaf_products
  28.2 1.2 %collective-permute-done.15.received = bf16[64,256]{1,0:T(8,128)(2,1)S(1)} collective-permute-done((bf16[64,256]{1,0:T(8,128)(2,1)S(1)}, bf16[64,256]{1,0:T(8,128)(2,1)S(1)}, u32[]{:S(2)}, u32[]{:S(2)}) %collective-permute-start.15) | collective-permute-done | bytes 32800 | tf_op jit(solution)/shard_map/ppermute | solution.py:35
  29.6 1.4 %collective-permute-start.19 = (bf16[64,256]{1,0:T(8,128)(2,1)S(1)}, bf16[64,256]{1,0:T(8,128)(2,1)S(1)}, u32[]{:S(2)}, u32[]{:S(2)}) collective-permute-start(bf16[64,256]{1,0:T(8,128)(2,1)S(1)} %shard_map.94), channel_id=1, source_target_pairs={{0,9},{1,8},{2,11},{3,10},{4,13},{5,12},{6,15},{7,14},{8,1},{9,0},... | collective-permute-start | bytes 98312 | tf_op jit(solution)/shard_map/ppermute | solution.py:35
  31.1 0.4 %collective-permute-start.20 = (bf16[64,256]{1,0:T(8,128)(2,1)S(1)}, bf16[64,256]{1,0:T(8,128)(2,1)S(1)}, u32[]{:S(2)}, u32[]{:S(2)}) collective-permute-start(bf16[64,256]{1,0:T(8,128)(2,1)S(1)} %collective-permute-done.15.received), channel_id=1, source_target_pairs={{0,8},{1,9},{2,10},{3,11},{4,12},{5,13},{6,14},{7,15},{8,0},{9,1},... | collective-permute-start | bytes 98312 | tf_op jit(solution)/shard_map/ppermute | solution.py:35
  31.4 0.4 %shard_map.89 = (f32[64,256]{1,0:T(8,128)S(1)}, bf16[64,256]{1,0:T(8,128)(2,1)S(1)}) custom-call(bf16[512,256]{1,0:T(8,128)(2,1)S(1)} %get-tuple-element.52.mine, bf16[512,256]{1,0:T(8,128)(2,1)S(1)} %collective-permute-done.6.mirror, bf16[384,256]{1,0:T(8,128)(2,1)S(1)} %shard_map.80.ends, bf16[384,256]{1,0:T(8,128)(2,1)S(1)} %collective-permute-done.9.mirror_ends, ...), custom_call_target="tpu_custom_call" | custom-call | flops 300000000 | bytes 1048576 | tf_op jit(solution)/shard_map/pallas_call | solution.py:40
  32.0 0.9 %collective-permute-done.19.refs_0_ = bf16[64,256]{1,0:T(8,128)(2,1)S(1)} collective-permute-done((bf16[64,256]{1,0:T(8,128)(2,1)S(1)}, bf16[64,256]{1,0:T(8,128)(2,1)S(1)}, u32[]{:S(2)}, u32[]{:S(2)}) %collective-permute-start.19) | collective-permute-done | bytes 32800 | tf_op jit(solution)/shard_map/ppermute | solution.py:35
  33.0 0.8 %shard_map.95 = (f32[64,128]{1,0:T(8,128)}, f32[5,64,256]{2,1,0:T(8,128)}) custom-call(f32[64,128]{1,0:T(8,128)S(1)} %shard_map.90.part, bf16[5,256,128]{2,1,0:T(8,128)(2,1)S(1)} %convolution_convert_fusion.leaf_products, bf16[64,256]{1,0:T(8,128)(2,1)S(1)} %collective-permute-done.19.refs_0_, bf16[64,256]{1,0:T(8,128)(2,1)S(1)} %collective-permute-done.20.refs_1_, ...), custom_call_target="tpu_custom_call" | custom-call | flops 300000000 | bytes 688128 | tf_op jit(solution)/shard_map/pallas_call | solution.py:40
  (46 shorter events, 2.8 us)
Async XLA Ops:
  0.6 1.1 %copy-start = (bf16[1,5,256,128]{3,2,1,0:T(8,128)(2,1)S(1)}, bf16[1,5,256,128]{3,2,1,0:T(8,128)(2,1)}, u32[]{:S(2)}) copy-start(bf16[1,5,256,128]{3,2,1,0:T(8,128)(2,1)} %param.8) | copy-start | bytes 983044
  0.6 4.3 %copy-start.1 = (bf16[1,5,256,256]{3,2,1,0:T(8,128)(2,1)S(1)}, bf16[1,5,256,256]{3,2,1,0:T(8,128)(2,1)}, u32[]{:S(2)}) copy-start(bf16[1,5,256,256]{3,2,1,0:T(8,128)(2,1)} %param.10) | copy-start | bytes 1966084
  0.7 4.6 %copy-start.3 = (bf16[1,4,1,2,256,256]{5,4,3,2,1,0:T(8,128)(2,1)S(1)}, bf16[1,4,1,2,256,256]{5,4,3,2,1,0:T(8,128)(2,1)}, u32[]{:S(2)}) copy-start(bf16[1,4,1,2,256,256]{5,4,3,2,1,0:T(8,128)(2,1)} %param.11) | copy-start | bytes 3145732
  2.0 5.3 %collective-permute-start = (bf16[64,256]{1,0:T(8,128)(2,1)S(1)}, bf16[64,256]{1,0:T(8,128)(2,1)S(1)}, u32[]{:S(2)}, u32[]{:S(2)}) collective-permute-start(bf16[64,256]{1,0:T(8,128)(2,1)S(1)} %fusion.2), channel_id=1, source_target_pairs={{0,1},{1,0},{2,3},{3,2},{4,5},{5,4},{6,7},{7,6},{8,9},{9,8},{10,11... | collective-permute-start | bytes 98312 | tf_op jit(solution)/shard_map/ppermute | solution.py:35
  5.2 2.0 %copy-start.2 = (f32[1,5,256,64]{2,3,1,0:T(8,128)S(1)}, f32[1,5,256,64]{2,3,1,0:T(8,128)}, u32[]{:S(2)}) copy-start(f32[1,5,256,64]{2,3,1,0:T(8,128)} %param.9) | copy-start | bytes 983044
  5.7 10.1 %collective-permute-start.6 = (bf16[512,256]{1,0:T(8,128)(2,1)S(1)}, bf16[512,256]{1,0:T(8,128)(2,1)S(1)}, u32[]{:S(2)}, u32[]{:S(2)}) collective-permute-start(bf16[512,256]{1,0:T(8,128)(2,1)S(1)} %get-tuple-element.52.mine), channel_id=1, source_target_pairs={{0,16},{1,17},{2,18},{3,19},{4,20},{5,21},{6,22},{7,23},{8,24},{9,... | collective-permute-start | bytes 786440 | tf_op jit(solution)/shard_map/ppermute | solution.py:35
  7.4 3.6 %collective-permute-start.3 = (bf16[320,256]{1,0:T(8,128)(2,1)S(1)}, bf16[320,256]{1,0:T(8,128)(2,1)S(1)}, u32[]{:S(2)}, u32[]{:S(2)}) collective-permute-start(bf16[320,256]{1,0:T(8,128)(2,1)S(1)} %get-tuple-element.48), channel_id=1, source_target_pairs={{0,8},{1,9},{2,10},{3,11},{4,12},{5,13},{6,14},{7,15},{8,0},{9,1},... | collective-permute-start | bytes 491528 | tf_op jit(solution)/shard_map/ppermute | solution.py:35
  7.5 3.5 %collective-permute-start.1 = (bf16[64,256]{1,0:T(8,128)(2,1)S(1)}, bf16[64,256]{1,0:T(8,128)(2,1)S(1)}, u32[]{:S(2)}, u32[]{:S(2)}) collective-permute-start(bf16[64,256]{1,0:T(8,128)(2,1)S(1)} %get-tuple-element.45), channel_id=1, source_target_pairs={{0,10},{1,11},{2,8},{3,9},{4,14},{5,15},{6,12},{7,13},{8,2},{9,3},... | collective-permute-start | bytes 98312 | tf_op jit(solution)/shard_map/ppermute | solution.py:35
  9.4 1.7 %collective-permute-start.2 = (bf16[64,256]{1,0:T(8,128)(2,1)S(1)}, bf16[64,256]{1,0:T(8,128)(2,1)S(1)}, u32[]{:S(2)}, u32[]{:S(2)}) collective-permute-start(bf16[64,256]{1,0:T(8,128)(2,1)S(1)} %get-tuple-element.46), channel_id=1, source_target_pairs={{0,8},{1,9},{2,10},{3,11},{4,12},{5,13},{6,14},{7,15},{8,0},{9,1},... | collective-permute-start | bytes 98312 | tf_op jit(solution)/shard_map/ppermute | solution.py:35
  9.4 8.3 %collective-permute-start.9 = (bf16[384,256]{1,0:T(8,128)(2,1)S(1)}, bf16[384,256]{1,0:T(8,128)(2,1)S(1)}, u32[]{:S(2)}, u32[]{:S(2)}) collective-permute-start(bf16[384,256]{1,0:T(8,128)(2,1)S(1)} %shard_map.80.ends), channel_id=1, source_target_pairs={{0,16},{1,17},{2,18},{3,19},{4,20},{5,21},{6,22},{7,23},{8,24},{9,... | collective-permute-start | bytes 589832 | tf_op jit(solution)/shard_map/ppermute | solution.py:35
  11.2 4.6 %collective-permute-start.4 = (bf16[64,256]{1,0:T(8,128)(2,1)S(1)}, bf16[64,256]{1,0:T(8,128)(2,1)S(1)}, u32[]{:S(2)}, u32[]{:S(2)}) collective-permute-start(bf16[64,256]{1,0:T(8,128)(2,1)S(1)} %get-tuple-element.50), channel_id=1, source_target_pairs={{0,12},{1,13},{2,14},{3,15},{4,8},{5,9},{6,10},{7,11},{8,4},{9,5},... | collective-permute-start | bytes 98312 | tf_op jit(solution)/shard_map/ppermute | solution.py:35
  14.2 1.6 %collective-permute-start.5 = (bf16[64,256]{1,0:T(8,128)(2,1)S(1)}, bf16[64,256]{1,0:T(8,128)(2,1)S(1)}, u32[]{:S(2)}, u32[]{:S(2)}) collective-permute-start(bf16[64,256]{1,0:T(8,128)(2,1)S(1)} %get-tuple-element.51), channel_id=1, source_target_pairs={{0,8},{1,9},{2,10},{3,11},{4,12},{5,13},{6,14},{7,15},{8,0},{9,1},... | collective-permute-start | bytes 98312 | tf_op jit(solution)/shard_map/ppermute | solution.py:35
  16.0 4.1 %collective-permute-start.7 = (bf16[128,256]{1,0:T(8,128)(2,1)S(1)}, bf16[128,256]{1,0:T(8,128)(2,1)S(1)}, u32[]{:S(2)}, u32[]{:S(2)}) collective-permute-start(bf16[128,256]{1,0:T(8,128)(2,1)S(1)} %shard_map.83.sent), channel_id=1, source_target_pairs={{0,24},{1,25},{2,26},{3,27},{4,28},{5,29},{6,30},{7,31},{8,16},{9,... | collective-permute-start | bytes 196616 | tf_op jit(solution)/shard_map/ppermute | solution.py:35
  17.6 2.9 %collective-permute-start.12 = (bf16[2,256,256]{2,1,0:T(8,128)(2,1)S(1)}, bf16[2,256,256]{2,1,0:T(8,128)(2,1)S(1)}, u32[]{:S(2)}, u32[]{:S(2)}) collective-permute-start(bf16[2,256,256]{2,1,0:T(8,128)(2,1)S(1)} %get-tuple-element.65), channel_id=1, source_target_pairs={{0,8},{1,9},{2,10},{3,11},{4,12},{5,13},{6,14},{7,15},{8,0},{9,1},... | collective-permute-start | bytes 786440 | tf_op jit(solution)/shard_map/ppermute | solution.py:35
  18.3 2.2 %collective-permute-start.10 = (bf16[704,256]{1,0:T(8,128)(2,1)S(1)}, bf16[704,256]{1,0:T(8,128)(2,1)S(1)}, u32[]{:S(2)}, u32[]{:S(2)}) collective-permute-start(bf16[704,256]{1,0:T(8,128)(2,1)S(1)} %shard_map.84.joined), channel_id=1, source_target_pairs={{0,8},{1,9},{2,10},{3,11},{4,12},{5,13},{6,14},{7,15},{8,0},{9,1},... | collective-permute-start | bytes 1081352 | tf_op jit(solution)/shard_map/ppermute | solution.py:35
  19.2 1.3 %collective-permute-start.11 = (f32[64,256]{1,0:T(8,128)S(1)}, f32[64,256]{1,0:T(8,128)S(1)}, u32[]{:S(2)}, u32[]{:S(2)}) collective-permute-start(f32[64,256]{1,0:T(8,128)S(1)} %shard_map.85), channel_id=1, source_target_pairs={{0,8},{1,9},{2,10},{3,11},{4,12},{5,13},{6,14},{7,15},{8,0},{9,1},... | collective-permute-start | bytes 196616 | tf_op jit(solution)/shard_map/ppermute | solution.py:35
  20.1 1.3 %collective-permute-start.8 = (bf16[128,256]{1,0:T(8,128)(2,1)S(1)}, bf16[128,256]{1,0:T(8,128)(2,1)S(1)}, u32[]{:S(2)}, u32[]{:S(2)}) collective-permute-start(bf16[128,256]{1,0:T(8,128)(2,1)S(1)} %collective-permute-done.7.across), channel_id=1, source_target_pairs={{0,8},{1,9},{2,10},{3,11},{4,12},{5,13},{6,14},{7,15},{8,0},{9,1},... | collective-permute-start | bytes 196616 | tf_op jit(solution)/shard_map/ppermute | solution.py:35
  21.5 4.3 %collective-permute-start.13 = (bf16[64,256]{1,0:T(8,128)(2,1)S(1)}, bf16[64,256]{1,0:T(8,128)(2,1)S(1)}, u32[]{:S(2)}, u32[]{:S(2)}) collective-permute-start(bf16[64,256]{1,0:T(8,128)(2,1)S(1)} %shard_map.87), channel_id=1, source_target_pairs={{0,12},{1,13},{2,14},{3,15},{4,8},{5,9},{6,10},{7,11},{8,4},{9,5},... | collective-permute-start | bytes 98312 | tf_op jit(solution)/shard_map/ppermute | solution.py:35
  23.9 1.9 %collective-permute-start.14 = (bf16[64,256]{1,0:T(8,128)(2,1)S(1)}, bf16[64,256]{1,0:T(8,128)(2,1)S(1)}, u32[]{:S(2)}, u32[]{:S(2)}) collective-permute-start(bf16[64,256]{1,0:T(8,128)(2,1)S(1)} %shard_map.87), channel_id=1, source_target_pairs={{0,8},{1,9},{2,10},{3,11},{4,12},{5,13},{6,14},{7,15},{8,0},{9,1},... | collective-permute-start | bytes 98312 | tf_op jit(solution)/shard_map/ppermute | solution.py:35
  24.7 3.5 %collective-permute-start.17 = (f32[64,256]{1,0:T(8,128)S(1)}, f32[64,256]{1,0:T(8,128)S(1)}, u32[]{:S(2)}, u32[]{:S(2)}) collective-permute-start(f32[64,256]{1,0:T(8,128)S(1)} %shard_map.93), channel_id=1, source_target_pairs={{0,8},{1,9},{2,10},{3,11},{4,12},{5,13},{6,14},{7,15},{8,0},{9,1},... | collective-permute-start | bytes 196616 | tf_op jit(solution)/shard_map/ppermute | solution.py:35
  25.1 3.1 %collective-permute-start.18 = (bf16[2,256,256]{2,1,0:T(8,128)(2,1)S(1)}, bf16[2,256,256]{2,1,0:T(8,128)(2,1)S(1)}, u32[]{:S(2)}, u32[]{:S(2)}) collective-permute-start(bf16[2,256,256]{2,1,0:T(8,128)(2,1)S(1)} %get-tuple-element.78), channel_id=1, source_target_pairs={{0,8},{1,9},{2,10},{3,11},{4,12},{5,13},{6,14},{7,15},{8,0},{9,1},... | collective-permute-start | bytes 786440 | tf_op jit(solution)/shard_map/ppermute | solution.py:35
  25.8 2.0 %copy-start.4 = (bf16[1,128,128]{2,1,0:T(8,128)(2,1)S(1)}, bf16[1,128,128]{2,1,0:T(8,128)(2,1)}, u32[]{:S(2)}) copy-start(bf16[1,128,128]{2,1,0:T(8,128)(2,1)} %param.7) | copy-start | bytes 98308
  26.0 3.4 %collective-permute-start.15 = (bf16[64,256]{1,0:T(8,128)(2,1)S(1)}, bf16[64,256]{1,0:T(8,128)(2,1)S(1)}, u32[]{:S(2)}, u32[]{:S(2)}) collective-permute-start(bf16[64,256]{1,0:T(8,128)(2,1)S(1)} %get-tuple-element.74), channel_id=1, source_target_pairs={{0,10},{1,11},{2,8},{3,9},{4,14},{5,15},{6,12},{7,13},{8,2},{9,3},... | collective-permute-start | bytes 98312 | tf_op jit(solution)/shard_map/ppermute | solution.py:35
  27.5 1.8 %collective-permute-start.16 = (bf16[64,256]{1,0:T(8,128)(2,1)S(1)}, bf16[64,256]{1,0:T(8,128)(2,1)S(1)}, u32[]{:S(2)}, u32[]{:S(2)}) collective-permute-start(bf16[64,256]{1,0:T(8,128)(2,1)S(1)} %get-tuple-element.74), channel_id=1, source_target_pairs={{0,8},{1,9},{2,10},{3,11},{4,12},{5,13},{6,14},{7,15},{8,0},{9,1},... | collective-permute-start | bytes 98312 | tf_op jit(solution)/shard_map/ppermute | solution.py:35
  29.6 3.4 %collective-permute-start.19 = (bf16[64,256]{1,0:T(8,128)(2,1)S(1)}, bf16[64,256]{1,0:T(8,128)(2,1)S(1)}, u32[]{:S(2)}, u32[]{:S(2)}) collective-permute-start(bf16[64,256]{1,0:T(8,128)(2,1)S(1)} %shard_map.94), channel_id=1, source_target_pairs={{0,9},{1,8},{2,11},{3,10},{4,13},{5,12},{6,15},{7,14},{8,1},{9,0},... | collective-permute-start | bytes 98312 | tf_op jit(solution)/shard_map/ppermute | solution.py:35
  30.9 2.0 %collective-permute-start.21 = (bf16[64,256]{1,0:T(8,128)(2,1)S(1)}, bf16[64,256]{1,0:T(8,128)(2,1)S(1)}, u32[]{:S(2)}, u32[]{:S(2)}) collective-permute-start(bf16[64,256]{1,0:T(8,128)(2,1)S(1)} %shard_map.94), channel_id=1, source_target_pairs={{0,8},{1,9},{2,10},{3,11},{4,12},{5,13},{6,14},{7,15},{8,0},{9,1},... | collective-permute-start | bytes 98312 | tf_op jit(solution)/shard_map/ppermute | solution.py:35
  31.1 1.9 %collective-permute-start.20 = (bf16[64,256]{1,0:T(8,128)(2,1)S(1)}, bf16[64,256]{1,0:T(8,128)(2,1)S(1)}, u32[]{:S(2)}, u32[]{:S(2)}) collective-permute-start(bf16[64,256]{1,0:T(8,128)(2,1)S(1)} %collective-permute-done.15.received), channel_id=1, source_target_pairs={{0,8},{1,9},{2,10},{3,11},{4,12},{5,13},{6,14},{7,15},{8,0},{9,1},... | collective-permute-start | bytes 98312 | tf_op jit(solution)/shard_map/ppermute | solution.py:35

commit v11 on v10

--- a/solution.py
+++ b/solution.py
@@ -22,6 +22,11 @@
 
 def gram(left, right):
     return lax.dot_general(left, right, (((0,), (0,)), ((), ())), preferred_element_type=F32)
+
+
+def deep(first, second, matrices):
+    depth, width = matrices.shape[1:]
+    return times(jnp.concatenate([first, second], axis=1), matrices[...].reshape(2 * depth, width))
 
 
 def turned(inverse, coupling):
@@ -59,17 +64,17 @@
     ahead[rows:] = terms[level + 1].astype(BF)
 
 
-def products_last(inverse, coupling, terms, values, out, out_turned, below, below_turned, folded, fixed, *, level):
+def products_last(inverse, coupling, terms, values, out, below, below_turned, maps, fixed, *, level):
     for side in range(2):
         out[side] = times(coupling[level, side], inverse[level]).astype(BF)
         below[side] = times(coupling[level - 1, side], inverse[level - 1]).astype(BF)
-        out_turned[side] = turned(inverse[level], coupling[level, side]).astype(BF)
+        maps[side, 1] = turned(inverse[level], coupling[level, side]).astype(BF)
     below_turned[...] = turned(inverse[level - 1], coupling[level - 1, 0]).astype(BF)
     for side in range(2):
-        folded[side] = times(below_turned[...], out_turned[side]).astype(BF)
+        maps[side, 0] = times(below_turned[...], maps[side, 1]).astype(BF)
     right = values[level].astype(BF)
-    fixed[0] = values[level + 1] - times(right, out_turned[0])
-    fixed[1] = terms[level + 1] + times(right, out_turned[1])
+    fixed[0] = values[level + 1] - times(right, maps[0, 1])
+    fixed[1] = terms[level + 1] + times(right, maps[1, 1])
 
 
 def top_gram(inverse, out):
@@ -130,10 +135,10 @@
     ahead[...] = (values[1] - times(change, product[0])).astype(BF)
 
 
-def forward_last(received, below, folded, product, fixed, out):
+def forward_last(received, below, maps, fixed, out):
     rows, arrived = received.shape[0], received[...].astype(BF)
-    out[:rows] = (fixed[1] - times(below[...], folded[1]) - times(arrived, product[1])).astype(BF)
-    out[rows:] = (fixed[0] + times(below[...], folded[0]) + times(arrived, product[0])).astype(BF)
+    out[:rows] = (fixed[1] - deep(below[...], arrived, maps[1])).astype(BF)
+    out[rows:] = (fixed[0] + deep(below[...], arrived, maps[0])).astype(BF)
 
 
 def solve_last(received, below, below_turned, inverse, values, solved, *, level):
@@ -260,8 +265,7 @@
 
 
 def back_both(received, known, solved, product, *outs):
-    value = solved[...] - times(known[...], product[0])
-    value = value - times(received[...].astype(BF), product[1])
+    value = solved[...] - deep(known[...], received[...].astype(BF), product)
     for out in outs:
         out[...] = value.astype(out.dtype)
 
@@ -346,7 +350,7 @@
             last = arrived(received)
             out = call(
                 forward_last, [((2 * cols, width), BF)],
-                last, below, folded, last_turned, fixed, cost=4,
+                last, below, maps, fixed, cost=4,
             )
             received = send(out, below_top, True)
         elif level == levels - 2:
@@ -386,9 +390,9 @@
                 )
             received = send(out, level + 1, across)
             if joined and level == core - 2:
-                product[core - 1], last_turned, product[core - 2], below_turned, folded, fixed = call(
+                product[core - 1], product[core - 2], below_turned, maps, fixed = call(
                     products_last,
-                    [pair, pair, pair, ((width, width), BF), pair, ((2, cols, width), F32)],
+                    [pair, pair, ((width, width), BF), ((2, 2, width, width), BF), ((2, cols, width), F32)],
                     after(inverse, out), coupling, terms, values, level=core - 1, cost=1,
                 )
             if level == 0:

time: 33.9 us -> 33.9 us (level)
  no operation moved by 1% of the time
where the time goes in v11:
time: 33.9 us; the launch traced here: 33.7 us
  starting transfers between devices  20.6 us (61%)
  Pallas kernels  6.03 us (18%)
  waiting for transfers between devices  4.79 us (14%)
  matrix products  1.52 us (4%)
  between operations  0.81 us (2%)
    ppermute x22, starting transfers between devices, exchange(): return lax.ppermute(value, ('gx', 'gy'), pairs)  20.6 us
    pallas_call x19, Pallas kernels, call(): pl.pallas_call(functools.partial(body, **static), out_shape=[jax.ShapeDty...  6.03 us
    ppermute x22, waiting for transfers between devices, exchange(): return lax.ppermute(value, ('gx', 'gy'), pairs)  4.79 us
    dot_general x1, matrix products, times_t(): lax.dot_general(values, matrix, (((1,), (1,)), ((), ())), preferred_eleme...  1.04 us
  transfers between devices with their start and end apart: 22, of which 7 were waited for; matrix products, arithmetic and copies ran while one was open for 1% of the time, Pallas kernels for 15%

profile of v11, /device:TPU:0, one launch (start us, length us, event | category | flops | bytes accessed | tf_op | source)
XLA Modules:
  0.0 33.7 jit_solution(4630205961293986547)
XLA Ops:
  0.7 1.0 %fusion.6.leaf = f32[64,128]{1,0:T(8,128)S(1)} fusion(f32[128,64]{0,1:T(8,128)} %param.6, bf16[1,128,128]{2,1,0:T(8,128)(2,1)} %param.7), kind=kOutput, calls=%fused_computation.9 | convolution fusion | flops 2105344 | bytes 98304 | tf_op jit(solution)/shard_map/dot_general | solution.py:20
  1.7 0.3 convolution_bitcast_fusion.terms
  2.0 3.0 %collective-permute-start = (bf16[64,256]{1,0:T(8,128)(2,1)S(1)}, bf16[64,256]{1,0:T(8,128)(2,1)S(1)}, u32[]{:S(2)}, u32[]{:S(2)}) collective-permute-start(bf16[64,256]{1,0:T(8,128)(2,1)S(1)} %fusion.2), channel_id=1, source_target_pairs={{0,1},{1,0},{2,3},{3,2},{4,5},{5,4},{6,7},{7,6},{8,9},{9,8},{10,11... | collective-permute-start | bytes 98312 | tf_op jit(solution)/shard_map/ppermute | solution.py:40
  5.0 0.2 shard_map.77.own_gram
  5.2 0.4 %shard_map.78 = (bf16[512,256]{1,0:T(8,128)(2,1)S(1)}, bf16[320,256]{1,0:T(8,128)(2,1)S(1)}, bf16[2,256,256]{2,1,0:T(8,128)(2,1)S(1)}, bf16[2,256,256]{2,1,0:T(8,128)(2,1)S(1)}) custom-call(bf16[5,256,256]{2,1,0:T(8,128)(2,1)S(1)} %bitcast.28, bf16[4,2,256,256]{3,2,1,0:T(8,128)(2,1)S(1)} %bitcast.39, f32[5,64,256]{2,1,0:T(8,128)S(1)} %convolution_bitcast_fusion.terms), custom_call_target="tpu_custom_call" | custom-call | flops 300000000 | bytes 2031616 | tf_op jit(solution)/shard_map/pallas_call | solution.py:45
  5.7 1.6 %collective-permute-start.6 = (bf16[512,256]{1,0:T(8,128)(2,1)S(1)}, bf16[512,256]{1,0:T(8,128)(2,1)S(1)}, u32[]{:S(2)}, u32[]{:S(2)}) collective-permute-start(bf16[512,256]{1,0:T(8,128)(2,1)S(1)} %get-tuple-element.51.mine), channel_id=1, source_target_pairs={{0,16},{1,17},{2,18},{3,19},{4,20},{5,21},{6,22},{7,23},{8,24},{9,... | collective-permute-start | bytes 786440 | tf_op jit(solution)/shard_map/ppermute | solution.py:40
  7.5 1.8 %collective-permute-start.1 = (bf16[64,256]{1,0:T(8,128)(2,1)S(1)}, bf16[64,256]{1,0:T(8,128)(2,1)S(1)}, u32[]{:S(2)}, u32[]{:S(2)}) collective-permute-start(bf16[64,256]{1,0:T(8,128)(2,1)S(1)} %get-tuple-element.44), channel_id=1, source_target_pairs={{0,10},{1,11},{2,8},{3,9},{4,14},{5,15},{6,12},{7,13},{8,2},{9,3},... | collective-permute-start | bytes 98312 | tf_op jit(solution)/shard_map/ppermute | solution.py:40
  9.4 1.6 %collective-permute-start.9 = (bf16[384,256]{1,0:T(8,128)(2,1)S(1)}, bf16[384,256]{1,0:T(8,128)(2,1)S(1)}, u32[]{:S(2)}, u32[]{:S(2)}) collective-permute-start(bf16[384,256]{1,0:T(8,128)(2,1)S(1)} %shard_map.80.ends), channel_id=1, source_target_pairs={{0,16},{1,17},{2,18},{3,19},{4,20},{5,21},{6,22},{7,23},{8,24},{9,... | collective-permute-start | bytes 589832 | tf_op jit(solution)/shard_map/ppermute | solution.py:40
  11.2 3.0 %collective-permute-start.4 = (bf16[64,256]{1,0:T(8,128)(2,1)S(1)}, bf16[64,256]{1,0:T(8,128)(2,1)S(1)}, u32[]{:S(2)}, u32[]{:S(2)}) collective-permute-start(bf16[64,256]{1,0:T(8,128)(2,1)S(1)} %get-tuple-element.49), channel_id=1, source_target_pairs={{0,12},{1,13},{2,14},{3,15},{4,8},{5,9},{6,10},{7,11},{8,4},{9,5},... | collective-permute-start | bytes 98312 | tf_op jit(solution)/shard_map/ppermute | solution.py:40
  14.2 0.6 %shard_map.82 = (bf16[2,256,256]{2,1,0:T(8,128)(2,1)S(1)}, bf16[2,256,256]{2,1,0:T(8,128)(2,1)S(1)}, bf16[256,256]{1,0:T(8,128)(2,1)S(1)}, bf16[2,2,256,256]{3,2,1,0:T(8,128)(2,1)S(1)}, f32[2,64,256]{2,1,0:T(8,128)S(1)}) custom-call(bf16[5,256,256]{2,1,0:T(8,128)(2,1)S(1)} %bitcast.29, bf16[4,2,256,256]{3,2,1,0:T(8,128)(2,1)S(1)} %bitcast.40, ...), custom_call_target="tpu_custom_call" | custom-call | flops 300000000 | bytes 2359296 | tf_op jit(solution)/shard_map/pallas_call | solution.py:45
  14.8 1.0 %collective-permute-done.4 = bf16[64,256]{1,0:T(8,128)(2,1)S(1)} collective-permute-done((bf16[64,256]{1,0:T(8,128)(2,1)S(1)}, bf16[64,256]{1,0:T(8,128)(2,1)S(1)}, u32[]{:S(2)}, u32[]{:S(2)}) %collective-permute-start.4) | collective-permute-done | bytes 32800 | tf_op jit(solution)/shard_map/ppermute | solution.py:40
  16.0 1.6 %collective-permute-start.7 = (bf16[128,256]{1,0:T(8,128)(2,1)S(1)}, bf16[128,256]{1,0:T(8,128)(2,1)S(1)}, u32[]{:S(2)}, u32[]{:S(2)}) collective-permute-start(bf16[128,256]{1,0:T(8,128)(2,1)S(1)} %shard_map.83.sent), channel_id=1, source_target_pairs={{0,24},{1,25},{2,26},{3,27},{4,28},{5,29},{6,30},{7,31},{8,16},{9,... | collective-permute-start | bytes 196616 | tf_op jit(solution)/shard_map/ppermute | solution.py:40
  17.7 0.6 %shard_map.84.joined = bf16[704,256]{1,0:T(8,128)(2,1)S(1)} custom-call(bf16[512,256]{1,0:T(8,128)(2,1)S(1)} %get-tuple-element.51.mine, bf16[512,256]{1,0:T(8,128)(2,1)S(1)} %collective-permute-done.6.mirror, bf16[384,256]{1,0:T(8,128)(2,1)S(1)} %shard_map.80.ends, bf16[384,256]{1,0:T(8,128)(2,1)S(1)} %collective-permute-done.9.mirror_ends, ...), custom_call_target="tpu_custom_call" | custom-call | flops 300000000 | bytes 1638400 | tf_op jit(solution)/shard_map/pallas_call | solution.py:45
  18.3 0.5 %collective-permute-start.10 = (bf16[704,256]{1,0:T(8,128)(2,1)S(1)}, bf16[704,256]{1,0:T(8,128)(2,1)S(1)}, u32[]{:S(2)}, u32[]{:S(2)}) collective-permute-start(bf16[704,256]{1,0:T(8,128)(2,1)S(1)} %shard_map.84.joined), channel_id=1, source_target_pairs={{0,8},{1,9},{2,10},{3,11},{4,12},{5,13},{6,14},{7,15},{8,0},{9,1},... | collective-permute-start | bytes 1081352 | tf_op jit(solution)/shard_map/ppermute | solution.py:40
  18.8 0.4 %shard_map.85 = f32[64,256]{1,0:T(8,128)S(1)} custom-call(f32[64,256]{1,0:T(8,128)S(1)} %convert_element_type.21.received, bf16[64,256]{1,0:T(8,128)(2,1)S(1)} %collective-permute-done.5.below.delta, bf16[256,256]{1,0:T(8,128)(2,1)S(1)} %get-tuple-element.60.below_turned, bf16[5,256,256]{2,1,0:T(8,128)(2,1)S(1)} %bitcast.31, f32[5,64,256]{2,1,0:T(8,128)S(1)} %bitcast.38), custom_call_target="tpu_custom_call" | custom-call | flops 3600000000 | bytes 1212416 | tf_op jit(solution)/shard_map/pallas_call | solution.py:45
  19.3 0.7 %collective-permute-done.7.across = bf16[128,256]{1,0:T(8,128)(2,1)S(1)} collective-permute-done((bf16[128,256]{1,0:T(8,128)(2,1)S(1)}, bf16[128,256]{1,0:T(8,128)(2,1)S(1)}, u32[]{:S(2)}, u32[]{:S(2)}) %collective-permute-start.7) | collective-permute-done | bytes 65568 | tf_op jit(solution)/shard_map/ppermute | solution.py:40
  20.3 0.2 collective-permute-done.11.solved
  20.5 0.6 %shard_map.86 = (f32[2,64,256]{2,1,0:T(8,128)S(1)}, bf16[2,64,256]{2,1,0:T(8,128)(2,1)S(1)}, bf16[2,256,256]{2,1,0:T(8,128)(2,1)S(1)}, f32[64,256]{1,0:T(8,128)S(1)}) custom-call(bf16[704,256]{1,0:T(8,128)(2,1)S(1)} %shard_map.84.joined, bf16[704,256]{1,0:T(8,128)(2,1)S(1)} %collective-permute-done.10.joined_mate, ...), custom_call_target="tpu_custom_call" | custom-call | flops 2700000000 | bytes 1114112 | tf_op jit(solution)/shard_map/pallas_call | solution.py:45
  21.5 2.4 %collective-permute-start.13 = (bf16[64,256]{1,0:T(8,128)(2,1)S(1)}, bf16[64,256]{1,0:T(8,128)(2,1)S(1)}, u32[]{:S(2)}, u32[]{:S(2)}) collective-permute-start(bf16[64,256]{1,0:T(8,128)(2,1)S(1)} %shard_map.87), channel_id=1, source_target_pairs={{0,12},{1,13},{2,14},{3,15},{4,8},{5,9},{6,10},{7,11},{8,4},{9,5},... | collective-permute-start | bytes 98312 | tf_op jit(solution)/shard_map/ppermute | solution.py:40
  24.1 0.3 shard_map.93
  24.4 0.3 shard_map.91.solved
  24.7 0.4 %collective-permute-start.17 = (f32[64,256]{1,0:T(8,128)S(1)}, f32[64,256]{1,0:T(8,128)S(1)}, u32[]{:S(2)}, u32[]{:S(2)}) collective-permute-start(f32[64,256]{1,0:T(8,128)S(1)} %shard_map.93), channel_id=1, source_target_pairs={{0,8},{1,9},{2,10},{3,11},{4,12},{5,13},{6,14},{7,15},{8,0},{9,1},... | collective-permute-start | bytes 196616 | tf_op jit(solution)/shard_map/ppermute | solution.py:40
  25.3 0.5 %collective-permute-done.13.refs_0_.received = bf16[64,256]{1,0:T(8,128)(2,1)S(1)} collective-permute-done((bf16[64,256]{1,0:T(8,128)(2,1)S(1)}, bf16[64,256]{1,0:T(8,128)(2,1)S(1)}, u32[]{:S(2)}, u32[]{:S(2)}) %collective-permute-start.13) | collective-permute-done | bytes 32800 | tf_op jit(solution)/shard_map/ppermute | solution.py:40
  26.0 1.6 %collective-permute-start.15 = (bf16[64,256]{1,0:T(8,128)(2,1)S(1)}, bf16[64,256]{1,0:T(8,128)(2,1)S(1)}, u32[]{:S(2)}, u32[]{:S(2)}) collective-permute-start(bf16[64,256]{1,0:T(8,128)(2,1)S(1)} %get-tuple-element.72), channel_id=1, source_target_pairs={{0,10},{1,11},{2,8},{3,9},{4,14},{5,15},{6,12},{7,13},{8,2},{9,3},... | collective-permute-start | bytes 98312 | tf_op jit(solution)/shard_map/ppermute | solution.py:40
  27.5 0.2 collective-permute-start.16
  27.8 0.2 convolution_convert_fusion.leaf_products
  28.2 1.2 %collective-permute-done.15.received = bf16[64,256]{1,0:T(8,128)(2,1)S(1)} collective-permute-done((bf16[64,256]{1,0:T(8,128)(2,1)S(1)}, bf16[64,256]{1,0:T(8,128)(2,1)S(1)}, u32[]{:S(2)}, u32[]{:S(2)}) %collective-permute-start.15) | collective-permute-done | bytes 32800 | tf_op jit(solution)/shard_map/ppermute | solution.py:40
  29.6 1.4 %collective-permute-start.19 = (bf16[64,256]{1,0:T(8,128)(2,1)S(1)}, bf16[64,256]{1,0:T(8,128)(2,1)S(1)}, u32[]{:S(2)}, u32[]{:S(2)}) collective-permute-start(bf16[64,256]{1,0:T(8,128)(2,1)S(1)} %shard_map.94), channel_id=1, source_target_pairs={{0,9},{1,8},{2,11},{3,10},{4,13},{5,12},{6,15},{7,14},{8,1},{9,0},... | collective-permute-start | bytes 98312 | tf_op jit(solution)/shard_map/ppermute | solution.py:40
  31.1 0.4 %collective-permute-start.20 = (bf16[64,256]{1,0:T(8,128)(2,1)S(1)}, bf16[64,256]{1,0:T(8,128)(2,1)S(1)}, u32[]{:S(2)}, u32[]{:S(2)}) collective-permute-start(bf16[64,256]{1,0:T(8,128)(2,1)S(1)} %collective-permute-done.15.received), channel_id=1, source_target_pairs={{0,8},{1,9},{2,10},{3,11},{4,12},{5,13},{6,14},{7,15},{8,0},{9,1},... | collective-permute-start | bytes 98312 | tf_op jit(solution)/shard_map/ppermute | solution.py:40
  31.4 0.4 %shard_map.89 = (f32[64,256]{1,0:T(8,128)S(1)}, bf16[64,256]{1,0:T(8,128)(2,1)S(1)}) custom-call(bf16[512,256]{1,0:T(8,128)(2,1)S(1)} %get-tuple-element.51.mine, bf16[512,256]{1,0:T(8,128)(2,1)S(1)} %collective-permute-done.6.mirror, bf16[384,256]{1,0:T(8,128)(2,1)S(1)} %shard_map.80.ends, bf16[384,256]{1,0:T(8,128)(2,1)S(1)} %collective-permute-done.9.mirror_ends, ...), custom_call_target="tpu_custom_call" | custom-call | flops 300000000 | bytes 1048576 | tf_op jit(solution)/shard_map/pallas_call | solution.py:45
  32.0 0.9 %collective-permute-done.19.refs_0_ = bf16[64,256]{1,0:T(8,128)(2,1)S(1)} collective-permute-done((bf16[64,256]{1,0:T(8,128)(2,1)S(1)}, bf16[64,256]{1,0:T(8,128)(2,1)S(1)}, u32[]{:S(2)}, u32[]{:S(2)}) %collective-permute-start.19) | collective-permute-done | bytes 32800 | tf_op jit(solution)/shard_map/ppermute | solution.py:40
  33.0 0.8 %shard_map.95 = (f32[64,128]{1,0:T(8,128)}, f32[5,64,256]{2,1,0:T(8,128)}) custom-call(f32[64,128]{1,0:T(8,128)S(1)} %shard_map.90.part, bf16[5,256,128]{2,1,0:T(8,128)(2,1)S(1)} %convolution_convert_fusion.leaf_products, bf16[64,256]{1,0:T(8,128)(2,1)S(1)} %collective-permute-done.19.refs_0_, bf16[64,256]{1,0:T(8,128)(2,1)S(1)} %collective-permute-done.20.refs_1_, ...), custom_call_target="tpu_custom_call" | custom-call | flops 300000000 | bytes 688128 | tf_op jit(solution)/shard_map/pallas_call | solution.py:45
  (46 shorter events, 2.8 us)
Async XLA Ops:
  0.6 1.1 %copy-start = (bf16[1,5,256,128]{3,2,1,0:T(8,128)(2,1)S(1)}, bf16[1,5,256,128]{3,2,1,0:T(8,128)(2,1)}, u32[]{:S(2)}) copy-start(bf16[1,5,256,128]{3,2,1,0:T(8,128)(2,1)} %param.8) | copy-start | bytes 983044
  0.6 4.3 %copy-start.1 = (bf16[1,5,256,256]{3,2,1,0:T(8,128)(2,1)S(1)}, bf16[1,5,256,256]{3,2,1,0:T(8,128)(2,1)}, u32[]{:S(2)}) copy-start(bf16[1,5,256,256]{3,2,1,0:T(8,128)(2,1)} %param.10) | copy-start | bytes 1966084
  0.7 4.6 %copy-start.3 = (bf16[1,4,1,2,256,256]{5,4,3,2,1,0:T(8,128)(2,1)S(1)}, bf16[1,4,1,2,256,256]{5,4,3,2,1,0:T(8,128)(2,1)}, u32[]{:S(2)}) copy-start(bf16[1,4,1,2,256,256]{5,4,3,2,1,0:T(8,128)(2,1)} %param.11) | copy-start | bytes 3145732
  2.0 5.3 %collective-permute-start = (bf16[64,256]{1,0:T(8,128)(2,1)S(1)}, bf16[64,256]{1,0:T(8,128)(2,1)S(1)}, u32[]{:S(2)}, u32[]{:S(2)}) collective-permute-start(bf16[64,256]{1,0:T(8,128)(2,1)S(1)} %fusion.2), channel_id=1, source_target_pairs={{0,1},{1,0},{2,3},{3,2},{4,5},{5,4},{6,7},{7,6},{8,9},{9,8},{10,11... | collective-permute-start | bytes 98312 | tf_op jit(solution)/shard_map/ppermute | solution.py:40
  5.2 2.0 %copy-start.2 = (f32[1,5,256,64]{2,3,1,0:T(8,128)S(1)}, f32[1,5,256,64]{2,3,1,0:T(8,128)}, u32[]{:S(2)}) copy-start(f32[1,5,256,64]{2,3,1,0:T(8,128)} %param.9) | copy-start | bytes 983044
  5.7 10.1 %collective-permute-start.6 = (bf16[512,256]{1,0:T(8,128)(2,1)S(1)}, bf16[512,256]{1,0:T(8,128)(2,1)S(1)}, u32[]{:S(2)}, u32[]{:S(2)}) collective-permute-start(bf16[512,256]{1,0:T(8,128)(2,1)S(1)} %get-tuple-element.51.mine), channel_id=1, source_target_pairs={{0,16},{1,17},{2,18},{3,19},{4,20},{5,21},{6,22},{7,23},{8,24},{9,... | collective-permute-start | bytes 786440 | tf_op jit(solution)/shard_map/ppermute | solution.py:40
  7.4 3.6 %collective-permute-start.3 = (bf16[320,256]{1,0:T(8,128)(2,1)S(1)}, bf16[320,256]{1,0:T(8,128)(2,1)S(1)}, u32[]{:S(2)}, u32[]{:S(2)}) collective-permute-start(bf16[320,256]{1,0:T(8,128)(2,1)S(1)} %get-tuple-element.47), channel_id=1, source_target_pairs={{0,8},{1,9},{2,10},{3,11},{4,12},{5,13},{6,14},{7,15},{8,0},{9,1},... | collective-permute-start | bytes 491528 | tf_op jit(solution)/shard_map/ppermute | solution.py:40
  7.5 3.5 %collective-permute-start.1 = (bf16[64,256]{1,0:T(8,128)(2,1)S(1)}, bf16[64,256]{1,0:T(8,128)(2,1)S(1)}, u32[]{:S(2)}, u32[]{:S(2)}) collective-permute-start(bf16[64,256]{1,0:T(8,128)(2,1)S(1)} %get-tuple-element.44), channel_id=1, source_target_pairs={{0,10},{1,11},{2,8},{3,9},{4,14},{5,15},{6,12},{7,13},{8,2},{9,3},... | collective-permute-start | bytes 98312 | tf_op jit(solution)/shard_map/ppermute | solution.py:40
  9.4 1.7 %collective-permute-start.2 = (bf16[64,256]{1,0:T(8,128)(2,1)S(1)}, bf16[64,256]{1,0:T(8,128)(2,1)S(1)}, u32[]{:S(2)}, u32[]{:S(2)}) collective-permute-start(bf16[64,256]{1,0:T(8,128)(2,1)S(1)} %get-tuple-element.45), channel_id=1, source_target_pairs={{0,8},{1,9},{2,10},{3,11},{4,12},{5,13},{6,14},{7,15},{8,0},{9,1},... | collective-permute-start | bytes 98312 | tf_op jit(solution)/shard_map/ppermute | solution.py:40
  9.4 8.3 %collective-permute-start.9 = (bf16[384,256]{1,0:T(8,128)(2,1)S(1)}, bf16[384,256]{1,0:T(8,128)(2,1)S(1)}, u32[]{:S(2)}, u32[]{:S(2)}) collective-permute-start(bf16[384,256]{1,0:T(8,128)(2,1)S(1)} %shard_map.80.ends), channel_id=1, source_target_pairs={{0,16},{1,17},{2,18},{3,19},{4,20},{5,21},{6,22},{7,23},{8,24},{9,... | collective-permute-start | bytes 589832 | tf_op jit(solution)/shard_map/ppermute | solution.py:40
  11.2 4.6 %collective-permute-start.4 = (bf16[64,256]{1,0:T(8,128)(2,1)S(1)}, bf16[64,256]{1,0:T(8,128)(2,1)S(1)}, u32[]{:S(2)}, u32[]{:S(2)}) collective-permute-start(bf16[64,256]{1,0:T(8,128)(2,1)S(1)} %get-tuple-element.49), channel_id=1, source_target_pairs={{0,12},{1,13},{2,14},{3,15},{4,8},{5,9},{6,10},{7,11},{8,4},{9,5},... | collective-permute-start | bytes 98312 | tf_op jit(solution)/shard_map/ppermute | solution.py:40
  14.2 1.6 %collective-permute-start.5 = (bf16[64,256]{1,0:T(8,128)(2,1)S(1)}, bf16[64,256]{1,0:T(8,128)(2,1)S(1)}, u32[]{:S(2)}, u32[]{:S(2)}) collective-permute-start(bf16[64,256]{1,0:T(8,128)(2,1)S(1)} %get-tuple-element.50), channel_id=1, source_target_pairs={{0,8},{1,9},{2,10},{3,11},{4,12},{5,13},{6,14},{7,15},{8,0},{9,1},... | collective-permute-start | bytes 98312 | tf_op jit(solution)/shard_map/ppermute | solution.py:40
  16.0 4.1 %collective-permute-start.7 = (bf16[128,256]{1,0:T(8,128)(2,1)S(1)}, bf16[128,256]{1,0:T(8,128)(2,1)S(1)}, u32[]{:S(2)}, u32[]{:S(2)}) collective-permute-start(bf16[128,256]{1,0:T(8,128)(2,1)S(1)} %shard_map.83.sent), channel_id=1, source_target_pairs={{0,24},{1,25},{2,26},{3,27},{4,28},{5,29},{6,30},{7,31},{8,16},{9,... | collective-permute-start | bytes 196616 | tf_op jit(solution)/shard_map/ppermute | solution.py:40
  17.6 2.9 %collective-permute-start.12 = (bf16[2,256,256]{2,1,0:T(8,128)(2,1)S(1)}, bf16[2,256,256]{2,1,0:T(8,128)(2,1)S(1)}, u32[]{:S(2)}, u32[]{:S(2)}) collective-permute-start(bf16[2,256,256]{2,1,0:T(8,128)(2,1)S(1)} %get-tuple-element.63), channel_id=1, source_target_pairs={{0,8},{1,9},{2,10},{3,11},{4,12},{5,13},{6,14},{7,15},{8,0},{9,1},... | collective-permute-start | bytes 786440 | tf_op jit(solution)/shard_map/ppermute | solution.py:40
  18.3 2.2 %collective-permute-start.10 = (bf16[704,256]{1,0:T(8,128)(2,1)S(1)}, bf16[704,256]{1,0:T(8,128)(2,1)S(1)}, u32[]{:S(2)}, u32[]{:S(2)}) collective-permute-start(bf16[704,256]{1,0:T(8,128)(2,1)S(1)} %shard_map.84.joined), channel_id=1, source_target_pairs={{0,8},{1,9},{2,10},{3,11},{4,12},{5,13},{6,14},{7,15},{8,0},{9,1},... | collective-permute-start | bytes 1081352 | tf_op jit(solution)/shard_map/ppermute | solution.py:40
  19.2 1.3 %collective-permute-start.11 = (f32[64,256]{1,0:T(8,128)S(1)}, f32[64,256]{1,0:T(8,128)S(1)}, u32[]{:S(2)}, u32[]{:S(2)}) collective-permute-start(f32[64,256]{1,0:T(8,128)S(1)} %shard_map.85), channel_id=1, source_target_pairs={{0,8},{1,9},{2,10},{3,11},{4,12},{5,13},{6,14},{7,15},{8,0},{9,1},... | collective-permute-start | bytes 196616 | tf_op jit(solution)/shard_map/ppermute | solution.py:40
  20.1 1.3 %collective-permute-start.8 = (bf16[128,256]{1,0:T(8,128)(2,1)S(1)}, bf16[128,256]{1,0:T(8,128)(2,1)S(1)}, u32[]{:S(2)}, u32[]{:S(2)}) collective-permute-start(bf16[128,256]{1,0:T(8,128)(2,1)S(1)} %collective-permute-done.7.across), channel_id=1, source_target_pairs={{0,8},{1,9},{2,10},{3,11},{4,12},{5,13},{6,14},{7,15},{8,0},{9,1},... | collective-permute-start | bytes 196616 | tf_op jit(solution)/shard_map/ppermute | solution.py:40
  21.5 4.3 %collective-permute-start.13 = (bf16[64,256]{1,0:T(8,128)(2,1)S(1)}, bf16[64,256]{1,0:T(8,128)(2,1)S(1)}, u32[]{:S(2)}, u32[]{:S(2)}) collective-permute-start(bf16[64,256]{1,0:T(8,128)(2,1)S(1)} %shard_map.87), channel_id=1, source_target_pairs={{0,12},{1,13},{2,14},{3,15},{4,8},{5,9},{6,10},{7,11},{8,4},{9,5},... | collective-permute-start | bytes 98312 | tf_op jit(solution)/shard_map/ppermute | solution.py:40
  23.9 1.9 %collective-permute-start.14 = (bf16[64,256]{1,0:T(8,128)(2,1)S(1)}, bf16[64,256]{1,0:T(8,128)(2,1)S(1)}, u32[]{:S(2)}, u32[]{:S(2)}) collective-permute-start(bf16[64,256]{1,0:T(8,128)(2,1)S(1)} %shard_map.87), channel_id=1, source_target_pairs={{0,8},{1,9},{2,10},{3,11},{4,12},{5,13},{6,14},{7,15},{8,0},{9,1},... | collective-permute-start | bytes 98312 | tf_op jit(solution)/shard_map/ppermute | solution.py:40
  24.7 3.5 %collective-permute-start.17 = (f32[64,256]{1,0:T(8,128)S(1)}, f32[64,256]{1,0:T(8,128)S(1)}, u32[]{:S(2)}, u32[]{:S(2)}) collective-permute-start(f32[64,256]{1,0:T(8,128)S(1)} %shard_map.93), channel_id=1, source_target_pairs={{0,8},{1,9},{2,10},{3,11},{4,12},{5,13},{6,14},{7,15},{8,0},{9,1},... | collective-permute-start | bytes 196616 | tf_op jit(solution)/shard_map/ppermute | solution.py:40
  25.1 3.1 %collective-permute-start.18 = (bf16[2,256,256]{2,1,0:T(8,128)(2,1)S(1)}, bf16[2,256,256]{2,1,0:T(8,128)(2,1)S(1)}, u32[]{:S(2)}, u32[]{:S(2)}) collective-permute-start(bf16[2,256,256]{2,1,0:T(8,128)(2,1)S(1)} %get-tuple-element.76), channel_id=1, source_target_pairs={{0,8},{1,9},{2,10},{3,11},{4,12},{5,13},{6,14},{7,15},{8,0},{9,1},... | collective-permute-start | bytes 786440 | tf_op jit(solution)/shard_map/ppermute | solution.py:40
  25.8 2.0 %copy-start.4 = (bf16[1,128,128]{2,1,0:T(8,128)(2,1)S(1)}, bf16[1,128,128]{2,1,0:T(8,128)(2,1)}, u32[]{:S(2)}) copy-start(bf16[1,128,128]{2,1,0:T(8,128)(2,1)} %param.7) | copy-start | bytes 98308
  26.0 3.4 %collective-permute-start.15 = (bf16[64,256]{1,0:T(8,128)(2,1)S(1)}, bf16[64,256]{1,0:T(8,128)(2,1)S(1)}, u32[]{:S(2)}, u32[]{:S(2)}) collective-permute-start(bf16[64,256]{1,0:T(8,128)(2,1)S(1)} %get-tuple-element.72), channel_id=1, source_target_pairs={{0,10},{1,11},{2,8},{3,9},{4,14},{5,15},{6,12},{7,13},{8,2},{9,3},... | collective-permute-start | bytes 98312 | tf_op jit(solution)/shard_map/ppermute | solution.py:40
  27.5 1.8 %collective-permute-start.16 = (bf16[64,256]{1,0:T(8,128)(2,1)S(1)}, bf16[64,256]{1,0:T(8,128)(2,1)S(1)}, u32[]{:S(2)}, u32[]{:S(2)}) collective-permute-start(bf16[64,256]{1,0:T(8,128)(2,1)S(1)} %get-tuple-element.72), channel_id=1, source_target_pairs={{0,8},{1,9},{2,10},{3,11},{4,12},{5,13},{6,14},{7,15},{8,0},{9,1},... | collective-permute-start | bytes 98312 | tf_op jit(solution)/shard_map/ppermute | solution.py:40
  29.6 3.4 %collective-permute-start.19 = (bf16[64,256]{1,0:T(8,128)(2,1)S(1)}, bf16[64,256]{1,0:T(8,128)(2,1)S(1)}, u32[]{:S(2)}, u32[]{:S(2)}) collective-permute-start(bf16[64,256]{1,0:T(8,128)(2,1)S(1)} %shard_map.94), channel_id=1, source_target_pairs={{0,9},{1,8},{2,11},{3,10},{4,13},{5,12},{6,15},{7,14},{8,1},{9,0},... | collective-permute-start | bytes 98312 | tf_op jit(solution)/shard_map/ppermute | solution.py:40
  30.9 2.0 %collective-permute-start.21 = (bf16[64,256]{1,0:T(8,128)(2,1)S(1)}, bf16[64,256]{1,0:T(8,128)(2,1)S(1)}, u32[]{:S(2)}, u32[]{:S(2)}) collective-permute-start(bf16[64,256]{1,0:T(8,128)(2,1)S(1)} %shard_map.94), channel_id=1, source_target_pairs={{0,8},{1,9},{2,10},{3,11},{4,12},{5,13},{6,14},{7,15},{8,0},{9,1},... | collective-permute-start | bytes 98312 | tf_op jit(solution)/shard_map/ppermute | solution.py:40
  31.1 1.9 %collective-permute-start.20 = (bf16[64,256]{1,0:T(8,128)(2,1)S(1)}, bf16[64,256]{1,0:T(8,128)(2,1)S(1)}, u32[]{:S(2)}, u32[]{:S(2)}) collective-permute-start(bf16[64,256]{1,0:T(8,128)(2,1)S(1)} %collective-permute-done.15.received), channel_id=1, source_target_pairs={{0,8},{1,9},{2,10},{3,11},{4,12},{5,13},{6,14},{7,15},{8,0},{9,1},... | collective-permute-start | bytes 98312 | tf_op jit(solution)/shard_map/ppermute | solution.py:40
